TPU v7x, 32 devices: a whole 2x2x4 slice. The times are simulated.
32 devices in a mesh: blk: 16 (over z, y, core), rows: 2 (over x).
Axes of the slice: x: 2, y: 2, z: 4, core: 2. Of those that a mesh axis runs over, the one named last changes fastest.
Arguments:
- matrix: bfloat16 [12288, 6144], P('rows', 'blk'), may hold values from -128 to 128
- plan: int32 [32], replicated, may hold values from 0 to 31, as said below
Outputs:
- next_matrix: bfloat16 [12288, 6144], P('rows', 'blk')
- off_ratio: float32 [], replicated
Inputs may be any that keep to these rules, and one draw needn't show every extreme that they name: `plan`: A permutation of the block numbers. Blocks 2 i and 2 i + 1 form pair i; of these two, one moves into a block of pair i + 1 and the other into a block of pair i - 1, counted around the closed cycle of pairs.
All inputs are finite; a program needn't handle non-finite values.
Results may differ from a plain program's by a relative error of at most 0.0027.
The roundings to bfloat16 on the way count: a program that leaves them out, or rounds other values in their place, can miss the bound.
Values may be sent and summed in bfloat16 or wider, within the bound.
No kernel may reach another device: no remote copies, remote signals or barrier semaphores. Data moves between devices by JAX's collectives and lax.ppermute only.
A program may use at most 64 MiB of HBM per device.

v0:
```python
import jax
import jax.numpy as jnp
from jax import lax
from jax.sharding import PartitionSpec as P

ROUNDS = 24


def shifted(value, axis, steps):
    count = lax.axis_size(axis)
    pairs = [(source, (source + steps) % count) for source in range(count)]
    return lax.ppermute(value, axis, pairs)


def advance_cols(values):
    size = values.shape[1]
    return jnp.concatenate(
        [values[:, 0:1], values[:, size - 1 : size], values[:, 1 : size - 1]], axis=1
    )


def advance_rows(values):
    size = values.shape[0]
    return jnp.concatenate([values[0:1], values[size - 1 : size], values[1 : size - 1]], axis=0)


def turn_cols(values, cosine, sine_val):
    half = values.shape[1] // 2
    lead_cols = values[:, :half]
    tail_cols = jnp.flip(values[:, half:], axis=1)
    new_lead = lead_cols * cosine + tail_cols * sine_val
    new_tail = tail_cols * cosine - lead_cols * sine_val
    return jnp.concatenate([new_lead, jnp.flip(new_tail, axis=1)], axis=1)


def turn_rows(values, cosine, sine_val):
    half = values.shape[0] // 2
    lead_rows = values[:half]
    tail_rows = jnp.flip(values[half:], axis=0)
    new_lead = lead_rows * cosine[:, None] + tail_rows * sine_val[:, None]
    new_tail = tail_rows * cosine[:, None] - lead_rows * sine_val[:, None]
    return jnp.concatenate([new_lead, jnp.flip(new_tail, axis=0)], axis=0)


def jacobi(gram_sum):
    size = gram_sum.shape[0]
    half = size // 2

    def rotate_once(turn_index, carry):
        gram_now, basis = carry
        diagonal = jnp.diagonal(gram_now)
        head_diag = diagonal[:half]
        tail_diag = jnp.flip(diagonal[half:])
        coupling = jnp.diagonal(jnp.flip(gram_now[:half, half:], axis=1))
        difference = head_diag - tail_diag
        sign_val = jnp.where(difference >= 0.0, 1.0, -1.0).astype(jnp.float32)
        angle = 0.5 * jnp.arctan2(2.0 * coupling * sign_val, jnp.abs(difference))
        cosine = jnp.cos(angle)
        sine_val = jnp.sin(angle)
        gram_now = turn_cols(gram_now, cosine, sine_val)
        gram_now = turn_rows(gram_now, cosine, sine_val)
        basis = turn_cols(basis, cosine, sine_val)
        gram_now = advance_rows(advance_cols(gram_now))
        basis = advance_cols(basis)
        return (gram_now, basis)

    start = (gram_sum, jnp.eye(size, dtype=jnp.float32))
    basis = lax.fori_loop(0, ROUNDS, rotate_once, start)[1]
    back = ROUNDS % (size - 1)
    return jnp.concatenate([basis[:, 0:1], jnp.roll(basis[:, 1:], -back, axis=1)], axis=1)


def inner_cols(left_side, right_side):
    return lax.dot_general(
        left_side, right_side, (((0,), (0,)), ((), ())), preferred_element_type=jnp.float32
    )


def on_device(matrix, plan):
    cycle_size = lax.axis_size("blk")
    position = lax.axis_index("blk")
    block_width = matrix.shape[1] // 2
    gram_sum = lax.psum(inner_cols(matrix, matrix), "rows")
    diag_sq = jnp.sum(jnp.diagonal(gram_sum) ** 2)
    off_sq = jnp.sum(gram_sum * gram_sum) - diag_sq
    off_total, diag_total = lax.psum((off_sq, diag_sq), "blk")
    off_ratio = jnp.sqrt(off_total / diag_total)
    rotation = jacobi(gram_sum).astype(jnp.bfloat16)
    my_dest = lax.dynamic_slice_in_dim(plan, 2 * position, 2)
    next_dev = (position + 1) % cycle_size
    right_first = my_dest[0] // 2 == next_dev
    rotated = jnp.dot(matrix, rotation, preferred_element_type=jnp.float32).astype(jnp.bfloat16)
    going_right = jnp.where(right_first, rotated[:, :block_width], rotated[:, block_width:])
    going_left = jnp.where(right_first, rotated[:, block_width:], rotated[:, :block_width])
    from_left = shifted(going_right, "blk", 1)
    from_right = shifted(going_left, "blk", -1)
    prev_dev = (position + cycle_size - 1) % cycle_size
    their_dest = lax.dynamic_slice_in_dim(plan, 2 * prev_dev, 2)
    in_slot = jnp.where(their_dest[0] // 2 == position, their_dest[0], their_dest[1]) % 2
    slot_zero = jnp.where(in_slot == 0, from_left, from_right)
    slot_one = jnp.where(in_slot == 0, from_right, from_left)
    return (jnp.concatenate([slot_zero, slot_one], axis=1), off_ratio)


def solution(mesh):
    in_specs = (P("rows", "blk"), P())
    out_specs = (P("rows", "blk"), P())
    return jax.shard_map(
        on_device, mesh=mesh, in_specs=in_specs, out_specs=out_specs, check_vma=False
    )
```

profile of v0, /device:TPU:1, one launch (start us, length us, event | category | flops | bytes accessed | tf_op | source)
XLA Modules:
  0.0 450.6 jit_solution(2094437050335173767)
XLA Ops:
  7.2 7.2 %fusion.21 = f32[384,384]{1,0:T(8,128)} fusion(bf16[6144,384]{1,0:T(8,128)(2,1)} %param.4), kind=kOutput, calls=%fused_computation.53 | convolution fusion | flops 1811939328 | bytes 5308416 | tf_op jit(solution)/shard_map/dot_general | solution.py:74
  14.8 31.9 %all-reduce.3.cloned.1.call-done = f32[384,384]{1,0:T(8,128)} async-done(((f32[384,384]{1,0:T(8,128)}), f32[384,384]{1,0:T(8,128)}) %all-reduce.3.cloned.1.call-update) | async-done | bytes 589840 | tf_op jit(solution)/shard_map/psum | solution.py:83
  46.7 1.1 copy.8
  47.8 298.1 %while.12 = (s32[]{:T(128)}, f32[384,384]{1,0:T(8,128)S(1)}, f32[384,384]{1,0:T(8,128)S(1)}, s32[]{:T(128)}) while((s32[]{:T(128)}, f32[384,384]{1,0:T(8,128)S(1)}, f32[384,384]{1,0:T(8,128)S(1)}, s32[]{:T(128)}) %tuple.52), condition=%wide.region_2.3_spmd, body=%wide.region_1.2_spmd.sunk | while | flops 3469634 | bytes 19504692 | solution.py:68
  47.8 3.4 gather_fusion
  51.5 0.6 reverse.13
  52.3 1.9 gather_fusion.1
  60.2 3.4 gather_fusion
  64.7 1.9 gather_fusion.1
  72.7 3.4 gather_fusion
  77.1 1.9 gather_fusion.1
  85.1 3.4 gather_fusion
  89.6 1.9 gather_fusion.1
  97.5 3.4 gather_fusion
  102.0 1.9 gather_fusion.1
  109.9 3.4 gather_fusion
  113.7 0.6 reverse.13
  114.4 1.9 gather_fusion.1
  122.3 3.4 gather_fusion
  126.8 1.9 gather_fusion.1
  134.8 3.4 gather_fusion
  139.2 1.9 gather_fusion.1
  147.2 3.4 gather_fusion
  151.7 1.9 gather_fusion.1
  159.6 3.4 gather_fusion
  164.1 1.9 gather_fusion.1
  172.0 3.4 gather_fusion
  176.5 1.9 gather_fusion.1
  184.5 3.4 gather_fusion
  188.9 1.9 gather_fusion.1
  196.9 3.4 gather_fusion
  201.4 1.9 gather_fusion.1
  209.3 3.4 gather_fusion
  213.8 1.9 gather_fusion.1
  221.7 3.4 gather_fusion
  226.2 1.9 gather_fusion.1
  234.2 3.4 gather_fusion
  237.9 0.6 reverse.13
  238.6 1.9 gather_fusion.1
  246.6 3.4 gather_fusion
  251.1 1.9 gather_fusion.1
  259.0 3.4 gather_fusion
  263.5 1.9 gather_fusion.1
  271.4 3.4 gather_fusion
  275.9 1.9 gather_fusion.1
  283.8 3.4 gather_fusion
  288.3 1.9 gather_fusion.1
  296.3 3.4 gather_fusion
  300.7 1.9 gather_fusion.1
  308.7 3.4 gather_fusion
  313.2 1.9 gather_fusion.1
  321.1 3.4 gather_fusion
  325.6 1.9 gather_fusion.1
  333.5 3.4 gather_fusion
  338.0 1.9 gather_fusion.1
  346.2 5.2 %fusion.8 = bf16[6144,384]{0,1:T(8,128)(2,1)S(1)} fusion(bf16[6144,384]{1,0:T(8,128)(2,1)} %param.4, bf16[384,24]{1,0:T(8,128)(2,1)S(1)} %slice.117, bf16[384,359]{1,0:T(8,128)(2,1)S(1)} %slice.116, bf16[384,1]{1,0:T(8,128)(2,1)S(1)} %slice.115), kind=kOutput, calls=%fused_computation.32 | convolution fusion | flops 1815183360 | bytes 9732096 | tf_op jit(solution)/shard_map/dot_general | solution.py:92
  351.5 2.5 broadcast_select_fusion.1
  354.0 1.8 collective-permute-start
  360.5 3.4 gather_fusion.2
  364.5 0.7 multiply_reduce_fusion
  366.5 63.6 %all-reduce = (f32[]{:T(128)}, f32[]{:T(128)}) all-reduce(f32[]{:T(128)S(6)} %sub.28, f32[]{:T(128)} %multiply_reduce_fusion.1), channel_id=1, replica_groups=mesh['blk'=16,'rows'=2] {'blk'}, use_global_device_ids=true, to_apply=%region_5.6 | all-reduce | flops 2 | bytes 16 | tf_op jit(solution)/shard_map/psum | solution.py:86
  431.4 2.0 broadcast_select_fusion.3
  433.4 2.6 pad_maximum_fusion.3
  436.1 6.6 %copy.5 = bf16[6144,384]{1,0:T(8,128)(2,1)} copy(bf16[6144,384]{0,1:T(8,128)(2,1)} %pad_maximum_fusion.3) | data formatting | bytes 9437184
  (735 shorter events, 165.1 us)
Async XLA Ops:
  7.2 7.3 %copy-start.1 = (s32[32]{0:T(128)S(1)}, s32[32]{0:T(128)}, u32[]{:S(2)}) copy-start(s32[32]{0:T(128)} %param.5) | copy-start | bytes 388
  7.2 39.5 %all-reduce.3.cloned.1.call-start = ((), (), s32[]{:S(2)}) async-start(), calls=%async_computation | async-start | bytes 1179648 | tf_op jit(solution)/shard_map/psum | solution.py:83
  351.4 9.0 %copy-start = (f32[384,384]{1,0:T(8,128)S(1)}, f32[384,384]{1,0:T(8,128)}, u32[]{:S(2)}) copy-start(f32[384,384]{1,0:T(8,128)} %all-reduce.3.cloned.1.call-done) | copy-start | bytes 1769476
  354.0 77.5 %collective-permute-start = (bf16[6144,192]{0,1:T(8,128)(2,1)}, bf16[6144,192]{0,1:T(8,128)(2,1)S(1)}, u32[]{:S(2)}, u32[]{:S(2)}) collective-permute-start(bf16[6144,192]{0,1:T(8,128)(2,1)} %get-tuple-element.52), channel_id=1, source_target_pairs={{0,2},{2,4},{4,6},{6,8},{8,10},{10,12},{12,14},{14,16},{16,18},{18... | collective-permute-start | bytes 7077896 | tf_op jit(solution)/shard_map/ppermute | solution.py:12
  355.7 75.7 %collective-permute-start.1 = (bf16[6144,192]{0,1:T(8,128)(2,1)}, bf16[6144,192]{0,1:T(8,128)(2,1)}, u32[]{:S(2)}, u32[]{:S(2)}) collective-permute-start(bf16[6144,192]{0,1:T(8,128)(2,1)} %get-tuple-element.53), channel_id=1, source_target_pairs={{0,30},{2,0},{4,2},{6,4},{8,6},{10,8},{12,10},{14,12},{16,14},{18,... | collective-permute-start | bytes 7077896 | tf_op jit(solution)/shard_map/ppermute | solution.py:12
Sparse Core Ops, SparseCore 0:
  14.6 32.0 all-reduce.2
where the time goes:
time: 453 us; the launch traced here: 451 us
  local copies, waits for them, and re-layouts  263 us (58%)
  blocking collectives  63.6 us (14%)
  other arithmetic  51.1 us (11%)
  waiting for transfers between devices  31.9 us (7%)
  between operations  22.1 us (5%)
  matrix products  12.4 us (3%)
    gather x24, local copies, waits for them, and re-layouts, rotate_once(): diagonal = jnp.diagonal(gram_now)  82.5 us
    while x216, local copies, waits for them, and re-layouts  80.5 us
    psum x1, blocking collectives, on_device(): off_total, diag_total = lax.psum((off_sq, diag_sq), 'blk')  63.6 us
    gather x24, local copies, waits for them, and re-layouts, rotate_once(): coupling = jnp.diagonal(jnp.flip(gram_now[:half, half:], axis=1))  45.9 us
    psum x1, waiting for transfers between devices, on_device(): gram_sum = lax.psum(inner_cols(matrix, matrix), 'rows')  31.9 us
    concatenate x48, other arithmetic, advance_cols(): jnp.concatenate([values[:, 0:1], values[:, size - 1:size], values[:, 1:si...  18.1 us
    rev x24, local copies, waits for them, and re-layouts, turn_rows(): tail_rows = jnp.flip(values[half:], axis=0)  13.6 us
    rev x24, local copies, waits for them, and re-layouts, turn_rows(): return jnp.concatenate([new_lead, jnp.flip(new_tail, axis=0)], axis=0)  13.6 us
  transfers between devices with their start and end apart: 3, of which 1 were waited for; matrix products, arithmetic and copies ran while one was open for 1% of the time, Pallas kernels for 0%

commit v1 on v0

v1 whole, which is shorter than its diff:
```python
import jax
import jax.numpy as jnp
from jax import lax
from jax.experimental import pallas as pl
from jax.experimental.pallas import tpu as pltpu
from jax.sharding import PartitionSpec as P

ROUNDS = 24
LANES = 128
SUBS = 8


def split_three(values):
    high = values.astype(jnp.bfloat16)
    rest = values - high.astype(jnp.float32)
    middle = rest.astype(jnp.bfloat16)
    low = (rest - middle.astype(jnp.float32)).astype(jnp.bfloat16)
    return high, middle, low


def dot32(left, right, dims=((1,), (0,))):
    return lax.dot_general(left, right, (dims, ((), ())), preferred_element_type=jnp.float32)


def slot_of_row(rows, groups, half):
    part = rows // half
    inside = rows % half
    index = (inside % SUBS) * groups + inside // SUBS
    return jnp.where(part == 0, index, 2 * half - 1 - index)


def slot_of_lane(lanes, half):
    part = lanes // (2 * LANES)
    odd = (lanes // LANES) % 2
    inside = lanes % LANES
    index = 2 * inside + odd
    slot = jnp.where(part == 0, index, 2 * half - 1 - index)
    return jnp.where(inside < half // 2, slot, -1)


def onehot(left, right):
    return jnp.where(left == right, 1.0, 0.0).astype(jnp.bfloat16)


def angles(head, tail, coupling):
    difference = head - tail
    sign_val = jnp.where(difference >= 0.0, 1.0, -1.0)
    across = 2.0 * coupling * sign_val
    along = jnp.abs(difference)
    scale = jnp.maximum(along, jnp.abs(across))
    empty = scale == 0.0
    inverse = 1.0 / jnp.where(empty, 1.0, scale)
    along = jnp.where(empty, 1.0, along * inverse)
    across = across * inverse
    square = along * along + across * across
    root = lax.rsqrt(square)
    root = root * (1.5 - 0.5 * square * root * root)
    cos_sq = 0.5 + 0.5 * (along * root)
    half_root = lax.rsqrt(cos_sq)
    half_root = half_root * (1.5 - 0.5 * cos_sq * half_root * half_root)
    return cos_sq * half_root, 0.5 * (across * root) * half_root


def jacobi_kernel(gram_ref, out_ref, gram_buf, basis_buf):
    size = gram_ref.shape[0]
    half = size // 2
    groups = half // SUBS
    last = groups - 1
    edge = half // 2 - 1
    lane_row = lax.broadcasted_iota(jnp.int32, (1, LANES), 1)
    lane = lax.broadcasted_iota(jnp.int32, (SUBS, LANES), 1)
    sub = lax.broadcasted_iota(jnp.int32, (SUBS, LANES), 0)
    spot = lane - sub * (groups // 2)

    def on_diag(group):
        return spot == group // 2

    row_slot = slot_of_row(lax.broadcasted_iota(jnp.int32, (size, 1), 0), groups, half)
    take_rows = onehot(row_slot, lax.broadcasted_iota(jnp.int32, (size, size), 1))
    lane_slot = slot_of_lane(lax.broadcasted_iota(jnp.int32, (1, 4 * LANES), 1), half)
    take_cols = onehot(lax.broadcasted_iota(jnp.int32, (size, 4 * LANES), 0), lane_slot)
    arranged = jnp.zeros((size, 4 * LANES), jnp.float32)
    for piece in split_three(gram_ref[...]):
        moved = dot32(take_rows, piece).astype(jnp.bfloat16)
        arranged = arranged + dot32(moved, take_cols)
    gram_buf[0] = arranged.reshape(2, groups, SUBS, 4 * LANES)
    basis_buf[0] = take_rows.astype(jnp.float32).reshape(2, groups, SUBS, size)

    zero = jnp.zeros((SUBS, LANES), jnp.float32)
    heads, tails, couplings = [zero, zero], [zero, zero], [zero, zero]
    for group in range(groups):
        odd = group % 2
        mask = on_diag(group)
        lead_cols = slice(odd * LANES, (odd + 1) * LANES)
        tail_cols = slice((2 + odd) * LANES, (3 + odd) * LANES)
        heads[odd] += jnp.where(mask, gram_buf[0, 0, group, :, lead_cols], 0.0)
        tails[odd] += jnp.where(mask, gram_buf[0, 1, group, :, tail_cols], 0.0)
        couplings[odd] += jnp.where(mask, gram_buf[0, 0, group, :, tail_cols], 0.0)

    def flat(values):
        return jnp.sum(values, axis=0, keepdims=True)

    def shift_lanes(lead, tail):
        lead0, lead1 = lead[:, :LANES], lead[:, LANES:]
        tail0, tail1 = tail[:, :LANES], tail[:, LANES:]
        here = lane[: lead.shape[0]]
        new_lead1 = jnp.where(here == 0, tail0, lead0)
        new_lead0 = jnp.where(here == 0, lead0, pltpu.roll(lead1, 1, 1))
        new_tail1 = jnp.where(here == edge, lead1, pltpu.roll(tail0, LANES - 1, 1))
        return new_lead0, new_lead1, tail1, new_tail1

    def turn(turn_index, carry):
        heads, tails, couplings = carry
        source = turn_index % 2
        target = 1 - source
        cosines, sines, new_heads, new_tails = [], [], [], []
        for odd in range(2):
            head, tail = heads[odd], tails[odd]
            coupling = flat(couplings[odd])
            cosine, sine_val = angles(head, tail, coupling)
            cosines.append(cosine)
            sines.append(sine_val)
            first = cosine * head + sine_val * coupling
            second = cosine * coupling + sine_val * tail
            new_heads.append(cosine * first + sine_val * second)
            first = cosine * coupling - sine_val * head
            second = cosine * tail - sine_val * coupling
            new_tails.append(cosine * second - sine_val * first)
        shifted_diag = shift_lanes(
            jnp.concatenate([jnp.broadcast_to(x, (SUBS, LANES)) for x in new_heads], axis=1),
            jnp.concatenate([jnp.broadcast_to(x, (SUBS, LANES)) for x in new_tails], axis=1),
        )
        shifted_diag = [x[:1] for x in shifted_diag]
        cos_lanes = [jnp.broadcast_to(x, (SUBS, LANES)) for x in cosines]
        sin_lanes = [jnp.broadcast_to(x, (SUBS, LANES)) for x in sines]
        cos_wide = jnp.concatenate(cos_lanes, axis=1)
        sin_wide = jnp.concatenate(sin_lanes, axis=1)

        def work(group):
            mask = on_diag(group)
            odd = group % 2
            cos_row = jnp.sum(jnp.where(mask, cos_lanes[odd], 0.0), axis=1, keepdims=True)
            sin_row = jnp.sum(jnp.where(mask, sin_lanes[odd], 0.0), axis=1, keepdims=True)

            def turned(part):
                values = gram_buf[source, part, group]
                lead, tail = values[:, : 2 * LANES], values[:, 2 * LANES :]
                return cos_wide * lead + sin_wide * tail, cos_wide * tail - sin_wide * lead

            top_lead, top_tail = turned(0)
            low_lead, low_tail = turned(1)
            top = shift_lanes(
                cos_row * top_lead + sin_row * low_lead, cos_row * top_tail + sin_row * low_tail
            )
            low = shift_lanes(
                cos_row * low_lead - sin_row * top_lead, cos_row * low_tail - sin_row * top_tail
            )
            lead = basis_buf[source, 0, group]
            tail = basis_buf[source, 1, group]
            base_top = cos_row * lead + sin_row * tail
            base_low = cos_row * tail - sin_row * lead
            return (
                list(top) + [base_top[:, i : i + LANES] for i in range(0, size, LANES)],
                list(low) + [base_low[:, i : i + LANES] for i in range(0, size, LANES)],
            )

        sums = [zero, zero]

        def store(part, group, values):
            for index, value in enumerate(values[:4]):
                gram_buf[target, part, group, :, index * LANES : (index + 1) * LANES] = value
            for index, value in enumerate(values[4:]):
                basis_buf[target, part, group, :, index * LANES : (index + 1) * LANES] = value
            if part == 0:
                odd = group % 2
                sums[odd] += jnp.where(on_diag(group), values[2 + odd], 0.0)

        first_top, first_low = work(0)
        last_top, last_low = work(last)
        store(0, 1, [jnp.where(sub == 0, y, x) for x, y in zip(first_top, first_low)])
        store(0, 0, [jnp.where(sub == 0, x, pltpu.roll(y, 1, 0)) for x, y in zip(first_top, last_top)])
        store(1, last, [
            jnp.where(sub == SUBS - 1, y, pltpu.roll(x, SUBS - 1, 0))
            for x, y in zip(first_low, last_top)
        ])
        store(1, last - 1, last_low)
        for group in range(1, last):
            top, low = work(group)
            store(0, group + 1, top)
            store(1, group - 1, low)
        return (
            (shifted_diag[0], shifted_diag[1]), (shifted_diag[2], shifted_diag[3]), tuple(sums)
        )

    start = (
        tuple(flat(x) for x in heads), tuple(flat(x) for x in tails), tuple(couplings)
    )
    lax.fori_loop(0, ROUNDS, turn, start)

    held = jnp.where(row_slot == 0, 0, 1 + (row_slot + (size - 2 - ROUNDS % (size - 1))) % (size - 1))
    place = onehot(held, lax.broadcasted_iota(jnp.int32, (size, size), 1))
    basis = basis_buf[ROUNDS % 2].reshape(size, size).astype(jnp.bfloat16)
    out_ref[...] = dot32(basis, place, ((0,), (0,))).astype(jnp.bfloat16)


def jacobi(gram_sum):
    size = gram_sum.shape[0]
    groups = size // 2 // SUBS
    return pl.pallas_call(
        jacobi_kernel,
        out_shape=jax.ShapeDtypeStruct((size, size), jnp.bfloat16),
        in_specs=[pl.BlockSpec(memory_space=pltpu.VMEM)],
        out_specs=pl.BlockSpec(memory_space=pltpu.VMEM),
        scratch_shapes=[
            pltpu.VMEM((2, 2, groups, SUBS, 4 * LANES), jnp.float32),
            pltpu.VMEM((2, 2, groups, SUBS, size), jnp.float32),
        ],
        compiler_params=pltpu.CompilerParams(vmem_limit_bytes=32 * 1024 * 1024),
        name="jacobi_turns",
    )(gram_sum)


def shifted(value, axis, steps):
    count = lax.axis_size(axis)
    pairs = [(source, (source + steps) % count) for source in range(count)]
    return lax.ppermute(value, axis, pairs)


def inner_cols(left_side, right_side):
    return lax.dot_general(
        left_side, right_side, (((0,), (0,)), ((), ())), preferred_element_type=jnp.float32
    )


def on_device(matrix, plan):
    cycle_size = lax.axis_size("blk")
    position = lax.axis_index("blk")
    block_width = matrix.shape[1] // 2
    gram_sum = lax.psum(inner_cols(matrix, matrix), "rows")
    diag_sq = jnp.sum(jnp.diagonal(gram_sum) ** 2)
    off_sq = jnp.sum(gram_sum * gram_sum) - diag_sq
    off_total, diag_total = lax.psum((off_sq, diag_sq), "blk")
    off_ratio = jnp.sqrt(off_total / diag_total)
    rotation = jacobi(gram_sum)
    my_dest = lax.dynamic_slice_in_dim(plan, 2 * position, 2)
    next_dev = (position + 1) % cycle_size
    right_first = my_dest[0] // 2 == next_dev
    rotated = jnp.dot(matrix, rotation, preferred_element_type=jnp.float32).astype(jnp.bfloat16)
    going_right = jnp.where(right_first, rotated[:, :block_width], rotated[:, block_width:])
    going_left = jnp.where(right_first, rotated[:, block_width:], rotated[:, :block_width])
    from_left = shifted(going_right, "blk", 1)
    from_right = shifted(going_left, "blk", -1)
    prev_dev = (position + cycle_size - 1) % cycle_size
    their_dest = lax.dynamic_slice_in_dim(plan, 2 * prev_dev, 2)
    in_slot = jnp.where(their_dest[0] // 2 == position, their_dest[0], their_dest[1]) % 2
    slot_zero = jnp.where(in_slot == 0, from_left, from_right)
    slot_one = jnp.where(in_slot == 0, from_right, from_left)
    return (jnp.concatenate([slot_zero, slot_one], axis=1), off_ratio)


def solution(mesh):
    in_specs = (P("rows", "blk"), P())
    out_specs = (P("rows", "blk"), P())
    return jax.shard_map(
        on_device, mesh=mesh, in_specs=in_specs, out_specs=out_specs, check_vma=False
    )
```

time: 453 us -> 213 us (0.47)
  local copies, waits for them, and re-layouts: 263 us -> 11.8 us
  Pallas kernels: 0 us -> 58.1 us
  other arithmetic: 51.1 us -> 8.48 us
    gather x48 -> x0, local copies, waits for them, and re-layouts: 128 us -> none  [the longest x24 82.5 us: rotate_once(): diagonal = jnp.diagonal(gram_now)]
    while x216 -> x0, local copies, waits for them, and re-layouts: 80.5 us -> none
    pallas_call x0 -> x1, Pallas kernels: none -> 58.1 us  [jacobi(): pl.pallas_call(jacobi_kernel, out_shape=jax.ShapeDtypeStruct((size, size)...]
    rev x48 -> x0, local copies, waits for them, and re-layouts: 27.2 us -> none  [the longest x24 13.6 us: turn_rows(): tail_rows = jnp.flip(values[half:], axis=0)]
    concatenate x144 -> x0, other arithmetic: 24.4 us -> none  [the longest x48 18.1 us: advance_cols(): jnp.concatenate([values[:, 0:1], values[:, size - 1:size], values[:, 1:si...]
    slice x195 -> x0, local copies, waits for them, and re-layouts: 14.5 us -> none  [the longest x48 8.02 us: turn_cols(): tail_cols = jnp.flip(values[:, half:], axis=1)]
    add x48 -> x0, other arithmetic: 12.5 us -> none  [the longest x24 6.87 us: turn_cols(): new_lead = lead_cols * cosine + tail_cols * sine_val]
  transfers between devices with their start and end apart: 3 -> 3, of which waited for: 1 -> 1; matrix products, arithmetic and copies ran while one was open for 1% -> 3% of each run, Pallas kernels for 0% -> 0%
where the time goes in v1:
time: 213 us; the launch traced here: 210 us
  blocking collectives  64.1 us (30%)
  Pallas kernels  58.1 us (27%)
  waiting for transfers between devices  32 us (15%)
  between operations  21.6 us (10%)
  matrix products  12.2 us (6%)
  local copies, waits for them, and re-layouts  11.8 us (6%)
  other arithmetic  8.48 us (4%)
    psum x1, blocking collectives, on_device(): off_total, diag_total = lax.psum((off_sq, diag_sq), 'blk')  64.1 us
    pallas_call x1, Pallas kernels, jacobi(): pl.pallas_call(jacobi_kernel, out_shape=jax.ShapeDtypeStruct((size, size)...  58.1 us
    psum x1, waiting for transfers between devices, on_device(): gram_sum = lax.psum(inner_cols(matrix, matrix), 'rows')  32 us
    unnamed x7, local copies, waits for them, and re-layouts  7.68 us
    dot_general x1, matrix products, inner_cols(): lax.dot_general(left_side, right_side, (((0,), (0,)), ((), ())), preferre...  7.21 us
    dot_general x1, matrix products, on_device(): jnp.dot(matrix, rotation, preferred_element_type=jnp.float32)  5 us
  transfers between devices with their start and end apart: 3, of which 1 were waited for; matrix products, arithmetic and copies ran while one was open for 3% of the time, Pallas kernels for 0%

profile of v1, /device:TPU:1, one launch (start us, length us, event | category | flops | bytes accessed | tf_op | source)
XLA Modules:
  0.0 210.0 jit_solution(1621118312241238458)
XLA Ops:
  7.2 0.0 copy-start.2
  7.2 0.0 all-reduce.3.cloned.1.call-start
  7.2 7.2 %fusion.3 = f32[384,384]{1,0:T(8,128)} fusion(bf16[6144,384]{1,0:T(8,128)(2,1)} %param.2), kind=kOutput, calls=%fused_computation.13 | convolution fusion | flops 1811939328 | bytes 5308416 | tf_op jit(solution)/shard_map/dot_general | solution.py:230
  14.4 0.0 all-reduce.3.cloned.1.call-update
  14.5 0.0 copy-done.2
  14.5 0.1 fusion.2
  14.7 32.0 %all-reduce.3.cloned.1.call-done.gram_ref = f32[384,384]{1,0:T(8,128)} async-done(((f32[384,384]{1,0:T(8,128)}), f32[384,384]{1,0:T(8,128)}) %all-reduce.3.cloned.1.call-update) | async-done | bytes 589840 | tf_op jit(solution)/shard_map/psum | solution.py:239
  46.7 0.0 copy-start
  46.7 1.1 copy-done
  47.8 58.1 %jacobi_turns.1 = bf16[384,384]{1,0:T(8,128)(2,1)S(1)} custom-call(f32[384,384]{1,0:T(8,128)S(1)} %copy-done), custom_call_target="tpu_custom_call" | custom-call | tf_op jit(solution)/shard_map/jacobi_turns/pallas_call | solution.py:209
  105.8 5.0 %fusion = bf16[6144,384]{0,1:T(8,128)(2,1)S(1)} fusion(bf16[384,384]{1,0:T(8,128)(2,1)S(1)} %jacobi_turns.1, bf16[6144,384]{1,0:T(8,128)(2,1)} %param.2), kind=kOutput, calls=%fused_computation.2 | convolution fusion | flops 1814298624 | bytes 9732096 | tf_op jit(solution)/shard_map/dot_general | solution.py:248
  110.8 0.0 copy-start.1
  110.9 2.5 %broadcast_select_fusion.1 = (bf16[6144,192]{0,1:T(8,128)(2,1)}, bf16[6144,192]{0,1:T(8,128)(2,1)}) fusion(pred[]{:T(512)S(6)} %eq.16, bf16[6144,384]{0,1:T(8,128)(2,1)S(1)} %fusion), kind=kLoop, calls=%fused_computation.5 | loop fusion | flops 2359296 | bytes 9437185 | tf_op jit(solution)/shard_map/jit(_where)/select_n | solution.py:249
  113.4 1.8 collective-permute-start
  115.1 0.0 collective-permute-start.1
  115.1 0.6 fusion.1
  119.4 0.0 copy-done.1
  119.4 3.4 %gather_fusion = f32[384]{0:T(512)S(1)} fusion(f32[384,384]{1,0:T(8,128)S(1)} %copy-done.1, s32[384]{0:T(512)S(1)} %or_reduce_fusion), kind=kCustom, calls=%fused_computation | custom fusion | bytes 6144 | tf_op jit(solution)/shard_map/jit(diagonal)/cond/branch_0_fun/gather | solution.py:240
  122.9 0.6 multiply_reduce_fusion.1
  123.5 0.7 multiply_reduce_fusion
  125.4 64.1 %all-reduce = (f32[]{:T(128)}, f32[]{:T(128)}) all-reduce(f32[]{:T(128)S(6)} %sub.16, f32[]{:T(128)} %multiply_reduce_fusion.1), channel_id=1, replica_groups=mesh['blk'=16,'rows'=2] {'blk'}, use_global_device_ids=true, to_apply=%region_3.4 | all-reduce | flops 2 | bytes 16 | tf_op jit(solution)/shard_map/psum | solution.py:242
  190.8 0.0 collective-permute-done
  190.8 0.0 collective-permute-done.1
  190.8 2.0 broadcast_select_fusion.3
  192.8 2.7 %pad_maximum_fusion = bf16[6144,384]{0,1:T(8,128)(2,1)} fusion(bf16[6144,192]{0,1:T(8,128)(2,1)S(1)} %get-tuple-element.9, bf16[6144,192]{0,1:T(8,128)(2,1)S(1)} %get-tuple-element.8), kind=kLoop, calls=%fused_computation.3 | loop fusion | flops 9437184 | bytes 9437184 | tf_op jit(solution)/shard_map/concatenate | solution.py:258
  195.5 6.6 %copy.5 = bf16[6144,384]{1,0:T(8,128)(2,1)} copy(bf16[6144,384]{0,1:T(8,128)(2,1)} %pad_maximum_fusion) | data formatting | bytes 9437184
  (1 shorter events, 0.0 us)
Async XLA Ops:
  7.2 7.3 %copy-start.2 = (s32[32]{0:T(128)S(1)}, s32[32]{0:T(128)}, u32[]{:S(2)}) copy-start(s32[32]{0:T(128)} %param.3) | copy-start | bytes 388
  7.2 39.5 %all-reduce.3.cloned.1.call-start = ((), (), s32[]{:S(2)}) async-start(), calls=%async_computation | async-start | bytes 1179648 | tf_op jit(solution)/shard_map/psum | solution.py:239
  46.7 1.1 copy-start
  110.8 8.6 %copy-start.1 = (f32[384,384]{1,0:T(8,128)S(1)}, f32[384,384]{1,0:T(8,128)}, u32[]{:S(2)}) copy-start(f32[384,384]{1,0:T(8,128)} %all-reduce.3.cloned.1.call-done.gram_ref) | copy-start | bytes 1769476
  113.4 77.5 %collective-permute-start = (bf16[6144,192]{0,1:T(8,128)(2,1)}, bf16[6144,192]{0,1:T(8,128)(2,1)S(1)}, u32[]{:S(2)}, u32[]{:S(2)}) collective-permute-start(bf16[6144,192]{0,1:T(8,128)(2,1)} %get-tuple-element.10), channel_id=1, source_target_pairs={{0,2},{2,4},{4,6},{6,8},{8,10},{10,12},{12,14},{14,16},{16,18},{18... | collective-permute-start | bytes 7077896 | tf_op jit(solution)/shard_map/ppermute | solution.py:226
  115.1 75.7 %collective-permute-start.1 = (bf16[6144,192]{0,1:T(8,128)(2,1)}, bf16[6144,192]{0,1:T(8,128)(2,1)}, u32[]{:S(2)}, u32[]{:S(2)}) collective-permute-start(bf16[6144,192]{0,1:T(8,128)(2,1)} %get-tuple-element.11), channel_id=1, source_target_pairs={{0,30},{2,0},{4,2},{6,4},{8,6},{10,8},{12,10},{14,12},{16,14},{18,... | collective-permute-start | bytes 7077896 | tf_op jit(solution)/shard_map/ppermute | solution.py:226
Sparse Core Ops, SparseCore 0:
  14.6 32.0 all-reduce.2

commit v2 on v1

--- a/solution.py
+++ b/solution.py
@@ -61,7 +61,7 @@
     return cos_sq * half_root, 0.5 * (across * root) * half_root
 
 
-def jacobi_kernel(gram_ref, out_ref, gram_buf, basis_buf):
+def jacobi_kernel(gram_ref, out_ref, gram_a, gram_b, basis_a, basis_b, cos_buf, sin_buf):
     size = gram_ref.shape[0]
     half = size // 2
     groups = half // SUBS
@@ -83,8 +83,8 @@
     for piece in split_three(gram_ref[...]):
         moved = dot32(take_rows, piece).astype(jnp.bfloat16)
         arranged = arranged + dot32(moved, take_cols)
-    gram_buf[0] = arranged.reshape(2, groups, SUBS, 4 * LANES)
-    basis_buf[0] = take_rows.astype(jnp.float32).reshape(2, groups, SUBS, size)
+    gram_a[...] = arranged.reshape(2, groups, SUBS, 4 * LANES)
+    basis_a[...] = take_rows.astype(jnp.float32).reshape(2, groups, SUBS, size)
 
     zero = jnp.zeros((SUBS, LANES), jnp.float32)
     heads, tails, couplings = [zero, zero], [zero, zero], [zero, zero]
@@ -93,9 +93,9 @@
         mask = on_diag(group)
         lead_cols = slice(odd * LANES, (odd + 1) * LANES)
         tail_cols = slice((2 + odd) * LANES, (3 + odd) * LANES)
-        heads[odd] += jnp.where(mask, gram_buf[0, 0, group, :, lead_cols], 0.0)
-        tails[odd] += jnp.where(mask, gram_buf[0, 1, group, :, tail_cols], 0.0)
-        couplings[odd] += jnp.where(mask, gram_buf[0, 0, group, :, tail_cols], 0.0)
+        heads[odd] += jnp.where(mask, gram_a[0, group, :, lead_cols], 0.0)
+        tails[odd] += jnp.where(mask, gram_a[1, group, :, tail_cols], 0.0)
+        couplings[odd] += jnp.where(mask, gram_a[0, group, :, tail_cols], 0.0)
 
     def flat(values):
         return jnp.sum(values, axis=0, keepdims=True)
@@ -109,10 +109,8 @@
         new_tail1 = jnp.where(here == edge, lead1, pltpu.roll(tail0, LANES - 1, 1))
         return new_lead0, new_lead1, tail1, new_tail1
 
-    def turn(turn_index, carry):
+    def turn(gram_from, gram_to, basis_from, basis_to, carry):
         heads, tails, couplings = carry
-        source = turn_index % 2
-        target = 1 - source
         cosines, sines, new_heads, new_tails = [], [], [], []
         for odd in range(2):
             head, tail = heads[odd], tails[odd]
@@ -136,14 +134,21 @@
         cos_wide = jnp.concatenate(cos_lanes, axis=1)
         sin_wide = jnp.concatenate(sin_lanes, axis=1)
 
-        def work(group):
+        for group in range(groups):
             mask = on_diag(group)
             odd = group % 2
-            cos_row = jnp.sum(jnp.where(mask, cos_lanes[odd], 0.0), axis=1, keepdims=True)
-            sin_row = jnp.sum(jnp.where(mask, sin_lanes[odd], 0.0), axis=1, keepdims=True)
+            for buf, lanes in ((cos_buf, cos_lanes[odd]), (sin_buf, sin_lanes[odd])):
+                picked = jnp.sum(jnp.where(mask, lanes, 0.0), axis=1, keepdims=True)
+                buf[group] = jnp.broadcast_to(picked, (SUBS, LANES))
+
+        def work(group):
+            cos_row = jnp.concatenate([cos_buf[group]] * 2, axis=1)
+            sin_row = jnp.concatenate([sin_buf[group]] * 2, axis=1)
+            cos_base = jnp.concatenate([cos_buf[group]] * (size // LANES), axis=1)
+            sin_base = jnp.concatenate([sin_buf[group]] * (size // LANES), axis=1)
 
             def turned(part):
-                values = gram_buf[source, part, group]
+                values = gram_from[part, group]
                 lead, tail = values[:, : 2 * LANES], values[:, 2 * LANES :]
                 return cos_wide * lead + sin_wide * tail, cos_wide * tail - sin_wide * lead
 
@@ -155,10 +160,10 @@
             low = shift_lanes(
                 cos_row * low_lead - sin_row * top_lead, cos_row * low_tail - sin_row * top_tail
             )
-            lead = basis_buf[source, 0, group]
-            tail = basis_buf[source, 1, group]
-            base_top = cos_row * lead + sin_row * tail
-            base_low = cos_row * tail - sin_row * lead
+            lead = basis_from[0, group]
+            tail = basis_from[1, group]
+            base_top = cos_base * lead + sin_base * tail
+            base_low = cos_base * tail - sin_base * lead
             return (
                 list(top) + [base_top[:, i : i + LANES] for i in range(0, size, LANES)],
                 list(low) + [base_low[:, i : i + LANES] for i in range(0, size, LANES)],
@@ -168,9 +173,9 @@
 
         def store(part, group, values):
             for index, value in enumerate(values[:4]):
-                gram_buf[target, part, group, :, index * LANES : (index + 1) * LANES] = value
+                gram_to[part, group, :, index * LANES : (index + 1) * LANES] = value
             for index, value in enumerate(values[4:]):
-                basis_buf[target, part, group, :, index * LANES : (index + 1) * LANES] = value
+                basis_to[part, group, :, index * LANES : (index + 1) * LANES] = value
             if part == 0:
                 odd = group % 2
                 sums[odd] += jnp.where(on_diag(group), values[2 + odd], 0.0)
@@ -195,11 +200,16 @@
     start = (
         tuple(flat(x) for x in heads), tuple(flat(x) for x in tails), tuple(couplings)
     )
-    lax.fori_loop(0, ROUNDS, turn, start)
+
+    def two_turns(_, carry):
+        carry = turn(gram_a, gram_b, basis_a, basis_b, carry)
+        return turn(gram_b, gram_a, basis_b, basis_a, carry)
+
+    lax.fori_loop(0, ROUNDS // 2, two_turns, start)
 
     held = jnp.where(row_slot == 0, 0, 1 + (row_slot + (size - 2 - ROUNDS % (size - 1))) % (size - 1))
     place = onehot(held, lax.broadcasted_iota(jnp.int32, (size, size), 1))
-    basis = basis_buf[ROUNDS % 2].reshape(size, size).astype(jnp.bfloat16)
+    basis = basis_a[...].reshape(size, size).astype(jnp.bfloat16)
     out_ref[...] = dot32(basis, place, ((0,), (0,))).astype(jnp.bfloat16)
 
 
@@ -212,8 +222,12 @@
         in_specs=[pl.BlockSpec(memory_space=pltpu.VMEM)],
         out_specs=pl.BlockSpec(memory_space=pltpu.VMEM),
         scratch_shapes=[
-            pltpu.VMEM((2, 2, groups, SUBS, 4 * LANES), jnp.float32),
-            pltpu.VMEM((2, 2, groups, SUBS, size), jnp.float32),
+            pltpu.VMEM((2, groups, SUBS, 4 * LANES), jnp.float32),
+            pltpu.VMEM((2, groups, SUBS, 4 * LANES), jnp.float32),
+            pltpu.VMEM((2, groups, SUBS, size), jnp.float32),
+            pltpu.VMEM((2, groups, SUBS, size), jnp.float32),
+            pltpu.VMEM((groups, SUBS, LANES), jnp.float32),
+            pltpu.VMEM((groups, SUBS, LANES), jnp.float32),
         ],
         compiler_params=pltpu.CompilerParams(vmem_limit_bytes=32 * 1024 * 1024),
         name="jacobi_turns",

time: 213 us -> 167 us (0.78)
  Pallas kernels: 58.1 us -> 11.9 us
    pallas_call x1, Pallas kernels: 58.1 us -> 11.9 us  [jacobi(): pl.pallas_call(jacobi_kernel, out_shape=jax.ShapeDtypeStruct((size, size)...]
where the time goes in v2:
time: 167 us; the launch traced here: 164 us
  blocking collectives  64.1 us (38%)
  waiting for transfers between devices  32 us (19%)
  between operations  21.6 us (13%)
  matrix products  12.2 us (7%)
  Pallas kernels  11.9 us (7%)
  local copies, waits for them, and re-layouts  11.8 us (7%)
  other arithmetic  8.48 us (5%)
  starting transfers between devices  1.8 us (1%)
    psum x1, blocking collectives, on_device(): off_total, diag_total = lax.psum((off_sq, diag_sq), 'blk')  64.1 us
    psum x1, waiting for transfers between devices, on_device(): gram_sum = lax.psum(inner_cols(matrix, matrix), 'rows')  32 us
    pallas_call x1, Pallas kernels, jacobi(): pl.pallas_call(jacobi_kernel, out_shape=jax.ShapeDtypeStruct((size, size)...  11.9 us
    unnamed x7, local copies, waits for them, and re-layouts  7.68 us
    dot_general x1, matrix products, inner_cols(): lax.dot_general(left_side, right_side, (((0,), (0,)), ((), ())), preferre...  7.21 us
    dot_general x1, matrix products, on_device(): jnp.dot(matrix, rotation, preferred_element_type=jnp.float32)  4.99 us
    gather x1, local copies, waits for them, and re-layouts, on_device(): diag_sq = jnp.sum(jnp.diagonal(gram_sum) ** 2)  3.45 us
  transfers between devices with their start and end apart: 3, of which 1 were waited for; matrix products, arithmetic and copies ran while one was open for 3% of the time, Pallas kernels for 0%

profile of v2, /device:TPU:1, one launch (start us, length us, event | category | flops | bytes accessed | tf_op | source)
XLA Modules:
  0.0 163.9 jit_solution(13255786643421597986)
XLA Ops:
  7.2 0.0 copy-start.2
  7.2 0.0 all-reduce.3.cloned.1.call-start
  7.2 7.2 %fusion.3 = f32[384,384]{1,0:T(8,128)} fusion(bf16[6144,384]{1,0:T(8,128)(2,1)} %param.2), kind=kOutput, calls=%fused_computation.13 | convolution fusion | flops 1811939328 | bytes 5308416 | tf_op jit(solution)/shard_map/dot_general | solution.py:244
  14.4 0.0 all-reduce.3.cloned.1.call-update
  14.5 0.0 copy-done.2
  14.5 0.1 fusion.2
  14.7 32.0 %all-reduce.3.cloned.1.call-done.gram_ref = f32[384,384]{1,0:T(8,128)} async-done(((f32[384,384]{1,0:T(8,128)}), f32[384,384]{1,0:T(8,128)}) %all-reduce.3.cloned.1.call-update) | async-done | bytes 589840 | tf_op jit(solution)/shard_map/psum | solution.py:253
  46.7 0.0 copy-start
  46.7 1.1 copy-done
  47.8 11.9 %jacobi_turns.1 = bf16[384,384]{1,0:T(8,128)(2,1)S(1)} custom-call(f32[384,384]{1,0:T(8,128)S(1)} %copy-done), custom_call_target="tpu_custom_call" | custom-call | tf_op jit(solution)/shard_map/jacobi_turns/pallas_call | solution.py:219
  59.7 5.0 %fusion = bf16[6144,384]{0,1:T(8,128)(2,1)S(1)} fusion(bf16[384,384]{1,0:T(8,128)(2,1)S(1)} %jacobi_turns.1, bf16[6144,384]{1,0:T(8,128)(2,1)} %param.2), kind=kOutput, calls=%fused_computation.2 | convolution fusion | flops 1814298624 | bytes 9732096 | tf_op jit(solution)/shard_map/dot_general | solution.py:262
  64.7 0.0 copy-start.1
  64.7 2.5 %broadcast_select_fusion.1 = (bf16[6144,192]{0,1:T(8,128)(2,1)}, bf16[6144,192]{0,1:T(8,128)(2,1)}) fusion(pred[]{:T(512)S(6)} %eq.16, bf16[6144,384]{0,1:T(8,128)(2,1)S(1)} %fusion), kind=kLoop, calls=%fused_computation.5 | loop fusion | flops 2359296 | bytes 9437185 | tf_op jit(solution)/shard_map/jit(_where)/select_n | solution.py:263
  67.2 1.8 %collective-permute-start = (bf16[6144,192]{0,1:T(8,128)(2,1)}, bf16[6144,192]{0,1:T(8,128)(2,1)S(1)}, u32[]{:S(2)}, u32[]{:S(2)}) collective-permute-start(bf16[6144,192]{0,1:T(8,128)(2,1)} %get-tuple-element.10), channel_id=1, source_target_pairs={{0,2},{2,4},{4,6},{6,8},{8,10},{10,12},{12,14},{14,16},{16,18},{18... | collective-permute-start | bytes 7077896 | tf_op jit(solution)/shard_map/ppermute | solution.py:240
  69.0 0.0 collective-permute-start.1
  69.0 0.6 fusion.1
  73.3 0.0 copy-done.1
  73.3 3.4 %gather_fusion = f32[384]{0:T(512)S(1)} fusion(f32[384,384]{1,0:T(8,128)S(1)} %copy-done.1, s32[384]{0:T(512)S(1)} %or_reduce_fusion), kind=kCustom, calls=%fused_computation | custom fusion | bytes 6144 | tf_op jit(solution)/shard_map/jit(diagonal)/cond/branch_0_fun/gather | solution.py:254
  76.8 0.6 multiply_reduce_fusion.1
  77.3 0.7 multiply_reduce_fusion
  79.3 64.1 %all-reduce = (f32[]{:T(128)}, f32[]{:T(128)}) all-reduce(f32[]{:T(128)S(6)} %sub.16, f32[]{:T(128)} %multiply_reduce_fusion.1), channel_id=1, replica_groups=mesh['blk'=16,'rows'=2] {'blk'}, use_global_device_ids=true, to_apply=%region_3.4 | all-reduce | flops 2 | bytes 16 | tf_op jit(solution)/shard_map/psum | solution.py:256
  144.7 0.0 collective-permute-done
  144.7 0.0 collective-permute-done.1
  144.7 2.0 %broadcast_select_fusion.3 = (bf16[6144,192]{0,1:T(8,128)(2,1)S(1)}, bf16[6144,192]{0,1:T(8,128)(2,1)S(1)}) fusion(bf16[6144,192]{0,1:T(8,128)(2,1)S(1)} %collective-permute-done, bf16[6144,192]{0,1:T(8,128)(2,1)} %collective-permute-done.1, pred[]{:T(512)S(6)} %eq.15), kind=kLoop, calls=%fused_computation.7 | loop fusion | flops 2359296 | bytes 9437185 | tf_op jit(solution)/shard_map/jit(_where)/select_n | solution.py:270
  146.7 2.7 %pad_maximum_fusion = bf16[6144,384]{0,1:T(8,128)(2,1)} fusion(bf16[6144,192]{0,1:T(8,128)(2,1)S(1)} %get-tuple-element.9, bf16[6144,192]{0,1:T(8,128)(2,1)S(1)} %get-tuple-element.8), kind=kLoop, calls=%fused_computation.3 | loop fusion | flops 9437184 | bytes 9437184 | tf_op jit(solution)/shard_map/concatenate | solution.py:272
  149.3 6.6 %copy.5 = bf16[6144,384]{1,0:T(8,128)(2,1)} copy(bf16[6144,384]{0,1:T(8,128)(2,1)} %pad_maximum_fusion) | data formatting | bytes 9437184
  (1 shorter events, 0.0 us)
Async XLA Ops:
  7.2 7.3 %copy-start.2 = (s32[32]{0:T(128)S(1)}, s32[32]{0:T(128)}, u32[]{:S(2)}) copy-start(s32[32]{0:T(128)} %param.3) | copy-start | bytes 388
  7.2 39.5 %all-reduce.3.cloned.1.call-start = ((), (), s32[]{:S(2)}) async-start(), calls=%async_computation | async-start | bytes 1179648 | tf_op jit(solution)/shard_map/psum | solution.py:253
  46.7 1.1 copy-start
  64.7 8.6 %copy-start.1 = (f32[384,384]{1,0:T(8,128)S(1)}, f32[384,384]{1,0:T(8,128)}, u32[]{:S(2)}) copy-start(f32[384,384]{1,0:T(8,128)} %all-reduce.3.cloned.1.call-done.gram_ref) | copy-start | bytes 1769476
  67.2 77.5 %collective-permute-start = (bf16[6144,192]{0,1:T(8,128)(2,1)}, bf16[6144,192]{0,1:T(8,128)(2,1)S(1)}, u32[]{:S(2)}, u32[]{:S(2)}) collective-permute-start(bf16[6144,192]{0,1:T(8,128)(2,1)} %get-tuple-element.10), channel_id=1, source_target_pairs={{0,2},{2,4},{4,6},{6,8},{8,10},{10,12},{12,14},{14,16},{16,18},{18... | collective-permute-start | bytes 7077896 | tf_op jit(solution)/shard_map/ppermute | solution.py:240
  69.0 75.7 %collective-permute-start.1 = (bf16[6144,192]{0,1:T(8,128)(2,1)}, bf16[6144,192]{0,1:T(8,128)(2,1)}, u32[]{:S(2)}, u32[]{:S(2)}) collective-permute-start(bf16[6144,192]{0,1:T(8,128)(2,1)} %get-tuple-element.11), channel_id=1, source_target_pairs={{0,30},{2,0},{4,2},{6,4},{8,6},{10,8},{12,10},{14,12},{16,14},{18,... | collective-permute-start | bytes 7077896 | tf_op jit(solution)/shard_map/ppermute | solution.py:240
Sparse Core Ops, SparseCore 0:
  14.6 32.0 all-reduce.2

commit v3 on v2

--- a/solution.py
+++ b/solution.py
@@ -8,6 +8,11 @@
 ROUNDS = 24
 LANES = 128
 SUBS = 8
+TILE = 512
+GRAM_TILE = 1024
+RAW_ROWS = 1024
+FIRST_ROWS = 3072
+VMEM_LIMIT = 32 * 1024 * 1024
 
 
 def split_three(values):
@@ -61,8 +66,36 @@
     return cos_sq * half_root, 0.5 * (across * root) * half_root
 
 
-def jacobi_kernel(gram_ref, out_ref, gram_a, gram_b, basis_a, basis_b, cos_buf, sin_buf):
-    size = gram_ref.shape[0]
+def full_gram(packed):
+    first = packed[:LANES]
+    block01, block02 = first[:, LANES : 2 * LANES], first[:, 2 * LANES :]
+    block12 = packed[LANES:, LANES : 2 * LANES]
+    second = jnp.concatenate([block01.T, packed[LANES:, : 2 * LANES]], axis=1)
+    third = jnp.concatenate([block02.T, block12.T, packed[LANES:, 2 * LANES :]], axis=1)
+    return jnp.concatenate([first, second, third], axis=0)
+
+
+def send_columns(lanes, base, slot, width):
+    section = lanes // LANES
+    lane = lanes % LANES
+    rest = width - LANES
+    main_start = base + jnp.where(slot == 0, 0, rest)
+    rest_start = base + jnp.where(slot == 0, LANES, 0)
+    high = (section // 2 + slot) % 2
+    inside = lane - high * (LANES - rest)
+    mixed = jnp.where((inside >= 0) & (inside < rest), rest_start + inside, -1)
+    return jnp.where(section == 1, main_start + lane, mixed)
+
+
+def jacobi_kernel(side_ref, *refs):
+    gram_refs, outs, scratch = refs[:-9], refs[-9:-6], refs[-6:]
+    jacobi_body(side_ref, gram_refs, *outs, *scratch)
+
+
+def jacobi_body(
+    side_ref, gram_refs, slow_ref, fast_ref, sums_ref, gram_a, gram_b, basis_a, basis_b, cos_buf, sin_buf
+):
+    size = gram_refs[0].shape[1]
     half = size // 2
     groups = half // SUBS
     last = groups - 1
@@ -80,7 +113,17 @@
     lane_slot = slot_of_lane(lax.broadcasted_iota(jnp.int32, (1, 4 * LANES), 1), half)
     take_cols = onehot(lax.broadcasted_iota(jnp.int32, (size, 4 * LANES), 0), lane_slot)
     arranged = jnp.zeros((size, 4 * LANES), jnp.float32)
-    for piece in split_three(gram_ref[...]):
+    packed = gram_refs[0][...]
+    for other in gram_refs[1:]:
+        packed = packed + other[...]
+    gram_sum = full_gram(packed)
+    squares = gram_sum * gram_sum
+    rows = lax.broadcasted_iota(jnp.int32, (size, size), 0)
+    cols = lax.broadcasted_iota(jnp.int32, (size, size), 1)
+    diag_sq = jnp.sum(jnp.where(rows == cols, squares, 0.0), keepdims=True)
+    off_sq = jnp.sum(squares, keepdims=True) - diag_sq
+    sums_ref[...] = jnp.where(sub == 0, off_sq, diag_sq)
+    for piece in split_three(gram_sum):
         moved = dot32(take_rows, piece).astype(jnp.bfloat16)
         arranged = arranged + dot32(moved, take_cols)
     gram_a[...] = arranged.reshape(2, groups, SUBS, 4 * LANES)
@@ -208,19 +251,26 @@
     lax.fori_loop(0, ROUNDS // 2, two_turns, start)
 
     held = jnp.where(row_slot == 0, 0, 1 + (row_slot + (size - 2 - ROUNDS % (size - 1))) % (size - 1))
-    place = onehot(held, lax.broadcasted_iota(jnp.int32, (size, size), 1))
     basis = basis_a[...].reshape(size, size).astype(jnp.bfloat16)
-    out_ref[...] = dot32(basis, place, ((0,), (0,))).astype(jnp.bfloat16)
-
-
-def jacobi(gram_sum):
-    size = gram_sum.shape[0]
+    lanes = lax.broadcasted_iota(jnp.int32, (1, size), 1)
+    for index, ref in enumerate((slow_ref, fast_ref)):
+        wanted = send_columns(lanes, side_ref[2 * index], side_ref[2 * index + 1], half)
+        ref[...] = dot32(basis, onehot(held, wanted), ((0,), (0,))).astype(jnp.bfloat16)
+
+
+def jacobi(side, grams):
+    size = grams[0].shape[1]
     groups = size // 2 // SUBS
     return pl.pallas_call(
         jacobi_kernel,
-        out_shape=jax.ShapeDtypeStruct((size, size), jnp.bfloat16),
-        in_specs=[pl.BlockSpec(memory_space=pltpu.VMEM)],
-        out_specs=pl.BlockSpec(memory_space=pltpu.VMEM),
+        out_shape=(
+            jax.ShapeDtypeStruct((size, size), jnp.bfloat16),
+            jax.ShapeDtypeStruct((size, size), jnp.bfloat16),
+            jax.ShapeDtypeStruct((SUBS, LANES), jnp.float32),
+        ),
+        in_specs=[pl.BlockSpec(memory_space=pltpu.SMEM)]
+        + [pl.BlockSpec(memory_space=pltpu.VMEM)] * len(grams),
+        out_specs=[pl.BlockSpec(memory_space=pltpu.VMEM)] * 3,
         scratch_shapes=[
             pltpu.VMEM((2, groups, SUBS, 4 * LANES), jnp.float32),
             pltpu.VMEM((2, groups, SUBS, 4 * LANES), jnp.float32),
@@ -229,47 +279,240 @@
             pltpu.VMEM((groups, SUBS, LANES), jnp.float32),
             pltpu.VMEM((groups, SUBS, LANES), jnp.float32),
         ],
-        compiler_params=pltpu.CompilerParams(vmem_limit_bytes=32 * 1024 * 1024),
+        compiler_params=pltpu.CompilerParams(vmem_limit_bytes=VMEM_LIMIT),
+        cost_estimate=pl.CostEstimate(
+            flops=ROUNDS * 20 * size * size * 30, bytes_accessed=8 * size * size, transcendentals=0
+        ),
         name="jacobi_turns",
-    )(gram_sum)
-
-
-def shifted(value, axis, steps):
+    )(side, *grams)
+
+
+def gram_kernel(matrix_ref, packed_ref, upper_ref, corner_ref):
+    step = pl.program_id(0)
+    values = matrix_ref[...]
+    right = values[:, 2 * LANES :]
+    upper = dot32(values[:, : 2 * LANES], values, ((0,), (0,)))
+    corner = dot32(right, right, ((0,), (0,)))
+
+    @pl.when(step == 0)
+    def _():
+        upper_ref[...] = upper
+        corner_ref[...] = corner
+
+    @pl.when(step > 0)
+    def _():
+        upper_ref[...] += upper
+        corner_ref[...] += corner
+
+    @pl.when(step == pl.num_programs(0) - 1)
+    def _():
+        packed_ref[:LANES] = upper_ref[:LANES]
+        packed_ref[LANES:, : 2 * LANES] = upper_ref[LANES:, LANES:]
+        packed_ref[LANES:, 2 * LANES :] = corner_ref[...]
+
+
+def gram_blocks(matrix):
+    rows, size = matrix.shape
+    return pl.pallas_call(
+        gram_kernel,
+        grid=(rows // GRAM_TILE,),
+        in_specs=[pl.BlockSpec((GRAM_TILE, size), lambda i: (i, 0))],
+        out_specs=pl.BlockSpec((2 * LANES, size), lambda i: (0, 0)),
+        out_shape=jax.ShapeDtypeStruct((2 * LANES, size), jnp.float32),
+        scratch_shapes=[
+            pltpu.VMEM((2 * LANES, size), jnp.float32),
+            pltpu.VMEM((LANES, LANES), jnp.float32),
+        ],
+        compiler_params=pltpu.CompilerParams(vmem_limit_bytes=VMEM_LIMIT),
+        cost_estimate=pl.CostEstimate(
+            flops=2 * rows * size * size, bytes_accessed=2 * rows * size, transcendentals=0
+        ),
+        name="gram_blocks",
+    )(matrix)
+
+
+def rotate_kernel(matrix_ref, turn_ref, packed_ref):
+    rows = matrix_ref.shape[0]
+    half = rows // 2
+    top = dot32(matrix_ref[:half], turn_ref[:, : 2 * LANES])
+    low = dot32(matrix_ref[half:], turn_ref[:, LANES:])
+    packed_ref[:half] = top[:, LANES:].astype(jnp.bfloat16)
+    packed_ref[half:rows] = low[:, :LANES].astype(jnp.bfloat16)
+    packed_ref[rows:] = (top[:, :LANES] + low[:, LANES:]).astype(jnp.bfloat16)
+
+
+def rotate_rows(matrix, turn, start, count):
+    size = matrix.shape[1]
+    first = start // TILE
+    pack = TILE + TILE // 2
+    return pl.pallas_call(
+        rotate_kernel,
+        grid=(count // TILE,),
+        in_specs=[
+            pl.BlockSpec((TILE, size), lambda i: (first + i, 0)),
+            pl.BlockSpec((size, size), lambda i: (0, 0)),
+        ],
+        out_specs=pl.BlockSpec((pack, LANES), lambda i: (i, 0)),
+        out_shape=jax.ShapeDtypeStruct((count // TILE * pack, LANES), jnp.bfloat16),
+        compiler_params=pltpu.CompilerParams(vmem_limit_bytes=VMEM_LIMIT),
+        cost_estimate=pl.CostEstimate(
+            flops=4 * count * size * LANES, bytes_accessed=3 * count * size, transcendentals=0
+        ),
+        name="rotate_rows",
+    )(matrix, turn)
+
+
+def low_lanes(slot, rows):
+    lane = lax.broadcasted_iota(jnp.int32, (rows, LANES), 1)
+    return (lane // (LANES // 2)) == slot
+
+
+def place_main(slot, out_ref, slow_main, fast_main):
+    @pl.when(slot == 0)
+    def _():
+        out_ref[:, :LANES] = slow_main
+        out_ref[:, 2 * LANES :] = fast_main
+
+    @pl.when(slot != 0)
+    def _():
+        out_ref[:, :LANES] = fast_main
+        out_ref[:, 2 * LANES :] = slow_main
+
+
+def place_kernel(slot_ref, slow_ref, fast_ref, *refs):
+    out_ref = refs[-1]
+    rows = out_ref.shape[0]
+    half = rows // 2
+    slot = slot_ref[0]
+    place_main(slot, out_ref, slow_ref[:rows], fast_ref[:rows])
+    slow = slow_ref[rows:].astype(jnp.float32)
+    fast = fast_ref[rows:].astype(jnp.float32)
+    mask = low_lanes(slot, half)
+    middle = slice(LANES, 2 * LANES)
+    out_ref[:half, middle] = jnp.where(mask, slow, fast).astype(jnp.bfloat16)
+    swapped = pltpu.roll(jnp.where(mask, fast, slow), LANES // 2, 1)
+    out_ref[half:, middle] = swapped.astype(jnp.bfloat16)
+
+
+def raw_kernel(slot_ref, raw_ref, turn_ref, fast_ref, *refs):
+    out_ref = refs[-1]
+    rows = out_ref.shape[0]
+    half = rows // 2
+    slot = slot_ref[0]
+    turned = dot32(raw_ref[...], turn_ref[...])
+    place_main(slot, out_ref, turned[:, LANES:].astype(jnp.bfloat16), fast_ref[:rows])
+    fast = fast_ref[rows:].astype(jnp.float32)
+    mask = low_lanes(slot, half)
+    middle = slice(LANES, 2 * LANES)
+    out_ref[:half, middle] = jnp.where(mask, turned[:half, :LANES], fast).astype(jnp.bfloat16)
+    swapped = pltpu.roll(fast, LANES // 2, 1)
+    out_ref[half:, middle] = jnp.where(mask, turned[half:, :LANES], swapped).astype(jnp.bfloat16)
+
+
+def fill_rows(kernel, slot, sources, specs, fast, held, shape, start, count):
+    first = start // TILE
+    pack = TILE + TILE // 2
+    operands = [slot, *sources, fast]
+    in_specs = [
+        pl.BlockSpec(memory_space=pltpu.SMEM),
+        *specs,
+        pl.BlockSpec((pack, LANES), lambda i: (first + i, 0)),
+    ]
+    aliases = {}
+    if held is not None:
+        aliases = {len(operands): 0}
+        operands.append(held)
+        in_specs.append(pl.BlockSpec(memory_space=pl.ANY))
+    return pl.pallas_call(
+        kernel,
+        grid=(count // TILE,),
+        in_specs=in_specs,
+        out_specs=pl.BlockSpec((TILE, shape[1]), lambda i: (first + i, 0)),
+        out_shape=jax.ShapeDtypeStruct(shape, jnp.bfloat16),
+        input_output_aliases=aliases,
+        compiler_params=pltpu.CompilerParams(vmem_limit_bytes=VMEM_LIMIT),
+        cost_estimate=pl.CostEstimate(
+            flops=count * shape[1], bytes_accessed=4 * count * shape[1], transcendentals=0
+        ),
+        name="fill_rows",
+    )(*operands)
+
+
+def swapped_with(value, axis, partner):
     count = lax.axis_size(axis)
-    pairs = [(source, (source + steps) % count) for source in range(count)]
-    return lax.ppermute(value, axis, pairs)
-
-
-def inner_cols(left_side, right_side):
-    return lax.dot_general(
-        left_side, right_side, (((0,), (0,)), ((), ())), preferred_element_type=jnp.float32
+    return lax.ppermute(value, axis, [(source, partner(source, count)) for source in range(count)])
+
+
+def slow_partner(source, count):
+    return (source + 1) % count if source % 2 else (source + count - 1) % count
+
+
+def fast_partner(source, count):
+    return source ^ 1
+
+
+def sends_and_slot(plan):
+    count = lax.axis_size("blk")
+    position = lax.axis_index("blk")
+    step = 2 * (position % 2) - 1
+    slow_dev = (position + step + count) % count
+    mine = lax.dynamic_slice_in_dim(plan, 2 * position, 2)
+    theirs = lax.dynamic_slice_in_dim(plan, 2 * slow_dev, 2)
+    first_slow = mine[0] // 2 == slow_dev
+    slow_to = jnp.where(first_slow, mine[0], mine[1])
+    fast_to = jnp.where(first_slow, mine[1], mine[0])
+    in_slot = jnp.where(theirs[0] // 2 == position, theirs[0], theirs[1]) % 2
+    return first_slow, slow_to % 2, fast_to % 2, in_slot
+
+
+def on_device(matrix, plan):
+    rows, size = matrix.shape
+    width = size // 2
+    first_slow, slow_slot, fast_slot, in_slot = sends_and_slot(plan)
+    zero = jnp.zeros((), jnp.int32)
+    side = jnp.stack([
+        jnp.where(first_slow, zero, width), slow_slot, jnp.where(first_slow, width, zero), fast_slot
+    ]).astype(jnp.int32)
+    slot = in_slot.astype(jnp.int32)[None]
+
+    raw = swapped_with(matrix[:RAW_ROWS], "blk", slow_partner)
+    own = gram_blocks(matrix)
+    if lax.axis_size("rows") == 2:
+        grams = [own, swapped_with(own, "rows", fast_partner)]
+    else:
+        grams = [lax.psum(own, "rows")]
+    slow_turn, fast_turn, sums = jacobi(side, grams)
+    totals = jnp.sum(lax.all_gather(sums, "blk"), axis=0)
+    off_ratio = jnp.sqrt(totals[0, 0] / totals[1, 0])
+
+    their_turn = swapped_with(slow_turn[:, : 2 * LANES], "blk", slow_partner)
+    spans = [(RAW_ROWS, FIRST_ROWS), (RAW_ROWS + FIRST_ROWS, rows - RAW_ROWS - FIRST_ROWS)]
+    arrived = [
+        swapped_with(rotate_rows(matrix, slow_turn, start, count), "blk", slow_partner)
+        for start, count in spans
+    ]
+    fast = swapped_with(rotate_rows(matrix, fast_turn, 0, rows), "blk", fast_partner)
+    shape = (rows, size)
+    pack = TILE + TILE // 2
+    result = fill_rows(
+        raw_kernel,
+        slot,
+        [raw, their_turn],
+        [
+            pl.BlockSpec((TILE, size), lambda i: (i, 0)),
+            pl.BlockSpec((size, 2 * LANES), lambda i: (0, 0)),
+        ],
+        fast, None, shape, 0, RAW_ROWS,
     )
-
-
-def on_device(matrix, plan):
-    cycle_size = lax.axis_size("blk")
-    position = lax.axis_index("blk")
-    block_width = matrix.shape[1] // 2
-    gram_sum = lax.psum(inner_cols(matrix, matrix), "rows")
-    diag_sq = jnp.sum(jnp.diagonal(gram_sum) ** 2)
-    off_sq = jnp.sum(gram_sum * gram_sum) - diag_sq
-    off_total, diag_total = lax.psum((off_sq, diag_sq), "blk")
-    off_ratio = jnp.sqrt(off_total / diag_total)
-    rotation = jacobi(gram_sum)
-    my_dest = lax.dynamic_slice_in_dim(plan, 2 * position, 2)
-    next_dev = (position + 1) % cycle_size
-    right_first = my_dest[0] // 2 == next_dev
-    rotated = jnp.dot(matrix, rotation, preferred_element_type=jnp.float32).astype(jnp.bfloat16)
-    going_right = jnp.where(right_first, rotated[:, :block_width], rotated[:, block_width:])
-    going_left = jnp.where(right_first, rotated[:, block_width:], rotated[:, :block_width])
-    from_left = shifted(going_right, "blk", 1)
-    from_right = shifted(going_left, "blk", -1)
-    prev_dev = (position + cycle_size - 1) % cycle_size
-    their_dest = lax.dynamic_slice_in_dim(plan, 2 * prev_dev, 2)
-    in_slot = jnp.where(their_dest[0] // 2 == position, their_dest[0], their_dest[1]) % 2
-    slot_zero = jnp.where(in_slot == 0, from_left, from_right)
-    slot_one = jnp.where(in_slot == 0, from_right, from_left)
-    return (jnp.concatenate([slot_zero, slot_one], axis=1), off_ratio)
+    for (start, count), slow in zip(spans, arrived):
+        result = fill_rows(
+            place_kernel,
+            slot,
+            [slow],
+            [pl.BlockSpec((pack, LANES), lambda i: (i, 0))],
+            fast, result, shape, start, count,
+        )
+    return result, off_ratio
 
 
 def solution(mesh):

time: 167 us -> 135 us (0.81); the launches traced: 164 us -> 134 us
  waiting for transfers between devices: 32 us -> 2.85 us
  Pallas kernels: 11.9 us -> 39.3 us
  matrix products: 12.2 us -> 0 us
  between operations: 21.6 us -> 12.1 us
  other arithmetic: 8.48 us -> 0.1 us
  local copies, waits for them, and re-layouts: 11.8 us -> 4.54 us
  starting transfers between devices: 1.8 us -> 6.88 us
  blocking collectives: 64.1 us -> 68.2 us
    all_gather x0 -> x1, blocking collectives: none -> 68.2 us  [on_device(): totals = jnp.sum(lax.all_gather(sums, 'blk'), axis=0)]
    psum x1 -> x0, blocking collectives: 64.1 us -> none  [on_device(): off_total, diag_total = lax.psum((off_sq, diag_sq), 'blk')]
    psum x1 -> x0, waiting for transfers between devices: 32 us -> none  [on_device(): gram_sum = lax.psum(inner_cols(matrix, matrix), 'rows')]
    pallas_call x1 -> x8, Pallas kernels: 11.9 us -> 39.3 us  [the longest x1 12.7 us: jacobi(): pl.pallas_call(jacobi_kernel, out_shape=(jax.ShapeDtypeStruct((size, size...]
    dot_general x2 -> x0, matrix products: 12.2 us -> none  [the longest x1 7.21 us: inner_cols(): lax.dot_general(left_side, right_side, (((0,), (0,)), ((), ())), preferre...]
    unnamed x7 -> x8, local copies, waits for them, and re-layouts: 7.68 us -> 2.34 us
    ppermute x2 -> x6, starting transfers between devices: 1.76 us -> 6.88 us  [swapped_with(): lax.ppermute(value, axis, [(source, partner(source, count)) for source in...]
    select_n x2 -> x0, other arithmetic: 4.47 us -> none  [the longest x1 2.5 us: on_device(): jnp.where(right_first, rotated[:, :block_width], rotated[:, block_width:])]
  transfers between devices with their start and end apart: 3 -> 6, of which waited for: 1 -> 1; matrix products, arithmetic and copies ran while one was open for 3% -> 2% of each run, Pallas kernels for 0% -> 10%
where the time goes in v3:
time: 135 us; the launch traced here: 134 us
  blocking collectives  68.2 us (51%)
  Pallas kernels  39.3 us (29%)
  between operations  12.1 us (9%)
  starting transfers between devices  6.88 us (5%)
  local copies, waits for them, and re-layouts  4.54 us (3%)
  waiting for transfers between devices  2.85 us (2%)
    all_gather x1, blocking collectives, on_device(): totals = jnp.sum(lax.all_gather(sums, 'blk'), axis=0)  68.2 us
    pallas_call x1, Pallas kernels, jacobi(): pl.pallas_call(jacobi_kernel, out_shape=(jax.ShapeDtypeStruct((size, size...  12.7 us
    pallas_call x3, Pallas kernels, rotate_rows(): pl.pallas_call(rotate_kernel, grid=(count // TILE,), in_specs=[pl.BlockSp...  11.7 us
    pallas_call x3, Pallas kernels, fill_rows(): pl.pallas_call(kernel, grid=(count // TILE,), in_specs=in_specs, out_spec...  11.3 us
    ppermute x6, starting transfers between devices, swapped_with(): lax.ppermute(value, axis, [(source, partner(source, count)) for source in...  6.88 us
    pallas_call x1, Pallas kernels, gram_blocks(): pl.pallas_call(gram_kernel, grid=(rows // GRAM_TILE,), in_specs=[pl.Block...  3.55 us
    ppermute x6, waiting for transfers between devices, swapped_with(): lax.ppermute(value, axis, [(source, partner(source, count)) for source in...  2.85 us
  transfers between devices with their start and end apart: 6, of which 1 were waited for; matrix products, arithmetic and copies ran while one was open for 2% of the time, Pallas kernels for 10%

profile of v3, /device:TPU:1, one launch (start us, length us, event | category | flops | bytes accessed | tf_op | source)
XLA Modules:
  0.0 133.9 jit_solution(17431517198007135099)
XLA Ops:
  0.6 0.0 copy-start
  0.6 2.3 %copy-done = bf16[6144,384]{1,0:T(8,128)(2,1)S(1)} copy-done((bf16[6144,384]{1,0:T(8,128)(2,1)S(1)}, bf16[6144,384]{1,0:T(8,128)(2,1)}, u32[]{:S(2)}) %copy-start) | copy-done | bytes 4718616
  3.0 0.0 copy-start.1
  3.0 0.0 slice-start
  3.0 3.5 %gram_blocks.1.refs_0_ = f32[256,384]{1,0:T(8,128)S(1)} custom-call(bf16[6144,384]{1,0:T(8,128)(2,1)S(1)} %copy-done), custom_call_target="tpu_custom_call" | custom-call | flops 1811939328 | bytes 4718592 | tf_op jit(solution)/shard_map/gram_blocks/pallas_call | solution.py:316
  6.5 2.1 %collective-permute-start = (f32[256,384]{1,0:T(8,128)S(1)}, f32[256,384]{1,0:T(8,128)S(1)}, u32[]{:S(2)}, u32[]{:S(2)}) collective-permute-start(f32[256,384]{1,0:T(8,128)S(1)} %gram_blocks.1.refs_0_), channel_id=1, source_target_pairs={{0,1},{1,0},{2,3},{3,2},{4,5},{5,4},{6,7},{7,6},{8,9},{9,8},{10,11... | collective-permute-start | bytes 1179656 | tf_op jit(solution)/shard_map/ppermute | solution.py:443
  8.6 0.0 copy-done.1
  8.6 0.1 fusion.2
  8.7 0.6 fusion.1
  14.6 0.1 pad_add_fusion.side_ref
  14.6 0.0 slice-start.1
  14.6 2.8 %collective-permute-done.refs_1_ = f32[256,384]{1,0:T(8,128)S(1)} collective-permute-done((f32[256,384]{1,0:T(8,128)S(1)}, f32[256,384]{1,0:T(8,128)S(1)}, u32[]{:S(2)}, u32[]{:S(2)}) %collective-permute-start) | collective-permute-done | bytes 393248 | tf_op jit(solution)/shard_map/ppermute | solution.py:443
  17.5 12.7 %jacobi_turns.1 = (bf16[384,384]{1,0:T(8,128)(2,1)S(1)}, bf16[384,384]{1,0:T(8,128)(2,1)S(1)}, f32[8,128]{1,0:T(8,128)S(1)}) custom-call(s32[4]{0:T(128)S(1)} %pad_add_fusion.side_ref, f32[256,384]{1,0:T(8,128)S(1)} %gram_blocks.1.refs_0_, f32[256,384]{1,0:T(8,128)S(1)} %collective-permute-done.refs_1_), custom_call_target="tpu_custom_call" | custom-call | flops 2123366400 | bytes 1179648 | tf_op jit(solution)/shard_map/jacobi_turns/pallas_call | solution.py:264
  30.2 0.0 slice-done
  30.2 0.0 slice-done.1
  30.2 6.2 %rotate_rows.4 = bf16[9216,128]{1,0:T(8,128)(2,1)} custom-call(bf16[6144,384]{1,0:T(8,128)(2,1)S(1)} %bitcast.13, bf16[384,384]{1,0:T(8,128)(2,1)S(1)} %get-tuple-element.6.turn_ref), custom_call_target="tpu_custom_call" | custom-call | flops 1207959552 | bytes 7077888 | tf_op jit(solution)/shard_map/rotate_rows/pallas_call | solution.py:348
  36.4 1.2 collective-permute-start.2
  37.6 3.2 %rotate_rows.5 = bf16[4608,128]{1,0:T(8,128)(2,1)} custom-call(bf16[6144,384]{1,0:T(8,128)(2,1)S(1)} %bitcast.13, bf16[384,384]{1,0:T(8,128)(2,1)S(1)} %get-tuple-element.5.turn_ref), custom_call_target="tpu_custom_call" | custom-call | flops 603979776 | bytes 3538944 | tf_op jit(solution)/shard_map/rotate_rows/pallas_call | solution.py:348
  40.9 1.4 %collective-permute-start.3 = (bf16[4608,128]{1,0:T(8,128)(2,1)}, bf16[4608,128]{1,0:T(8,128)(2,1)}, u32[]{:S(2)}, u32[]{:S(2)}) collective-permute-start(bf16[4608,128]{1,0:T(8,128)(2,1)} %rotate_rows.5), channel_id=1, source_target_pairs={{0,30},{2,4},{4,2},{6,8},{8,6},{10,12},{12,10},{14,16},{16,14},{18... | collective-permute-start | bytes 3538952 | tf_op jit(solution)/shard_map/ppermute | solution.py:443
  42.3 0.9 slice.32
  43.2 0.4 collective-permute-start.4
  43.6 2.3 %rotate_rows.3 = bf16[3072,128]{1,0:T(8,128)(2,1)} custom-call(bf16[6144,384]{1,0:T(8,128)(2,1)S(1)} %bitcast.13, bf16[384,384]{1,0:T(8,128)(2,1)S(1)} %get-tuple-element.5.turn_ref), custom_call_target="tpu_custom_call" | custom-call | flops 402653184 | bytes 2359296 | tf_op jit(solution)/shard_map/rotate_rows/pallas_call | solution.py:348
  45.8 1.4 %collective-permute-start.1 = (bf16[3072,128]{1,0:T(8,128)(2,1)}, bf16[3072,128]{1,0:T(8,128)(2,1)}, u32[]{:S(2)}, u32[]{:S(2)}) collective-permute-start(bf16[3072,128]{1,0:T(8,128)(2,1)} %rotate_rows.3), channel_id=1, source_target_pairs={{0,30},{2,4},{4,2},{6,8},{8,6},{10,12},{12,10},{14,16},{16,14},{18... | collective-permute-start | bytes 2359304 | tf_op jit(solution)/shard_map/ppermute | solution.py:443
  51.0 0.4 collective-permute-start.5
  51.4 68.2 %all-gather = f32[128,128]{1,0:T(8,128)S(1)} all-gather(f32[8,128]{1,0:T(8,128)S(1)} %get-tuple-element.7), channel_id=2, replica_groups=mesh['blk'=16,'rows'=2] {'blk'}, dimensions={0}, use_global_device_ids=true | all-gather | bytes 69632 | tf_op jit(solution)/shard_map/all_gather | solution.py:485
  119.6 0.5 fusion
  121.5 0.0 collective-permute-done.5.turn_ref
  121.5 0.0 collective-permute-done.4.raw_ref
  121.5 0.0 collective-permute-done.2.fast_ref
  121.5 2.6 %fill_rows.3.refs_0_ = bf16[6144,384]{1,0:T(8,128)(2,1)} custom-call(s32[1]{0:T(128)} %bitcast.2.slot_ref, bf16[1024,384]{1,0:T(8,128)(2,1)} %collective-permute-done.4.raw_ref, bf16[384,256]{1,0:T(8,128)(2,1)S(1)} %collective-permute-done.5.turn_ref, bf16[9216,128]{1,0:T(8,128)(2,1)S(1)} %collective-permute-done.2.fast_ref), custom_call_target="tpu_custom_call" | custom-call | flops 393216 | bytes 1572864 | tf_op jit(solution)/shard_map/fill_rows/pallas_call | solution.py:426
  124.1 0.0 collective-permute-done.3.slow_ref
  124.1 5.0 %fill_rows.4.refs_0_ = bf16[6144,384]{1,0:T(8,128)(2,1)} custom-call(s32[1]{0:T(128)} %bitcast.2.slot_ref, bf16[4608,128]{1,0:T(8,128)(2,1)} %collective-permute-done.3.slow_ref, bf16[9216,128]{1,0:T(8,128)(2,1)S(1)} %collective-permute-done.2.fast_ref, bf16[6144,384]{1,0:T(8,128)(2,1)} %fill_rows.3.refs_0_), custom_call_target="tpu_custom_call", output_to_operand_aliasing={{}: (3, {})} | custom-call | flops 1179648 | bytes 4718592 | tf_op jit(solution)/shard_map/fill_rows/pallas_call | solution.py:426
  129.1 0.0 collective-permute-done.1.slow_ref
  129.1 3.7 %fill_rows.5 = bf16[6144,384]{1,0:T(8,128)(2,1)} custom-call(s32[1]{0:T(128)} %bitcast.2.slot_ref, bf16[3072,128]{1,0:T(8,128)(2,1)} %collective-permute-done.1.slow_ref, bf16[9216,128]{1,0:T(8,128)(2,1)S(1)} %collective-permute-done.2.fast_ref, bf16[6144,384]{1,0:T(8,128)(2,1)} %fill_rows.4.refs_0_), custom_call_target="tpu_custom_call", output_to_operand_aliasing={{}: (3, {})} | custom-call | flops 786432 | bytes 3145728 | tf_op jit(solution)/shard_map/fill_rows/pallas_call | solution.py:426
  (3 shorter events, 0.0 us)
Async XLA Ops:
  0.6 2.3 %copy-start = (bf16[6144,384]{1,0:T(8,128)(2,1)S(1)}, bf16[6144,384]{1,0:T(8,128)(2,1)}, u32[]{:S(2)}) copy-start(bf16[6144,384]{1,0:T(8,128)(2,1)} %matrix_ref.7) | copy-start | bytes 14155780
  3.0 5.7 %copy-start.1 = (s32[32]{0:T(128)S(1)}, s32[32]{0:T(128)}, u32[]{:S(2)}) copy-start(s32[32]{0:T(128)} %param.3) | copy-start | bytes 388
  3.0 27.2 %slice-start = ((s8[4718592]{0:T(1024)(128)(4,1)}), s8[524288]{0:T(1024)(128)(4,1)S(1)}, s32[]{:S(2)}) async-start(s8[4718592]{0:T(1024)(128)(4,1)} %bitcast.12), calls=%async_computation | async-start | bytes 1048576
  6.5 10.9 %collective-permute-start = (f32[256,384]{1,0:T(8,128)S(1)}, f32[256,384]{1,0:T(8,128)S(1)}, u32[]{:S(2)}, u32[]{:S(2)}) collective-permute-start(f32[256,384]{1,0:T(8,128)S(1)} %gram_blocks.1.refs_0_), channel_id=1, source_target_pairs={{0,1},{1,0},{2,3},{3,2},{4,5},{5,4},{6,7},{7,6},{8,9},{9,8},{10,11... | collective-permute-start | bytes 1179656 | tf_op jit(solution)/shard_map/ppermute | solution.py:443
  14.6 15.6 %slice-start.1 = ((s8[4718592]{0:T(1024)(128)(4,1)}), s8[4194304]{0:T(1024)(128)(4,1)S(1)}, s32[]{:S(2)}) async-start(s8[4718592]{0:T(1024)(128)(4,1)} %bitcast.12), calls=%async_computation.1 | async-start | bytes 8388608
  36.4 85.1 %collective-permute-start.2 = (bf16[9216,128]{1,0:T(8,128)(2,1)}, bf16[9216,128]{1,0:T(8,128)(2,1)S(1)}, u32[]{:S(2)}, u32[]{:S(2)}) collective-permute-start(bf16[9216,128]{1,0:T(8,128)(2,1)} %rotate_rows.4), channel_id=1, source_target_pairs={{0,2},{2,0},{4,6},{6,4},{8,10},{10,8},{12,14},{14,12},{16,18},{18,... | collective-permute-start | bytes 7077896 | tf_op jit(solution)/shard_map/ppermute | solution.py:443
  40.9 83.2 %collective-permute-start.3 = (bf16[4608,128]{1,0:T(8,128)(2,1)}, bf16[4608,128]{1,0:T(8,128)(2,1)}, u32[]{:S(2)}, u32[]{:S(2)}) collective-permute-start(bf16[4608,128]{1,0:T(8,128)(2,1)} %rotate_rows.5), channel_id=1, source_target_pairs={{0,30},{2,4},{4,2},{6,8},{8,6},{10,12},{12,10},{14,16},{16,14},{18... | collective-permute-start | bytes 3538952 | tf_op jit(solution)/shard_map/ppermute | solution.py:443
  43.2 78.3 %collective-permute-start.4 = (bf16[1024,384]{1,0:T(8,128)(2,1)}, bf16[1024,384]{1,0:T(8,128)(2,1)}, u32[]{:S(2)}, u32[]{:S(2)}) collective-permute-start(bf16[1024,384]{1,0:T(8,128)(2,1)} %slice.32), channel_id=1, source_target_pairs={{0,30},{2,4},{4,2},{6,8},{8,6},{10,12},{12,10},{14,16},{16,14},{18... | collective-permute-start | bytes 2359304 | tf_op jit(solution)/shard_map/ppermute | solution.py:443
  45.8 83.3 %collective-permute-start.1 = (bf16[3072,128]{1,0:T(8,128)(2,1)}, bf16[3072,128]{1,0:T(8,128)(2,1)}, u32[]{:S(2)}, u32[]{:S(2)}) collective-permute-start(bf16[3072,128]{1,0:T(8,128)(2,1)} %rotate_rows.3), channel_id=1, source_target_pairs={{0,30},{2,4},{4,2},{6,8},{8,6},{10,12},{12,10},{14,16},{16,14},{18... | collective-permute-start | bytes 2359304 | tf_op jit(solution)/shard_map/ppermute | solution.py:443
  51.0 70.5 %collective-permute-start.5 = (bf16[384,256]{1,0:T(8,128)(2,1)S(1)}, bf16[384,256]{1,0:T(8,128)(2,1)S(1)}, u32[]{:S(2)}, u32[]{:S(2)}) collective-permute-start(bf16[384,256]{1,0:T(8,128)(2,1)S(1)} %slice.33), channel_id=1, source_target_pairs={{0,30},{2,4},{4,2},{6,8},{8,6},{10,12},{12,10},{14,16},{16,14},{18... | collective-permute-start | bytes 589832 | tf_op jit(solution)/shard_map/ppermute | solution.py:443

commit v4 on v3

--- a/solution.py
+++ b/solution.py
@@ -8,11 +8,13 @@
 ROUNDS = 24
 LANES = 128
 SUBS = 8
-TILE = 512
+UNIT = 512
+PACK = UNIT + UNIT // 2
 GRAM_TILE = 1024
 RAW_ROWS = 1024
 FIRST_ROWS = 3072
 VMEM_LIMIT = 32 * 1024 * 1024
+GRAM_VMEM_LIMIT = 60 * 1024 * 1024
 
 
 def split_three(values):
@@ -87,13 +89,26 @@
     return jnp.where(section == 1, main_start + lane, mixed)
 
 
-def jacobi_kernel(side_ref, *refs):
-    gram_refs, outs, scratch = refs[:-9], refs[-9:-6], refs[-6:]
-    jacobi_body(side_ref, gram_refs, *outs, *scratch)
+def moves(plan_ref):
+    count = plan_ref.shape[0] // 2
+    position = lax.axis_index("blk")
+    slow_dev = lax.rem(position + 2 * lax.rem(position, 2) - 1 + count, count)
+    mine = plan_ref[2 * position], plan_ref[2 * position + 1]
+    theirs = plan_ref[2 * slow_dev], plan_ref[2 * slow_dev + 1]
+    first_slow = mine[0] // 2 == slow_dev
+    slow_slot = lax.rem(jnp.where(first_slow, mine[0], mine[1]), 2)
+    fast_slot = lax.rem(jnp.where(first_slow, mine[1], mine[0]), 2)
+    in_slot = lax.rem(jnp.where(theirs[0] // 2 == position, theirs[0], theirs[1]), 2)
+    return first_slow, slow_slot, fast_slot, in_slot
+
+
+def jacobi_kernel(plan_ref, *refs):
+    jacobi_body(plan_ref, refs[:-10], *refs[-10:])
 
 
 def jacobi_body(
-    side_ref, gram_refs, slow_ref, fast_ref, sums_ref, gram_a, gram_b, basis_a, basis_b, cos_buf, sin_buf
+    plan_ref, gram_refs, slow_ref, fast_ref, send_ref, sums_ref,
+    gram_a, gram_b, basis_a, basis_b, cos_buf, sin_buf,
 ):
     size = gram_refs[0].shape[1]
     half = size // 2
@@ -253,12 +268,15 @@
     held = jnp.where(row_slot == 0, 0, 1 + (row_slot + (size - 2 - ROUNDS % (size - 1))) % (size - 1))
     basis = basis_a[...].reshape(size, size).astype(jnp.bfloat16)
     lanes = lax.broadcasted_iota(jnp.int32, (1, size), 1)
-    for index, ref in enumerate((slow_ref, fast_ref)):
-        wanted = send_columns(lanes, side_ref[2 * index], side_ref[2 * index + 1], half)
+    first_slow, slow_slot, fast_slot, _ = moves(plan_ref)
+    slow_base = jnp.where(first_slow, 0, half)
+    for ref, base, slot in ((slow_ref, slow_base, slow_slot), (fast_ref, half - slow_base, fast_slot)):
+        wanted = send_columns(lanes, base, slot, half)
         ref[...] = dot32(basis, onehot(held, wanted), ((0,), (0,))).astype(jnp.bfloat16)
-
-
-def jacobi(side, grams):
+    send_ref[...] = slow_ref[:, : 2 * LANES]
+
+
+def jacobi(plan, grams):
     size = grams[0].shape[1]
     groups = size // 2 // SUBS
     return pl.pallas_call(
@@ -266,11 +284,12 @@
         out_shape=(
             jax.ShapeDtypeStruct((size, size), jnp.bfloat16),
             jax.ShapeDtypeStruct((size, size), jnp.bfloat16),
+            jax.ShapeDtypeStruct((size, 2 * LANES), jnp.bfloat16),
             jax.ShapeDtypeStruct((SUBS, LANES), jnp.float32),
         ),
         in_specs=[pl.BlockSpec(memory_space=pltpu.SMEM)]
         + [pl.BlockSpec(memory_space=pltpu.VMEM)] * len(grams),
-        out_specs=[pl.BlockSpec(memory_space=pltpu.VMEM)] * 3,
+        out_specs=[pl.BlockSpec(memory_space=pltpu.VMEM)] * 4,
         scratch_shapes=[
             pltpu.VMEM((2, groups, SUBS, 4 * LANES), jnp.float32),
             pltpu.VMEM((2, groups, SUBS, 4 * LANES), jnp.float32),
@@ -281,10 +300,10 @@
         ],
         compiler_params=pltpu.CompilerParams(vmem_limit_bytes=VMEM_LIMIT),
         cost_estimate=pl.CostEstimate(
-            flops=ROUNDS * 20 * size * size * 30, bytes_accessed=8 * size * size, transcendentals=0
+            flops=size * size, bytes_accessed=8 * size * size, transcendentals=0
         ),
         name="jacobi_turns",
-    )(side, *grams)
+    )(plan, *grams)
 
 
 def gram_kernel(matrix_ref, packed_ref, upper_ref, corner_ref):
@@ -323,7 +342,7 @@
             pltpu.VMEM((2 * LANES, size), jnp.float32),
             pltpu.VMEM((LANES, LANES), jnp.float32),
         ],
-        compiler_params=pltpu.CompilerParams(vmem_limit_bytes=VMEM_LIMIT),
+        compiler_params=pltpu.CompilerParams(vmem_limit_bytes=GRAM_VMEM_LIMIT),
         cost_estimate=pl.CostEstimate(
             flops=2 * rows * size * size, bytes_accessed=2 * rows * size, transcendentals=0
         ),
@@ -332,28 +351,29 @@
 
 
 def rotate_kernel(matrix_ref, turn_ref, packed_ref):
-    rows = matrix_ref.shape[0]
-    half = rows // 2
-    top = dot32(matrix_ref[:half], turn_ref[:, : 2 * LANES])
-    low = dot32(matrix_ref[half:], turn_ref[:, LANES:])
-    packed_ref[:half] = top[:, LANES:].astype(jnp.bfloat16)
-    packed_ref[half:rows] = low[:, :LANES].astype(jnp.bfloat16)
-    packed_ref[rows:] = (top[:, :LANES] + low[:, LANES:]).astype(jnp.bfloat16)
-
-
-def rotate_rows(matrix, turn, start, count):
+    half = UNIT // 2
+    for unit in range(matrix_ref.shape[0] // UNIT):
+        start, at = unit * UNIT, unit * PACK
+        top = dot32(matrix_ref[start : start + half], turn_ref[:, : 2 * LANES])
+        low = dot32(matrix_ref[start + half : start + UNIT], turn_ref[:, LANES:])
+        packed_ref[at : at + half] = top[:, LANES:].astype(jnp.bfloat16)
+        packed_ref[at + half : at + UNIT] = low[:, :LANES].astype(jnp.bfloat16)
+        packed_ref[at + UNIT : at + PACK] = (top[:, :LANES] + low[:, LANES:]).astype(jnp.bfloat16)
+
+
+def rotate_rows(matrix, turn, start, count, tile):
     size = matrix.shape[1]
-    first = start // TILE
-    pack = TILE + TILE // 2
+    first = start // tile
+    pack = tile // UNIT * PACK
     return pl.pallas_call(
         rotate_kernel,
-        grid=(count // TILE,),
+        grid=(count // tile,),
         in_specs=[
-            pl.BlockSpec((TILE, size), lambda i: (first + i, 0)),
+            pl.BlockSpec((tile, size), lambda i: (first + i, 0)),
             pl.BlockSpec((size, size), lambda i: (0, 0)),
         ],
         out_specs=pl.BlockSpec((pack, LANES), lambda i: (i, 0)),
-        out_shape=jax.ShapeDtypeStruct((count // TILE * pack, LANES), jnp.bfloat16),
+        out_shape=jax.ShapeDtypeStruct((count // UNIT * PACK, LANES), jnp.bfloat16),
         compiler_params=pltpu.CompilerParams(vmem_limit_bytes=VMEM_LIMIT),
         cost_estimate=pl.CostEstimate(
             flops=4 * count * size * LANES, bytes_accessed=3 * count * size, transcendentals=0
@@ -362,57 +382,63 @@
     )(matrix, turn)
 
 
-def low_lanes(slot, rows):
-    lane = lax.broadcasted_iota(jnp.int32, (rows, LANES), 1)
-    return (lane // (LANES // 2)) == slot
-
-
-def place_main(slot, out_ref, slow_main, fast_main):
+def place_main(slot, out_ref, rows, slow_main, fast_main):
     @pl.when(slot == 0)
     def _():
-        out_ref[:, :LANES] = slow_main
-        out_ref[:, 2 * LANES :] = fast_main
+        out_ref[rows, :LANES] = slow_main
+        out_ref[rows, 2 * LANES :] = fast_main
 
     @pl.when(slot != 0)
     def _():
-        out_ref[:, :LANES] = fast_main
-        out_ref[:, 2 * LANES :] = slow_main
-
-
-def place_kernel(slot_ref, slow_ref, fast_ref, *refs):
+        out_ref[rows, :LANES] = fast_main
+        out_ref[rows, 2 * LANES :] = slow_main
+
+
+def slot_lanes(slot):
+    lane = lax.broadcasted_iota(jnp.int32, (UNIT // 2, LANES), 1)
+    return (lane // (LANES // 2)) == slot
+
+
+def place_kernel(plan_ref, slow_ref, fast_ref, *refs):
     out_ref = refs[-1]
-    rows = out_ref.shape[0]
-    half = rows // 2
-    slot = slot_ref[0]
-    place_main(slot, out_ref, slow_ref[:rows], fast_ref[:rows])
-    slow = slow_ref[rows:].astype(jnp.float32)
-    fast = fast_ref[rows:].astype(jnp.float32)
-    mask = low_lanes(slot, half)
+    half = UNIT // 2
+    slot = moves(plan_ref)[3]
+    mask = slot_lanes(slot)
     middle = slice(LANES, 2 * LANES)
-    out_ref[:half, middle] = jnp.where(mask, slow, fast).astype(jnp.bfloat16)
-    swapped = pltpu.roll(jnp.where(mask, fast, slow), LANES // 2, 1)
-    out_ref[half:, middle] = swapped.astype(jnp.bfloat16)
-
-
-def raw_kernel(slot_ref, raw_ref, turn_ref, fast_ref, *refs):
+    for unit in range(out_ref.shape[0] // UNIT):
+        start, at = unit * UNIT, unit * PACK
+        main, rest = slice(at, at + UNIT), slice(at + UNIT, at + PACK)
+        place_main(slot, out_ref, slice(start, start + UNIT), slow_ref[main], fast_ref[main])
+        slow = slow_ref[rest].astype(jnp.float32)
+        fast = fast_ref[rest].astype(jnp.float32)
+        out_ref[start : start + half, middle] = jnp.where(mask, slow, fast).astype(jnp.bfloat16)
+        swapped = pltpu.roll(jnp.where(mask, fast, slow), LANES // 2, 1)
+        out_ref[start + half : start + UNIT, middle] = swapped.astype(jnp.bfloat16)
+
+
+def raw_kernel(plan_ref, raw_ref, turn_ref, fast_ref, *refs):
     out_ref = refs[-1]
-    rows = out_ref.shape[0]
-    half = rows // 2
-    slot = slot_ref[0]
-    turned = dot32(raw_ref[...], turn_ref[...])
-    place_main(slot, out_ref, turned[:, LANES:].astype(jnp.bfloat16), fast_ref[:rows])
-    fast = fast_ref[rows:].astype(jnp.float32)
-    mask = low_lanes(slot, half)
+    half = UNIT // 2
+    slot = moves(plan_ref)[3]
+    mask = slot_lanes(slot)
     middle = slice(LANES, 2 * LANES)
-    out_ref[:half, middle] = jnp.where(mask, turned[:half, :LANES], fast).astype(jnp.bfloat16)
-    swapped = pltpu.roll(fast, LANES // 2, 1)
-    out_ref[half:, middle] = jnp.where(mask, turned[half:, :LANES], swapped).astype(jnp.bfloat16)
-
-
-def fill_rows(kernel, slot, sources, specs, fast, held, shape, start, count):
-    first = start // TILE
-    pack = TILE + TILE // 2
-    operands = [slot, *sources, fast]
+    for unit in range(out_ref.shape[0] // UNIT):
+        start, at = unit * UNIT, unit * PACK
+        rows = slice(start, start + UNIT)
+        turned = dot32(raw_ref[rows], turn_ref[...])
+        main = turned[:, LANES:].astype(jnp.bfloat16)
+        place_main(slot, out_ref, rows, main, fast_ref[at : at + UNIT])
+        fast = fast_ref[at + UNIT : at + PACK].astype(jnp.float32)
+        top = jnp.where(mask, turned[:half, :LANES], fast)
+        out_ref[start : start + half, middle] = top.astype(jnp.bfloat16)
+        low = jnp.where(mask, turned[half:, :LANES], pltpu.roll(fast, LANES // 2, 1))
+        out_ref[start + half : start + UNIT, middle] = low.astype(jnp.bfloat16)
+
+
+def fill_rows(kernel, plan, sources, specs, fast, held, shape, start, count, tile):
+    first = start // tile
+    pack = tile // UNIT * PACK
+    operands = [plan, *sources, fast]
     in_specs = [
         pl.BlockSpec(memory_space=pltpu.SMEM),
         *specs,
@@ -425,9 +451,9 @@
         in_specs.append(pl.BlockSpec(memory_space=pl.ANY))
     return pl.pallas_call(
         kernel,
-        grid=(count // TILE,),
+        grid=(count // tile,),
         in_specs=in_specs,
-        out_specs=pl.BlockSpec((TILE, shape[1]), lambda i: (first + i, 0)),
+        out_specs=pl.BlockSpec((tile, shape[1]), lambda i: (first + i, 0)),
         out_shape=jax.ShapeDtypeStruct(shape, jnp.bfloat16),
         input_output_aliases=aliases,
         compiler_params=pltpu.CompilerParams(vmem_limit_bytes=VMEM_LIMIT),
@@ -451,67 +477,51 @@
     return source ^ 1
 
 
-def sends_and_slot(plan):
-    count = lax.axis_size("blk")
-    position = lax.axis_index("blk")
-    step = 2 * (position % 2) - 1
-    slow_dev = (position + step + count) % count
-    mine = lax.dynamic_slice_in_dim(plan, 2 * position, 2)
-    theirs = lax.dynamic_slice_in_dim(plan, 2 * slow_dev, 2)
-    first_slow = mine[0] // 2 == slow_dev
-    slow_to = jnp.where(first_slow, mine[0], mine[1])
-    fast_to = jnp.where(first_slow, mine[1], mine[0])
-    in_slot = jnp.where(theirs[0] // 2 == position, theirs[0], theirs[1]) % 2
-    return first_slow, slow_to % 2, fast_to % 2, in_slot
+def sum_over(values, axis):
+    count = lax.axis_size(axis)
+    step = 1
+    while step < count:
+        values = values + swapped_with(values, axis, lambda source, _, step=step: source ^ step)
+        step *= 2
+    return values
 
 
 def on_device(matrix, plan):
     rows, size = matrix.shape
-    width = size // 2
-    first_slow, slow_slot, fast_slot, in_slot = sends_and_slot(plan)
-    zero = jnp.zeros((), jnp.int32)
-    side = jnp.stack([
-        jnp.where(first_slow, zero, width), slow_slot, jnp.where(first_slow, width, zero), fast_slot
-    ]).astype(jnp.int32)
-    slot = in_slot.astype(jnp.int32)[None]
-
     raw = swapped_with(matrix[:RAW_ROWS], "blk", slow_partner)
     own = gram_blocks(matrix)
     if lax.axis_size("rows") == 2:
         grams = [own, swapped_with(own, "rows", fast_partner)]
     else:
         grams = [lax.psum(own, "rows")]
-    slow_turn, fast_turn, sums = jacobi(side, grams)
-    totals = jnp.sum(lax.all_gather(sums, "blk"), axis=0)
+    slow_turn, fast_turn, send_turn, sums = jacobi(plan, grams)
+
+    their_turn = swapped_with(send_turn, "blk", slow_partner)
+    spans = [
+        (RAW_ROWS, FIRST_ROWS, FIRST_ROWS // 3),
+        (RAW_ROWS + FIRST_ROWS, rows - RAW_ROWS - FIRST_ROWS, RAW_ROWS),
+    ]
+    packs = [rotate_rows(matrix, slow_turn, *span) for span in spans]
+    arrived = [swapped_with(pack, "blk", slow_partner) for pack in packs]
+    fast_turn, raw, _ = lax.optimization_barrier((fast_turn, raw, packs))
+    fast_pack = rotate_rows(matrix, fast_turn, 0, rows, rows // 4)
+    fast = swapped_with(fast_pack, "blk", fast_partner)
+    sums, _ = lax.optimization_barrier((sums, fast_pack))
+    totals = sum_over(sums, "blk")
     off_ratio = jnp.sqrt(totals[0, 0] / totals[1, 0])
 
-    their_turn = swapped_with(slow_turn[:, : 2 * LANES], "blk", slow_partner)
-    spans = [(RAW_ROWS, FIRST_ROWS), (RAW_ROWS + FIRST_ROWS, rows - RAW_ROWS - FIRST_ROWS)]
-    arrived = [
-        swapped_with(rotate_rows(matrix, slow_turn, start, count), "blk", slow_partner)
-        for start, count in spans
+    shape = (rows, size)
+    raw_specs = [
+        pl.BlockSpec((UNIT, size), lambda i: (i, 0)),
+        pl.BlockSpec((size, 2 * LANES), lambda i: (0, 0)),
     ]
-    fast = swapped_with(rotate_rows(matrix, fast_turn, 0, rows), "blk", fast_partner)
-    shape = (rows, size)
-    pack = TILE + TILE // 2
     result = fill_rows(
-        raw_kernel,
-        slot,
-        [raw, their_turn],
-        [
-            pl.BlockSpec((TILE, size), lambda i: (i, 0)),
-            pl.BlockSpec((size, 2 * LANES), lambda i: (0, 0)),
-        ],
-        fast, None, shape, 0, RAW_ROWS,
+        raw_kernel, plan, [raw, their_turn], raw_specs, fast, None, shape, 0, RAW_ROWS, UNIT
     )
-    for (start, count), slow in zip(spans, arrived):
-        result = fill_rows(
-            place_kernel,
-            slot,
-            [slow],
-            [pl.BlockSpec((pack, LANES), lambda i: (i, 0))],
-            fast, result, shape, start, count,
-        )
+    for span, slow in zip(spans, arrived):
+        pack = span[2] // UNIT * PACK
+        specs = [pl.BlockSpec((pack, LANES), lambda i: (i, 0))]
+        result = fill_rows(place_kernel, plan, [slow], specs, fast, result, shape, *span)
     return result, off_ratio
 
 

time: 135 us -> 112 us (0.83)
  the two profiles are of different devices: /device:TPU:1 before, /device:TPU:0 now
where the time goes in v4:
time: 112 us
  waiting for transfers between devices  54 us (48%)
  Pallas kernels  31 us (28%)
  starting transfers between devices  18.7 us (17%)
  local copies, waits for them, and re-layouts  5.07 us (5%)
  between operations  3.24 us (3%)
    ppermute x10, waiting for transfers between devices, swapped_with(): lax.ppermute(value, axis, [(source, partner(source, count)) for source in...  54 us
    ppermute x10, starting transfers between devices, swapped_with(): lax.ppermute(value, axis, [(source, partner(source, count)) for source in...  18.7 us
    pallas_call x1, Pallas kernels, jacobi(): pl.pallas_call(jacobi_kernel, out_shape=(jax.ShapeDtypeStruct((size, size...  12.7 us
    pallas_call x3, Pallas kernels, fill_rows(): pl.pallas_call(kernel, grid=(count // tile,), in_specs=in_specs, out_spec...  7.03 us
    pallas_call x1, Pallas kernels, gram_blocks(): pl.pallas_call(gram_kernel, grid=(rows // GRAM_TILE,), in_specs=[pl.Block...  6.64 us
    pallas_call x3, Pallas kernels, rotate_rows(): pl.pallas_call(rotate_kernel, grid=(count // tile,), in_specs=[pl.BlockSp...  4.58 us
    unnamed x6, local copies, waits for them, and re-layouts  3.33 us
  transfers between devices with their start and end apart: 10, of which 5 were waited for; matrix products, arithmetic and copies ran while one was open for 0% of the time, Pallas kernels for 24%

profile of v4, /device:TPU:0, one launch (start us, length us, event | category | flops | bytes accessed | tf_op | source)
XLA Modules:
  0.0 112.0 jit_solution(2948082343174875436)
XLA Ops:
  0.6 0.0 copy-start.2
  0.6 1.2 %slice.9 = bf16[1024,384]{1,0:T(8,128)(2,1)S(1)} slice(bf16[6144,384]{1,0:T(8,128)(2,1)} %matrix_ref.7), slice={[0:1024], [0:384]} | slice | bytes 1572864 | tf_op jit(solution)/shard_map/slice | solution.py:491
  1.9 5.5 %collective-permute-start.2 = (bf16[1024,384]{1,0:T(8,128)(2,1)S(1)}, bf16[1024,384]{1,0:T(8,128)(2,1)S(1)}, u32[]{:S(2)}, u32[]{:S(2)}) collective-permute-start(bf16[1024,384]{1,0:T(8,128)(2,1)S(1)} %slice.9), channel_id=1, source_target_pairs={{0,30},{2,4},{4,2},{6,8},{8,6},{10,12},{12,10},{14,16},{16,14},{18... | collective-permute-start | bytes 2359304 | tf_op jit(solution)/shard_map/ppermute | solution.py:469
  7.4 6.6 %gram_blocks.1.refs_0_ = f32[256,384]{1,0:T(8,128)} custom-call(bf16[6144,384]{1,0:T(8,128)(2,1)} %matrix_ref.7), custom_call_target="tpu_custom_call" | custom-call | flops 1811939328 | bytes 4718592 | tf_op jit(solution)/shard_map/gram_blocks/pallas_call | solution.py:335
  14.0 1.5 %collective-permute-start = (f32[256,384]{1,0:T(8,128)}, f32[256,384]{1,0:T(8,128)S(1)}, u32[]{:S(2)}, u32[]{:S(2)}) collective-permute-start(f32[256,384]{1,0:T(8,128)} %gram_blocks.1.refs_0_), channel_id=1, source_target_pairs={{0,1},{1,0},{2,3},{3,2},{4,5},{5,4},{6,7},{7,6},{8,9},{9,8},{10,11... | collective-permute-start | bytes 1179656 | tf_op jit(solution)/shard_map/ppermute | solution.py:469
  15.5 7.4 %collective-permute-done.refs_1_ = f32[256,384]{1,0:T(8,128)S(1)} collective-permute-done((f32[256,384]{1,0:T(8,128)}, f32[256,384]{1,0:T(8,128)S(1)}, u32[]{:S(2)}, u32[]{:S(2)}) %collective-permute-start) | collective-permute-done | bytes 393248 | tf_op jit(solution)/shard_map/ppermute | solution.py:469
  22.9 0.0 copy-done.2
  22.9 0.0 copy-start.1
  22.9 1.0 copy-done.1
  23.9 12.7 %jacobi_turns.1 = (bf16[384,384]{1,0:T(8,128)(2,1)S(1)}, bf16[384,384]{1,0:T(8,128)(2,1)S(1)}, bf16[384,256]{1,0:T(8,128)(2,1)S(1)}, f32[8,128]{1,0:T(8,128)S(1)}) custom-call(s32[32]{0:T(128)S(1)} %copy-done.2, f32[256,384]{1,0:T(8,128)S(1)} %copy-done.1, f32[256,384]{1,0:T(8,128)S(1)} %collective-permute-done.refs_1_), custom_call_target="tpu_custom_call" | custom-call | flops 147456 | bytes 1179648 | tf_op jit(solution)/shard_map/jacobi_turns/pallas_call | solution.py:282
  36.6 0.0 copy-start
  36.6 2.3 %copy-done = bf16[6144,384]{1,0:T(8,128)(2,1)S(1)} copy-done((bf16[6144,384]{1,0:T(8,128)(2,1)S(1)}, bf16[6144,384]{1,0:T(8,128)(2,1)}, u32[]{:S(2)}) %copy-start) | copy-done | bytes 4718616
  39.0 0.9 rotate_rows.3
  39.8 1.3 %rotate_rows.4 = bf16[4608,128]{1,0:T(8,128)(2,1)S(1)} custom-call(bf16[6144,384]{1,0:T(8,128)(2,1)S(1)} %copy-done, bf16[384,384]{1,0:T(8,128)(2,1)S(1)} %get-tuple-element.9.turn_ref), custom_call_target="tpu_custom_call" | custom-call | flops 603979776 | bytes 3538944 | tf_op jit(solution)/shard_map/rotate_rows/pallas_call | solution.py:368
  41.2 0.0 collective-permute-done.2.raw_ref
  41.2 2.4 %rotate_rows.5 = bf16[9216,128]{1,0:T(8,128)(2,1)S(1)} custom-call(bf16[6144,384]{1,0:T(8,128)(2,1)S(1)} %copy-done, bf16[384,384]{1,0:T(8,128)(2,1)S(1)} %get-tuple-element.11.turn_ref), custom_call_target="tpu_custom_call" | custom-call | flops 1207959552 | bytes 7077888 | tf_op jit(solution)/shard_map/rotate_rows/pallas_call | solution.py:368
  43.6 0.1 collective-permute-start.3
  43.6 3.0 %collective-permute-start.4 = (bf16[4608,128]{1,0:T(8,128)(2,1)S(1)}, bf16[4608,128]{1,0:T(8,128)(2,1)S(1)}, u32[]{:S(2)}, u32[]{:S(2)}) collective-permute-start(bf16[4608,128]{1,0:T(8,128)(2,1)S(1)} %rotate_rows.4), channel_id=1, source_target_pairs={{0,30},{2,4},{4,2},{6,8},{8,6},{10,12},{12,10},{14,16},{16,14},{18... | collective-permute-start | bytes 3538952 | tf_op jit(solution)/shard_map/ppermute | solution.py:469
  46.7 1.5 %collective-permute-start.1 = (bf16[3072,128]{1,0:T(8,128)(2,1)S(1)}, bf16[3072,128]{1,0:T(8,128)(2,1)S(1)}, u32[]{:S(2)}, u32[]{:S(2)}) collective-permute-start(bf16[3072,128]{1,0:T(8,128)(2,1)S(1)} %rotate_rows.3), channel_id=1, source_target_pairs={{0,30},{2,4},{4,2},{6,8},{8,6},{10,12},{12,10},{14,16},{16,14},{18... | collective-permute-start | bytes 2359304 | tf_op jit(solution)/shard_map/ppermute | solution.py:469
  48.2 3.0 %collective-permute-start.5 = (bf16[384,256]{1,0:T(8,128)(2,1)S(1)}, bf16[384,256]{1,0:T(8,128)(2,1)S(1)}, u32[]{:S(2)}, u32[]{:S(2)}) collective-permute-start(bf16[384,256]{1,0:T(8,128)(2,1)S(1)} %get-tuple-element.13), channel_id=1, source_target_pairs={{0,30},{2,4},{4,2},{6,8},{8,6},{10,12},{12,10},{14,16},{16,14},{18... | collective-permute-start | bytes 589832 | tf_op jit(solution)/shard_map/ppermute | solution.py:469
  51.1 0.0 collective-permute-start.6
  51.1 1.2 %collective-permute-done.6 = f32[8,128]{1,0:T(8,128)S(1)} collective-permute-done((f32[8,128]{1,0:T(8,128)S(1)}, f32[8,128]{1,0:T(8,128)S(1)}, u32[]{:S(2)}, u32[]{:S(2)}) %collective-permute-start.6) | collective-permute-done | bytes 4128 | tf_op jit(solution)/shard_map/ppermute | solution.py:469
  52.3 0.0 collective-permute-start.7
  52.3 41.4 %collective-permute-done.7 = f32[8,128]{1,0:T(8,128)S(1)} collective-permute-done((f32[8,128]{1,0:T(8,128)S(1)}, f32[8,128]{1,0:T(8,128)S(1)}, u32[]{:S(2)}, u32[]{:S(2)}) %collective-permute-start.7) | collective-permute-done | bytes 4128 | tf_op jit(solution)/shard_map/ppermute | solution.py:469
  93.8 1.6 %collective-permute-start.8 = (f32[8,128]{1,0:T(8,128)S(1)}, f32[8,128]{1,0:T(8,128)S(1)}, u32[]{:S(2)}, u32[]{:S(2)}) collective-permute-start(f32[8,128]{1,0:T(8,128)S(1)} %add.13), channel_id=1, source_target_pairs={{0,8},{2,10},{4,12},{6,14},{8,0},{10,2},{12,4},{14,6},{16,24},{18,... | collective-permute-start | bytes 12296 | tf_op jit(solution)/shard_map/ppermute | solution.py:469
  95.3 2.0 %collective-permute-done.8 = f32[8,128]{1,0:T(8,128)S(1)} collective-permute-done((f32[8,128]{1,0:T(8,128)S(1)}, f32[8,128]{1,0:T(8,128)S(1)}, u32[]{:S(2)}, u32[]{:S(2)}) %collective-permute-start.8) | collective-permute-done | bytes 4128 | tf_op jit(solution)/shard_map/ppermute | solution.py:469
  97.4 2.6 %collective-permute-start.9 = (f32[8,128]{1,0:T(8,128)S(1)}, f32[8,128]{1,0:T(8,128)S(1)}, u32[]{:S(2)}, u32[]{:S(2)}) collective-permute-start(f32[8,128]{1,0:T(8,128)S(1)} %add.14), channel_id=1, source_target_pairs={{0,16},{2,18},{4,20},{6,22},{8,24},{10,26},{12,28},{14,30},{16,0},... | collective-permute-start | bytes 12296 | tf_op jit(solution)/shard_map/ppermute | solution.py:469
  99.9 1.9 %collective-permute-done.9 = f32[8,128]{1,0:T(8,128)S(1)} collective-permute-done((f32[8,128]{1,0:T(8,128)S(1)}, f32[8,128]{1,0:T(8,128)S(1)}, u32[]{:S(2)}, u32[]{:S(2)}) %collective-permute-start.9) | collective-permute-done | bytes 4128 | tf_op jit(solution)/shard_map/ppermute | solution.py:469
  101.9 0.5 fusion
  103.8 0.0 collective-permute-done.5.turn_ref
  103.8 0.0 collective-permute-done.3.fast_ref
  103.8 2.1 %fill_rows.3.refs_0_ = bf16[6144,384]{1,0:T(8,128)(2,1)} custom-call(s32[32]{0:T(128)S(1)} %copy-done.2, bf16[1024,384]{1,0:T(8,128)(2,1)S(1)} %collective-permute-done.2.raw_ref, bf16[384,256]{1,0:T(8,128)(2,1)S(1)} %collective-permute-done.5.turn_ref, bf16[9216,128]{1,0:T(8,128)(2,1)S(1)} %collective-permute-done.3.fast_ref), custom_call_target="tpu_custom_call" | custom-call | flops 393216 | bytes 1572864 | tf_op jit(solution)/shard_map/fill_rows/pallas_call | solution.py:452
  105.9 0.0 collective-permute-done.4.slow_ref
  105.9 2.9 %fill_rows.4.refs_0_ = bf16[6144,384]{1,0:T(8,128)(2,1)} custom-call(s32[32]{0:T(128)S(1)} %copy-done.2, bf16[4608,128]{1,0:T(8,128)(2,1)S(1)} %collective-permute-done.4.slow_ref, bf16[9216,128]{1,0:T(8,128)(2,1)S(1)} %collective-permute-done.3.fast_ref, bf16[6144,384]{1,0:T(8,128)(2,1)} %fill_rows.3.refs_0_), custom_call_target="tpu_custom_call", output_to_operand_aliasing={{}: (3, {})} | custom-call | flops 1179648 | bytes 4718592 | tf_op jit(solution)/shard_map/fill_rows/pallas_call | solution.py:452
  108.8 0.0 collective-permute-done.1.slow_ref
  108.8 2.0 %fill_rows.5 = bf16[6144,384]{1,0:T(8,128)(2,1)} custom-call(s32[32]{0:T(128)S(1)} %copy-done.2, bf16[3072,128]{1,0:T(8,128)(2,1)S(1)} %collective-permute-done.1.slow_ref, bf16[9216,128]{1,0:T(8,128)(2,1)S(1)} %collective-permute-done.3.fast_ref, bf16[6144,384]{1,0:T(8,128)(2,1)} %fill_rows.4.refs_0_), custom_call_target="tpu_custom_call", output_to_operand_aliasing={{}: (3, {})} | custom-call | flops 786432 | bytes 3145728 | tf_op jit(solution)/shard_map/fill_rows/pallas_call | solution.py:452
  (4 shorter events, 0.0 us)
Async XLA Ops:
  0.6 22.3 %copy-start.2 = (s32[32]{0:T(128)S(1)}, s32[32]{0:T(128)}, u32[]{:S(2)}) copy-start(s32[32]{0:T(128)} %plan_ref.7) | copy-start | bytes 388
  1.9 39.3 %collective-permute-start.2 = (bf16[1024,384]{1,0:T(8,128)(2,1)S(1)}, bf16[1024,384]{1,0:T(8,128)(2,1)S(1)}, u32[]{:S(2)}, u32[]{:S(2)}) collective-permute-start(bf16[1024,384]{1,0:T(8,128)(2,1)S(1)} %slice.9), channel_id=1, source_target_pairs={{0,30},{2,4},{4,2},{6,8},{8,6},{10,12},{12,10},{14,16},{16,14},{18... | collective-permute-start | bytes 2359304 | tf_op jit(solution)/shard_map/ppermute | solution.py:469
  14.0 8.9 %collective-permute-start = (f32[256,384]{1,0:T(8,128)}, f32[256,384]{1,0:T(8,128)S(1)}, u32[]{:S(2)}, u32[]{:S(2)}) collective-permute-start(f32[256,384]{1,0:T(8,128)} %gram_blocks.1.refs_0_), channel_id=1, source_target_pairs={{0,1},{1,0},{2,3},{3,2},{4,5},{5,4},{6,7},{7,6},{8,9},{9,8},{10,11... | collective-permute-start | bytes 1179656 | tf_op jit(solution)/shard_map/ppermute | solution.py:469
  22.9 1.0 copy-start.1
  36.6 2.3 %copy-start = (bf16[6144,384]{1,0:T(8,128)(2,1)S(1)}, bf16[6144,384]{1,0:T(8,128)(2,1)}, u32[]{:S(2)}) copy-start(bf16[6144,384]{1,0:T(8,128)(2,1)} %matrix_ref.7) | copy-start | bytes 14155780
  43.6 60.2 %collective-permute-start.3 = (bf16[9216,128]{1,0:T(8,128)(2,1)S(1)}, bf16[9216,128]{1,0:T(8,128)(2,1)S(1)}, u32[]{:S(2)}, u32[]{:S(2)}) collective-permute-start(bf16[9216,128]{1,0:T(8,128)(2,1)S(1)} %rotate_rows.5), channel_id=1, source_target_pairs={{0,2},{2,0},{4,6},{6,4},{8,10},{10,8},{12,14},{14,12},{16,18},{18,... | collective-permute-start | bytes 7077896 | tf_op jit(solution)/shard_map/ppermute | solution.py:469
  43.6 62.3 %collective-permute-start.4 = (bf16[4608,128]{1,0:T(8,128)(2,1)S(1)}, bf16[4608,128]{1,0:T(8,128)(2,1)S(1)}, u32[]{:S(2)}, u32[]{:S(2)}) collective-permute-start(bf16[4608,128]{1,0:T(8,128)(2,1)S(1)} %rotate_rows.4), channel_id=1, source_target_pairs={{0,30},{2,4},{4,2},{6,8},{8,6},{10,12},{12,10},{14,16},{16,14},{18... | collective-permute-start | bytes 3538952 | tf_op jit(solution)/shard_map/ppermute | solution.py:469
  46.7 62.1 %collective-permute-start.1 = (bf16[3072,128]{1,0:T(8,128)(2,1)S(1)}, bf16[3072,128]{1,0:T(8,128)(2,1)S(1)}, u32[]{:S(2)}, u32[]{:S(2)}) collective-permute-start(bf16[3072,128]{1,0:T(8,128)(2,1)S(1)} %rotate_rows.3), channel_id=1, source_target_pairs={{0,30},{2,4},{4,2},{6,8},{8,6},{10,12},{12,10},{14,16},{16,14},{18... | collective-permute-start | bytes 2359304 | tf_op jit(solution)/shard_map/ppermute | solution.py:469
  48.2 55.6 %collective-permute-start.5 = (bf16[384,256]{1,0:T(8,128)(2,1)S(1)}, bf16[384,256]{1,0:T(8,128)(2,1)S(1)}, u32[]{:S(2)}, u32[]{:S(2)}) collective-permute-start(bf16[384,256]{1,0:T(8,128)(2,1)S(1)} %get-tuple-element.13), channel_id=1, source_target_pairs={{0,30},{2,4},{4,2},{6,8},{8,6},{10,12},{12,10},{14,16},{16,14},{18... | collective-permute-start | bytes 589832 | tf_op jit(solution)/shard_map/ppermute | solution.py:469
  51.1 1.2 %collective-permute-start.6 = (f32[8,128]{1,0:T(8,128)S(1)}, f32[8,128]{1,0:T(8,128)S(1)}, u32[]{:S(2)}, u32[]{:S(2)}) collective-permute-start(f32[8,128]{1,0:T(8,128)S(1)} %get-tuple-element.15), channel_id=1, source_target_pairs={{0,2},{2,0},{4,6},{6,4},{8,10},{10,8},{12,14},{14,12},{16,18},{18,... | collective-permute-start | bytes 12296 | tf_op jit(solution)/shard_map/ppermute | solution.py:469
  52.3 41.4 %collective-permute-start.7 = (f32[8,128]{1,0:T(8,128)S(1)}, f32[8,128]{1,0:T(8,128)S(1)}, u32[]{:S(2)}, u32[]{:S(2)}) collective-permute-start(f32[8,128]{1,0:T(8,128)S(1)} %add.12), channel_id=1, source_target_pairs={{0,4},{2,6},{4,0},{6,2},{8,12},{10,14},{12,8},{14,10},{16,20},{18,... | collective-permute-start | bytes 12296 | tf_op jit(solution)/shard_map/ppermute | solution.py:469
  93.8 3.6 %collective-permute-start.8 = (f32[8,128]{1,0:T(8,128)S(1)}, f32[8,128]{1,0:T(8,128)S(1)}, u32[]{:S(2)}, u32[]{:S(2)}) collective-permute-start(f32[8,128]{1,0:T(8,128)S(1)} %add.13), channel_id=1, source_target_pairs={{0,8},{2,10},{4,12},{6,14},{8,0},{10,2},{12,4},{14,6},{16,24},{18,... | collective-permute-start | bytes 12296 | tf_op jit(solution)/shard_map/ppermute | solution.py:469
  97.4 4.5 %collective-permute-start.9 = (f32[8,128]{1,0:T(8,128)S(1)}, f32[8,128]{1,0:T(8,128)S(1)}, u32[]{:S(2)}, u32[]{:S(2)}) collective-permute-start(f32[8,128]{1,0:T(8,128)S(1)} %add.14), channel_id=1, source_target_pairs={{0,16},{2,18},{4,20},{6,22},{8,24},{10,26},{12,28},{14,30},{16,0},... | collective-permute-start | bytes 12296 | tf_op jit(solution)/shard_map/ppermute | solution.py:469

commit v5 on v4

--- a/solution.py
+++ b/solution.py
@@ -1,3 +1,5 @@
+import functools
+
 import jax
 import jax.numpy as jnp
 from jax import lax
@@ -10,11 +12,13 @@
 SUBS = 8
 UNIT = 512
 PACK = UNIT + UNIT // 2
-GRAM_TILE = 1024
-RAW_ROWS = 1024
+GRAM_TILE = 512
+RAW_ROWS = 1536
 FIRST_ROWS = 3072
+ROTATE_TILE = 1536
+FILL_TILE = 512
 VMEM_LIMIT = 32 * 1024 * 1024
-GRAM_VMEM_LIMIT = 60 * 1024 * 1024
+GRAM_VMEM_LIMIT = 58 * 1024 * 1024
 
 
 def split_three(values):
@@ -103,11 +107,11 @@
 
 
 def jacobi_kernel(plan_ref, *refs):
-    jacobi_body(plan_ref, refs[:-10], *refs[-10:])
+    jacobi_body(plan_ref, refs[:-9], *refs[-9:])
 
 
 def jacobi_body(
-    plan_ref, gram_refs, slow_ref, fast_ref, send_ref, sums_ref,
+    plan_ref, gram_refs, slow_ref, fast_ref, send_ref,
     gram_a, gram_b, basis_a, basis_b, cos_buf, sin_buf,
 ):
     size = gram_refs[0].shape[1]
@@ -132,12 +136,6 @@
     for other in gram_refs[1:]:
         packed = packed + other[...]
     gram_sum = full_gram(packed)
-    squares = gram_sum * gram_sum
-    rows = lax.broadcasted_iota(jnp.int32, (size, size), 0)
-    cols = lax.broadcasted_iota(jnp.int32, (size, size), 1)
-    diag_sq = jnp.sum(jnp.where(rows == cols, squares, 0.0), keepdims=True)
-    off_sq = jnp.sum(squares, keepdims=True) - diag_sq
-    sums_ref[...] = jnp.where(sub == 0, off_sq, diag_sq)
     for piece in split_three(gram_sum):
         moved = dot32(take_rows, piece).astype(jnp.bfloat16)
         arranged = arranged + dot32(moved, take_cols)
@@ -285,11 +283,10 @@
             jax.ShapeDtypeStruct((size, size), jnp.bfloat16),
             jax.ShapeDtypeStruct((size, size), jnp.bfloat16),
             jax.ShapeDtypeStruct((size, 2 * LANES), jnp.bfloat16),
-            jax.ShapeDtypeStruct((SUBS, LANES), jnp.float32),
         ),
         in_specs=[pl.BlockSpec(memory_space=pltpu.SMEM)]
         + [pl.BlockSpec(memory_space=pltpu.VMEM)] * len(grams),
-        out_specs=[pl.BlockSpec(memory_space=pltpu.VMEM)] * 4,
+        out_specs=[pl.BlockSpec(memory_space=pltpu.VMEM)] * 3,
         scratch_shapes=[
             pltpu.VMEM((2, groups, SUBS, 4 * LANES), jnp.float32),
             pltpu.VMEM((2, groups, SUBS, 4 * LANES), jnp.float32),
@@ -300,47 +297,88 @@
         ],
         compiler_params=pltpu.CompilerParams(vmem_limit_bytes=VMEM_LIMIT),
         cost_estimate=pl.CostEstimate(
-            flops=size * size, bytes_accessed=8 * size * size, transcendentals=0
+            flops=ROUNDS * 600 * size * size, bytes_accessed=8 * size * size, transcendentals=0
         ),
         name="jacobi_turns",
     )(plan, *grams)
 
 
-def gram_kernel(matrix_ref, packed_ref, upper_ref, corner_ref):
-    step = pl.program_id(0)
-    values = matrix_ref[...]
-    right = values[:, 2 * LANES :]
-    upper = dot32(values[:, : 2 * LANES], values, ((0,), (0,)))
-    corner = dot32(right, right, ((0,), (0,)))
-
-    @pl.when(step == 0)
-    def _():
-        upper_ref[...] = upper
-        corner_ref[...] = corner
-
-    @pl.when(step > 0)
-    def _():
-        upper_ref[...] += upper
-        corner_ref[...] += corner
-
-    @pl.when(step == pl.num_programs(0) - 1)
-    def _():
-        packed_ref[:LANES] = upper_ref[:LANES]
-        packed_ref[LANES:, : 2 * LANES] = upper_ref[LANES:, LANES:]
-        packed_ref[LANES:, 2 * LANES :] = corner_ref[...]
+def sums_kernel(*refs):
+    sums_ref = refs[-1]
+    packed = refs[0][...]
+    for other in refs[1:-1]:
+        packed = packed + other[...]
+    squares = packed * packed
+    total = jnp.zeros((1, 1), jnp.float32)
+    diag_sq = jnp.zeros((1, 1), jnp.float32)
+    rows = lax.broadcasted_iota(jnp.int32, (LANES, LANES), 0)
+    cols = lax.broadcasted_iota(jnp.int32, (LANES, LANES), 1)
+    for row, col, weight in (
+        (0, 0, 1.0), (0, 1, 2.0), (0, 2, 2.0), (1, 0, 1.0), (1, 1, 2.0), (1, 2, 1.0)
+    ):
+        block = squares[row * LANES : (row + 1) * LANES, col * LANES : (col + 1) * LANES]
+        total = total + weight * jnp.sum(block, keepdims=True)
+        if weight == 1.0:
+            diag_sq = diag_sq + jnp.sum(jnp.where(rows == cols, block, 0.0), keepdims=True)
+    sub = lax.broadcasted_iota(jnp.int32, (SUBS, LANES), 0)
+    sums_ref[...] = jnp.where(sub == 0, total - diag_sq, diag_sq)
+
+
+def gram_sums(grams):
+    return pl.pallas_call(
+        sums_kernel,
+        out_shape=jax.ShapeDtypeStruct((SUBS, LANES), jnp.float32),
+        in_specs=[pl.BlockSpec(memory_space=pltpu.VMEM)] * len(grams),
+        out_specs=pl.BlockSpec(memory_space=pltpu.VMEM),
+        name="gram_sums",
+    )(*grams)
+
+
+def gram_kernel(matrix_ref, packed_ref, raw_ref, held, upper_ref, corner_ref, sems, raw_sem):
+    rows = held.shape[0]
+    copies = []
+    for index in range(rows // GRAM_TILE):
+        part = pl.ds(index * GRAM_TILE, GRAM_TILE)
+        copies.append(pltpu.make_async_copy(matrix_ref.at[part], held.at[part], sems.at[index]))
+        copies[-1].start()
+    early = pl.ds(0, RAW_ROWS)
+    leave = pltpu.make_async_copy(held.at[early], raw_ref, raw_sem)
+    for index, copy in enumerate(copies):
+        copy.wait()
+        if (index + 1) * GRAM_TILE == RAW_ROWS:
+            leave.start()
+        values = held[index * GRAM_TILE : (index + 1) * GRAM_TILE]
+        right = values[:, 2 * LANES :]
+        upper = dot32(values[:, : 2 * LANES], values, ((0,), (0,)))
+        corner = dot32(right, right, ((0,), (0,)))
+        if index == 0:
+            upper_ref[...] = upper
+            corner_ref[...] = corner
+        else:
+            upper_ref[...] += upper
+            corner_ref[...] += corner
+    packed_ref[:LANES] = upper_ref[:LANES]
+    packed_ref[LANES:, : 2 * LANES] = upper_ref[LANES:, LANES:]
+    packed_ref[LANES:, 2 * LANES :] = corner_ref[...]
+    leave.wait()
 
 
 def gram_blocks(matrix):
     rows, size = matrix.shape
     return pl.pallas_call(
         gram_kernel,
-        grid=(rows // GRAM_TILE,),
-        in_specs=[pl.BlockSpec((GRAM_TILE, size), lambda i: (i, 0))],
-        out_specs=pl.BlockSpec((2 * LANES, size), lambda i: (0, 0)),
-        out_shape=jax.ShapeDtypeStruct((2 * LANES, size), jnp.float32),
+        in_specs=[pl.BlockSpec(memory_space=pl.ANY)],
+        out_specs=[pl.BlockSpec(memory_space=pltpu.VMEM), pl.BlockSpec(memory_space=pl.ANY)],
+        out_shape=(
+            jax.ShapeDtypeStruct((2 * LANES, size), jnp.float32),
+            jax.ShapeDtypeStruct((RAW_ROWS, size), jnp.bfloat16),
+        ),
         scratch_shapes=[
+            pltpu.VMEM((rows, size), jnp.bfloat16),
             pltpu.VMEM((2 * LANES, size), jnp.float32),
             pltpu.VMEM((LANES, LANES), jnp.float32),
+            pltpu.SemaphoreType.DMA((rows // GRAM_TILE,)),
+            pltpu.SemaphoreType.DMA,
         ],
         compiler_params=pltpu.CompilerParams(vmem_limit_bytes=GRAM_VMEM_LIMIT),
         cost_estimate=pl.CostEstimate(
@@ -350,36 +388,54 @@
     )(matrix)
 
 
-def rotate_kernel(matrix_ref, turn_ref, packed_ref):
+def pack_unit(values, turn, packed_ref, at):
     half = UNIT // 2
-    for unit in range(matrix_ref.shape[0] // UNIT):
-        start, at = unit * UNIT, unit * PACK
-        top = dot32(matrix_ref[start : start + half], turn_ref[:, : 2 * LANES])
-        low = dot32(matrix_ref[start + half : start + UNIT], turn_ref[:, LANES:])
-        packed_ref[at : at + half] = top[:, LANES:].astype(jnp.bfloat16)
-        packed_ref[at + half : at + UNIT] = low[:, :LANES].astype(jnp.bfloat16)
-        packed_ref[at + UNIT : at + PACK] = (top[:, :LANES] + low[:, LANES:]).astype(jnp.bfloat16)
-
-
-def rotate_rows(matrix, turn, start, count, tile):
-    size = matrix.shape[1]
-    first = start // tile
-    pack = tile // UNIT * PACK
+    top = dot32(values[:half], turn[:, : 2 * LANES])
+    low = dot32(values[half:], turn[:, LANES:])
+    packed_ref[at : at + half] = top[:, LANES:].astype(jnp.bfloat16)
+    packed_ref[at + half : at + UNIT] = low[:, :LANES].astype(jnp.bfloat16)
+    packed_ref[at + UNIT : at + PACK] = (top[:, :LANES] + low[:, LANES:]).astype(jnp.bfloat16)
+
+
+def rotate_kernel(ranges, matrix_ref, slow_ref, fast_ref, fast_pack_ref, *slow_packs):
+    step = pl.program_id(0)
+    units = matrix_ref.shape[0] // UNIT
+    for unit in range(units):
+        values = matrix_ref[unit * UNIT : (unit + 1) * UNIT]
+        pack_unit(values, fast_ref[...], fast_pack_ref, unit * PACK)
+    for (first, count), pack_ref in zip(ranges, slow_packs):
+        @pl.when((step >= first) & (step < first + count))
+        def _(pack_ref=pack_ref):
+            for unit in range(units):
+                values = matrix_ref[unit * UNIT : (unit + 1) * UNIT]
+                pack_unit(values, slow_ref[...], pack_ref, unit * PACK)
+
+
+def rotate_all(matrix, slow_turn, fast_turn, spans):
+    rows, size = matrix.shape
+    pack = ROTATE_TILE // UNIT * PACK
+    ranges = [(start // ROTATE_TILE, count // ROTATE_TILE) for start, count, _ in spans]
+    packs = [rows] + [count for _, count, _ in spans]
+    turn_spec = pl.BlockSpec((size, size), lambda i: (0, 0))
+
+    def slow_spec(first, count):
+        return pl.BlockSpec((pack, LANES), lambda i: (jnp.clip(i - first, 0, count - 1), 0))
+
     return pl.pallas_call(
-        rotate_kernel,
-        grid=(count // tile,),
-        in_specs=[
-            pl.BlockSpec((tile, size), lambda i: (first + i, 0)),
-            pl.BlockSpec((size, size), lambda i: (0, 0)),
+        functools.partial(rotate_kernel, ranges),
+        grid=(rows // ROTATE_TILE,),
+        in_specs=[pl.BlockSpec((ROTATE_TILE, size), lambda i: (i, 0)), turn_spec, turn_spec],
+        out_specs=[pl.BlockSpec((pack, LANES), lambda i: (i, 0))]
+        + [slow_spec(*part) for part in ranges],
+        out_shape=[
+            jax.ShapeDtypeStruct((count // UNIT * PACK, LANES), jnp.bfloat16) for count in packs
         ],
-        out_specs=pl.BlockSpec((pack, LANES), lambda i: (i, 0)),
-        out_shape=jax.ShapeDtypeStruct((count // UNIT * PACK, LANES), jnp.bfloat16),
         compiler_params=pltpu.CompilerParams(vmem_limit_bytes=VMEM_LIMIT),
         cost_estimate=pl.CostEstimate(
-            flops=4 * count * size * LANES, bytes_accessed=3 * count * size, transcendentals=0
+            flops=8 * rows * size * LANES, bytes_accessed=6 * rows * size, transcendentals=0
         ),
         name="rotate_rows",
-    )(matrix, turn)
+    )(matrix, slow_turn, fast_turn)
 
 
 def place_main(slot, out_ref, rows, slow_main, fast_main):
@@ -477,37 +533,34 @@
     return source ^ 1
 
 
-def sum_over(values, axis):
-    count = lax.axis_size(axis)
-    step = 1
-    while step < count:
-        values = values + swapped_with(values, axis, lambda source, _, step=step: source ^ step)
-        step *= 2
-    return values
+def add_swapped(values, step):
+    return values + swapped_with(values, "blk", lambda source, _: source ^ step)
 
 
 def on_device(matrix, plan):
     rows, size = matrix.shape
-    raw = swapped_with(matrix[:RAW_ROWS], "blk", slow_partner)
-    own = gram_blocks(matrix)
+    own, early = gram_blocks(matrix)
     if lax.axis_size("rows") == 2:
         grams = [own, swapped_with(own, "rows", fast_partner)]
     else:
         grams = [lax.psum(own, "rows")]
-    slow_turn, fast_turn, send_turn, sums = jacobi(plan, grams)
+    raw = swapped_with(early, "blk", slow_partner)
+    totals = add_swapped(gram_sums(grams), 2)
+    slow_turn, fast_turn, send_turn = jacobi(plan, grams)
+    slow_turn, totals = lax.optimization_barrier((slow_turn, totals))
 
     their_turn = swapped_with(send_turn, "blk", slow_partner)
-    spans = [
-        (RAW_ROWS, FIRST_ROWS, FIRST_ROWS // 3),
-        (RAW_ROWS + FIRST_ROWS, rows - RAW_ROWS - FIRST_ROWS, RAW_ROWS),
-    ]
-    packs = [rotate_rows(matrix, slow_turn, *span) for span in spans]
+    last_rows = rows - RAW_ROWS - FIRST_ROWS
+    spans = [(RAW_ROWS, FIRST_ROWS, ROTATE_TILE), (RAW_ROWS + FIRST_ROWS, last_rows, FILL_TILE)]
+    fast_pack, *packs = rotate_all(matrix, slow_turn, fast_turn, spans)
     arrived = [swapped_with(pack, "blk", slow_partner) for pack in packs]
-    fast_turn, raw, _ = lax.optimization_barrier((fast_turn, raw, packs))
-    fast_pack = rotate_rows(matrix, fast_turn, 0, rows, rows // 4)
+    fast_pack, raw = lax.optimization_barrier((fast_pack, raw))
     fast = swapped_with(fast_pack, "blk", fast_partner)
-    sums, _ = lax.optimization_barrier((sums, fast_pack))
-    totals = sum_over(sums, "blk")
+    step = 1
+    while step < lax.axis_size("blk"):
+        if step != 2:
+            totals = add_swapped(totals, step)
+        step *= 2
     off_ratio = jnp.sqrt(totals[0, 0] / totals[1, 0])
 
     shape = (rows, size)

time: 112 us -> 97.3 us (0.87)
  the two profiles are of different devices: /device:TPU:0 before, /device:TPU:1 now
where the time goes in v5:
time: 97.3 us; the launch traced here: 97.1 us
  waiting for transfers between devices  40.7 us (42%)
  Pallas kernels  32.4 us (33%)
  starting transfers between devices  17.4 us (18%)
  local copies, waits for them, and re-layouts  3.26 us (3%)
  between operations  3.23 us (3%)
    ppermute x10, waiting for transfers between devices, swapped_with(): lax.ppermute(value, axis, [(source, partner(source, count)) for source in...  40.7 us
    ppermute x10, starting transfers between devices, swapped_with(): lax.ppermute(value, axis, [(source, partner(source, count)) for source in...  17.4 us
    pallas_call x1, Pallas kernels, jacobi(): pl.pallas_call(jacobi_kernel, out_shape=(jax.ShapeDtypeStruct((size, size...  12.7 us
    pallas_call x3, Pallas kernels, fill_rows(): pl.pallas_call(kernel, grid=(count // tile,), in_specs=in_specs, out_spec...  7.6 us
    pallas_call x1, Pallas kernels, gram_blocks(): pl.pallas_call(gram_kernel, in_specs=[pl.BlockSpec(memory_space=pl.ANY)],...  6.19 us
    pallas_call x1, Pallas kernels, rotate_all(): pl.pallas_call(functools.partial(rotate_kernel, ranges), grid=(rows // RO...  4.08 us
    unnamed x12, local copies, waits for them, and re-layouts  2.74 us
  transfers between devices with their start and end apart: 10, of which 5 were waited for; matrix products, arithmetic and copies ran while one was open for 1% of the time, Pallas kernels for 25%

profile of v5, /device:TPU:1, one launch (start us, length us, event | category | flops | bytes accessed | tf_op | source)
XLA Modules:
  0.0 97.1 jit_solution(16699337410871708720)
XLA Ops:
  0.6 0.0 copy-start.3
  0.6 6.2 %gram_blocks.1 = (f32[256,384]{1,0:T(8,128)}, bf16[1536,384]{1,0:T(8,128)(2,1)}) custom-call(bf16[6144,384]{1,0:T(8,128)(2,1)} %matrix_ref.3), custom_call_target="tpu_custom_call" | custom-call | flops 1811939328 | bytes 4718592 | tf_op jit(solution)/shard_map/gram_blocks/pallas_call | solution.py:368
  6.8 2.7 %collective-permute-start.3 = (bf16[1536,384]{1,0:T(8,128)(2,1)}, bf16[1536,384]{1,0:T(8,128)(2,1)S(1)}, u32[]{:S(2)}, u32[]{:S(2)}) collective-permute-start(bf16[1536,384]{1,0:T(8,128)(2,1)} %get-tuple-element.20), channel_id=1, source_target_pairs={{0,30},{2,4},{4,2},{6,8},{8,6},{10,12},{12,10},{14,16},{16,14},{18... | collective-permute-start | bytes 3538952 | tf_op jit(solution)/shard_map/ppermute | solution.py:525
  9.5 1.2 %collective-permute-start = (f32[256,384]{1,0:T(8,128)}, f32[256,384]{1,0:T(8,128)S(1)}, u32[]{:S(2)}, u32[]{:S(2)}) collective-permute-start(f32[256,384]{1,0:T(8,128)} %get-tuple-element.14.refs_0_), channel_id=1, source_target_pairs={{0,1},{1,0},{2,3},{3,2},{4,5},{5,4},{6,7},{7,6},{8,9},{9,8},{10,11... | collective-permute-start | bytes 1179656 | tf_op jit(solution)/shard_map/ppermute | solution.py:525
  10.7 6.7 %collective-permute-done.refs_1_ = f32[256,384]{1,0:T(8,128)S(1)} collective-permute-done((f32[256,384]{1,0:T(8,128)}, f32[256,384]{1,0:T(8,128)S(1)}, u32[]{:S(2)}, u32[]{:S(2)}) %collective-permute-start) | collective-permute-done | bytes 393248 | tf_op jit(solution)/shard_map/ppermute | solution.py:525
  17.5 0.0 copy-start.1
  17.5 0.7 copy-done.1
  18.2 1.9 %gram_sums.1 = f32[8,128]{1,0:T(8,128)} custom-call(f32[256,384]{1,0:T(8,128)} %get-tuple-element.14.refs_0_, f32[256,384]{1,0:T(8,128)} %copy-done.1), custom_call_target="tpu_custom_call" | custom-call | tf_op jit(solution)/shard_map/gram_sums/pallas_call | solution.py:328
  20.1 4.1 %collective-permute-start.1 = (f32[8,128]{1,0:T(8,128)}, f32[8,128]{1,0:T(8,128)S(1)}, u32[]{:S(2)}, u32[]{:S(2)}) collective-permute-start(f32[8,128]{1,0:T(8,128)} %gram_sums.1), channel_id=1, source_target_pairs={{0,4},{2,6},{4,0},{6,2},{8,12},{10,14},{12,8},{14,10},{16,20},{18,... | collective-permute-start | bytes 12296 | tf_op jit(solution)/shard_map/ppermute | solution.py:525
  24.2 0.0 copy-done.3
  24.2 0.0 copy-start
  24.2 1.0 %copy-done = f32[256,384]{1,0:T(8,128)S(1)} copy-done((f32[256,384]{1,0:T(8,128)S(1)}, f32[256,384]{1,0:T(8,128)}, u32[]{:S(2)}) %copy-start) | copy-done | bytes 393240
  25.2 0.0 copy-start.2
  25.2 1.0 %copy-done.2 = f32[256,384]{1,0:T(8,128)S(1)} copy-done((f32[256,384]{1,0:T(8,128)S(1)}, f32[256,384]{1,0:T(8,128)}, u32[]{:S(2)}) %copy-start.2) | copy-done | bytes 393240
  26.2 0.0 copy-start.5
  26.2 0.0 copy-start.4
  26.2 12.7 %jacobi_turns.1 = (bf16[384,384]{1,0:T(8,128)(2,1)S(1)}, bf16[384,384]{1,0:T(8,128)(2,1)S(1)}, bf16[384,256]{1,0:T(8,128)(2,1)S(1)}) custom-call(s32[32]{0:T(128)S(1)} %copy-done.3, f32[256,384]{1,0:T(8,128)S(1)} %copy-done, f32[256,384]{1,0:T(8,128)S(1)} %copy-done.2), custom_call_target="tpu_custom_call" | custom-call | flops 2123366400 | bytes 1179648 | tf_op jit(solution)/shard_map/jacobi_turns/pallas_call | solution.py:280
  38.9 0.0 collective-permute-done.1
  38.9 0.0 copy-done.5
  38.9 0.0 copy-done.4
  38.9 4.1 %rotate_rows.1 = (bf16[9216,128]{1,0:T(8,128)(2,1)S(1)}, bf16[4608,128]{1,0:T(8,128)(2,1)S(1)}, bf16[2304,128]{1,0:T(8,128)(2,1)S(1)}) custom-call(bf16[6144,384]{1,0:T(8,128)(2,1)S(1)} %copy-done.4, bf16[384,384]{1,0:T(8,128)(2,1)S(1)} %get-tuple-element.16.slow_ref, bf16[384,384]{1,0:T(8,128)(2,1)S(1)} %get-tuple-element.17.fast_ref), custom_call_target="tpu_custom_call" | custom-call | flops 2415919104 | bytes 14155776 | tf_op jit(solution)/shard_map/rotate_rows/pallas_call | solution.py:424
  43.0 0.0 collective-permute-done.3.raw_ref
  43.0 0.2 collective-permute-start.4
  43.2 1.3 %collective-permute-start.5 = (bf16[4608,128]{1,0:T(8,128)(2,1)S(1)}, bf16[4608,128]{1,0:T(8,128)(2,1)S(1)}, u32[]{:S(2)}, u32[]{:S(2)}) collective-permute-start(bf16[4608,128]{1,0:T(8,128)(2,1)S(1)} %get-tuple-element.22), channel_id=1, source_target_pairs={{0,30},{2,4},{4,2},{6,8},{8,6},{10,12},{12,10},{14,16},{16,14},{18... | collective-permute-start | bytes 3538952 | tf_op jit(solution)/shard_map/ppermute | solution.py:525
  44.5 0.4 collective-permute-start.2
  44.9 1.3 %collective-permute-start.6 = (bf16[384,256]{1,0:T(8,128)(2,1)S(1)}, bf16[384,256]{1,0:T(8,128)(2,1)S(1)}, u32[]{:S(2)}, u32[]{:S(2)}) collective-permute-start(bf16[384,256]{1,0:T(8,128)(2,1)S(1)} %get-tuple-element.24), channel_id=1, source_target_pairs={{0,30},{2,4},{4,2},{6,8},{8,6},{10,12},{12,10},{14,16},{16,14},{18... | collective-permute-start | bytes 589832 | tf_op jit(solution)/shard_map/ppermute | solution.py:525
  46.3 6.2 %collective-permute-start.7 = (f32[8,128]{1,0:T(8,128)S(1)}, f32[8,128]{1,0:T(8,128)S(1)}, u32[]{:S(2)}, u32[]{:S(2)}) collective-permute-start(f32[8,128]{1,0:T(8,128)S(1)} %add.12), channel_id=1, source_target_pairs={{0,2},{2,0},{4,6},{6,4},{8,10},{10,8},{12,14},{14,12},{16,18},{18,... | collective-permute-start | bytes 12296 | tf_op jit(solution)/shard_map/ppermute | solution.py:525
  52.4 0.8 collective-permute-done.7
  53.3 0.0 collective-permute-start.8
  53.3 2.9 %collective-permute-done.8 = f32[8,128]{1,0:T(8,128)S(1)} collective-permute-done((f32[8,128]{1,0:T(8,128)S(1)}, f32[8,128]{1,0:T(8,128)S(1)}, u32[]{:S(2)}, u32[]{:S(2)}) %collective-permute-start.8) | collective-permute-done | bytes 4128 | tf_op jit(solution)/shard_map/ppermute | solution.py:525
  56.1 0.0 collective-permute-start.9
  56.1 3.8 %collective-permute-done.9 = f32[8,128]{1,0:T(8,128)S(1)} collective-permute-done((f32[8,128]{1,0:T(8,128)S(1)}, f32[8,128]{1,0:T(8,128)S(1)}, u32[]{:S(2)}, u32[]{:S(2)}) %collective-permute-start.9) | collective-permute-done | bytes 4128 | tf_op jit(solution)/shard_map/ppermute | solution.py:525
  59.9 0.5 fusion
  61.8 26.5 %collective-permute-done.6.turn_ref = bf16[384,256]{1,0:T(8,128)(2,1)S(1)} collective-permute-done((bf16[384,256]{1,0:T(8,128)(2,1)S(1)}, bf16[384,256]{1,0:T(8,128)(2,1)S(1)}, u32[]{:S(2)}, u32[]{:S(2)}) %collective-permute-start.6) | collective-permute-done | bytes 196640 | tf_op jit(solution)/shard_map/ppermute | solution.py:525
  88.3 0.0 collective-permute-done.4.fast_ref
  88.3 2.8 %fill_rows.3.refs_0_ = bf16[6144,384]{1,0:T(8,128)(2,1)} custom-call(s32[32]{0:T(128)S(1)} %copy-done.3, bf16[1536,384]{1,0:T(8,128)(2,1)S(1)} %collective-permute-done.3.raw_ref, bf16[384,256]{1,0:T(8,128)(2,1)S(1)} %collective-permute-done.6.turn_ref, bf16[9216,128]{1,0:T(8,128)(2,1)S(1)} %collective-permute-done.4.fast_ref), custom_call_target="tpu_custom_call" | custom-call | flops 589824 | bytes 2359296 | tf_op jit(solution)/shard_map/fill_rows/pallas_call | solution.py:508
  91.2 0.0 collective-permute-done.5.slow_ref
  91.2 2.4 %fill_rows.4.refs_0_ = bf16[6144,384]{1,0:T(8,128)(2,1)} custom-call(s32[32]{0:T(128)S(1)} %copy-done.3, bf16[4608,128]{1,0:T(8,128)(2,1)S(1)} %collective-permute-done.5.slow_ref, bf16[9216,128]{1,0:T(8,128)(2,1)S(1)} %collective-permute-done.4.fast_ref, bf16[6144,384]{1,0:T(8,128)(2,1)} %fill_rows.3.refs_0_), custom_call_target="tpu_custom_call", output_to_operand_aliasing={{}: (3, {})} | custom-call | flops 1179648 | bytes 4718592 | tf_op jit(solution)/shard_map/fill_rows/pallas_call | solution.py:508
  93.5 0.0 collective-permute-done.2.slow_ref
  93.5 2.4 %fill_rows.5 = bf16[6144,384]{1,0:T(8,128)(2,1)} custom-call(s32[32]{0:T(128)S(1)} %copy-done.3, bf16[2304,128]{1,0:T(8,128)(2,1)S(1)} %collective-permute-done.2.slow_ref, bf16[9216,128]{1,0:T(8,128)(2,1)S(1)} %collective-permute-done.4.fast_ref, bf16[6144,384]{1,0:T(8,128)(2,1)} %fill_rows.4.refs_0_), custom_call_target="tpu_custom_call", output_to_operand_aliasing={{}: (3, {})} | custom-call | flops 589824 | bytes 2359296 | tf_op jit(solution)/shard_map/fill_rows/pallas_call | solution.py:508
  (4 shorter events, 0.0 us)
Async XLA Ops:
  0.6 23.5 %copy-start.3 = (s32[32]{0:T(128)S(1)}, s32[32]{0:T(128)}, u32[]{:S(2)}) copy-start(s32[32]{0:T(128)} %plan_ref.7) | copy-start | bytes 388
  6.8 36.1 %collective-permute-start.3 = (bf16[1536,384]{1,0:T(8,128)(2,1)}, bf16[1536,384]{1,0:T(8,128)(2,1)S(1)}, u32[]{:S(2)}, u32[]{:S(2)}) collective-permute-start(bf16[1536,384]{1,0:T(8,128)(2,1)} %get-tuple-element.20), channel_id=1, source_target_pairs={{0,30},{2,4},{4,2},{6,8},{8,6},{10,12},{12,10},{14,16},{16,14},{18... | collective-permute-start | bytes 3538952 | tf_op jit(solution)/shard_map/ppermute | solution.py:525
  9.5 7.9 %collective-permute-start = (f32[256,384]{1,0:T(8,128)}, f32[256,384]{1,0:T(8,128)S(1)}, u32[]{:S(2)}, u32[]{:S(2)}) collective-permute-start(f32[256,384]{1,0:T(8,128)} %get-tuple-element.14.refs_0_), channel_id=1, source_target_pairs={{0,1},{1,0},{2,3},{3,2},{4,5},{5,4},{6,7},{7,6},{8,9},{9,8},{10,11... | collective-permute-start | bytes 1179656 | tf_op jit(solution)/shard_map/ppermute | solution.py:525
  17.5 0.7 copy-start.1
  20.1 18.8 %collective-permute-start.1 = (f32[8,128]{1,0:T(8,128)}, f32[8,128]{1,0:T(8,128)S(1)}, u32[]{:S(2)}, u32[]{:S(2)}) collective-permute-start(f32[8,128]{1,0:T(8,128)} %gram_sums.1), channel_id=1, source_target_pairs={{0,4},{2,6},{4,0},{6,2},{8,12},{10,14},{12,8},{14,10},{16,20},{18,... | collective-permute-start | bytes 12296 | tf_op jit(solution)/shard_map/ppermute | solution.py:525
  24.2 1.0 %copy-start = (f32[256,384]{1,0:T(8,128)S(1)}, f32[256,384]{1,0:T(8,128)}, u32[]{:S(2)}) copy-start(f32[256,384]{1,0:T(8,128)} %get-tuple-element.14.refs_0_) | copy-start | bytes 1179652
  25.2 1.0 %copy-start.2 = (f32[256,384]{1,0:T(8,128)S(1)}, f32[256,384]{1,0:T(8,128)}, u32[]{:S(2)}) copy-start(f32[256,384]{1,0:T(8,128)} %copy-done.1) | copy-start | bytes 1179652
  26.2 12.7 %copy-start.5 = (f32[8,128]{1,0:T(8,128)S(1)}, f32[8,128]{1,0:T(8,128)}, u32[]{:S(2)}) copy-start(f32[8,128]{1,0:T(8,128)} %gram_sums.1) | copy-start | bytes 12292
  26.2 12.7 %copy-start.4 = (bf16[6144,384]{1,0:T(8,128)(2,1)S(1)}, bf16[6144,384]{1,0:T(8,128)(2,1)}, u32[]{:S(2)}) copy-start(bf16[6144,384]{1,0:T(8,128)(2,1)} %matrix_ref.3) | copy-start | bytes 14155780
  43.0 45.3 %collective-permute-start.4 = (bf16[9216,128]{1,0:T(8,128)(2,1)S(1)}, bf16[9216,128]{1,0:T(8,128)(2,1)S(1)}, u32[]{:S(2)}, u32[]{:S(2)}) collective-permute-start(bf16[9216,128]{1,0:T(8,128)(2,1)S(1)} %get-tuple-element.21), channel_id=1, source_target_pairs={{0,2},{2,0},{4,6},{6,4},{8,10},{10,8},{12,14},{14,12},{16,18},{18,... | collective-permute-start | bytes 7077896 | tf_op jit(solution)/shard_map/ppermute | solution.py:525
  43.2 48.0 %collective-permute-start.5 = (bf16[4608,128]{1,0:T(8,128)(2,1)S(1)}, bf16[4608,128]{1,0:T(8,128)(2,1)S(1)}, u32[]{:S(2)}, u32[]{:S(2)}) collective-permute-start(bf16[4608,128]{1,0:T(8,128)(2,1)S(1)} %get-tuple-element.22), channel_id=1, source_target_pairs={{0,30},{2,4},{4,2},{6,8},{8,6},{10,12},{12,10},{14,16},{16,14},{18... | collective-permute-start | bytes 3538952 | tf_op jit(solution)/shard_map/ppermute | solution.py:525
  44.5 49.0 %collective-permute-start.2 = (bf16[2304,128]{1,0:T(8,128)(2,1)S(1)}, bf16[2304,128]{1,0:T(8,128)(2,1)S(1)}, u32[]{:S(2)}, u32[]{:S(2)}) collective-permute-start(bf16[2304,128]{1,0:T(8,128)(2,1)S(1)} %get-tuple-element.18), channel_id=1, source_target_pairs={{0,30},{2,4},{4,2},{6,8},{8,6},{10,12},{12,10},{14,16},{16,14},{18... | collective-permute-start | bytes 1769480 | tf_op jit(solution)/shard_map/ppermute | solution.py:525
  44.9 43.4 %collective-permute-start.6 = (bf16[384,256]{1,0:T(8,128)(2,1)S(1)}, bf16[384,256]{1,0:T(8,128)(2,1)S(1)}, u32[]{:S(2)}, u32[]{:S(2)}) collective-permute-start(bf16[384,256]{1,0:T(8,128)(2,1)S(1)} %get-tuple-element.24), channel_id=1, source_target_pairs={{0,30},{2,4},{4,2},{6,8},{8,6},{10,12},{12,10},{14,16},{16,14},{18... | collective-permute-start | bytes 589832 | tf_op jit(solution)/shard_map/ppermute | solution.py:525
  46.3 7.0 %collective-permute-start.7 = (f32[8,128]{1,0:T(8,128)S(1)}, f32[8,128]{1,0:T(8,128)S(1)}, u32[]{:S(2)}, u32[]{:S(2)}) collective-permute-start(f32[8,128]{1,0:T(8,128)S(1)} %add.12), channel_id=1, source_target_pairs={{0,2},{2,0},{4,6},{6,4},{8,10},{10,8},{12,14},{14,12},{16,18},{18,... | collective-permute-start | bytes 12296 | tf_op jit(solution)/shard_map/ppermute | solution.py:525
  53.3 2.9 %collective-permute-start.8 = (f32[8,128]{1,0:T(8,128)S(1)}, f32[8,128]{1,0:T(8,128)S(1)}, u32[]{:S(2)}, u32[]{:S(2)}) collective-permute-start(f32[8,128]{1,0:T(8,128)S(1)} %add.13), channel_id=1, source_target_pairs={{0,8},{2,10},{4,12},{6,14},{8,0},{10,2},{12,4},{14,6},{16,24},{18,... | collective-permute-start | bytes 12296 | tf_op jit(solution)/shard_map/ppermute | solution.py:525
  56.1 3.8 %collective-permute-start.9 = (f32[8,128]{1,0:T(8,128)S(1)}, f32[8,128]{1,0:T(8,128)S(1)}, u32[]{:S(2)}, u32[]{:S(2)}) collective-permute-start(f32[8,128]{1,0:T(8,128)S(1)} %add.14), channel_id=1, source_target_pairs={{0,16},{2,18},{4,20},{6,22},{8,24},{10,26},{12,28},{14,30},{16,0},... | collective-permute-start | bytes 12296 | tf_op jit(solution)/shard_map/ppermute | solution.py:525

commit v6 on v5

--- a/solution.py
+++ b/solution.py
@@ -1,5 +1,3 @@
-import functools
-
 import jax
 import jax.numpy as jnp
 from jax import lax
@@ -14,10 +12,10 @@
 PACK = UNIT + UNIT // 2
 GRAM_TILE = 512
 RAW_ROWS = 1536
-FIRST_ROWS = 3072
-ROTATE_TILE = 1536
-FILL_TILE = 512
+LAST_ROWS = 1024
+IN_FLIGHT = 3
 VMEM_LIMIT = 32 * 1024 * 1024
+JACOBI_VMEM_LIMIT = 30 * 1024 * 1024
 GRAM_VMEM_LIMIT = 58 * 1024 * 1024
 
 
@@ -93,6 +91,32 @@
     return jnp.where(section == 1, main_start + lane, mixed)
 
 
+def block_sums(packed):
+    squares = packed * packed
+    total = jnp.zeros((1, 1), jnp.float32)
+    diag_sq = jnp.zeros((1, 1), jnp.float32)
+    rows = lax.broadcasted_iota(jnp.int32, (LANES, LANES), 0)
+    cols = lax.broadcasted_iota(jnp.int32, (LANES, LANES), 1)
+    for row, col, weight in (
+        (0, 0, 1.0), (0, 1, 2.0), (0, 2, 2.0), (1, 0, 1.0), (1, 1, 2.0), (1, 2, 1.0)
+    ):
+        block = squares[row * LANES : (row + 1) * LANES, col * LANES : (col + 1) * LANES]
+        total = total + weight * jnp.sum(block, keepdims=True)
+        if weight == 1.0:
+            diag_sq = diag_sq + jnp.sum(jnp.where(rows == cols, block, 0.0), keepdims=True)
+    sub = lax.broadcasted_iota(jnp.int32, (SUBS, LANES), 0)
+    return jnp.where(sub == 0, total - diag_sq, diag_sq)
+
+
+def pack_unit(values, turn, packed_ref, at):
+    half = UNIT // 2
+    top = dot32(values[:half], turn[:, : 2 * LANES])
+    low = dot32(values[half:], turn[:, LANES:])
+    packed_ref[at : at + half] = top[:, LANES:].astype(jnp.bfloat16)
+    packed_ref[at + half : at + UNIT] = low[:, :LANES].astype(jnp.bfloat16)
+    packed_ref[at + UNIT : at + PACK] = (top[:, :LANES] + low[:, LANES:]).astype(jnp.bfloat16)
+
+
 def moves(plan_ref):
     count = plan_ref.shape[0] // 2
     position = lax.axis_index("blk")
@@ -107,13 +131,15 @@
 
 
 def jacobi_kernel(plan_ref, *refs):
-    jacobi_body(plan_ref, refs[:-9], *refs[-9:])
+    jacobi_body(plan_ref, refs[:-14], *refs[-14:])
 
 
 def jacobi_body(
-    plan_ref, gram_refs, slow_ref, fast_ref, send_ref,
-    gram_a, gram_b, basis_a, basis_b, cos_buf, sin_buf,
+    plan_ref, gram_refs, matrix_ref, first_ref, last_ref, fast_ref, sums_ref,
+    gram_a, gram_b, basis_a, basis_b, cos_buf, sin_buf, held, packs, sems,
 ):
+    matrix_copy = pltpu.make_async_copy(matrix_ref.at[pl.ds(RAW_ROWS, held.shape[0])], held, sems.at[0])
+    matrix_copy.start()
     size = gram_refs[0].shape[1]
     half = size // 2
     groups = half // SUBS
@@ -136,6 +162,7 @@
     for other in gram_refs[1:]:
         packed = packed + other[...]
     gram_sum = full_gram(packed)
+    sums_ref[...] = block_sums(packed)
     for piece in split_three(gram_sum):
         moved = dot32(take_rows, piece).astype(jnp.bfloat16)
         arranged = arranged + dot32(moved, take_cols)
@@ -263,30 +290,60 @@
 
     lax.fori_loop(0, ROUNDS // 2, two_turns, start)
 
-    held = jnp.where(row_slot == 0, 0, 1 + (row_slot + (size - 2 - ROUNDS % (size - 1))) % (size - 1))
+    held_slot = jnp.where(row_slot == 0, 0, 1 + (row_slot + (size - 2 - ROUNDS % (size - 1))) % (size - 1))
     basis = basis_a[...].reshape(size, size).astype(jnp.bfloat16)
     lanes = lax.broadcasted_iota(jnp.int32, (1, size), 1)
     first_slow, slow_slot, fast_slot, _ = moves(plan_ref)
     slow_base = jnp.where(first_slow, 0, half)
-    for ref, base, slot in ((slow_ref, slow_base, slow_slot), (fast_ref, half - slow_base, fast_slot)):
-        wanted = send_columns(lanes, base, slot, half)
-        ref[...] = dot32(basis, onehot(held, wanted), ((0,), (0,))).astype(jnp.bfloat16)
-    send_ref[...] = slow_ref[:, : 2 * LANES]
-
-
-def jacobi(plan, grams):
-    size = grams[0].shape[1]
+    def turned(base, slot):
+        place = onehot(held_slot, send_columns(lanes, base, slot, half))
+        return dot32(basis, place, ((0,), (0,))).astype(jnp.bfloat16)
+
+    fast_ref[...] = turned(half - slow_base, fast_slot)[:, : 2 * LANES]
+    slow = turned(slow_base, slow_slot)
+    packs[:size] = slow[:, :LANES]
+    packs[size : 2 * size] = slow[:, LANES : 2 * LANES]
+    matrix_copy.wait()
+    copies = []
+
+    def leave(start, count, ref):
+        copies.append(
+            pltpu.make_async_copy(packs.at[pl.ds(start, count)], ref, sems.at[1 + len(copies)])
+        )
+        copies[-1].start()
+
+    first_count = first_ref.shape[0]
+    leave(0, PACK, first_ref.at[pl.ds(0, PACK)])
+    for unit in range(held.shape[0] // UNIT):
+        at = (1 + unit) * PACK
+        pack_unit(held[unit * UNIT : (unit + 1) * UNIT], slow, packs, at)
+        if at < first_count:
+            leave(at, PACK, first_ref.at[pl.ds(at, PACK)])
+        else:
+            leave(at, PACK, last_ref.at[pl.ds(at - first_count, PACK)])
+    for copy in copies:
+        copy.wait()
+
+
+def jacobi(plan, grams, matrix):
+    rows, size = matrix.shape
     groups = size // 2 // SUBS
+    moved = rows - RAW_ROWS
+    blocks = 1 + moved // UNIT
+    last = LAST_ROWS // UNIT * PACK
     return pl.pallas_call(
         jacobi_kernel,
         out_shape=(
-            jax.ShapeDtypeStruct((size, size), jnp.bfloat16),
-            jax.ShapeDtypeStruct((size, size), jnp.bfloat16),
+            jax.ShapeDtypeStruct((blocks * PACK - last, LANES), jnp.bfloat16),
+            jax.ShapeDtypeStruct((last, LANES), jnp.bfloat16),
             jax.ShapeDtypeStruct((size, 2 * LANES), jnp.bfloat16),
+            jax.ShapeDtypeStruct((SUBS, LANES), jnp.float32),
         ),
         in_specs=[pl.BlockSpec(memory_space=pltpu.SMEM)]
-        + [pl.BlockSpec(memory_space=pltpu.VMEM)] * len(grams),
-        out_specs=[pl.BlockSpec(memory_space=pltpu.VMEM)] * 3,
+        + [pl.BlockSpec(memory_space=pltpu.VMEM)] * len(grams)
+        + [pl.BlockSpec(memory_space=pl.ANY)],
+        out_specs=[pl.BlockSpec(memory_space=pl.ANY)] * 2
+        + [pl.BlockSpec(memory_space=pltpu.VMEM)] * 2,
         scratch_shapes=[
             pltpu.VMEM((2, groups, SUBS, 4 * LANES), jnp.float32),
             pltpu.VMEM((2, groups, SUBS, 4 * LANES), jnp.float32),
@@ -294,44 +351,16 @@
             pltpu.VMEM((2, groups, SUBS, size), jnp.float32),
             pltpu.VMEM((groups, SUBS, LANES), jnp.float32),
             pltpu.VMEM((groups, SUBS, LANES), jnp.float32),
+            pltpu.VMEM((moved, size), jnp.bfloat16),
+            pltpu.VMEM((blocks * PACK, LANES), jnp.bfloat16),
+            pltpu.SemaphoreType.DMA((1 + blocks,)),
         ],
-        compiler_params=pltpu.CompilerParams(vmem_limit_bytes=VMEM_LIMIT),
+        compiler_params=pltpu.CompilerParams(vmem_limit_bytes=JACOBI_VMEM_LIMIT),
         cost_estimate=pl.CostEstimate(
-            flops=ROUNDS * 600 * size * size, bytes_accessed=8 * size * size, transcendentals=0
+            flops=ROUNDS * 600 * size * size, bytes_accessed=4 * rows * size, transcendentals=0
         ),
         name="jacobi_turns",
-    )(plan, *grams)
-
-
-def sums_kernel(*refs):
-    sums_ref = refs[-1]
-    packed = refs[0][...]
-    for other in refs[1:-1]:
-        packed = packed + other[...]
-    squares = packed * packed
-    total = jnp.zeros((1, 1), jnp.float32)
-    diag_sq = jnp.zeros((1, 1), jnp.float32)
-    rows = lax.broadcasted_iota(jnp.int32, (LANES, LANES), 0)
-    cols = lax.broadcasted_iota(jnp.int32, (LANES, LANES), 1)
-    for row, col, weight in (
-        (0, 0, 1.0), (0, 1, 2.0), (0, 2, 2.0), (1, 0, 1.0), (1, 1, 2.0), (1, 2, 1.0)
-    ):
-        block = squares[row * LANES : (row + 1) * LANES, col * LANES : (col + 1) * LANES]
-        total = total + weight * jnp.sum(block, keepdims=True)
-        if weight == 1.0:
-            diag_sq = diag_sq + jnp.sum(jnp.where(rows == cols, block, 0.0), keepdims=True)
-    sub = lax.broadcasted_iota(jnp.int32, (SUBS, LANES), 0)
-    sums_ref[...] = jnp.where(sub == 0, total - diag_sq, diag_sq)
-
-
-def gram_sums(grams):
-    return pl.pallas_call(
-        sums_kernel,
-        out_shape=jax.ShapeDtypeStruct((SUBS, LANES), jnp.float32),
-        in_specs=[pl.BlockSpec(memory_space=pltpu.VMEM)] * len(grams),
-        out_specs=pl.BlockSpec(memory_space=pltpu.VMEM),
-        name="gram_sums",
-    )(*grams)
+    )(plan, *grams, matrix)
 
 
 def gram_kernel(matrix_ref, packed_ref, raw_ref, held, upper_ref, corner_ref, sems, raw_sem):
@@ -340,11 +369,14 @@
     for index in range(rows // GRAM_TILE):
         part = pl.ds(index * GRAM_TILE, GRAM_TILE)
         copies.append(pltpu.make_async_copy(matrix_ref.at[part], held.at[part], sems.at[index]))
-        copies[-1].start()
+    for copy in copies[:IN_FLIGHT]:
+        copy.start()
     early = pl.ds(0, RAW_ROWS)
     leave = pltpu.make_async_copy(held.at[early], raw_ref, raw_sem)
     for index, copy in enumerate(copies):
         copy.wait()
+        if index + IN_FLIGHT < len(copies):
+            copies[index + IN_FLIGHT].start()
         if (index + 1) * GRAM_TILE == RAW_ROWS:
             leave.start()
         values = held[index * GRAM_TILE : (index + 1) * GRAM_TILE]
@@ -388,128 +420,68 @@
     )(matrix)
 
 
-def pack_unit(values, turn, packed_ref, at):
-    half = UNIT // 2
-    top = dot32(values[:half], turn[:, : 2 * LANES])
-    low = dot32(values[half:], turn[:, LANES:])
-    packed_ref[at : at + half] = top[:, LANES:].astype(jnp.bfloat16)
-    packed_ref[at + half : at + UNIT] = low[:, :LANES].astype(jnp.bfloat16)
-    packed_ref[at + UNIT : at + PACK] = (top[:, :LANES] + low[:, LANES:]).astype(jnp.bfloat16)
-
-
-def rotate_kernel(ranges, matrix_ref, slow_ref, fast_ref, fast_pack_ref, *slow_packs):
-    step = pl.program_id(0)
-    units = matrix_ref.shape[0] // UNIT
-    for unit in range(units):
-        values = matrix_ref[unit * UNIT : (unit + 1) * UNIT]
-        pack_unit(values, fast_ref[...], fast_pack_ref, unit * PACK)
-    for (first, count), pack_ref in zip(ranges, slow_packs):
-        @pl.when((step >= first) & (step < first + count))
-        def _(pack_ref=pack_ref):
-            for unit in range(units):
-                values = matrix_ref[unit * UNIT : (unit + 1) * UNIT]
-                pack_unit(values, slow_ref[...], pack_ref, unit * PACK)
-
-
-def rotate_all(matrix, slow_turn, fast_turn, spans):
-    rows, size = matrix.shape
-    pack = ROTATE_TILE // UNIT * PACK
-    ranges = [(start // ROTATE_TILE, count // ROTATE_TILE) for start, count, _ in spans]
-    packs = [rows] + [count for _, count, _ in spans]
-    turn_spec = pl.BlockSpec((size, size), lambda i: (0, 0))
-
-    def slow_spec(first, count):
-        return pl.BlockSpec((pack, LANES), lambda i: (jnp.clip(i - first, 0, count - 1), 0))
-
-    return pl.pallas_call(
-        functools.partial(rotate_kernel, ranges),
-        grid=(rows // ROTATE_TILE,),
-        in_specs=[pl.BlockSpec((ROTATE_TILE, size), lambda i: (i, 0)), turn_spec, turn_spec],
-        out_specs=[pl.BlockSpec((pack, LANES), lambda i: (i, 0))]
-        + [slow_spec(*part) for part in ranges],
-        out_shape=[
-            jax.ShapeDtypeStruct((count // UNIT * PACK, LANES), jnp.bfloat16) for count in packs
-        ],
-        compiler_params=pltpu.CompilerParams(vmem_limit_bytes=VMEM_LIMIT),
-        cost_estimate=pl.CostEstimate(
-            flops=8 * rows * size * LANES, bytes_accessed=6 * rows * size, transcendentals=0
-        ),
-        name="rotate_rows",
-    )(matrix, slow_turn, fast_turn)
-
-
-def place_main(slot, out_ref, rows, slow_main, fast_main):
+def place_main(slot, out_ref, slow_main, fast_main):
     @pl.when(slot == 0)
     def _():
-        out_ref[rows, :LANES] = slow_main
-        out_ref[rows, 2 * LANES :] = fast_main
+        out_ref[:, :LANES] = slow_main
+        out_ref[:, 2 * LANES :] = fast_main
 
     @pl.when(slot != 0)
     def _():
-        out_ref[rows, :LANES] = fast_main
-        out_ref[rows, 2 * LANES :] = slow_main
-
-
-def slot_lanes(slot):
-    lane = lax.broadcasted_iota(jnp.int32, (UNIT // 2, LANES), 1)
-    return (lane // (LANES // 2)) == slot
-
-
-def place_kernel(plan_ref, slow_ref, fast_ref, *refs):
+        out_ref[:, :LANES] = fast_main
+        out_ref[:, 2 * LANES :] = slow_main
+
+
+def fill_kernel(plan_ref, slow_ref, near_ref, near_turn_ref, *refs):
     out_ref = refs[-1]
     half = UNIT // 2
     slot = moves(plan_ref)[3]
-    mask = slot_lanes(slot)
     middle = slice(LANES, 2 * LANES)
-    for unit in range(out_ref.shape[0] // UNIT):
-        start, at = unit * UNIT, unit * PACK
-        main, rest = slice(at, at + UNIT), slice(at + UNIT, at + PACK)
-        place_main(slot, out_ref, slice(start, start + UNIT), slow_ref[main], fast_ref[main])
-        slow = slow_ref[rest].astype(jnp.float32)
-        fast = fast_ref[rest].astype(jnp.float32)
-        out_ref[start : start + half, middle] = jnp.where(mask, slow, fast).astype(jnp.bfloat16)
-        swapped = pltpu.roll(jnp.where(mask, fast, slow), LANES // 2, 1)
-        out_ref[start + half : start + UNIT, middle] = swapped.astype(jnp.bfloat16)
-
-
-def raw_kernel(plan_ref, raw_ref, turn_ref, fast_ref, *refs):
-    out_ref = refs[-1]
-    half = UNIT // 2
+    near = dot32(near_ref[...], near_turn_ref[...])
+    place_main(slot, out_ref, slow_ref[:UNIT], near[:, LANES:].astype(jnp.bfloat16))
+    lane = lax.broadcasted_iota(jnp.int32, (half, LANES), 1)
+    mask = (lane // (LANES // 2)) == slot
+    slow = slow_ref[UNIT:].astype(jnp.float32)
+    top = jnp.where(mask, slow, near[:half, :LANES])
+    low = jnp.where(mask, pltpu.roll(slow, LANES // 2, 1), near[half:, :LANES])
+    out_ref[:half, middle] = top.astype(jnp.bfloat16)
+    out_ref[half:, middle] = low.astype(jnp.bfloat16)
+
+
+def raw_kernel(plan_ref, slow_ref, slow_turn_ref, near_ref, near_turn_ref, out_ref):
+    size = slow_ref.shape[1]
     slot = moves(plan_ref)[3]
-    mask = slot_lanes(slot)
-    middle = slice(LANES, 2 * LANES)
-    for unit in range(out_ref.shape[0] // UNIT):
-        start, at = unit * UNIT, unit * PACK
-        rows = slice(start, start + UNIT)
-        turned = dot32(raw_ref[rows], turn_ref[...])
-        main = turned[:, LANES:].astype(jnp.bfloat16)
-        place_main(slot, out_ref, rows, main, fast_ref[at : at + UNIT])
-        fast = fast_ref[at + UNIT : at + PACK].astype(jnp.float32)
-        top = jnp.where(mask, turned[:half, :LANES], fast)
-        out_ref[start : start + half, middle] = top.astype(jnp.bfloat16)
-        low = jnp.where(mask, turned[half:, :LANES], pltpu.roll(fast, LANES // 2, 1))
-        out_ref[start + half : start + UNIT, middle] = low.astype(jnp.bfloat16)
-
-
-def fill_rows(kernel, plan, sources, specs, fast, held, shape, start, count, tile):
-    first = start // tile
-    pack = tile // UNIT * PACK
-    operands = [plan, *sources, fast]
+    near = dot32(near_ref[...], near_turn_ref[...])
+    mixed = dot32(slow_ref[...], slow_turn_ref[:size])
+    main = dot32(slow_ref[...], slow_turn_ref[size:])
+    place_main(slot, out_ref, main.astype(jnp.bfloat16), near[:, LANES:].astype(jnp.bfloat16))
+    lane = lax.broadcasted_iota(jnp.int32, mixed.shape, 1)
+    mask = (lane // (LANES // 2)) == slot
+    middle = jnp.where(mask, mixed, near[:, :LANES])
+    out_ref[:, LANES : 2 * LANES] = middle.astype(jnp.bfloat16)
+
+
+def fill_rows(kernel, plan, sources, specs, near, near_turn, result, start, count):
+    shape = near.shape
+    first = start // UNIT
+    operands = [plan, *sources, near, near_turn]
+    row_spec = pl.BlockSpec((UNIT, shape[1]), lambda i: (first + i, 0))
     in_specs = [
         pl.BlockSpec(memory_space=pltpu.SMEM),
         *specs,
-        pl.BlockSpec((pack, LANES), lambda i: (first + i, 0)),
+        row_spec,
+        pl.BlockSpec(near_turn.shape, lambda i: (0, 0)),
     ]
     aliases = {}
-    if held is not None:
+    if result is not None:
         aliases = {len(operands): 0}
-        operands.append(held)
+        operands.append(result)
         in_specs.append(pl.BlockSpec(memory_space=pl.ANY))
     return pl.pallas_call(
         kernel,
-        grid=(count // tile,),
+        grid=(count // UNIT,),
         in_specs=in_specs,
-        out_specs=pl.BlockSpec((tile, shape[1]), lambda i: (first + i, 0)),
+        out_specs=row_spec,
         out_shape=jax.ShapeDtypeStruct(shape, jnp.bfloat16),
         input_output_aliases=aliases,
         compiler_params=pltpu.CompilerParams(vmem_limit_bytes=VMEM_LIMIT),
@@ -533,48 +505,62 @@
     return source ^ 1
 
 
-def add_swapped(values, step):
-    return values + swapped_with(values, "blk", lambda source, _: source ^ step)
+def permuted(value, pairs):
+    return lax.ppermute(value, "blk", pairs)
+
+
+def cycle_sums(sums):
+    count = lax.axis_size("blk")
+    outer = [place for place in range(count) if place % 4 in (0, 3)]
+    inner = [place for place in range(count) if place % 4 in (1, 2)]
+    is_outer = (lax.axis_index("blk") + 1) % 4 < 2
+    sums = sums + permuted(sums, [(place, place ^ 1) for place in range(count)])
+    sums = sums + permuted(sums, [(place, place ^ 3) for place in outer])
+    moved = permuted(sums, [(place, place ^ 1) for place in outer])
+    sums = jnp.where(is_outer, sums, moved)
+    step = 4
+    while step < count:
+        sums = sums + permuted(sums, [(place, place ^ step) for place in inner])
+        step *= 2
+    moved = permuted(sums, [(place, place ^ 1) for place in inner])
+    return jnp.where(is_outer, moved, sums)
 
 
 def on_device(matrix, plan):
     rows, size = matrix.shape
     own, early = gram_blocks(matrix)
+    matrix_after = matrix
     if lax.axis_size("rows") == 2:
-        grams = [own, swapped_with(own, "rows", fast_partner)]
+        other = swapped_with(own, "rows", fast_partner)
+        matrix_after, other = lax.optimization_barrier((matrix, other))
+        grams = [own, other]
     else:
         grams = [lax.psum(own, "rows")]
     raw = swapped_with(early, "blk", slow_partner)
-    totals = add_swapped(gram_sums(grams), 2)
-    slow_turn, fast_turn, send_turn = jacobi(plan, grams)
-    slow_turn, totals = lax.optimization_barrier((slow_turn, totals))
-
-    their_turn = swapped_with(send_turn, "blk", slow_partner)
-    last_rows = rows - RAW_ROWS - FIRST_ROWS
-    spans = [(RAW_ROWS, FIRST_ROWS, ROTATE_TILE), (RAW_ROWS + FIRST_ROWS, last_rows, FILL_TILE)]
-    fast_pack, *packs = rotate_all(matrix, slow_turn, fast_turn, spans)
-    arrived = [swapped_with(pack, "blk", slow_partner) for pack in packs]
-    fast_pack, raw = lax.optimization_barrier((fast_pack, raw))
-    fast = swapped_with(fast_pack, "blk", fast_partner)
-    step = 1
-    while step < lax.axis_size("blk"):
-        if step != 2:
-            totals = add_swapped(totals, step)
-        step *= 2
+    near = swapped_with(matrix_after, "blk", fast_partner)
+    first, last, near_turn, sums = jacobi(plan, grams, matrix)
+    near_turn, sums, raw, near = lax.optimization_barrier((near_turn, sums, raw, near))
+
+    first = swapped_with(first, "blk", slow_partner)
+    last = swapped_with(last, "blk", slow_partner)
+    near_turn = swapped_with(near_turn, "blk", fast_partner)
+    totals = cycle_sums(sums)
     off_ratio = jnp.sqrt(totals[0, 0] / totals[1, 0])
 
-    shape = (rows, size)
-    raw_specs = [
-        pl.BlockSpec((UNIT, size), lambda i: (i, 0)),
-        pl.BlockSpec((size, 2 * LANES), lambda i: (0, 0)),
-    ]
+    turn_spec = pl.BlockSpec((PACK, LANES), lambda i: (0, 0))
+    raw_spec = pl.BlockSpec((UNIT, size), lambda i: (i, 0))
+    first_spec = pl.BlockSpec((PACK, LANES), lambda i: (1 + i, 0))
+    last_spec = pl.BlockSpec((PACK, LANES), lambda i: (i, 0))
+    middle = rows - RAW_ROWS - LAST_ROWS
     result = fill_rows(
-        raw_kernel, plan, [raw, their_turn], raw_specs, fast, None, shape, 0, RAW_ROWS, UNIT
+        raw_kernel, plan, [raw, first], [raw_spec, turn_spec], near, near_turn, None, 0, RAW_ROWS
     )
-    for span, slow in zip(spans, arrived):
-        pack = span[2] // UNIT * PACK
-        specs = [pl.BlockSpec((pack, LANES), lambda i: (i, 0))]
-        result = fill_rows(place_kernel, plan, [slow], specs, fast, result, shape, *span)
+    result = fill_rows(
+        fill_kernel, plan, [first], [first_spec], near, near_turn, result, RAW_ROWS, middle
+    )
+    result = fill_rows(
+        fill_kernel, plan, [last], [last_spec], near, near_turn, result, rows - LAST_ROWS, LAST_ROWS
+    )
     return result, off_ratio
 
 

time: 97.3 us -> 106 us (1.089); the launches traced: 97.1 us -> 104 us
  waiting for transfers between devices: 40.7 us -> 44.4 us
  local copies, waits for them, and re-layouts: 3.26 us -> 6.05 us
    ppermute x0 -> x6, starting transfers between devices: none -> 11.3 us  [permuted(): return lax.ppermute(value, 'blk', pairs)]
    ppermute x10 -> x6, starting transfers between devices: 17.4 us -> 6.67 us  [swapped_with(): lax.ppermute(value, axis, [(source, partner(source, count)) for source in...]
    ppermute x0 -> x6, waiting for transfers between devices: none -> 7.6 us  [permuted(): return lax.ppermute(value, 'blk', pairs)]
    ppermute x10 -> x6, waiting for transfers between devices: 40.7 us -> 36.8 us  [swapped_with(): lax.ppermute(value, axis, [(source, partner(source, count)) for source in...]
    unnamed x12 -> x10, local copies, waits for them, and re-layouts: 2.74 us -> 5.46 us
    pallas_call x6 -> x4, Pallas kernels: 26.3 us -> 25.2 us  [the longest x1 14.7 us: jacobi(): pl.pallas_call(jacobi_kernel, out_shape=(jax.ShapeDtypeStruct((blocks * P...]
  transfers between devices with their start and end apart: 10 -> 12, of which waited for: 5 -> 7; matrix products, arithmetic and copies ran while one was open for 1% -> 1% of each run, Pallas kernels for 25% -> 22%
where the time goes in v6:
time: 106 us; the launch traced here: 104 us
  waiting for transfers between devices  44.4 us (42%)
  Pallas kernels  31.7 us (30%)
  starting transfers between devices  18 us (17%)
  local copies, waits for them, and re-layouts  6.05 us (6%)
  between operations  3.32 us (3%)
    ppermute x6, waiting for transfers between devices, swapped_with(): lax.ppermute(value, axis, [(source, partner(source, count)) for source in...  36.8 us
    pallas_call x1, Pallas kernels, jacobi(): pl.pallas_call(jacobi_kernel, out_shape=(jax.ShapeDtypeStruct((blocks * P...  14.7 us
    ppermute x6, starting transfers between devices, permuted(): return lax.ppermute(value, 'blk', pairs)  11.3 us
    pallas_call x3, Pallas kernels, fill_rows(): pl.pallas_call(kernel, grid=(count // UNIT,), in_specs=in_specs, out_spec...  10.5 us
    ppermute x6, waiting for transfers between devices, permuted(): return lax.ppermute(value, 'blk', pairs)  7.6 us
    ppermute x6, starting transfers between devices, swapped_with(): lax.ppermute(value, axis, [(source, partner(source, count)) for source in...  6.67 us
    pallas_call x1, Pallas kernels, gram_blocks(): pl.pallas_call(gram_kernel, in_specs=[pl.BlockSpec(memory_space=pl.ANY)],...  6.43 us
    unnamed x10, local copies, waits for them, and re-layouts  5.46 us
  transfers between devices with their start and end apart: 12, of which 7 were waited for; matrix products, arithmetic and copies ran while one was open for 1% of the time, Pallas kernels for 22%

profile of v6, /device:TPU:1, one launch (start us, length us, event | category | flops | bytes accessed | tf_op | source)
XLA Modules:
  0.0 103.5 jit_solution(13337242487004152663)
XLA Ops:
  0.6 0.0 copy-start.3
  0.6 6.4 %gram_blocks.1 = (f32[256,384]{1,0:T(8,128)}, bf16[1536,384]{1,0:T(8,128)(2,1)}) custom-call(bf16[6144,384]{1,0:T(8,128)(2,1)} %refs_2_.1), custom_call_target="tpu_custom_call" | custom-call | flops 1811939328 | bytes 4718592 | tf_op jit(solution)/shard_map/gram_blocks/pallas_call | solution.py:400
  7.1 2.1 %collective-permute-start = (f32[256,384]{1,0:T(8,128)}, f32[256,384]{1,0:T(8,128)S(1)}, u32[]{:S(2)}, u32[]{:S(2)}) collective-permute-start(f32[256,384]{1,0:T(8,128)} %get-tuple-element.14.refs_0_), channel_id=1, source_target_pairs={{0,1},{1,0},{2,3},{3,2},{4,5},{5,4},{6,7},{7,6},{8,9},{9,8},{10,11... | collective-permute-start | bytes 1179656 | tf_op jit(solution)/shard_map/ppermute | solution.py:497
  9.2 9.1 %collective-permute-done.refs_1_ = f32[256,384]{1,0:T(8,128)S(1)} collective-permute-done((f32[256,384]{1,0:T(8,128)}, f32[256,384]{1,0:T(8,128)S(1)}, u32[]{:S(2)}, u32[]{:S(2)}) %collective-permute-start) | collective-permute-done | bytes 393248 | tf_op jit(solution)/shard_map/ppermute | solution.py:497
  18.2 1.2 %collective-permute-start.3 = (bf16[6144,384]{1,0:T(8,128)(2,1)}, bf16[6144,384]{1,0:T(8,128)(2,1)S(1)}, u32[]{:S(2)}, u32[]{:S(2)}) collective-permute-start(bf16[6144,384]{1,0:T(8,128)(2,1)} %refs_2_.1), channel_id=1, source_target_pairs={{0,2},{2,0},{4,6},{6,4},{8,10},{10,8},{12,14},{14,12},{16,18},{18,... | collective-permute-start | bytes 14155784 | tf_op jit(solution)/shard_map/ppermute | solution.py:497
  19.5 1.4 %collective-permute-start.2 = (bf16[1536,384]{1,0:T(8,128)(2,1)}, bf16[1536,384]{1,0:T(8,128)(2,1)S(1)}, u32[]{:S(2)}, u32[]{:S(2)}) collective-permute-start(bf16[1536,384]{1,0:T(8,128)(2,1)} %get-tuple-element.19), channel_id=1, source_target_pairs={{0,30},{2,4},{4,2},{6,8},{8,6},{10,12},{12,10},{14,16},{16,14},{18... | collective-permute-start | bytes 3538952 | tf_op jit(solution)/shard_map/ppermute | solution.py:497
  20.8 0.0 copy-done.3
  20.9 0.0 copy-start.4
  20.9 1.0 copy-done.4
  21.8 14.7 %jacobi_turns.1 = (bf16[6144,128]{1,0:T(8,128)(2,1)}, bf16[1536,128]{1,0:T(8,128)(2,1)S(1)}, bf16[384,256]{1,0:T(8,128)(2,1)S(1)}, f32[8,128]{1,0:T(8,128)S(1)}) custom-call(s32[32]{0:T(128)S(1)} %copy-done.3, f32[256,384]{1,0:T(8,128)S(1)} %copy-done.4, f32[256,384]{1,0:T(8,128)S(1)} %collective-permute-done.refs_1_, bf16[6144,384]{1,0:T(8,128)(2,1)} %refs_2_.1), custom_call_target="tpu_custom_call" | custom-call | flops 2123366400 | bytes 9437184 | tf_op jit(solution)/shard_map/jacobi_turns/pallas_call | solution.py:334
  36.6 0.4 collective-permute-start.5
  37.0 27.8 %collective-permute-done.2.slow_ref = bf16[1536,384]{1,0:T(8,128)(2,1)S(1)} collective-permute-done((bf16[1536,384]{1,0:T(8,128)(2,1)}, bf16[1536,384]{1,0:T(8,128)(2,1)S(1)}, u32[]{:S(2)}, u32[]{:S(2)}) %collective-permute-start.2) | collective-permute-done | bytes 1179680 | tf_op jit(solution)/shard_map/ppermute | solution.py:497
  64.8 0.0 collective-permute-done.3.near_ref
  64.8 0.0 copy-start
  64.8 2.1 %copy-done = bf16[6144,384]{1,0:T(8,128)(2,1)} copy-done((bf16[6144,384]{1,0:T(8,128)(2,1)}, bf16[6144,384]{1,0:T(8,128)(2,1)S(1)}, u32[]{:S(2)}) %copy-start) | copy-done | bytes 4718616
  66.9 0.0 collective-permute-start.6
  66.9 1.2 %collective-permute-done.6 = f32[8,128]{1,0:T(8,128)S(1)} collective-permute-done((f32[8,128]{1,0:T(8,128)S(1)}, f32[8,128]{1,0:T(8,128)S(1)}, u32[]{:S(2)}, u32[]{:S(2)}) %collective-permute-start.6) | collective-permute-done | bytes 4128 | tf_op jit(solution)/shard_map/ppermute | solution.py:509
  68.1 0.7 collective-permute-start.7
  68.8 0.0 collective-permute-done.7
  68.8 1.3 %collective-permute-start.8 = (f32[8,128]{1,0:T(8,128)S(1)}, f32[8,128]{1,0:T(8,128)S(1)}, u32[]{:S(2)}, u32[]{:S(2)}) collective-permute-start(f32[8,128]{1,0:T(8,128)S(1)} %add.22), channel_id=1, source_target_pairs={{0,2},{6,4},{8,10},{14,12},{16,18},{22,20},{24,26},{30,28},{1,3},{... | collective-permute-start | bytes 12296 | tf_op jit(solution)/shard_map/ppermute | solution.py:509
  70.1 1.4 %collective-permute-start.1 = (bf16[1536,128]{1,0:T(8,128)(2,1)S(1)}, bf16[1536,128]{1,0:T(8,128)(2,1)S(1)}, u32[]{:S(2)}, u32[]{:S(2)}) collective-permute-start(bf16[1536,128]{1,0:T(8,128)(2,1)S(1)} %get-tuple-element.16), channel_id=1, source_target_pairs={{0,30},{2,4},{4,2},{6,8},{8,6},{10,12},{12,10},{14,16},{16,14},{18... | collective-permute-start | bytes 1179656 | tf_op jit(solution)/shard_map/ppermute | solution.py:497
  71.5 3.7 %collective-permute-done.8 = f32[8,128]{1,0:T(8,128)S(1)} collective-permute-done((f32[8,128]{1,0:T(8,128)S(1)}, f32[8,128]{1,0:T(8,128)S(1)}, u32[]{:S(2)}, u32[]{:S(2)}) %collective-permute-start.8) | collective-permute-done | bytes 4128 | tf_op jit(solution)/shard_map/ppermute | solution.py:509
  75.2 3.4 %collective-permute-start.9 = (f32[8,128]{1,0:T(8,128)S(1)}, f32[8,128]{1,0:T(8,128)S(1)}, u32[]{:S(2)}, u32[]{:S(2)}) collective-permute-start(f32[8,128]{1,0:T(8,128)S(1)} %broadcast_select_fusion.1), channel_id=1, source_target_pairs={{2,10},{4,12},{10,2},{12,4},{18,26},{20,28},{26,18},{28,20},{3,11}... | collective-permute-start | bytes 12296 | tf_op jit(solution)/shard_map/ppermute | solution.py:509
  78.7 1.1 %collective-permute-done.9 = f32[8,128]{1,0:T(8,128)S(1)} collective-permute-done((f32[8,128]{1,0:T(8,128)S(1)}, f32[8,128]{1,0:T(8,128)S(1)}, u32[]{:S(2)}, u32[]{:S(2)}) %collective-permute-start.9) | collective-permute-done | bytes 4128 | tf_op jit(solution)/shard_map/ppermute | solution.py:509
  79.7 4.6 %collective-permute-start.10 = (f32[8,128]{1,0:T(8,128)S(1)}, f32[8,128]{1,0:T(8,128)S(1)}, u32[]{:S(2)}, u32[]{:S(2)}) collective-permute-start(f32[8,128]{1,0:T(8,128)S(1)} %add.23), channel_id=1, source_target_pairs={{2,18},{4,20},{10,26},{12,28},{18,2},{20,4},{26,10},{28,12},{3,19}... | collective-permute-start | bytes 12296 | tf_op jit(solution)/shard_map/ppermute | solution.py:509
  84.4 1.0 collective-permute-done.10
  85.4 1.3 %collective-permute-start.11 = (f32[8,128]{1,0:T(8,128)S(1)}, f32[8,128]{1,0:T(8,128)S(1)}, u32[]{:S(2)}, u32[]{:S(2)}) collective-permute-start(f32[8,128]{1,0:T(8,128)S(1)} %add.24), channel_id=1, source_target_pairs={{2,0},{4,6},{10,8},{12,14},{18,16},{20,22},{26,24},{28,30},{3,1},{... | collective-permute-start | bytes 12296 | tf_op jit(solution)/shard_map/ppermute | solution.py:509
  86.7 0.1 collective-permute-start.4
  86.7 0.7 collective-permute-done.11
  87.5 0.6 fusion
  89.5 0.0 collective-permute-done.5.slow_turn_ref.slow_ref
  89.5 0.0 collective-permute-done.4.near_turn_ref
  89.5 0.0 copy-start.1
  89.5 2.3 %copy-done.1 = bf16[6144,384]{1,0:T(8,128)(2,1)S(1)} copy-done((bf16[6144,384]{1,0:T(8,128)(2,1)S(1)}, bf16[6144,384]{1,0:T(8,128)(2,1)}, u32[]{:S(2)}) %copy-start.1) | copy-done | bytes 4718616
  91.8 0.0 copy-start.2
  91.8 3.2 %fill_rows.3.refs_0_ = bf16[6144,384]{1,0:T(8,128)(2,1)} custom-call(s32[32]{0:T(128)S(1)} %copy-done.3, bf16[1536,384]{1,0:T(8,128)(2,1)S(1)} %collective-permute-done.2.slow_ref, bf16[6144,128]{1,0:T(8,128)(2,1)S(1)} %collective-permute-done.5.slow_turn_ref.slow_ref, bf16[6144,384]{1,0:T(8,128)(2,1)S(1)} %copy-done.1, ...), custom_call_target="tpu_custom_call" | custom-call | flops 589824 | bytes 2359296 | tf_op jit(solution)/shard_map/fill_rows/pallas_call | solution.py:480
  95.0 0.0 copy-done.2
  95.0 5.2 %fill_rows.4.refs_0_ = bf16[6144,384]{1,0:T(8,128)(2,1)} custom-call(s32[32]{0:T(128)S(1)} %copy-done.3, bf16[6144,128]{1,0:T(8,128)(2,1)S(1)} %collective-permute-done.5.slow_turn_ref.slow_ref, bf16[6144,384]{1,0:T(8,128)(2,1)S(1)} %copy-done.2, bf16[384,256]{1,0:T(8,128)(2,1)S(1)} %collective-permute-done.4.near_turn_ref, ...), custom_call_target="tpu_custom_call", output_to_operand_aliasing={{}: (4, {})} | custom-call | flops 1376256 | bytes 5505024 | tf_op jit(solution)/shard_map/fill_rows/pallas_call | solution.py:480
  100.2 0.0 collective-permute-done.1.slow_ref
  100.2 2.1 %fill_rows.5 = bf16[6144,384]{1,0:T(8,128)(2,1)} custom-call(s32[32]{0:T(128)S(1)} %copy-done.3, bf16[1536,128]{1,0:T(8,128)(2,1)S(1)} %collective-permute-done.1.slow_ref, bf16[6144,384]{1,0:T(8,128)(2,1)S(1)} %copy-done.2, bf16[384,256]{1,0:T(8,128)(2,1)S(1)} %collective-permute-done.4.near_turn_ref, ...), custom_call_target="tpu_custom_call", output_to_operand_aliasing={{}: (4, {})} | custom-call | flops 393216 | bytes 1572864 | tf_op jit(solution)/shard_map/fill_rows/pallas_call | solution.py:480
  (6 shorter events, 0.0 us)
Async XLA Ops:
  0.6 20.2 %copy-start.3 = (s32[32]{0:T(128)S(1)}, s32[32]{0:T(128)}, u32[]{:S(2)}) copy-start(s32[32]{0:T(128)} %plan_ref.7) | copy-start | bytes 388
  7.1 11.2 %collective-permute-start = (f32[256,384]{1,0:T(8,128)}, f32[256,384]{1,0:T(8,128)S(1)}, u32[]{:S(2)}, u32[]{:S(2)}) collective-permute-start(f32[256,384]{1,0:T(8,128)} %get-tuple-element.14.refs_0_), channel_id=1, source_target_pairs={{0,1},{1,0},{2,3},{3,2},{4,5},{5,4},{6,7},{7,6},{8,9},{9,8},{10,11... | collective-permute-start | bytes 1179656 | tf_op jit(solution)/shard_map/ppermute | solution.py:497
  18.2 46.6 %collective-permute-start.3 = (bf16[6144,384]{1,0:T(8,128)(2,1)}, bf16[6144,384]{1,0:T(8,128)(2,1)S(1)}, u32[]{:S(2)}, u32[]{:S(2)}) collective-permute-start(bf16[6144,384]{1,0:T(8,128)(2,1)} %refs_2_.1), channel_id=1, source_target_pairs={{0,2},{2,0},{4,6},{6,4},{8,10},{10,8},{12,14},{14,12},{16,18},{18,... | collective-permute-start | bytes 14155784 | tf_op jit(solution)/shard_map/ppermute | solution.py:497
  19.5 45.3 %collective-permute-start.2 = (bf16[1536,384]{1,0:T(8,128)(2,1)}, bf16[1536,384]{1,0:T(8,128)(2,1)S(1)}, u32[]{:S(2)}, u32[]{:S(2)}) collective-permute-start(bf16[1536,384]{1,0:T(8,128)(2,1)} %get-tuple-element.19), channel_id=1, source_target_pairs={{0,30},{2,4},{4,2},{6,8},{8,6},{10,12},{12,10},{14,16},{16,14},{18... | collective-permute-start | bytes 3538952 | tf_op jit(solution)/shard_map/ppermute | solution.py:497
  20.9 1.0 copy-start.4
  36.6 52.9 %collective-permute-start.5 = (bf16[6144,128]{1,0:T(8,128)(2,1)}, bf16[6144,128]{1,0:T(8,128)(2,1)S(1)}, u32[]{:S(2)}, u32[]{:S(2)}) collective-permute-start(bf16[6144,128]{1,0:T(8,128)(2,1)} %get-tuple-element.23), channel_id=1, source_target_pairs={{0,30},{2,4},{4,2},{6,8},{8,6},{10,12},{12,10},{14,16},{16,14},{18... | collective-permute-start | bytes 4718600 | tf_op jit(solution)/shard_map/ppermute | solution.py:497
  64.8 2.1 %copy-start = (bf16[6144,384]{1,0:T(8,128)(2,1)}, bf16[6144,384]{1,0:T(8,128)(2,1)S(1)}, u32[]{:S(2)}) copy-start(bf16[6144,384]{1,0:T(8,128)(2,1)S(1)} %collective-permute-done.3.near_ref) | copy-start | bytes 14155780
  66.9 1.2 %collective-permute-start.6 = (f32[8,128]{1,0:T(8,128)S(1)}, f32[8,128]{1,0:T(8,128)S(1)}, u32[]{:S(2)}, u32[]{:S(2)}) collective-permute-start(f32[8,128]{1,0:T(8,128)S(1)} %get-tuple-element.25), channel_id=1, source_target_pairs={{0,2},{2,0},{4,6},{6,4},{8,10},{10,8},{12,14},{14,12},{16,18},{18,... | collective-permute-start | bytes 12296 | tf_op jit(solution)/shard_map/ppermute | solution.py:509
  68.1 0.7 collective-permute-start.7
  68.8 6.4 %collective-permute-start.8 = (f32[8,128]{1,0:T(8,128)S(1)}, f32[8,128]{1,0:T(8,128)S(1)}, u32[]{:S(2)}, u32[]{:S(2)}) collective-permute-start(f32[8,128]{1,0:T(8,128)S(1)} %add.22), channel_id=1, source_target_pairs={{0,2},{6,4},{8,10},{14,12},{16,18},{22,20},{24,26},{30,28},{1,3},{... | collective-permute-start | bytes 12296 | tf_op jit(solution)/shard_map/ppermute | solution.py:509
  70.1 30.1 %collective-permute-start.1 = (bf16[1536,128]{1,0:T(8,128)(2,1)S(1)}, bf16[1536,128]{1,0:T(8,128)(2,1)S(1)}, u32[]{:S(2)}, u32[]{:S(2)}) collective-permute-start(bf16[1536,128]{1,0:T(8,128)(2,1)S(1)} %get-tuple-element.16), channel_id=1, source_target_pairs={{0,30},{2,4},{4,2},{6,8},{8,6},{10,12},{12,10},{14,16},{16,14},{18... | collective-permute-start | bytes 1179656 | tf_op jit(solution)/shard_map/ppermute | solution.py:497
  75.2 4.5 %collective-permute-start.9 = (f32[8,128]{1,0:T(8,128)S(1)}, f32[8,128]{1,0:T(8,128)S(1)}, u32[]{:S(2)}, u32[]{:S(2)}) collective-permute-start(f32[8,128]{1,0:T(8,128)S(1)} %broadcast_select_fusion.1), channel_id=1, source_target_pairs={{2,10},{4,12},{10,2},{12,4},{18,26},{20,28},{26,18},{28,20},{3,11}... | collective-permute-start | bytes 12296 | tf_op jit(solution)/shard_map/ppermute | solution.py:509
  79.7 5.6 %collective-permute-start.10 = (f32[8,128]{1,0:T(8,128)S(1)}, f32[8,128]{1,0:T(8,128)S(1)}, u32[]{:S(2)}, u32[]{:S(2)}) collective-permute-start(f32[8,128]{1,0:T(8,128)S(1)} %add.23), channel_id=1, source_target_pairs={{2,18},{4,20},{10,26},{12,28},{18,2},{20,4},{26,10},{28,12},{3,19}... | collective-permute-start | bytes 12296 | tf_op jit(solution)/shard_map/ppermute | solution.py:509
  85.4 2.1 %collective-permute-start.11 = (f32[8,128]{1,0:T(8,128)S(1)}, f32[8,128]{1,0:T(8,128)S(1)}, u32[]{:S(2)}, u32[]{:S(2)}) collective-permute-start(f32[8,128]{1,0:T(8,128)S(1)} %add.24), channel_id=1, source_target_pairs={{2,0},{4,6},{10,8},{12,14},{18,16},{20,22},{26,24},{28,30},{3,1},{... | collective-permute-start | bytes 12296 | tf_op jit(solution)/shard_map/ppermute | solution.py:509
  86.7 2.8 %collective-permute-start.4 = (bf16[384,256]{1,0:T(8,128)(2,1)S(1)}, bf16[384,256]{1,0:T(8,128)(2,1)S(1)}, u32[]{:S(2)}, u32[]{:S(2)}) collective-permute-start(bf16[384,256]{1,0:T(8,128)(2,1)S(1)} %get-tuple-element.22), channel_id=1, source_target_pairs={{0,2},{2,0},{4,6},{6,4},{8,10},{10,8},{12,14},{14,12},{16,18},{18,... | collective-permute-start | bytes 589832 | tf_op jit(solution)/shard_map/ppermute | solution.py:497
  89.5 2.3 %copy-start.1 = (bf16[6144,384]{1,0:T(8,128)(2,1)S(1)}, bf16[6144,384]{1,0:T(8,128)(2,1)}, u32[]{:S(2)}) copy-start(bf16[6144,384]{1,0:T(8,128)(2,1)} %copy-done) | copy-start | bytes 14155780
  91.8 3.2 %copy-start.2 = (bf16[6144,384]{1,0:T(8,128)(2,1)S(1)}, bf16[6144,384]{1,0:T(8,128)(2,1)}, u32[]{:S(2)}) copy-start(bf16[6144,384]{1,0:T(8,128)(2,1)} %copy-done) | copy-start | bytes 14155780

commit v7 on v6

--- a/solution.py
+++ b/solution.py
@@ -10,10 +10,11 @@
 SUBS = 8
 UNIT = 512
 PACK = UNIT + UNIT // 2
-GRAM_TILE = 512
+GRAM_PARTS = (512, 1024)
+GRAM_TILE = 1536
 RAW_ROWS = 1536
-LAST_ROWS = 1024
-IN_FLIGHT = 3
+LAST_ROWS = 2560
+IN_FLIGHT = 2
 VMEM_LIMIT = 32 * 1024 * 1024
 JACOBI_VMEM_LIMIT = 30 * 1024 * 1024
 GRAM_VMEM_LIMIT = 58 * 1024 * 1024
@@ -357,17 +358,28 @@
         ],
         compiler_params=pltpu.CompilerParams(vmem_limit_bytes=JACOBI_VMEM_LIMIT),
         cost_estimate=pl.CostEstimate(
-            flops=ROUNDS * 600 * size * size, bytes_accessed=4 * rows * size, transcendentals=0
+            flops=size, bytes_accessed=size, transcendentals=0
         ),
         name="jacobi_turns",
     )(plan, *grams, matrix)
 
 
+def gram_spans(rows):
+    spans = []
+    start = 0
+    while start < rows:
+        wanted = GRAM_PARTS[len(spans)] if len(spans) < len(GRAM_PARTS) else GRAM_TILE
+        spans.append((start, min(wanted, rows - start)))
+        start += spans[-1][1]
+    return spans
+
+
 def gram_kernel(matrix_ref, packed_ref, raw_ref, held, upper_ref, corner_ref, sems, raw_sem):
     rows = held.shape[0]
     copies = []
-    for index in range(rows // GRAM_TILE):
-        part = pl.ds(index * GRAM_TILE, GRAM_TILE)
+    spans = gram_spans(rows)
+    for index, (start, count) in enumerate(spans):
+        part = pl.ds(start, count)
         copies.append(pltpu.make_async_copy(matrix_ref.at[part], held.at[part], sems.at[index]))
     for copy in copies[:IN_FLIGHT]:
         copy.start()
@@ -377,9 +389,10 @@
         copy.wait()
         if index + IN_FLIGHT < len(copies):
             copies[index + IN_FLIGHT].start()
-        if (index + 1) * GRAM_TILE == RAW_ROWS:
+        start, count = spans[index]
+        if start + count == RAW_ROWS:
             leave.start()
-        values = held[index * GRAM_TILE : (index + 1) * GRAM_TILE]
+        values = held[start : start + count]
         right = values[:, 2 * LANES :]
         upper = dot32(values[:, : 2 * LANES], values, ((0,), (0,)))
         corner = dot32(right, right, ((0,), (0,)))
@@ -409,7 +422,7 @@
             pltpu.VMEM((rows, size), jnp.bfloat16),
             pltpu.VMEM((2 * LANES, size), jnp.float32),
             pltpu.VMEM((LANES, LANES), jnp.float32),
-            pltpu.SemaphoreType.DMA((rows // GRAM_TILE,)),
+            pltpu.SemaphoreType.DMA((len(gram_spans(rows)),)),
             pltpu.SemaphoreType.DMA,
         ],
         compiler_params=pltpu.CompilerParams(vmem_limit_bytes=GRAM_VMEM_LIMIT),
@@ -529,17 +542,16 @@
 def on_device(matrix, plan):
     rows, size = matrix.shape
     own, early = gram_blocks(matrix)
-    matrix_after = matrix
+    matrix_after, own = lax.optimization_barrier((matrix, own))
     if lax.axis_size("rows") == 2:
         other = swapped_with(own, "rows", fast_partner)
-        matrix_after, other = lax.optimization_barrier((matrix, other))
         grams = [own, other]
     else:
         grams = [lax.psum(own, "rows")]
     raw = swapped_with(early, "blk", slow_partner)
     near = swapped_with(matrix_after, "blk", fast_partner)
     first, last, near_turn, sums = jacobi(plan, grams, matrix)
-    near_turn, sums, raw, near = lax.optimization_barrier((near_turn, sums, raw, near))
+    near_turn, raw, near = lax.optimization_barrier((near_turn, raw, near))
 
     first = swapped_with(first, "blk", slow_partner)
     last = swapped_with(last, "blk", slow_partner)

time: 106 us -> 94.7 us (0.89); the launches traced: 104 us -> 93.9 us
  waiting for transfers between devices: 44.4 us -> 34.8 us
  local copies, waits for them, and re-layouts: 6.05 us -> 1.52 us
  starting transfers between devices: 18 us -> 20.5 us
  Pallas kernels: 31.7 us -> 33.8 us
    ppermute x6, waiting for transfers between devices: 36.8 us -> 6.15 us  [swapped_with(): lax.ppermute(value, axis, [(source, partner(source, count)) for source in...]
    ppermute x6, waiting for transfers between devices: 7.6 us -> 28.6 us  [permuted(): return lax.ppermute(value, 'blk', pairs)]
    unnamed x10 -> x4, local copies, waits for them, and re-layouts: 5.46 us -> 1 us
    pallas_call x3, Pallas kernels: 10.5 us -> 13.7 us  [fill_rows(): pl.pallas_call(kernel, grid=(count // UNIT,), in_specs=in_specs, out_spec...]
    ppermute x6, starting transfers between devices: 6.67 us -> 8.6 us  [swapped_with(): lax.ppermute(value, axis, [(source, partner(source, count)) for source in...]
    pallas_call x1, Pallas kernels: 6.43 us -> 5.35 us  [gram_blocks(): pl.pallas_call(gram_kernel, in_specs=[pl.BlockSpec(memory_space=pl.ANY)],...]
  transfers between devices with their start and end apart: 12 -> 12, of which waited for: 7 -> 6; matrix products, arithmetic and copies ran while one was open for 1% -> 1% of each run, Pallas kernels for 22% -> 25%
where the time goes in v7:
time: 94.7 us; the launch traced here: 93.9 us
  waiting for transfers between devices  34.8 us (37%)
  Pallas kernels  33.8 us (36%)
  starting transfers between devices  20.5 us (22%)
  between operations  3.28 us (3%)
  local copies, waits for them, and re-layouts  1.52 us (2%)
    ppermute x6, waiting for transfers between devices, permuted(): return lax.ppermute(value, 'blk', pairs)  28.6 us
    pallas_call x1, Pallas kernels, jacobi(): pl.pallas_call(jacobi_kernel, out_shape=(jax.ShapeDtypeStruct((blocks * P...  14.7 us
    pallas_call x3, Pallas kernels, fill_rows(): pl.pallas_call(kernel, grid=(count // UNIT,), in_specs=in_specs, out_spec...  13.7 us
    ppermute x6, starting transfers between devices, permuted(): return lax.ppermute(value, 'blk', pairs)  11.9 us
    ppermute x6, starting transfers between devices, swapped_with(): lax.ppermute(value, axis, [(source, partner(source, count)) for source in...  8.6 us
    ppermute x6, waiting for transfers between devices, swapped_with(): lax.ppermute(value, axis, [(source, partner(source, count)) for source in...  6.15 us
    pallas_call x1, Pallas kernels, gram_blocks(): pl.pallas_call(gram_kernel, in_specs=[pl.BlockSpec(memory_space=pl.ANY)],...  5.35 us
  transfers between devices with their start and end apart: 12, of which 6 were waited for; matrix products, arithmetic and copies ran while one was open for 1% of the time, Pallas kernels for 25%

profile of v7, /device:TPU:1, one launch (start us, length us, event | category | flops | bytes accessed | tf_op | source)
XLA Modules:
  0.0 93.9 jit_solution(10601693130519869349)
XLA Ops:
  0.6 0.0 copy-start.1
  0.6 5.3 %gram_blocks.1 = (f32[256,384]{1,0:T(8,128)}, bf16[1536,384]{1,0:T(8,128)(2,1)}) custom-call(bf16[6144,384]{1,0:T(8,128)(2,1)} %refs_2_.1), custom_call_target="tpu_custom_call" | custom-call | flops 1811939328 | bytes 4718592 | tf_op jit(solution)/shard_map/gram_blocks/pallas_call | solution.py:413
  6.0 0.1 collective-permute-start.3
  6.1 2.7 %collective-permute-start.2 = (bf16[1536,384]{1,0:T(8,128)(2,1)}, bf16[1536,384]{1,0:T(8,128)(2,1)S(1)}, u32[]{:S(2)}, u32[]{:S(2)}) collective-permute-start(bf16[1536,384]{1,0:T(8,128)(2,1)} %get-tuple-element.17), channel_id=1, source_target_pairs={{0,30},{2,4},{4,2},{6,8},{8,6},{10,12},{12,10},{14,16},{16,14},{18... | collective-permute-start | bytes 3538952 | tf_op jit(solution)/shard_map/ppermute | solution.py:510
  8.8 1.2 %collective-permute-start = (f32[256,384]{1,0:T(8,128)}, f32[256,384]{1,0:T(8,128)S(1)}, u32[]{:S(2)}, u32[]{:S(2)}) collective-permute-start(f32[256,384]{1,0:T(8,128)} %get-tuple-element.14.refs_0_), channel_id=1, source_target_pairs={{0,1},{1,0},{2,3},{3,2},{4,5},{5,4},{6,7},{7,6},{8,9},{9,8},{10,11... | collective-permute-start | bytes 1179656 | tf_op jit(solution)/shard_map/ppermute | solution.py:510
  10.0 6.1 %collective-permute-done.refs_1_ = f32[256,384]{1,0:T(8,128)S(1)} collective-permute-done((f32[256,384]{1,0:T(8,128)}, f32[256,384]{1,0:T(8,128)S(1)}, u32[]{:S(2)}, u32[]{:S(2)}) %collective-permute-start) | collective-permute-done | bytes 393248 | tf_op jit(solution)/shard_map/ppermute | solution.py:510
  16.1 0.0 copy-done.1
  16.1 0.0 copy-start
  16.1 1.0 %copy-done = f32[256,384]{1,0:T(8,128)S(1)} copy-done((f32[256,384]{1,0:T(8,128)S(1)}, f32[256,384]{1,0:T(8,128)}, u32[]{:S(2)}) %copy-start) | copy-done | bytes 393240
  17.1 14.7 %jacobi_turns.1 = (bf16[3840,128]{1,0:T(8,128)(2,1)}, bf16[3840,128]{1,0:T(8,128)(2,1)}, bf16[384,256]{1,0:T(8,128)(2,1)S(1)}, f32[8,128]{1,0:T(8,128)S(1)}) custom-call(s32[32]{0:T(128)S(1)} %copy-done.1, f32[256,384]{1,0:T(8,128)S(1)} %copy-done, f32[256,384]{1,0:T(8,128)S(1)} %collective-permute-done.refs_1_, bf16[6144,384]{1,0:T(8,128)(2,1)} %refs_2_.1), custom_call_target="tpu_custom_call" | custom-call | flops 384 | bytes 384 | tf_op jit(solution)/shard_map/jacobi_turns/pallas_call | solution.py:335
  31.9 4.5 %collective-permute-start.5 = (bf16[3840,128]{1,0:T(8,128)(2,1)}, bf16[3840,128]{1,0:T(8,128)(2,1)S(1)}, u32[]{:S(2)}, u32[]{:S(2)}) collective-permute-start(bf16[3840,128]{1,0:T(8,128)(2,1)} %get-tuple-element.21), channel_id=1, source_target_pairs={{0,30},{2,4},{4,2},{6,8},{8,6},{10,12},{12,10},{14,16},{16,14},{18... | collective-permute-start | bytes 2949128 | tf_op jit(solution)/shard_map/ppermute | solution.py:510
  36.3 0.1 collective-permute-start.1
  36.4 4.4 %collective-permute-start.6 = (f32[8,128]{1,0:T(8,128)S(1)}, f32[8,128]{1,0:T(8,128)S(1)}, u32[]{:S(2)}, u32[]{:S(2)}) collective-permute-start(f32[8,128]{1,0:T(8,128)S(1)} %get-tuple-element.23), channel_id=1, source_target_pairs={{0,2},{2,0},{4,6},{6,4},{8,10},{10,8},{12,14},{14,12},{16,18},{18,... | collective-permute-start | bytes 12296 | tf_op jit(solution)/shard_map/ppermute | solution.py:522
  40.8 0.8 collective-permute-done.6
  41.6 0.6 collective-permute-start.7
  42.2 0.0 collective-permute-done.7
  42.3 1.3 %collective-permute-start.8 = (f32[8,128]{1,0:T(8,128)S(1)}, f32[8,128]{1,0:T(8,128)S(1)}, u32[]{:S(2)}, u32[]{:S(2)}) collective-permute-start(f32[8,128]{1,0:T(8,128)S(1)} %add.22), channel_id=1, source_target_pairs={{0,2},{6,4},{8,10},{14,12},{16,18},{22,20},{24,26},{30,28},{1,3},{... | collective-permute-start | bytes 12296 | tf_op jit(solution)/shard_map/ppermute | solution.py:522
  43.6 21.9 %collective-permute-done.8 = f32[8,128]{1,0:T(8,128)S(1)} collective-permute-done((f32[8,128]{1,0:T(8,128)S(1)}, f32[8,128]{1,0:T(8,128)S(1)}, u32[]{:S(2)}, u32[]{:S(2)}) %collective-permute-start.8) | collective-permute-done | bytes 4128 | tf_op jit(solution)/shard_map/ppermute | solution.py:522
  65.5 1.9 %collective-permute-start.9 = (f32[8,128]{1,0:T(8,128)S(1)}, f32[8,128]{1,0:T(8,128)S(1)}, u32[]{:S(2)}, u32[]{:S(2)}) collective-permute-start(f32[8,128]{1,0:T(8,128)S(1)} %broadcast_select_fusion.1), channel_id=1, source_target_pairs={{2,10},{4,12},{10,2},{12,4},{18,26},{20,28},{26,18},{28,20},{3,11}... | collective-permute-start | bytes 12296 | tf_op jit(solution)/shard_map/ppermute | solution.py:522
  67.4 2.4 %collective-permute-done.9 = f32[8,128]{1,0:T(8,128)S(1)} collective-permute-done((f32[8,128]{1,0:T(8,128)S(1)}, f32[8,128]{1,0:T(8,128)S(1)}, u32[]{:S(2)}, u32[]{:S(2)}) %collective-permute-start.9) | collective-permute-done | bytes 4128 | tf_op jit(solution)/shard_map/ppermute | solution.py:522
  69.8 2.4 %collective-permute-start.10 = (f32[8,128]{1,0:T(8,128)S(1)}, f32[8,128]{1,0:T(8,128)S(1)}, u32[]{:S(2)}, u32[]{:S(2)}) collective-permute-start(f32[8,128]{1,0:T(8,128)S(1)} %add.23), channel_id=1, source_target_pairs={{2,18},{4,20},{10,26},{12,28},{18,2},{20,4},{26,10},{28,12},{3,19}... | collective-permute-start | bytes 12296 | tf_op jit(solution)/shard_map/ppermute | solution.py:522
  72.2 2.8 %collective-permute-done.10 = f32[8,128]{1,0:T(8,128)S(1)} collective-permute-done((f32[8,128]{1,0:T(8,128)S(1)}, f32[8,128]{1,0:T(8,128)S(1)}, u32[]{:S(2)}, u32[]{:S(2)}) %collective-permute-start.10) | collective-permute-done | bytes 4128 | tf_op jit(solution)/shard_map/ppermute | solution.py:522
  75.0 1.3 %collective-permute-start.11 = (f32[8,128]{1,0:T(8,128)S(1)}, f32[8,128]{1,0:T(8,128)S(1)}, u32[]{:S(2)}, u32[]{:S(2)}) collective-permute-start(f32[8,128]{1,0:T(8,128)S(1)} %add.24), channel_id=1, source_target_pairs={{2,0},{4,6},{10,8},{12,14},{18,16},{20,22},{26,24},{28,30},{3,1},{... | collective-permute-start | bytes 12296 | tf_op jit(solution)/shard_map/ppermute | solution.py:522
  76.3 0.0 collective-permute-done.2.slow_ref
  76.3 0.0 collective-permute-done.3.near_ref
  76.3 0.1 collective-permute-start.4
  76.4 0.7 collective-permute-done.11
  77.1 0.5 fusion
  79.0 0.0 collective-permute-done.5.slow_turn_ref.slow_ref
  79.0 0.0 collective-permute-done.4.near_turn_ref
  79.1 4.1 %fill_rows.3.refs_0_ = bf16[6144,384]{1,0:T(8,128)(2,1)} custom-call(s32[32]{0:T(128)S(1)} %copy-done.1, bf16[1536,384]{1,0:T(8,128)(2,1)S(1)} %collective-permute-done.2.slow_ref, bf16[3840,128]{1,0:T(8,128)(2,1)S(1)} %collective-permute-done.5.slow_turn_ref.slow_ref, bf16[6144,384]{1,0:T(8,128)(2,1)} %collective-permute-done.3.near_ref, ...), custom_call_target="tpu_custom_call" | custom-call | flops 589824 | bytes 2359296 | tf_op jit(solution)/shard_map/fill_rows/pallas_call | solution.py:493
  83.1 4.3 %fill_rows.4.refs_0_ = bf16[6144,384]{1,0:T(8,128)(2,1)} custom-call(s32[32]{0:T(128)S(1)} %copy-done.1, bf16[3840,128]{1,0:T(8,128)(2,1)S(1)} %collective-permute-done.5.slow_turn_ref.slow_ref, bf16[6144,384]{1,0:T(8,128)(2,1)} %collective-permute-done.3.near_ref, ...), custom_call_target="tpu_custom_call", output_to_operand_aliasing={{}: (4, {})} | custom-call | flops 786432 | bytes 3145728 | tf_op jit(solution)/shard_map/fill_rows/pallas_call | solution.py:493
  87.5 0.0 collective-permute-done.1.slow_ref
  87.5 5.3 %fill_rows.5 = bf16[6144,384]{1,0:T(8,128)(2,1)} custom-call(s32[32]{0:T(128)S(1)} %copy-done.1, bf16[3840,128]{1,0:T(8,128)(2,1)S(1)} %collective-permute-done.1.slow_ref, bf16[6144,384]{1,0:T(8,128)(2,1)} %collective-permute-done.3.near_ref, bf16[384,256]{1,0:T(8,128)(2,1)S(1)} %collective-permute-done.4.near_turn_ref, ...), custom_call_target="tpu_custom_call", output_to_operand_aliasing={{}: (4, {})} | custom-call | flops 983040 | bytes 3932160 | tf_op jit(solution)/shard_map/fill_rows/pallas_call | solution.py:493
  (6 shorter events, 0.0 us)
Async XLA Ops:
  0.6 15.5 %copy-start.1 = (s32[32]{0:T(128)S(1)}, s32[32]{0:T(128)}, u32[]{:S(2)}) copy-start(s32[32]{0:T(128)} %plan_ref.7) | copy-start | bytes 388
  6.0 70.3 %collective-permute-start.3 = (bf16[6144,384]{1,0:T(8,128)(2,1)}, bf16[6144,384]{1,0:T(8,128)(2,1)}, u32[]{:S(2)}, u32[]{:S(2)}) collective-permute-start(bf16[6144,384]{1,0:T(8,128)(2,1)} %refs_2_.1), channel_id=1, source_target_pairs={{0,2},{2,0},{4,6},{6,4},{8,10},{10,8},{12,14},{14,12},{16,18},{18,... | collective-permute-start | bytes 14155784 | tf_op jit(solution)/shard_map/ppermute | solution.py:510
  6.1 70.2 %collective-permute-start.2 = (bf16[1536,384]{1,0:T(8,128)(2,1)}, bf16[1536,384]{1,0:T(8,128)(2,1)S(1)}, u32[]{:S(2)}, u32[]{:S(2)}) collective-permute-start(bf16[1536,384]{1,0:T(8,128)(2,1)} %get-tuple-element.17), channel_id=1, source_target_pairs={{0,30},{2,4},{4,2},{6,8},{8,6},{10,12},{12,10},{14,16},{16,14},{18... | collective-permute-start | bytes 3538952 | tf_op jit(solution)/shard_map/ppermute | solution.py:510
  8.8 7.3 %collective-permute-start = (f32[256,384]{1,0:T(8,128)}, f32[256,384]{1,0:T(8,128)S(1)}, u32[]{:S(2)}, u32[]{:S(2)}) collective-permute-start(f32[256,384]{1,0:T(8,128)} %get-tuple-element.14.refs_0_), channel_id=1, source_target_pairs={{0,1},{1,0},{2,3},{3,2},{4,5},{5,4},{6,7},{7,6},{8,9},{9,8},{10,11... | collective-permute-start | bytes 1179656 | tf_op jit(solution)/shard_map/ppermute | solution.py:510
  16.1 1.0 %copy-start = (f32[256,384]{1,0:T(8,128)S(1)}, f32[256,384]{1,0:T(8,128)}, u32[]{:S(2)}) copy-start(f32[256,384]{1,0:T(8,128)} %get-tuple-element.14.refs_0_) | copy-start | bytes 1179652
  31.9 47.2 %collective-permute-start.5 = (bf16[3840,128]{1,0:T(8,128)(2,1)}, bf16[3840,128]{1,0:T(8,128)(2,1)S(1)}, u32[]{:S(2)}, u32[]{:S(2)}) collective-permute-start(bf16[3840,128]{1,0:T(8,128)(2,1)} %get-tuple-element.21), channel_id=1, source_target_pairs={{0,30},{2,4},{4,2},{6,8},{8,6},{10,12},{12,10},{14,16},{16,14},{18... | collective-permute-start | bytes 2949128 | tf_op jit(solution)/shard_map/ppermute | solution.py:510
  36.3 51.1 %collective-permute-start.1 = (bf16[3840,128]{1,0:T(8,128)(2,1)}, bf16[3840,128]{1,0:T(8,128)(2,1)S(1)}, u32[]{:S(2)}, u32[]{:S(2)}) collective-permute-start(bf16[3840,128]{1,0:T(8,128)(2,1)} %get-tuple-element.15), channel_id=1, source_target_pairs={{0,30},{2,4},{4,2},{6,8},{8,6},{10,12},{12,10},{14,16},{16,14},{18... | collective-permute-start | bytes 2949128 | tf_op jit(solution)/shard_map/ppermute | solution.py:510
  36.4 5.2 %collective-permute-start.6 = (f32[8,128]{1,0:T(8,128)S(1)}, f32[8,128]{1,0:T(8,128)S(1)}, u32[]{:S(2)}, u32[]{:S(2)}) collective-permute-start(f32[8,128]{1,0:T(8,128)S(1)} %get-tuple-element.23), channel_id=1, source_target_pairs={{0,2},{2,0},{4,6},{6,4},{8,10},{10,8},{12,14},{14,12},{16,18},{18,... | collective-permute-start | bytes 12296 | tf_op jit(solution)/shard_map/ppermute | solution.py:522
  41.6 0.7 collective-permute-start.7
  42.3 23.2 %collective-permute-start.8 = (f32[8,128]{1,0:T(8,128)S(1)}, f32[8,128]{1,0:T(8,128)S(1)}, u32[]{:S(2)}, u32[]{:S(2)}) collective-permute-start(f32[8,128]{1,0:T(8,128)S(1)} %add.22), channel_id=1, source_target_pairs={{0,2},{6,4},{8,10},{14,12},{16,18},{22,20},{24,26},{30,28},{1,3},{... | collective-permute-start | bytes 12296 | tf_op jit(solution)/shard_map/ppermute | solution.py:522
  65.5 4.3 %collective-permute-start.9 = (f32[8,128]{1,0:T(8,128)S(1)}, f32[8,128]{1,0:T(8,128)S(1)}, u32[]{:S(2)}, u32[]{:S(2)}) collective-permute-start(f32[8,128]{1,0:T(8,128)S(1)} %broadcast_select_fusion.1), channel_id=1, source_target_pairs={{2,10},{4,12},{10,2},{12,4},{18,26},{20,28},{26,18},{28,20},{3,11}... | collective-permute-start | bytes 12296 | tf_op jit(solution)/shard_map/ppermute | solution.py:522
  69.8 5.2 %collective-permute-start.10 = (f32[8,128]{1,0:T(8,128)S(1)}, f32[8,128]{1,0:T(8,128)S(1)}, u32[]{:S(2)}, u32[]{:S(2)}) collective-permute-start(f32[8,128]{1,0:T(8,128)S(1)} %add.23), channel_id=1, source_target_pairs={{2,18},{4,20},{10,26},{12,28},{18,2},{20,4},{26,10},{28,12},{3,19}... | collective-permute-start | bytes 12296 | tf_op jit(solution)/shard_map/ppermute | solution.py:522
  75.0 2.1 %collective-permute-start.11 = (f32[8,128]{1,0:T(8,128)S(1)}, f32[8,128]{1,0:T(8,128)S(1)}, u32[]{:S(2)}, u32[]{:S(2)}) collective-permute-start(f32[8,128]{1,0:T(8,128)S(1)} %add.24), channel_id=1, source_target_pairs={{2,0},{4,6},{10,8},{12,14},{18,16},{20,22},{26,24},{28,30},{3,1},{... | collective-permute-start | bytes 12296 | tf_op jit(solution)/shard_map/ppermute | solution.py:522
  76.3 2.7 %collective-permute-start.4 = (bf16[384,256]{1,0:T(8,128)(2,1)S(1)}, bf16[384,256]{1,0:T(8,128)(2,1)S(1)}, u32[]{:S(2)}, u32[]{:S(2)}) collective-permute-start(bf16[384,256]{1,0:T(8,128)(2,1)S(1)} %get-tuple-element.20), channel_id=1, source_target_pairs={{0,2},{2,0},{4,6},{6,4},{8,10},{10,8},{12,14},{14,12},{16,18},{18,... | collective-permute-start | bytes 589832 | tf_op jit(solution)/shard_map/ppermute | solution.py:510

commit v8 on v7

--- a/solution.py
+++ b/solution.py
@@ -10,10 +10,12 @@
 SUBS = 8
 UNIT = 512
 PACK = UNIT + UNIT // 2
-GRAM_PARTS = (512, 1024)
-GRAM_TILE = 1536
-RAW_ROWS = 1536
-LAST_ROWS = 2560
+GRAM_PARTS = (512, 1536)
+GRAM_TILE = 2048
+RAW_ROWS = 2048
+LAST_ROWS = 2048
+FILL_TILE = 1024
+SUM_ROWS = 16
 IN_FLIGHT = 2
 VMEM_LIMIT = 32 * 1024 * 1024
 JACOBI_VMEM_LIMIT = 30 * 1024 * 1024
@@ -105,8 +107,11 @@
         total = total + weight * jnp.sum(block, keepdims=True)
         if weight == 1.0:
             diag_sq = diag_sq + jnp.sum(jnp.where(rows == cols, block, 0.0), keepdims=True)
-    sub = lax.broadcasted_iota(jnp.int32, (SUBS, LANES), 0)
-    return jnp.where(sub == 0, total - diag_sq, diag_sq)
+    row = lax.broadcasted_iota(jnp.int32, (SUM_ROWS, LANES), 0)
+    pieces = jnp.zeros((SUM_ROWS, LANES), jnp.float32)
+    for index, piece in enumerate(split_three(total - diag_sq) + split_three(diag_sq)):
+        pieces = jnp.where(row == index, piece.astype(jnp.float32), pieces)
+    return pieces.astype(jnp.bfloat16)
 
 
 def pack_unit(values, turn, packed_ref, at):
@@ -313,8 +318,12 @@
         )
         copies[-1].start()
 
-    first_count = first_ref.shape[0]
+    first_count = first_ref.shape[0] - SUM_ROWS
     leave(0, PACK, first_ref.at[pl.ds(0, PACK)])
+    copies.append(
+        pltpu.make_async_copy(sums_ref, first_ref.at[pl.ds(first_count, SUM_ROWS)], sems.at[2])
+    )
+    copies[-1].start()
     for unit in range(held.shape[0] // UNIT):
         at = (1 + unit) * PACK
         pack_unit(held[unit * UNIT : (unit + 1) * UNIT], slow, packs, at)
@@ -335,10 +344,10 @@
     return pl.pallas_call(
         jacobi_kernel,
         out_shape=(
-            jax.ShapeDtypeStruct((blocks * PACK - last, LANES), jnp.bfloat16),
+            jax.ShapeDtypeStruct((blocks * PACK - last + SUM_ROWS, LANES), jnp.bfloat16),
             jax.ShapeDtypeStruct((last, LANES), jnp.bfloat16),
             jax.ShapeDtypeStruct((size, 2 * LANES), jnp.bfloat16),
-            jax.ShapeDtypeStruct((SUBS, LANES), jnp.float32),
+            jax.ShapeDtypeStruct((SUM_ROWS, LANES), jnp.bfloat16),
         ),
         in_specs=[pl.BlockSpec(memory_space=pltpu.SMEM)]
         + [pl.BlockSpec(memory_space=pltpu.VMEM)] * len(grams)
@@ -354,7 +363,7 @@
             pltpu.VMEM((groups, SUBS, LANES), jnp.float32),
             pltpu.VMEM((moved, size), jnp.bfloat16),
             pltpu.VMEM((blocks * PACK, LANES), jnp.bfloat16),
-            pltpu.SemaphoreType.DMA((1 + blocks,)),
+            pltpu.SemaphoreType.DMA((2 + blocks,)),
         ],
         compiler_params=pltpu.CompilerParams(vmem_limit_bytes=JACOBI_VMEM_LIMIT),
         cost_estimate=pl.CostEstimate(
@@ -433,57 +442,66 @@
     )(matrix)
 
 
-def place_main(slot, out_ref, slow_main, fast_main):
+def place_main(slot, out_ref, rows, slow_main, near_main):
     @pl.when(slot == 0)
     def _():
-        out_ref[:, :LANES] = slow_main
-        out_ref[:, 2 * LANES :] = fast_main
+        out_ref[rows, :LANES] = slow_main
+        out_ref[rows, 2 * LANES :] = near_main
 
     @pl.when(slot != 0)
     def _():
-        out_ref[:, :LANES] = fast_main
-        out_ref[:, 2 * LANES :] = slow_main
-
-
-def fill_kernel(plan_ref, slow_ref, near_ref, near_turn_ref, *refs):
-    out_ref = refs[-1]
+        out_ref[rows, :LANES] = near_main
+        out_ref[rows, 2 * LANES :] = slow_main
+
+
+def slot_lanes(slot, rows):
+    lane = lax.broadcasted_iota(jnp.int32, (rows, LANES), 1)
+    return (lane // (LANES // 2)) == slot
+
+
+def fill_kernel(plan_ref, near_ref, near_turn_ref, *refs):
+    slow_refs, out_ref = refs[:-2], refs[-1]
     half = UNIT // 2
     slot = moves(plan_ref)[3]
+    mask = slot_lanes(slot, half)
     middle = slice(LANES, 2 * LANES)
-    near = dot32(near_ref[...], near_turn_ref[...])
-    place_main(slot, out_ref, slow_ref[:UNIT], near[:, LANES:].astype(jnp.bfloat16))
-    lane = lax.broadcasted_iota(jnp.int32, (half, LANES), 1)
-    mask = (lane // (LANES // 2)) == slot
-    slow = slow_ref[UNIT:].astype(jnp.float32)
-    top = jnp.where(mask, slow, near[:half, :LANES])
-    low = jnp.where(mask, pltpu.roll(slow, LANES // 2, 1), near[half:, :LANES])
-    out_ref[:half, middle] = top.astype(jnp.bfloat16)
-    out_ref[half:, middle] = low.astype(jnp.bfloat16)
-
-
-def raw_kernel(plan_ref, slow_ref, slow_turn_ref, near_ref, near_turn_ref, out_ref):
+    for unit, slow_ref in enumerate(slow_refs):
+        start = unit * UNIT
+        rows = slice(start, start + UNIT)
+        near = dot32(near_ref[rows], near_turn_ref[...])
+        place_main(slot, out_ref, rows, slow_ref[:UNIT], near[:, LANES:].astype(jnp.bfloat16))
+        slow = slow_ref[UNIT:].astype(jnp.float32)
+        top = jnp.where(mask, slow, near[:half, :LANES])
+        low = jnp.where(mask, pltpu.roll(slow, LANES // 2, 1), near[half:, :LANES])
+        out_ref[start : start + half, middle] = top.astype(jnp.bfloat16)
+        out_ref[start + half : start + UNIT, middle] = low.astype(jnp.bfloat16)
+
+
+def raw_kernel(plan_ref, near_ref, near_turn_ref, slow_ref, slow_turn_ref, out_ref):
     size = slow_ref.shape[1]
     slot = moves(plan_ref)[3]
-    near = dot32(near_ref[...], near_turn_ref[...])
-    mixed = dot32(slow_ref[...], slow_turn_ref[:size])
-    main = dot32(slow_ref[...], slow_turn_ref[size:])
-    place_main(slot, out_ref, main.astype(jnp.bfloat16), near[:, LANES:].astype(jnp.bfloat16))
-    lane = lax.broadcasted_iota(jnp.int32, mixed.shape, 1)
-    mask = (lane // (LANES // 2)) == slot
-    middle = jnp.where(mask, mixed, near[:, :LANES])
-    out_ref[:, LANES : 2 * LANES] = middle.astype(jnp.bfloat16)
+    mask = slot_lanes(slot, UNIT)
+    slow_turn = jnp.concatenate([slow_turn_ref[:size], slow_turn_ref[size:]], axis=1)
+    for unit in range(out_ref.shape[0] // UNIT):
+        rows = slice(unit * UNIT, (unit + 1) * UNIT)
+        near = dot32(near_ref[rows], near_turn_ref[...])
+        slow = dot32(slow_ref[rows], slow_turn)
+        near_main = near[:, LANES:].astype(jnp.bfloat16)
+        place_main(slot, out_ref, rows, slow[:, LANES:].astype(jnp.bfloat16), near_main)
+        middle = jnp.where(mask, slow[:, :LANES], near[:, :LANES])
+        out_ref[rows, LANES : 2 * LANES] = middle.astype(jnp.bfloat16)
 
 
 def fill_rows(kernel, plan, sources, specs, near, near_turn, result, start, count):
     shape = near.shape
-    first = start // UNIT
-    operands = [plan, *sources, near, near_turn]
-    row_spec = pl.BlockSpec((UNIT, shape[1]), lambda i: (first + i, 0))
+    first = start // FILL_TILE
+    operands = [plan, near, near_turn, *sources]
+    row_spec = pl.BlockSpec((FILL_TILE, shape[1]), lambda i: (first + i, 0))
     in_specs = [
         pl.BlockSpec(memory_space=pltpu.SMEM),
-        *specs,
         row_spec,
         pl.BlockSpec(near_turn.shape, lambda i: (0, 0)),
+        *specs,
     ]
     aliases = {}
     if result is not None:
@@ -492,7 +510,7 @@
         in_specs.append(pl.BlockSpec(memory_space=pl.ANY))
     return pl.pallas_call(
         kernel,
-        grid=(count // UNIT,),
+        grid=(count // FILL_TILE,),
         in_specs=in_specs,
         out_specs=row_spec,
         out_shape=jax.ShapeDtypeStruct(shape, jnp.bfloat16),
@@ -522,21 +540,35 @@
     return lax.ppermute(value, "blk", pairs)
 
 
-def cycle_sums(sums):
+def joined(pieces):
+    values = pieces.astype(jnp.float32)
+    row = lax.broadcasted_iota(jnp.int32, (SUBS, LANES), 0)
+    off = values[0:1] + values[1:2] + values[2:3]
+    diag = values[3:4] + values[4:5] + values[5:6]
+    return jnp.where(row == 0, off, diag)
+
+
+def add_pairs(left, right):
+    total = left[0] + right[0]
+    moved = total - left[0]
+    lost = (left[0] - (total - moved)) + (right[0] - moved)
+    small = left[1] + right[1] + lost
+    high = total + small
+    return high, small - (high - total)
+
+
+def cycle_sums(mine, theirs):
     count = lax.axis_size("blk")
-    outer = [place for place in range(count) if place % 4 in (0, 3)]
-    inner = [place for place in range(count) if place % 4 in (1, 2)]
-    is_outer = (lax.axis_index("blk") + 1) % 4 < 2
-    sums = sums + permuted(sums, [(place, place ^ 1) for place in range(count)])
-    sums = sums + permuted(sums, [(place, place ^ 3) for place in outer])
-    moved = permuted(sums, [(place, place ^ 1) for place in outer])
-    sums = jnp.where(is_outer, sums, moved)
-    step = 4
+    zero = jnp.zeros((SUBS, LANES), jnp.float32)
+    sums = add_pairs((joined(mine), zero), (joined(theirs), zero))
+    step = 1
     while step < count:
-        sums = sums + permuted(sums, [(place, place ^ step) for place in inner])
+        if step != 2:
+            pairs = [(place, place ^ step) for place in range(count)]
+            moved = permuted(jnp.concatenate(sums, axis=0), pairs)
+            sums = add_pairs(sums, (moved[:SUBS], moved[SUBS:]))
         step *= 2
-    moved = permuted(sums, [(place, place ^ 1) for place in inner])
-    return jnp.where(is_outer, moved, sums)
+    return sums[0]
 
 
 def on_device(matrix, plan):
@@ -556,22 +588,31 @@
     first = swapped_with(first, "blk", slow_partner)
     last = swapped_with(last, "blk", slow_partner)
     near_turn = swapped_with(near_turn, "blk", fast_partner)
-    totals = cycle_sums(sums)
+    theirs = first[first.shape[0] - SUM_ROWS :]
+    theirs, near_turn = lax.optimization_barrier((theirs, near_turn))
+    totals = cycle_sums(sums, theirs)
     off_ratio = jnp.sqrt(totals[0, 0] / totals[1, 0])
 
+    def pack_specs(skip):
+        units = FILL_TILE // UNIT
+        return [
+            pl.BlockSpec((PACK, LANES), lambda i, unit=unit: (skip + units * i + unit, 0))
+            for unit in range(units)
+        ]
+
+    units = FILL_TILE // UNIT
     turn_spec = pl.BlockSpec((PACK, LANES), lambda i: (0, 0))
-    raw_spec = pl.BlockSpec((UNIT, size), lambda i: (i, 0))
-    first_spec = pl.BlockSpec((PACK, LANES), lambda i: (1 + i, 0))
-    last_spec = pl.BlockSpec((PACK, LANES), lambda i: (i, 0))
+    raw_spec = pl.BlockSpec((FILL_TILE, size), lambda i: (i, 0))
     middle = rows - RAW_ROWS - LAST_ROWS
     result = fill_rows(
         raw_kernel, plan, [raw, first], [raw_spec, turn_spec], near, near_turn, None, 0, RAW_ROWS
     )
     result = fill_rows(
-        fill_kernel, plan, [first], [first_spec], near, near_turn, result, RAW_ROWS, middle
+        fill_kernel, plan, [first] * units, pack_specs(1), near, near_turn, result, RAW_ROWS, middle
     )
     result = fill_rows(
-        fill_kernel, plan, [last], [last_spec], near, near_turn, result, rows - LAST_ROWS, LAST_ROWS
+        fill_kernel, plan, [last] * units, pack_specs(0), near, near_turn, result,
+        rows - LAST_ROWS, LAST_ROWS,
     )
     return result, off_ratio
 

time: 94.7 us -> 96.6 us (1.020); the launches traced: 93.9 us -> 94.8 us
  waiting for transfers between devices: 34.8 us -> 40.3 us
  starting transfers between devices: 20.5 us -> 15.4 us
    ppermute x6, waiting for transfers between devices: 6.15 us -> 38.1 us  [swapped_with(): lax.ppermute(value, axis, [(source, partner(source, count)) for source in...]
    ppermute x6 -> x3, waiting for transfers between devices: 28.6 us -> 2.2 us  [permuted(): return lax.ppermute(value, 'blk', pairs)]
    ppermute x6 -> x3, starting transfers between devices: 11.9 us -> 4.48 us  [permuted(): return lax.ppermute(value, 'blk', pairs)]
    pallas_call x3, Pallas kernels: 13.7 us -> 10.2 us  [fill_rows(): pl.pallas_call(kernel, grid=(count // FILL_TILE,), in_specs=in_specs, out...]
    pallas_call x1, Pallas kernels: 14.7 us -> 17.5 us  [jacobi(): pl.pallas_call(jacobi_kernel, out_shape=(jax.ShapeDtypeStruct((blocks * P...]
    ppermute x6, starting transfers between devices: 8.6 us -> 10.9 us  [swapped_with(): lax.ppermute(value, axis, [(source, partner(source, count)) for source in...]
    pallas_call x1, Pallas kernels: 5.35 us -> 6.33 us  [gram_blocks(): pl.pallas_call(gram_kernel, in_specs=[pl.BlockSpec(memory_space=pl.ANY)],...]
  transfers between devices with their start and end apart: 12 -> 9, of which waited for: 6 -> 5; matrix products, arithmetic and copies ran while one was open for 1% -> 0% of each run, Pallas kernels for 25% -> 29%
where the time goes in v8:
time: 96.6 us; the launch traced here: 94.8 us
  waiting for transfers between devices  40.3 us (42%)
  Pallas kernels  34 us (35%)
  starting transfers between devices  15.4 us (16%)
  between operations  3.26 us (3%)
  local copies, waits for them, and re-layouts  1.6 us (2%)
    ppermute x6, waiting for transfers between devices, swapped_with(): lax.ppermute(value, axis, [(source, partner(source, count)) for source in...  38.1 us
    pallas_call x1, Pallas kernels, jacobi(): pl.pallas_call(jacobi_kernel, out_shape=(jax.ShapeDtypeStruct((blocks * P...  17.5 us
    ppermute x6, starting transfers between devices, swapped_with(): lax.ppermute(value, axis, [(source, partner(source, count)) for source in...  10.9 us
    pallas_call x3, Pallas kernels, fill_rows(): pl.pallas_call(kernel, grid=(count // FILL_TILE,), in_specs=in_specs, out...  10.2 us
    pallas_call x1, Pallas kernels, gram_blocks(): pl.pallas_call(gram_kernel, in_specs=[pl.BlockSpec(memory_space=pl.ANY)],...  6.33 us
    ppermute x3, starting transfers between devices, permuted(): return lax.ppermute(value, 'blk', pairs)  4.48 us
    ppermute x3, waiting for transfers between devices, permuted(): return lax.ppermute(value, 'blk', pairs)  2.2 us
  transfers between devices with their start and end apart: 9, of which 5 were waited for; matrix products, arithmetic and copies ran while one was open for 0% of the time, Pallas kernels for 29%

profile of v8, /device:TPU:1, one launch (start us, length us, event | category | flops | bytes accessed | tf_op | source)
XLA Modules:
  0.0 94.8 jit_solution(10720847923240347179)
XLA Ops:
  0.6 0.0 copy-start
  0.6 0.0 copy-start.2
  0.6 6.3 %gram_blocks.1 = (f32[256,384]{1,0:T(8,128)}, bf16[2048,384]{1,0:T(8,128)(2,1)}) custom-call(bf16[6144,384]{1,0:T(8,128)(2,1)} %refs_2_.1), custom_call_target="tpu_custom_call" | custom-call | flops 1811939328 | bytes 4718592 | tf_op jit(solution)/shard_map/gram_blocks/pallas_call | solution.py:422
  7.0 0.0 copy-done
  7.0 0.1 collective-permute-start.2
  7.1 2.7 %collective-permute-start.1 = (bf16[2048,384]{1,0:T(8,128)(2,1)}, bf16[2048,384]{1,0:T(8,128)(2,1)S(1)}, u32[]{:S(2)}, u32[]{:S(2)}) collective-permute-start(bf16[2048,384]{1,0:T(8,128)(2,1)} %get-tuple-element.18), channel_id=1, source_target_pairs={{0,30},{2,4},{4,2},{6,8},{8,6},{10,12},{12,10},{14,16},{16,14},{18... | collective-permute-start | bytes 4718600 | tf_op jit(solution)/shard_map/ppermute | solution.py:528
  9.8 1.2 %collective-permute-start = (f32[256,384]{1,0:T(8,128)}, f32[256,384]{1,0:T(8,128)S(1)}, u32[]{:S(2)}, u32[]{:S(2)}) collective-permute-start(f32[256,384]{1,0:T(8,128)} %get-tuple-element.16.refs_0_), channel_id=1, source_target_pairs={{0,1},{1,0},{2,3},{3,2},{4,5},{5,4},{6,7},{7,6},{8,9},{9,8},{10,11... | collective-permute-start | bytes 1179656 | tf_op jit(solution)/shard_map/ppermute | solution.py:528
  11.0 6.1 %collective-permute-done.refs_1_ = f32[256,384]{1,0:T(8,128)S(1)} collective-permute-done((f32[256,384]{1,0:T(8,128)}, f32[256,384]{1,0:T(8,128)S(1)}, u32[]{:S(2)}, u32[]{:S(2)}) %collective-permute-start) | collective-permute-done | bytes 393248 | tf_op jit(solution)/shard_map/ppermute | solution.py:528
  17.1 0.0 copy-done.2
  17.1 0.0 copy-start.1
  17.1 1.0 %copy-done.1 = f32[256,384]{1,0:T(8,128)S(1)} copy-done((f32[256,384]{1,0:T(8,128)S(1)}, f32[256,384]{1,0:T(8,128)}, u32[]{:S(2)}) %copy-start.1) | copy-done | bytes 393240
  18.1 17.5 %jacobi_turns.1 = (bf16[3856,128]{1,0:T(8,128)(2,1)S(1)}, bf16[3072,128]{1,0:T(8,128)(2,1)S(1)}, bf16[384,256]{1,0:T(8,128)(2,1)S(1)}, bf16[16,128]{1,0:T(8,128)(2,1)S(1)}) custom-call(s32[32]{0:T(128)S(1)} %copy-done.2, f32[256,384]{1,0:T(8,128)S(1)} %copy-done.1, f32[256,384]{1,0:T(8,128)S(1)} %collective-permute-done.refs_1_, bf16[6144,384]{1,0:T(8,128)(2,1)S(1)} %copy-done), custom_call_target="tpu_custom_call" | custom-call | flops 384 | bytes 384 | tf_op jit(solution)/shard_map/jacobi_turns/pallas_call | solution.py:344
  35.6 4.5 %collective-permute-start.3 = (bf16[3856,128]{1,0:T(8,128)(2,1)S(1)}, bf16[3856,128]{1,0:T(8,128)(2,1)S(1)}, u32[]{:S(2)}, u32[]{:S(2)}) collective-permute-start(bf16[3856,128]{1,0:T(8,128)(2,1)S(1)} %get-tuple-element.21), channel_id=1, source_target_pairs={{0,30},{2,4},{4,2},{6,8},{8,6},{10,12},{12,10},{14,16},{16,14},{18... | collective-permute-start | bytes 2961416 | tf_op jit(solution)/shard_map/ppermute | solution.py:528
  40.1 14.8 %collective-permute-done.1.slow_ref = bf16[2048,384]{1,0:T(8,128)(2,1)S(1)} collective-permute-done((bf16[2048,384]{1,0:T(8,128)(2,1)}, bf16[2048,384]{1,0:T(8,128)(2,1)S(1)}, u32[]{:S(2)}, u32[]{:S(2)}) %collective-permute-start.1) | collective-permute-done | bytes 1572896 | tf_op jit(solution)/shard_map/ppermute | solution.py:528
  54.9 0.0 collective-permute-done.2.near_ref
  54.9 0.0 collective-permute-start.4
  54.9 2.4 %collective-permute-start.5 = (bf16[3072,128]{1,0:T(8,128)(2,1)S(1)}, bf16[3072,128]{1,0:T(8,128)(2,1)S(1)}, u32[]{:S(2)}, u32[]{:S(2)}) collective-permute-start(bf16[3072,128]{1,0:T(8,128)(2,1)S(1)} %get-tuple-element.24), channel_id=1, source_target_pairs={{0,30},{2,4},{4,2},{6,8},{8,6},{10,12},{12,10},{14,16},{16,14},{18... | collective-permute-start | bytes 2359304 | tf_op jit(solution)/shard_map/ppermute | solution.py:528
  57.3 17.2 %collective-permute-done.3.slow_turn_ref.refs_0_.refs_1_ = bf16[3856,128]{1,0:T(8,128)(2,1)S(1)} collective-permute-done((bf16[3856,128]{1,0:T(8,128)(2,1)S(1)}, bf16[3856,128]{1,0:T(8,128)(2,1)S(1)}, u32[]{:S(2)}, u32[]{:S(2)}) %collective-permute-start.3) | collective-permute-done | bytes 987168 | tf_op jit(solution)/shard_map/ppermute | solution.py:528
  74.5 0.0 collective-permute-done.4.near_turn_ref
  74.5 0.1 fusion.1
  74.6 0.0 collective-permute-start.6
  74.7 1.2 %collective-permute-done.6 = f32[16,128]{1,0:T(8,128)S(1)} collective-permute-done((f32[16,128]{1,0:T(8,128)S(1)}, f32[16,128]{1,0:T(8,128)S(1)}, u32[]{:S(2)}, u32[]{:S(2)}) %collective-permute-start.6) | collective-permute-done | bytes 8224 | tf_op jit(solution)/shard_map/ppermute | solution.py:540
  75.8 0.1 subtract_subtract_fusion.1
  75.9 1.9 %collective-permute-start.7 = (f32[16,128]{1,0:T(8,128)S(1)}, f32[16,128]{1,0:T(8,128)S(1)}, u32[]{:S(2)}, u32[]{:S(2)}) collective-permute-start(f32[16,128]{1,0:T(8,128)S(1)} %pad_maximum_fusion.1), channel_id=1, source_target_pairs={{0,8},{2,10},{4,12},{6,14},{8,0},{10,2},{12,4},{14,6},{16,24},{18,... | collective-permute-start | bytes 24584 | tf_op jit(solution)/shard_map/ppermute | solution.py:540
  77.8 1.0 %collective-permute-done.7 = f32[16,128]{1,0:T(8,128)S(1)} collective-permute-done((f32[16,128]{1,0:T(8,128)S(1)}, f32[16,128]{1,0:T(8,128)S(1)}, u32[]{:S(2)}, u32[]{:S(2)}) %collective-permute-start.7) | collective-permute-done | bytes 8224 | tf_op jit(solution)/shard_map/ppermute | solution.py:540
  78.9 2.5 %collective-permute-start.8 = (f32[16,128]{1,0:T(8,128)S(1)}, f32[16,128]{1,0:T(8,128)S(1)}, u32[]{:S(2)}, u32[]{:S(2)}) collective-permute-start(f32[16,128]{1,0:T(8,128)S(1)} %pad_maximum_fusion.2), channel_id=1, source_target_pairs={{0,16},{2,18},{4,20},{6,22},{8,24},{10,26},{12,28},{14,30},{16,0},... | collective-permute-start | bytes 24584 | tf_op jit(solution)/shard_map/ppermute | solution.py:540
  81.4 3.4 %fill_rows.3.refs_2_ = bf16[6144,384]{1,0:T(8,128)(2,1)} custom-call(s32[32]{0:T(128)S(1)} %copy-done.2, bf16[6144,384]{1,0:T(8,128)(2,1)S(1)} %collective-permute-done.2.near_ref, bf16[384,256]{1,0:T(8,128)(2,1)S(1)} %collective-permute-done.4.near_turn_ref, bf16[2048,384]{1,0:T(8,128)(2,1)S(1)} %collective-permute-done.1.slow_ref, ...), custom_call_target="tpu_custom_call" | custom-call | flops 786432 | bytes 3145728 | tf_op jit(solution)/shard_map/fill_rows/pallas_call | solution.py:511
  84.9 3.4 %fill_rows.4.refs_2_ = bf16[6144,384]{1,0:T(8,128)(2,1)} custom-call(s32[32]{0:T(128)S(1)} %copy-done.2, bf16[6144,384]{1,0:T(8,128)(2,1)S(1)} %collective-permute-done.2.near_ref, bf16[384,256]{1,0:T(8,128)(2,1)S(1)} %collective-permute-done.4.near_turn_ref, ...), custom_call_target="tpu_custom_call", output_to_operand_aliasing={{}: (5, {})} | custom-call | flops 786432 | bytes 3145728 | tf_op jit(solution)/shard_map/fill_rows/pallas_call | solution.py:511
  88.2 0.0 collective-permute-done.5.refs_0_.refs_1_
  88.2 3.4 %fill_rows.5 = bf16[6144,384]{1,0:T(8,128)(2,1)} custom-call(s32[32]{0:T(128)S(1)} %copy-done.2, bf16[6144,384]{1,0:T(8,128)(2,1)S(1)} %collective-permute-done.2.near_ref, bf16[384,256]{1,0:T(8,128)(2,1)S(1)} %collective-permute-done.4.near_turn_ref, bf16[3072,128]{1,0:T(8,128)(2,1)S(1)} %collective-permute-done.5.refs_0_.refs_1_, ...), custom_call_target="tpu_custom_call", output_to_operand_aliasing={{}: (5, {})} | custom-call | flops 786432 | bytes 3145728 | tf_op jit(solution)/shard_map/fill_rows/pallas_call | solution.py:511
  91.6 0.0 collective-permute-done.8
  91.6 0.6 fusion.17
  (10 shorter events, 0.1 us)
Async XLA Ops:
  0.6 6.4 %copy-start = (bf16[6144,384]{1,0:T(8,128)(2,1)S(1)}, bf16[6144,384]{1,0:T(8,128)(2,1)}, u32[]{:S(2)}) copy-start(bf16[6144,384]{1,0:T(8,128)(2,1)} %refs_2_.1) | copy-start | bytes 14155780
  0.6 16.5 %copy-start.2 = (s32[32]{0:T(128)S(1)}, s32[32]{0:T(128)}, u32[]{:S(2)}) copy-start(s32[32]{0:T(128)} %plan_ref.7) | copy-start | bytes 388
  7.0 47.9 %collective-permute-start.2 = (bf16[6144,384]{1,0:T(8,128)(2,1)S(1)}, bf16[6144,384]{1,0:T(8,128)(2,1)S(1)}, u32[]{:S(2)}, u32[]{:S(2)}) collective-permute-start(bf16[6144,384]{1,0:T(8,128)(2,1)S(1)} %copy-done), channel_id=1, source_target_pairs={{0,2},{2,0},{4,6},{6,4},{8,10},{10,8},{12,14},{14,12},{16,18},{18,... | collective-permute-start | bytes 14155784 | tf_op jit(solution)/shard_map/ppermute | solution.py:528
  7.1 47.8 %collective-permute-start.1 = (bf16[2048,384]{1,0:T(8,128)(2,1)}, bf16[2048,384]{1,0:T(8,128)(2,1)S(1)}, u32[]{:S(2)}, u32[]{:S(2)}) collective-permute-start(bf16[2048,384]{1,0:T(8,128)(2,1)} %get-tuple-element.18), channel_id=1, source_target_pairs={{0,30},{2,4},{4,2},{6,8},{8,6},{10,12},{12,10},{14,16},{16,14},{18... | collective-permute-start | bytes 4718600 | tf_op jit(solution)/shard_map/ppermute | solution.py:528
  9.8 7.3 %collective-permute-start = (f32[256,384]{1,0:T(8,128)}, f32[256,384]{1,0:T(8,128)S(1)}, u32[]{:S(2)}, u32[]{:S(2)}) collective-permute-start(f32[256,384]{1,0:T(8,128)} %get-tuple-element.16.refs_0_), channel_id=1, source_target_pairs={{0,1},{1,0},{2,3},{3,2},{4,5},{5,4},{6,7},{7,6},{8,9},{9,8},{10,11... | collective-permute-start | bytes 1179656 | tf_op jit(solution)/shard_map/ppermute | solution.py:528
  17.1 1.0 %copy-start.1 = (f32[256,384]{1,0:T(8,128)S(1)}, f32[256,384]{1,0:T(8,128)}, u32[]{:S(2)}) copy-start(f32[256,384]{1,0:T(8,128)} %get-tuple-element.16.refs_0_) | copy-start | bytes 1179652
  35.6 38.9 %collective-permute-start.3 = (bf16[3856,128]{1,0:T(8,128)(2,1)S(1)}, bf16[3856,128]{1,0:T(8,128)(2,1)S(1)}, u32[]{:S(2)}, u32[]{:S(2)}) collective-permute-start(bf16[3856,128]{1,0:T(8,128)(2,1)S(1)} %get-tuple-element.21), channel_id=1, source_target_pairs={{0,30},{2,4},{4,2},{6,8},{8,6},{10,12},{12,10},{14,16},{16,14},{18... | collective-permute-start | bytes 2961416 | tf_op jit(solution)/shard_map/ppermute | solution.py:528
  54.9 19.6 %collective-permute-start.4 = (bf16[384,256]{1,0:T(8,128)(2,1)S(1)}, bf16[384,256]{1,0:T(8,128)(2,1)S(1)}, u32[]{:S(2)}, u32[]{:S(2)}) collective-permute-start(bf16[384,256]{1,0:T(8,128)(2,1)S(1)} %get-tuple-element.22), channel_id=1, source_target_pairs={{0,2},{2,0},{4,6},{6,4},{8,10},{10,8},{12,14},{14,12},{16,18},{18,... | collective-permute-start | bytes 589832 | tf_op jit(solution)/shard_map/ppermute | solution.py:528
  54.9 33.3 %collective-permute-start.5 = (bf16[3072,128]{1,0:T(8,128)(2,1)S(1)}, bf16[3072,128]{1,0:T(8,128)(2,1)S(1)}, u32[]{:S(2)}, u32[]{:S(2)}) collective-permute-start(bf16[3072,128]{1,0:T(8,128)(2,1)S(1)} %get-tuple-element.24), channel_id=1, source_target_pairs={{0,30},{2,4},{4,2},{6,8},{8,6},{10,12},{12,10},{14,16},{16,14},{18... | collective-permute-start | bytes 2359304 | tf_op jit(solution)/shard_map/ppermute | solution.py:528
  74.6 1.2 %collective-permute-start.6 = (f32[16,128]{1,0:T(8,128)S(1)}, f32[16,128]{1,0:T(8,128)S(1)}, u32[]{:S(2)}, u32[]{:S(2)}) collective-permute-start(f32[16,128]{1,0:T(8,128)S(1)} %pad_maximum_fusion), channel_id=1, source_target_pairs={{0,2},{2,0},{4,6},{6,4},{8,10},{10,8},{12,14},{14,12},{16,18},{18,... | collective-permute-start | bytes 24584 | tf_op jit(solution)/shard_map/ppermute | solution.py:540
  75.9 2.9 %collective-permute-start.7 = (f32[16,128]{1,0:T(8,128)S(1)}, f32[16,128]{1,0:T(8,128)S(1)}, u32[]{:S(2)}, u32[]{:S(2)}) collective-permute-start(f32[16,128]{1,0:T(8,128)S(1)} %pad_maximum_fusion.1), channel_id=1, source_target_pairs={{0,8},{2,10},{4,12},{6,14},{8,0},{10,2},{12,4},{14,6},{16,24},{18,... | collective-permute-start | bytes 24584 | tf_op jit(solution)/shard_map/ppermute | solution.py:540
  78.9 12.7 %collective-permute-start.8 = (f32[16,128]{1,0:T(8,128)S(1)}, f32[16,128]{1,0:T(8,128)S(1)}, u32[]{:S(2)}, u32[]{:S(2)}) collective-permute-start(f32[16,128]{1,0:T(8,128)S(1)} %pad_maximum_fusion.2), channel_id=1, source_target_pairs={{0,16},{2,18},{4,20},{6,22},{8,24},{10,26},{12,28},{14,30},{16,0},... | collective-permute-start | bytes 24584 | tf_op jit(solution)/shard_map/ppermute | solution.py:540

commit v9 on v8

--- a/solution.py
+++ b/solution.py
@@ -10,16 +10,15 @@
 SUBS = 8
 UNIT = 512
 PACK = UNIT + UNIT // 2
-GRAM_PARTS = (512, 1536)
-GRAM_TILE = 2048
-RAW_ROWS = 2048
-LAST_ROWS = 2048
-FILL_TILE = 1024
+GRAM_PARTS = (512, 1024)
+GRAM_TILE = 1536
+RAW_ROWS = 1536
+LAST_ROWS = 1536
+FILL_TILE = 512
 SUM_ROWS = 16
 IN_FLIGHT = 2
-VMEM_LIMIT = 32 * 1024 * 1024
-JACOBI_VMEM_LIMIT = 30 * 1024 * 1024
-GRAM_VMEM_LIMIT = 58 * 1024 * 1024
+VMEM_LIMIT = 60 * 1024 * 1024
+FILL_VMEM_LIMIT = 32 * 1024 * 1024
 
 
 def split_three(values):
@@ -137,13 +136,19 @@
 
 
 def jacobi_kernel(plan_ref, *refs):
-    jacobi_body(plan_ref, refs[:-14], *refs[-14:])
+    jacobi_body(plan_ref, refs[:-17], *refs[-17:])
 
 
 def jacobi_body(
-    plan_ref, gram_refs, matrix_ref, first_ref, last_ref, fast_ref, sums_ref,
-    gram_a, gram_b, basis_a, basis_b, cos_buf, sin_buf, held, packs, sems,
+    plan_ref, gram_refs, matrix_ref, head_ref, first_ref, last_ref, fast_ref, sums_ref,
+    gram_a, gram_b, basis_a, basis_b, cos_buf, sin_buf, held, packs, gram_held, gram_sems, sems,
 ):
+    gram_copies = [
+        pltpu.make_async_copy(ref, gram_held.at[index], gram_sems.at[index])
+        for index, ref in enumerate(gram_refs)
+    ]
+    for copy in gram_copies:
+        copy.start()
     matrix_copy = pltpu.make_async_copy(matrix_ref.at[pl.ds(RAW_ROWS, held.shape[0])], held, sems.at[0])
     matrix_copy.start()
     size = gram_refs[0].shape[1]
@@ -164,9 +169,11 @@
     lane_slot = slot_of_lane(lax.broadcasted_iota(jnp.int32, (1, 4 * LANES), 1), half)
     take_cols = onehot(lax.broadcasted_iota(jnp.int32, (size, 4 * LANES), 0), lane_slot)
     arranged = jnp.zeros((size, 4 * LANES), jnp.float32)
-    packed = gram_refs[0][...]
-    for other in gram_refs[1:]:
-        packed = packed + other[...]
+    for copy in gram_copies:
+        copy.wait()
+    packed = gram_held[0]
+    for index in range(1, len(gram_refs)):
+        packed = packed + gram_held[index]
     gram_sum = full_gram(packed)
     sums_ref[...] = block_sums(packed)
     for piece in split_three(gram_sum):
@@ -318,19 +325,18 @@
         )
         copies[-1].start()
 
-    first_count = first_ref.shape[0] - SUM_ROWS
-    leave(0, PACK, first_ref.at[pl.ds(0, PACK)])
-    copies.append(
-        pltpu.make_async_copy(sums_ref, first_ref.at[pl.ds(first_count, SUM_ROWS)], sems.at[2])
-    )
+    leave(0, PACK, head_ref.at[pl.ds(0, PACK)])
+    copies.append(pltpu.make_async_copy(sums_ref, head_ref.at[pl.ds(PACK, SUM_ROWS)], sems.at[2]))
     copies[-1].start()
+    first_count = first_ref.shape[0]
     for unit in range(held.shape[0] // UNIT):
         at = (1 + unit) * PACK
         pack_unit(held[unit * UNIT : (unit + 1) * UNIT], slow, packs, at)
-        if at < first_count:
-            leave(at, PACK, first_ref.at[pl.ds(at, PACK)])
+        place = unit * PACK
+        if place < first_count:
+            leave(at, PACK, first_ref.at[pl.ds(place, PACK)])
         else:
-            leave(at, PACK, last_ref.at[pl.ds(at - first_count, PACK)])
+            leave(at, PACK, last_ref.at[pl.ds(place - first_count, PACK)])
     for copy in copies:
         copy.wait()
 
@@ -344,15 +350,15 @@
     return pl.pallas_call(
         jacobi_kernel,
         out_shape=(
-            jax.ShapeDtypeStruct((blocks * PACK - last + SUM_ROWS, LANES), jnp.bfloat16),
+            jax.ShapeDtypeStruct((PACK + SUM_ROWS, LANES), jnp.bfloat16),
+            jax.ShapeDtypeStruct(((blocks - 1) * PACK - last, LANES), jnp.bfloat16),
             jax.ShapeDtypeStruct((last, LANES), jnp.bfloat16),
             jax.ShapeDtypeStruct((size, 2 * LANES), jnp.bfloat16),
             jax.ShapeDtypeStruct((SUM_ROWS, LANES), jnp.bfloat16),
         ),
         in_specs=[pl.BlockSpec(memory_space=pltpu.SMEM)]
-        + [pl.BlockSpec(memory_space=pltpu.VMEM)] * len(grams)
-        + [pl.BlockSpec(memory_space=pl.ANY)],
-        out_specs=[pl.BlockSpec(memory_space=pl.ANY)] * 2
+        + [pl.BlockSpec(memory_space=pl.ANY)] * (len(grams) + 1),
+        out_specs=[pl.BlockSpec(memory_space=pl.ANY)] * 3
         + [pl.BlockSpec(memory_space=pltpu.VMEM)] * 2,
         scratch_shapes=[
             pltpu.VMEM((2, groups, SUBS, 4 * LANES), jnp.float32),
@@ -363,9 +369,11 @@
             pltpu.VMEM((groups, SUBS, LANES), jnp.float32),
             pltpu.VMEM((moved, size), jnp.bfloat16),
             pltpu.VMEM((blocks * PACK, LANES), jnp.bfloat16),
+            pltpu.VMEM((len(grams), 2 * LANES, size), jnp.float32),
+            pltpu.SemaphoreType.DMA((len(grams),)),
             pltpu.SemaphoreType.DMA((2 + blocks,)),
         ],
-        compiler_params=pltpu.CompilerParams(vmem_limit_bytes=JACOBI_VMEM_LIMIT),
+        compiler_params=pltpu.CompilerParams(vmem_limit_bytes=VMEM_LIMIT),
         cost_estimate=pl.CostEstimate(
             flops=size, bytes_accessed=size, transcendentals=0
         ),
@@ -434,7 +442,7 @@
             pltpu.SemaphoreType.DMA((len(gram_spans(rows)),)),
             pltpu.SemaphoreType.DMA,
         ],
-        compiler_params=pltpu.CompilerParams(vmem_limit_bytes=GRAM_VMEM_LIMIT),
+        compiler_params=pltpu.CompilerParams(vmem_limit_bytes=VMEM_LIMIT),
         cost_estimate=pl.CostEstimate(
             flops=2 * rows * size * size, bytes_accessed=2 * rows * size, transcendentals=0
         ),
@@ -515,7 +523,7 @@
         out_specs=row_spec,
         out_shape=jax.ShapeDtypeStruct(shape, jnp.bfloat16),
         input_output_aliases=aliases,
-        compiler_params=pltpu.CompilerParams(vmem_limit_bytes=VMEM_LIMIT),
+        compiler_params=pltpu.CompilerParams(vmem_limit_bytes=FILL_VMEM_LIMIT),
         cost_estimate=pl.CostEstimate(
             flops=count * shape[1], bytes_accessed=4 * count * shape[1], transcendentals=0
         ),
@@ -582,14 +590,14 @@
         grams = [lax.psum(own, "rows")]
     raw = swapped_with(early, "blk", slow_partner)
     near = swapped_with(matrix_after, "blk", fast_partner)
-    first, last, near_turn, sums = jacobi(plan, grams, matrix)
-    near_turn, raw, near = lax.optimization_barrier((near_turn, raw, near))
-
+    head, first, last, near_turn, sums = jacobi(plan, grams, matrix)
+
+    head = swapped_with(head, "blk", slow_partner)
     first = swapped_with(first, "blk", slow_partner)
     last = swapped_with(last, "blk", slow_partner)
     near_turn = swapped_with(near_turn, "blk", fast_partner)
-    theirs = first[first.shape[0] - SUM_ROWS :]
-    theirs, near_turn = lax.optimization_barrier((theirs, near_turn))
+    theirs = head[PACK:]
+    theirs, near_turn, raw, near = lax.optimization_barrier((theirs, near_turn, raw, near))
     totals = cycle_sums(sums, theirs)
     off_ratio = jnp.sqrt(totals[0, 0] / totals[1, 0])
 
@@ -605,10 +613,10 @@
     raw_spec = pl.BlockSpec((FILL_TILE, size), lambda i: (i, 0))
     middle = rows - RAW_ROWS - LAST_ROWS
     result = fill_rows(
-        raw_kernel, plan, [raw, first], [raw_spec, turn_spec], near, near_turn, None, 0, RAW_ROWS
+        raw_kernel, plan, [raw, head], [raw_spec, turn_spec], near, near_turn, None, 0, RAW_ROWS
     )
     result = fill_rows(
-        fill_kernel, plan, [first] * units, pack_specs(1), near, near_turn, result, RAW_ROWS, middle
+        fill_kernel, plan, [first] * units, pack_specs(0), near, near_turn, result, RAW_ROWS, middle
     )
     result = fill_rows(
         fill_kernel, plan, [last] * units, pack_specs(0), near, near_turn, result,

time: 96.6 us -> 90.5 us (0.937); the launches traced: 94.8 us -> 90 us
  waiting for transfers between devices: 40.3 us -> 18.9 us
  starting transfers between devices: 15.4 us -> 30.2 us
  Pallas kernels: 34 us -> 35.5 us
    ppermute x6 -> x7, waiting for transfers between devices: 38.1 us -> 16.6 us  [swapped_with(): lax.ppermute(value, axis, [(source, partner(source, count)) for source in...]
    ppermute x3, starting transfers between devices: 4.48 us -> 19 us  [permuted(): return lax.ppermute(value, 'blk', pairs)]
    pallas_call x3, Pallas kernels: 10.2 us -> 13.6 us  [fill_rows(): pl.pallas_call(kernel, grid=(count // FILL_TILE,), in_specs=in_specs, out...]
    pallas_call x1, Pallas kernels: 17.5 us -> 16.5 us  [jacobi(): pl.pallas_call(jacobi_kernel, out_shape=(jax.ShapeDtypeStruct((PACK + SUM...]
    pallas_call x1, Pallas kernels: 6.33 us -> 5.35 us  [gram_blocks(): pl.pallas_call(gram_kernel, in_specs=[pl.BlockSpec(memory_space=pl.ANY)],...]
    ppermute x6 -> x7, starting transfers between devices: 10.9 us -> 11.2 us  [swapped_with(): lax.ppermute(value, axis, [(source, partner(source, count)) for source in...]
  transfers between devices with their start and end apart: 9 -> 10, of which waited for: 5 -> 6; matrix products, arithmetic and copies ran while one was open for 0% -> 1% of each run, Pallas kernels for 29% -> 33%
where the time goes in v9:
time: 90.5 us; the launch traced here: 90 us
  Pallas kernels  35.5 us (39%)
  starting transfers between devices  30.2 us (33%)
  waiting for transfers between devices  18.9 us (21%)
  between operations  3.24 us (4%)
  local copies, waits for them, and re-layouts  1.36 us (2%)
  other arithmetic  0.91 us (1%)
    ppermute x3, starting transfers between devices, permuted(): return lax.ppermute(value, 'blk', pairs)  19 us
    ppermute x7, waiting for transfers between devices, swapped_with(): lax.ppermute(value, axis, [(source, partner(source, count)) for source in...  16.6 us
    pallas_call x1, Pallas kernels, jacobi(): pl.pallas_call(jacobi_kernel, out_shape=(jax.ShapeDtypeStruct((PACK + SUM...  16.5 us
    pallas_call x3, Pallas kernels, fill_rows(): pl.pallas_call(kernel, grid=(count // FILL_TILE,), in_specs=in_specs, out...  13.6 us
    ppermute x7, starting transfers between devices, swapped_with(): lax.ppermute(value, axis, [(source, partner(source, count)) for source in...  11.2 us
    pallas_call x1, Pallas kernels, gram_blocks(): pl.pallas_call(gram_kernel, in_specs=[pl.BlockSpec(memory_space=pl.ANY)],...  5.35 us
    ppermute x3, waiting for transfers between devices, permuted(): return lax.ppermute(value, 'blk', pairs)  2.26 us
  transfers between devices with their start and end apart: 10, of which 6 were waited for; matrix products, arithmetic and copies ran while one was open for 1% of the time, Pallas kernels for 33%

profile of v9, /device:TPU:1, one launch (start us, length us, event | category | flops | bytes accessed | tf_op | source)
XLA Modules:
  0.0 90.0 jit_solution(3131872422945820007)
XLA Ops:
  0.6 0.0 copy-start
  0.6 5.4 %gram_blocks.1 = (f32[256,384]{1,0:T(8,128)}, bf16[1536,384]{1,0:T(8,128)(2,1)}) custom-call(bf16[6144,384]{1,0:T(8,128)(2,1)} %refs_2_.1), custom_call_target="tpu_custom_call" | custom-call | flops 1811939328 | bytes 4718592 | tf_op jit(solution)/shard_map/gram_blocks/pallas_call | solution.py:430
  6.0 0.1 collective-permute-start.4
  6.1 2.7 %collective-permute-start.3 = (bf16[1536,384]{1,0:T(8,128)(2,1)}, bf16[1536,384]{1,0:T(8,128)(2,1)S(1)}, u32[]{:S(2)}, u32[]{:S(2)}) collective-permute-start(bf16[1536,384]{1,0:T(8,128)(2,1)} %get-tuple-element.19), channel_id=1, source_target_pairs={{0,30},{2,4},{4,2},{6,8},{8,6},{10,12},{12,10},{14,16},{16,14},{18... | collective-permute-start | bytes 3538952 | tf_op jit(solution)/shard_map/ppermute | solution.py:536
  8.8 1.2 %collective-permute-start = (f32[256,384]{1,0:T(8,128)}, f32[256,384]{1,0:T(8,128)S(1)}, u32[]{:S(2)}, u32[]{:S(2)}) collective-permute-start(f32[256,384]{1,0:T(8,128)} %get-tuple-element.16.refs_0_), channel_id=1, source_target_pairs={{0,1},{1,0},{2,3},{3,2},{4,5},{5,4},{6,7},{7,6},{8,9},{9,8},{10,11... | collective-permute-start | bytes 1179656 | tf_op jit(solution)/shard_map/ppermute | solution.py:536
  10.0 6.1 %collective-permute-done.refs_1_ = f32[256,384]{1,0:T(8,128)S(1)} collective-permute-done((f32[256,384]{1,0:T(8,128)}, f32[256,384]{1,0:T(8,128)S(1)}, u32[]{:S(2)}, u32[]{:S(2)}) %collective-permute-start) | collective-permute-done | bytes 393248 | tf_op jit(solution)/shard_map/ppermute | solution.py:536
  16.1 0.0 copy-start.1
  16.1 0.8 copy-done.1
  16.9 16.5 %jacobi_turns.1 = (bf16[784,128]{1,0:T(8,128)(2,1)}, bf16[4608,128]{1,0:T(8,128)(2,1)}, bf16[2304,128]{1,0:T(8,128)(2,1)}, bf16[384,256]{1,0:T(8,128)(2,1)}, bf16[16,128]{1,0:T(8,128)(2,1)}) custom-call(s32[32]{0:T(128)} %plan_ref.7, f32[256,384]{1,0:T(8,128)} %get-tuple-element.16.refs_0_, f32[256,384]{1,0:T(8,128)} %copy-done.1, bf16[6144,384]{1,0:T(8,128)(2,1)} %refs_2_.1), custom_call_target="tpu_custom_call" | custom-call | flops 384 | bytes 384 | tf_op jit(solution)/shard_map/jacobi_turns/pallas_call | solution.py:350
  33.4 4.5 %collective-permute-start.1 = (bf16[784,128]{1,0:T(8,128)(2,1)}, bf16[784,128]{1,0:T(8,128)(2,1)S(1)}, u32[]{:S(2)}, u32[]{:S(2)}) collective-permute-start(bf16[784,128]{1,0:T(8,128)(2,1)} %get-tuple-element.17), channel_id=1, source_target_pairs={{0,30},{2,4},{4,2},{6,8},{8,6},{10,12},{12,10},{14,16},{16,14},{18... | collective-permute-start | bytes 602120 | tf_op jit(solution)/shard_map/ppermute | solution.py:536
  37.8 2.0 %collective-permute-start.2 = (bf16[384,256]{1,0:T(8,128)(2,1)}, bf16[384,256]{1,0:T(8,128)(2,1)S(1)}, u32[]{:S(2)}, u32[]{:S(2)}) collective-permute-start(bf16[384,256]{1,0:T(8,128)(2,1)} %get-tuple-element.18), channel_id=1, source_target_pairs={{0,2},{2,0},{4,6},{6,4},{8,10},{10,8},{12,14},{14,12},{16,18},{18,... | collective-permute-start | bytes 589832 | tf_op jit(solution)/shard_map/ppermute | solution.py:536
  39.8 0.7 convert_element_type.6
  40.5 0.8 collective-permute-start.6
  41.3 1.7 %collective-permute-done.1.slow_turn_ref = bf16[784,128]{1,0:T(8,128)(2,1)S(1)} collective-permute-done((bf16[784,128]{1,0:T(8,128)(2,1)}, bf16[784,128]{1,0:T(8,128)(2,1)S(1)}, u32[]{:S(2)}, u32[]{:S(2)}) %collective-permute-start.1) | collective-permute-done | bytes 200736 | tf_op jit(solution)/shard_map/ppermute | solution.py:536
  43.0 0.0 collective-permute-done.2.near_turn_ref
  43.0 0.0 collective-permute-done.3.slow_ref
  43.0 0.0 collective-permute-done.4.near_ref
  43.0 0.1 fusion.1
  43.1 3.0 %collective-permute-start.7 = (f32[16,128]{1,0:T(8,128)S(1)}, f32[16,128]{1,0:T(8,128)S(1)}, u32[]{:S(2)}, u32[]{:S(2)}) collective-permute-start(f32[16,128]{1,0:T(8,128)S(1)} %pad_maximum_fusion), channel_id=1, source_target_pairs={{0,2},{2,0},{4,6},{6,4},{8,10},{10,8},{12,14},{14,12},{16,18},{18,... | collective-permute-start | bytes 24584 | tf_op jit(solution)/shard_map/ppermute | solution.py:548
  46.2 0.0 collective-permute-start.5
  46.2 0.8 collective-permute-done.7
  47.0 0.1 subtract_subtract_fusion.1
  47.1 13.5 %collective-permute-start.8 = (f32[16,128]{1,0:T(8,128)S(1)}, f32[16,128]{1,0:T(8,128)S(1)}, u32[]{:S(2)}, u32[]{:S(2)}) collective-permute-start(f32[16,128]{1,0:T(8,128)S(1)} %pad_maximum_fusion.1), channel_id=1, source_target_pairs={{0,8},{2,10},{4,12},{6,14},{8,0},{10,2},{12,4},{14,6},{16,24},{18,... | collective-permute-start | bytes 24584 | tf_op jit(solution)/shard_map/ppermute | solution.py:548
  60.6 1.4 %collective-permute-done.8 = f32[16,128]{1,0:T(8,128)S(1)} collective-permute-done((f32[16,128]{1,0:T(8,128)S(1)}, f32[16,128]{1,0:T(8,128)S(1)}, u32[]{:S(2)}, u32[]{:S(2)}) %collective-permute-start.8) | collective-permute-done | bytes 8224 | tf_op jit(solution)/shard_map/ppermute | solution.py:548
  62.0 2.4 %collective-permute-start.9 = (f32[16,128]{1,0:T(8,128)S(1)}, f32[16,128]{1,0:T(8,128)S(1)}, u32[]{:S(2)}, u32[]{:S(2)}) collective-permute-start(f32[16,128]{1,0:T(8,128)S(1)} %pad_maximum_fusion.2), channel_id=1, source_target_pairs={{0,16},{2,18},{4,20},{6,22},{8,24},{10,26},{12,28},{14,30},{16,0},... | collective-permute-start | bytes 24584 | tf_op jit(solution)/shard_map/ppermute | solution.py:548
  64.5 0.0 copy-done
  64.5 3.9 %fill_rows.3.refs_1_ = bf16[6144,384]{1,0:T(8,128)(2,1)} custom-call(s32[32]{0:T(128)S(1)} %copy-done, bf16[6144,384]{1,0:T(8,128)(2,1)} %collective-permute-done.4.near_ref, bf16[384,256]{1,0:T(8,128)(2,1)S(1)} %collective-permute-done.2.near_turn_ref, bf16[1536,384]{1,0:T(8,128)(2,1)S(1)} %collective-permute-done.3.slow_ref, ...), custom_call_target="tpu_custom_call" | custom-call | flops 589824 | bytes 2359296 | tf_op jit(solution)/shard_map/fill_rows/pallas_call | solution.py:519
  68.4 8.4 %collective-permute-done.6.refs_0_ = bf16[4608,128]{1,0:T(8,128)(2,1)S(1)} collective-permute-done((bf16[4608,128]{1,0:T(8,128)(2,1)}, bf16[4608,128]{1,0:T(8,128)(2,1)S(1)}, u32[]{:S(2)}, u32[]{:S(2)}) %collective-permute-start.6) | collective-permute-done | bytes 1179680 | tf_op jit(solution)/shard_map/ppermute | solution.py:536
  76.8 6.0 %fill_rows.4.refs_1_ = bf16[6144,384]{1,0:T(8,128)(2,1)} custom-call(s32[32]{0:T(128)S(1)} %copy-done, bf16[6144,384]{1,0:T(8,128)(2,1)} %collective-permute-done.4.near_ref, bf16[384,256]{1,0:T(8,128)(2,1)S(1)} %collective-permute-done.2.near_turn_ref, bf16[4608,128]{1,0:T(8,128)(2,1)S(1)} %collective-permute-done.6.refs_0_, ...), custom_call_target="tpu_custom_call", output_to_operand_aliasing={{}: (4, {})} | custom-call | flops 1179648 | bytes 4718592 | tf_op jit(solution)/shard_map/fill_rows/pallas_call | solution.py:519
  82.8 0.4 collective-permute-done.5.refs_0_
  83.1 3.7 %fill_rows.5 = bf16[6144,384]{1,0:T(8,128)(2,1)} custom-call(s32[32]{0:T(128)S(1)} %copy-done, bf16[6144,384]{1,0:T(8,128)(2,1)} %collective-permute-done.4.near_ref, bf16[384,256]{1,0:T(8,128)(2,1)S(1)} %collective-permute-done.2.near_turn_ref, bf16[2304,128]{1,0:T(8,128)(2,1)S(1)} %collective-permute-done.5.refs_0_, ...), custom_call_target="tpu_custom_call", output_to_operand_aliasing={{}: (4, {})} | custom-call | flops 589824 | bytes 2359296 | tf_op jit(solution)/shard_map/fill_rows/pallas_call | solution.py:519
  86.9 0.0 collective-permute-done.9
  86.9 0.6 fusion.17
  (9 shorter events, 0.1 us)
Async XLA Ops:
  0.6 63.9 %copy-start = (s32[32]{0:T(128)S(1)}, s32[32]{0:T(128)}, u32[]{:S(2)}) copy-start(s32[32]{0:T(128)} %plan_ref.7) | copy-start | bytes 388
  6.0 37.0 %collective-permute-start.4 = (bf16[6144,384]{1,0:T(8,128)(2,1)}, bf16[6144,384]{1,0:T(8,128)(2,1)}, u32[]{:S(2)}, u32[]{:S(2)}) collective-permute-start(bf16[6144,384]{1,0:T(8,128)(2,1)} %refs_2_.1), channel_id=1, source_target_pairs={{0,2},{2,0},{4,6},{6,4},{8,10},{10,8},{12,14},{14,12},{16,18},{18,... | collective-permute-start | bytes 14155784 | tf_op jit(solution)/shard_map/ppermute | solution.py:536
  6.1 36.9 %collective-permute-start.3 = (bf16[1536,384]{1,0:T(8,128)(2,1)}, bf16[1536,384]{1,0:T(8,128)(2,1)S(1)}, u32[]{:S(2)}, u32[]{:S(2)}) collective-permute-start(bf16[1536,384]{1,0:T(8,128)(2,1)} %get-tuple-element.19), channel_id=1, source_target_pairs={{0,30},{2,4},{4,2},{6,8},{8,6},{10,12},{12,10},{14,16},{16,14},{18... | collective-permute-start | bytes 3538952 | tf_op jit(solution)/shard_map/ppermute | solution.py:536
  8.8 7.3 %collective-permute-start = (f32[256,384]{1,0:T(8,128)}, f32[256,384]{1,0:T(8,128)S(1)}, u32[]{:S(2)}, u32[]{:S(2)}) collective-permute-start(f32[256,384]{1,0:T(8,128)} %get-tuple-element.16.refs_0_), channel_id=1, source_target_pairs={{0,1},{1,0},{2,3},{3,2},{4,5},{5,4},{6,7},{7,6},{8,9},{9,8},{10,11... | collective-permute-start | bytes 1179656 | tf_op jit(solution)/shard_map/ppermute | solution.py:536
  16.1 0.8 copy-start.1
  33.4 9.6 %collective-permute-start.1 = (bf16[784,128]{1,0:T(8,128)(2,1)}, bf16[784,128]{1,0:T(8,128)(2,1)S(1)}, u32[]{:S(2)}, u32[]{:S(2)}) collective-permute-start(bf16[784,128]{1,0:T(8,128)(2,1)} %get-tuple-element.17), channel_id=1, source_target_pairs={{0,30},{2,4},{4,2},{6,8},{8,6},{10,12},{12,10},{14,16},{16,14},{18... | collective-permute-start | bytes 602120 | tf_op jit(solution)/shard_map/ppermute | solution.py:536
  37.8 5.2 %collective-permute-start.2 = (bf16[384,256]{1,0:T(8,128)(2,1)}, bf16[384,256]{1,0:T(8,128)(2,1)S(1)}, u32[]{:S(2)}, u32[]{:S(2)}) collective-permute-start(bf16[384,256]{1,0:T(8,128)(2,1)} %get-tuple-element.18), channel_id=1, source_target_pairs={{0,2},{2,0},{4,6},{6,4},{8,10},{10,8},{12,14},{14,12},{16,18},{18,... | collective-permute-start | bytes 589832 | tf_op jit(solution)/shard_map/ppermute | solution.py:536
  40.5 36.3 %collective-permute-start.6 = (bf16[4608,128]{1,0:T(8,128)(2,1)}, bf16[4608,128]{1,0:T(8,128)(2,1)S(1)}, u32[]{:S(2)}, u32[]{:S(2)}) collective-permute-start(bf16[4608,128]{1,0:T(8,128)(2,1)} %get-tuple-element.24), channel_id=1, source_target_pairs={{0,30},{2,4},{4,2},{6,8},{8,6},{10,12},{12,10},{14,16},{16,14},{18... | collective-permute-start | bytes 3538952 | tf_op jit(solution)/shard_map/ppermute | solution.py:536
  43.1 3.9 %collective-permute-start.7 = (f32[16,128]{1,0:T(8,128)S(1)}, f32[16,128]{1,0:T(8,128)S(1)}, u32[]{:S(2)}, u32[]{:S(2)}) collective-permute-start(f32[16,128]{1,0:T(8,128)S(1)} %pad_maximum_fusion), channel_id=1, source_target_pairs={{0,2},{2,0},{4,6},{6,4},{8,10},{10,8},{12,14},{14,12},{16,18},{18,... | collective-permute-start | bytes 24584 | tf_op jit(solution)/shard_map/ppermute | solution.py:548
  46.2 36.9 %collective-permute-start.5 = (bf16[2304,128]{1,0:T(8,128)(2,1)}, bf16[2304,128]{1,0:T(8,128)(2,1)S(1)}, u32[]{:S(2)}, u32[]{:S(2)}) collective-permute-start(bf16[2304,128]{1,0:T(8,128)(2,1)} %get-tuple-element.23), channel_id=1, source_target_pairs={{0,30},{2,4},{4,2},{6,8},{8,6},{10,12},{12,10},{14,16},{16,14},{18... | collective-permute-start | bytes 1769480 | tf_op jit(solution)/shard_map/ppermute | solution.py:536
  47.1 14.9 %collective-permute-start.8 = (f32[16,128]{1,0:T(8,128)S(1)}, f32[16,128]{1,0:T(8,128)S(1)}, u32[]{:S(2)}, u32[]{:S(2)}) collective-permute-start(f32[16,128]{1,0:T(8,128)S(1)} %pad_maximum_fusion.1), channel_id=1, source_target_pairs={{0,8},{2,10},{4,12},{6,14},{8,0},{10,2},{12,4},{14,6},{16,24},{18,... | collective-permute-start | bytes 24584 | tf_op jit(solution)/shard_map/ppermute | solution.py:548
  62.0 24.8 %collective-permute-start.9 = (f32[16,128]{1,0:T(8,128)S(1)}, f32[16,128]{1,0:T(8,128)S(1)}, u32[]{:S(2)}, u32[]{:S(2)}) collective-permute-start(f32[16,128]{1,0:T(8,128)S(1)} %pad_maximum_fusion.2), channel_id=1, source_target_pairs={{0,16},{2,18},{4,20},{6,22},{8,24},{10,26},{12,28},{14,30},{16,0},... | collective-permute-start | bytes 24584 | tf_op jit(solution)/shard_map/ppermute | solution.py:548

commit v10 on v9

--- a/solution.py
+++ b/solution.py
@@ -14,7 +14,7 @@
 GRAM_TILE = 1536
 RAW_ROWS = 1536
 LAST_ROWS = 1536
-FILL_TILE = 512
+WIDE_TILE = 1536
 SUM_ROWS = 16
 IN_FLIGHT = 2
 VMEM_LIMIT = 60 * 1024 * 1024
@@ -150,7 +150,6 @@
     for copy in gram_copies:
         copy.start()
     matrix_copy = pltpu.make_async_copy(matrix_ref.at[pl.ds(RAW_ROWS, held.shape[0])], held, sems.at[0])
-    matrix_copy.start()
     size = gram_refs[0].shape[1]
     half = size // 2
     groups = half // SUBS
@@ -171,6 +170,7 @@
     arranged = jnp.zeros((size, 4 * LANES), jnp.float32)
     for copy in gram_copies:
         copy.wait()
+    matrix_copy.start()
     packed = gram_held[0]
     for index in range(1, len(gram_refs)):
         packed = packed + gram_held[index]
@@ -312,7 +312,7 @@
         place = onehot(held_slot, send_columns(lanes, base, slot, half))
         return dot32(basis, place, ((0,), (0,))).astype(jnp.bfloat16)
 
-    fast_ref[...] = turned(half - slow_base, fast_slot)[:, : 2 * LANES]
+    fast_ref[...] = turned(half - slow_base, fast_slot)
     slow = turned(slow_base, slow_slot)
     packs[:size] = slow[:, :LANES]
     packs[size : 2 * size] = slow[:, LANES : 2 * LANES]
@@ -353,7 +353,7 @@
             jax.ShapeDtypeStruct((PACK + SUM_ROWS, LANES), jnp.bfloat16),
             jax.ShapeDtypeStruct(((blocks - 1) * PACK - last, LANES), jnp.bfloat16),
             jax.ShapeDtypeStruct((last, LANES), jnp.bfloat16),
-            jax.ShapeDtypeStruct((size, 2 * LANES), jnp.bfloat16),
+            jax.ShapeDtypeStruct((size, size), jnp.bfloat16),
             jax.ShapeDtypeStruct((SUM_ROWS, LANES), jnp.bfloat16),
         ),
         in_specs=[pl.BlockSpec(memory_space=pltpu.SMEM)]
@@ -467,48 +467,74 @@
     return (lane // (LANES // 2)) == slot
 
 
-def fill_kernel(plan_ref, near_ref, near_turn_ref, *refs):
-    slow_refs, out_ref = refs[:-2], refs[-1]
+def near_kernel(near_ref, turn_ref, packed_ref):
+    for unit in range(near_ref.shape[0] // UNIT):
+        values = near_ref[unit * UNIT : (unit + 1) * UNIT]
+        pack_unit(values, turn_ref[...], packed_ref, unit * PACK)
+
+
+def rotate_near(near, turn):
+    rows, size = near.shape
+    pack = WIDE_TILE // UNIT * PACK
+    return pl.pallas_call(
+        near_kernel,
+        grid=(rows // WIDE_TILE,),
+        in_specs=[
+            pl.BlockSpec((WIDE_TILE, size), lambda i: (i, 0)),
+            pl.BlockSpec((size, size), lambda i: (0, 0)),
+        ],
+        out_specs=pl.BlockSpec((pack, LANES), lambda i: (i, 0)),
+        out_shape=jax.ShapeDtypeStruct((rows // UNIT * PACK, LANES), jnp.bfloat16),
+        compiler_params=pltpu.CompilerParams(vmem_limit_bytes=FILL_VMEM_LIMIT),
+        cost_estimate=pl.CostEstimate(flops=size, bytes_accessed=size, transcendentals=0),
+        name="rotate_near",
+    )(near, turn)
+
+
+def fill_kernel(plan_ref, near_ref, slow_ref, *refs):
+    out_ref = refs[-1]
     half = UNIT // 2
     slot = moves(plan_ref)[3]
     mask = slot_lanes(slot, half)
     middle = slice(LANES, 2 * LANES)
-    for unit, slow_ref in enumerate(slow_refs):
-        start = unit * UNIT
+    for unit in range(out_ref.shape[0] // UNIT):
+        start, at = unit * UNIT, unit * PACK
         rows = slice(start, start + UNIT)
-        near = dot32(near_ref[rows], near_turn_ref[...])
-        place_main(slot, out_ref, rows, slow_ref[:UNIT], near[:, LANES:].astype(jnp.bfloat16))
-        slow = slow_ref[UNIT:].astype(jnp.float32)
-        top = jnp.where(mask, slow, near[:half, :LANES])
-        low = jnp.where(mask, pltpu.roll(slow, LANES // 2, 1), near[half:, :LANES])
+        main, rest = slice(at, at + UNIT), slice(at + UNIT, at + PACK)
+        place_main(slot, out_ref, rows, slow_ref[main], near_ref[main])
+        slow = slow_ref[rest].astype(jnp.float32)
+        near = near_ref[rest].astype(jnp.float32)
+        out_ref[start : start + half, middle] = jnp.where(mask, slow, near).astype(jnp.bfloat16)
+        low = pltpu.roll(jnp.where(mask, near, slow), LANES // 2, 1)
+        out_ref[start + half : start + UNIT, middle] = low.astype(jnp.bfloat16)
+
+
+def raw_kernel(plan_ref, near_ref, slow_ref, slow_turn_ref, out_ref):
+    size = slow_ref.shape[1]
+    half = UNIT // 2
+    slot = moves(plan_ref)[3]
+    mask = slot_lanes(slot, half)
+    middle = slice(LANES, 2 * LANES)
+    slow_turn = jnp.concatenate([slow_turn_ref[:size], slow_turn_ref[size:]], axis=1)
+    for unit in range(out_ref.shape[0] // UNIT):
+        start, at = unit * UNIT, unit * PACK
+        rows = slice(start, start + UNIT)
+        slow = dot32(slow_ref[rows], slow_turn)
+        slow_main = slow[:, LANES:].astype(jnp.bfloat16)
+        place_main(slot, out_ref, rows, slow_main, near_ref[at : at + UNIT])
+        near = near_ref[at + UNIT : at + PACK].astype(jnp.float32)
+        top = jnp.where(mask, slow[:half, :LANES], near)
+        low = jnp.where(mask, slow[half:, :LANES], pltpu.roll(near, LANES // 2, 1))
         out_ref[start : start + half, middle] = top.astype(jnp.bfloat16)
         out_ref[start + half : start + UNIT, middle] = low.astype(jnp.bfloat16)
 
 
-def raw_kernel(plan_ref, near_ref, near_turn_ref, slow_ref, slow_turn_ref, out_ref):
-    size = slow_ref.shape[1]
-    slot = moves(plan_ref)[3]
-    mask = slot_lanes(slot, UNIT)
-    slow_turn = jnp.concatenate([slow_turn_ref[:size], slow_turn_ref[size:]], axis=1)
-    for unit in range(out_ref.shape[0] // UNIT):
-        rows = slice(unit * UNIT, (unit + 1) * UNIT)
-        near = dot32(near_ref[rows], near_turn_ref[...])
-        slow = dot32(slow_ref[rows], slow_turn)
-        near_main = near[:, LANES:].astype(jnp.bfloat16)
-        place_main(slot, out_ref, rows, slow[:, LANES:].astype(jnp.bfloat16), near_main)
-        middle = jnp.where(mask, slow[:, :LANES], near[:, :LANES])
-        out_ref[rows, LANES : 2 * LANES] = middle.astype(jnp.bfloat16)
-
-
-def fill_rows(kernel, plan, sources, specs, near, near_turn, result, start, count):
-    shape = near.shape
-    first = start // FILL_TILE
-    operands = [plan, near, near_turn, *sources]
-    row_spec = pl.BlockSpec((FILL_TILE, shape[1]), lambda i: (first + i, 0))
+def fill_rows(kernel, plan, sources, specs, near_pack, result, shape, start, count, tile):
+    first = start // tile
+    operands = [plan, near_pack, *sources]
     in_specs = [
         pl.BlockSpec(memory_space=pltpu.SMEM),
-        row_spec,
-        pl.BlockSpec(near_turn.shape, lambda i: (0, 0)),
+        pl.BlockSpec((tile // UNIT * PACK, LANES), lambda i: (first + i, 0)),
         *specs,
     ]
     aliases = {}
@@ -518,9 +544,9 @@
         in_specs.append(pl.BlockSpec(memory_space=pl.ANY))
     return pl.pallas_call(
         kernel,
-        grid=(count // FILL_TILE,),
+        grid=(count // tile,),
         in_specs=in_specs,
-        out_specs=row_spec,
+        out_specs=pl.BlockSpec((tile, shape[1]), lambda i: (first + i, 0)),
         out_shape=jax.ShapeDtypeStruct(shape, jnp.bfloat16),
         input_output_aliases=aliases,
         compiler_params=pltpu.CompilerParams(vmem_limit_bytes=FILL_VMEM_LIMIT),
@@ -596,31 +622,30 @@
     first = swapped_with(first, "blk", slow_partner)
     last = swapped_with(last, "blk", slow_partner)
     near_turn = swapped_with(near_turn, "blk", fast_partner)
+    near_pack = rotate_near(near, near_turn)
     theirs = head[PACK:]
-    theirs, near_turn, raw, near = lax.optimization_barrier((theirs, near_turn, raw, near))
+    theirs, near_pack, raw = lax.optimization_barrier((theirs, near_pack, raw))
     totals = cycle_sums(sums, theirs)
     off_ratio = jnp.sqrt(totals[0, 0] / totals[1, 0])
 
-    def pack_specs(skip):
-        units = FILL_TILE // UNIT
-        return [
-            pl.BlockSpec((PACK, LANES), lambda i, unit=unit: (skip + units * i + unit, 0))
-            for unit in range(units)
-        ]
-
-    units = FILL_TILE // UNIT
+    shape = (rows, size)
     turn_spec = pl.BlockSpec((PACK, LANES), lambda i: (0, 0))
-    raw_spec = pl.BlockSpec((FILL_TILE, size), lambda i: (i, 0))
+    raw_spec = pl.BlockSpec((UNIT, size), lambda i: (i, 0))
+    wide_spec = pl.BlockSpec((WIDE_TILE // UNIT * PACK, LANES), lambda i: (i, 0))
+    last_spec = pl.BlockSpec((PACK, LANES), lambda i: (i, 0))
     middle = rows - RAW_ROWS - LAST_ROWS
     result = fill_rows(
-        raw_kernel, plan, [raw, head], [raw_spec, turn_spec], near, near_turn, None, 0, RAW_ROWS
+        raw_kernel, plan, [raw, head], [raw_spec, turn_spec], near_pack, None, shape,
+        0, RAW_ROWS, UNIT,
     )
     result = fill_rows(
-        fill_kernel, plan, [first] * units, pack_specs(0), near, near_turn, result, RAW_ROWS, middle
+        fill_kernel, plan, [first], [wide_spec], near_pack, result, shape,
+        RAW_ROWS, middle, WIDE_TILE,
     )
+    result, off_ratio = lax.optimization_barrier((result, off_ratio))
     result = fill_rows(
-        fill_kernel, plan, [last] * units, pack_specs(0), near, near_turn, result,
-        rows - LAST_ROWS, LAST_ROWS,
+        fill_kernel, plan, [last], [last_spec], near_pack, result, shape,
+        rows - LAST_ROWS, LAST_ROWS, UNIT,
     )
     return result, off_ratio
 

time: 90.5 us -> 87.3 us (0.965)
  starting transfers between devices: 30.2 us -> 16.8 us
  waiting for transfers between devices: 18.9 us -> 30.5 us
  Pallas kernels: 35.5 us -> 34.1 us
    ppermute x3, starting transfers between devices: 19 us -> 5.27 us  [permuted(): return lax.ppermute(value, 'blk', pairs)]
    ppermute x7, waiting for transfers between devices: 16.6 us -> 29.4 us  [swapped_with(): lax.ppermute(value, axis, [(source, partner(source, count)) for source in...]
    pallas_call x3 -> x4, Pallas kernels: 13.6 us -> 12 us  [the longest x3 7.62 us: fill_rows(): pl.pallas_call(kernel, grid=(count // tile,), in_specs=in_specs, out_spec...]
    ppermute x3, waiting for transfers between devices: 2.26 us -> 1.16 us  [permuted(): return lax.ppermute(value, 'blk', pairs)]
  transfers between devices with their start and end apart: 10 -> 10, of which waited for: 6 -> 5; matrix products, arithmetic and copies ran while one was open for 1% -> 2% of each run, Pallas kernels for 33% -> 30%
where the time goes in v10:
time: 87.3 us; the launch traced here: 87 us
  Pallas kernels  34.1 us (39%)
  waiting for transfers between devices  30.5 us (35%)
  starting transfers between devices  16.8 us (19%)
  between operations  3.28 us (4%)
  local copies, waits for them, and re-layouts  1.36 us (2%)
  other arithmetic  0.9 us (1%)
    ppermute x7, waiting for transfers between devices, swapped_with(): lax.ppermute(value, axis, [(source, partner(source, count)) for source in...  29.4 us
    pallas_call x1, Pallas kernels, jacobi(): pl.pallas_call(jacobi_kernel, out_shape=(jax.ShapeDtypeStruct((PACK + SUM...  16.7 us
    ppermute x7, starting transfers between devices, swapped_with(): lax.ppermute(value, axis, [(source, partner(source, count)) for source in...  11.6 us
    pallas_call x3, Pallas kernels, fill_rows(): pl.pallas_call(kernel, grid=(count // tile,), in_specs=in_specs, out_spec...  7.62 us
    pallas_call x1, Pallas kernels, gram_blocks(): pl.pallas_call(gram_kernel, in_specs=[pl.BlockSpec(memory_space=pl.ANY)],...  5.36 us
    ppermute x3, starting transfers between devices, permuted(): return lax.ppermute(value, 'blk', pairs)  5.27 us
    pallas_call x1, Pallas kernels, rotate_near(): pl.pallas_call(near_kernel, grid=(rows // WIDE_TILE,), in_specs=[pl.Block...  4.41 us
  transfers between devices with their start and end apart: 10, of which 5 were waited for; matrix products, arithmetic and copies ran while one was open for 2% of the time, Pallas kernels for 30%

profile of v10, /device:TPU:1, one launch (start us, length us, event | category | flops | bytes accessed | tf_op | source)
XLA Modules:
  0.0 87.0 jit_solution(14220455233048223274)
XLA Ops:
  0.6 5.4 %gram_blocks.1 = (f32[256,384]{1,0:T(8,128)}, bf16[1536,384]{1,0:T(8,128)(2,1)}) custom-call(bf16[6144,384]{1,0:T(8,128)(2,1)} %refs_2_.1), custom_call_target="tpu_custom_call" | custom-call | flops 1811939328 | bytes 4718592 | tf_op jit(solution)/shard_map/gram_blocks/pallas_call | solution.py:430
  6.0 0.1 collective-permute-start.2
  6.1 2.7 %collective-permute-start.4 = (bf16[1536,384]{1,0:T(8,128)(2,1)}, bf16[1536,384]{1,0:T(8,128)(2,1)S(1)}, u32[]{:S(2)}, u32[]{:S(2)}) collective-permute-start(bf16[1536,384]{1,0:T(8,128)(2,1)} %get-tuple-element.21), channel_id=1, source_target_pairs={{0,30},{2,4},{4,2},{6,8},{8,6},{10,12},{12,10},{14,16},{16,14},{18... | collective-permute-start | bytes 3538952 | tf_op jit(solution)/shard_map/ppermute | solution.py:562
  8.8 1.2 %collective-permute-start = (f32[256,384]{1,0:T(8,128)}, f32[256,384]{1,0:T(8,128)S(1)}, u32[]{:S(2)}, u32[]{:S(2)}) collective-permute-start(f32[256,384]{1,0:T(8,128)} %get-tuple-element.17.refs_0_), channel_id=1, source_target_pairs={{0,1},{1,0},{2,3},{3,2},{4,5},{5,4},{6,7},{7,6},{8,9},{9,8},{10,11... | collective-permute-start | bytes 1179656 | tf_op jit(solution)/shard_map/ppermute | solution.py:562
  10.0 6.2 %collective-permute-done.refs_1_ = f32[256,384]{1,0:T(8,128)S(1)} collective-permute-done((f32[256,384]{1,0:T(8,128)}, f32[256,384]{1,0:T(8,128)S(1)}, u32[]{:S(2)}, u32[]{:S(2)}) %collective-permute-start) | collective-permute-done | bytes 393248 | tf_op jit(solution)/shard_map/ppermute | solution.py:562
  16.1 0.0 copy-start.1
  16.1 0.7 copy-done.1
  16.9 16.7 %jacobi_turns.1 = (bf16[784,128]{1,0:T(8,128)(2,1)}, bf16[4608,128]{1,0:T(8,128)(2,1)}, bf16[2304,128]{1,0:T(8,128)(2,1)}, bf16[384,384]{1,0:T(8,128)(2,1)}, bf16[16,128]{1,0:T(8,128)(2,1)}) custom-call(s32[32]{0:T(128)} %plan_ref.7, f32[256,384]{1,0:T(8,128)} %get-tuple-element.17.refs_0_, f32[256,384]{1,0:T(8,128)} %copy-done.1, bf16[6144,384]{1,0:T(8,128)(2,1)} %refs_2_.1), custom_call_target="tpu_custom_call" | custom-call | flops 384 | bytes 384 | tf_op jit(solution)/shard_map/jacobi_turns/pallas_call | solution.py:350
  33.6 0.0 copy-start.2
  33.6 0.0 copy-start
  33.6 4.4 %collective-permute-start.3 = (bf16[384,384]{1,0:T(8,128)(2,1)}, bf16[384,384]{1,0:T(8,128)(2,1)S(1)}, u32[]{:S(2)}, u32[]{:S(2)}) collective-permute-start(bf16[384,384]{1,0:T(8,128)(2,1)} %get-tuple-element.20), channel_id=1, source_target_pairs={{0,2},{2,0},{4,6},{6,4},{8,10},{10,8},{12,14},{14,12},{16,18},{18,... | collective-permute-start | bytes 884744 | tf_op jit(solution)/shard_map/ppermute | solution.py:562
  38.1 0.6 collective-permute-start.1
  38.7 0.7 convert_element_type.6
  39.4 1.1 %collective-permute-start.6 = (bf16[4608,128]{1,0:T(8,128)(2,1)}, bf16[4608,128]{1,0:T(8,128)(2,1)S(1)}, u32[]{:S(2)}, u32[]{:S(2)}) collective-permute-start(bf16[4608,128]{1,0:T(8,128)(2,1)} %get-tuple-element.24), channel_id=1, source_target_pairs={{0,30},{2,4},{4,2},{6,8},{8,6},{10,12},{12,10},{14,16},{16,14},{18... | collective-permute-start | bytes 3538952 | tf_op jit(solution)/shard_map/ppermute | solution.py:562
  40.5 16.0 %collective-permute-done.1.slow_turn_ref = bf16[784,128]{1,0:T(8,128)(2,1)S(1)} collective-permute-done((bf16[784,128]{1,0:T(8,128)(2,1)}, bf16[784,128]{1,0:T(8,128)(2,1)S(1)}, u32[]{:S(2)}, u32[]{:S(2)}) %collective-permute-start.1) | collective-permute-done | bytes 200736 | tf_op jit(solution)/shard_map/ppermute | solution.py:562
  56.5 0.0 collective-permute-done.3.turn_ref
  56.5 0.0 collective-permute-done.2.near_ref
  56.5 4.4 %rotate_near.1.near_ref = bf16[9216,128]{1,0:T(8,128)(2,1)S(1)} custom-call(bf16[6144,384]{1,0:T(8,128)(2,1)} %collective-permute-done.2.near_ref, bf16[384,384]{1,0:T(8,128)(2,1)S(1)} %collective-permute-done.3.turn_ref), custom_call_target="tpu_custom_call" | custom-call | flops 384 | bytes 384 | tf_op jit(solution)/shard_map/rotate_near/pallas_call | solution.py:479
  60.9 0.0 collective-permute-done.4.slow_ref
  61.0 0.1 fusion.1
  61.1 0.0 collective-permute-start.7
  61.1 1.2 %collective-permute-done.7 = f32[16,128]{1,0:T(8,128)S(1)} collective-permute-done((f32[16,128]{1,0:T(8,128)S(1)}, f32[16,128]{1,0:T(8,128)S(1)}, u32[]{:S(2)}, u32[]{:S(2)}) %collective-permute-start.7) | collective-permute-done | bytes 8224 | tf_op jit(solution)/shard_map/ppermute | solution.py:574
  62.3 0.1 subtract_subtract_fusion.1
  62.4 3.0 %collective-permute-start.8 = (f32[16,128]{1,0:T(8,128)S(1)}, f32[16,128]{1,0:T(8,128)S(1)}, u32[]{:S(2)}, u32[]{:S(2)}) collective-permute-start(f32[16,128]{1,0:T(8,128)S(1)} %pad_maximum_fusion.1), channel_id=1, source_target_pairs={{0,8},{2,10},{4,12},{6,14},{8,0},{10,2},{12,4},{14,6},{16,24},{18,... | collective-permute-start | bytes 24584 | tf_op jit(solution)/shard_map/ppermute | solution.py:574
  65.4 0.0 copy-done.2
  65.4 1.4 %collective-permute-start.5 = (bf16[2304,128]{1,0:T(8,128)(2,1)S(1)}, bf16[2304,128]{1,0:T(8,128)(2,1)S(1)}, u32[]{:S(2)}, u32[]{:S(2)}) collective-permute-start(bf16[2304,128]{1,0:T(8,128)(2,1)S(1)} %copy-done.2), channel_id=1, source_target_pairs={{0,30},{2,4},{4,2},{6,8},{8,6},{10,12},{12,10},{14,16},{16,14},{18... | collective-permute-start | bytes 1769480 | tf_op jit(solution)/shard_map/ppermute | solution.py:562
  66.8 0.0 collective-permute-done.8
  66.8 2.2 %collective-permute-start.9 = (f32[16,128]{1,0:T(8,128)S(1)}, f32[16,128]{1,0:T(8,128)S(1)}, u32[]{:S(2)}, u32[]{:S(2)}) collective-permute-start(f32[16,128]{1,0:T(8,128)S(1)} %pad_maximum_fusion.2), channel_id=1, source_target_pairs={{0,16},{2,18},{4,20},{6,22},{8,24},{10,26},{12,28},{14,30},{16,0},... | collective-permute-start | bytes 24584 | tf_op jit(solution)/shard_map/ppermute | solution.py:574
  69.0 0.0 copy-done
  69.0 2.8 %fill_rows.3.refs_0_ = bf16[6144,384]{1,0:T(8,128)(2,1)} custom-call(s32[32]{0:T(128)S(1)} %copy-done, bf16[9216,128]{1,0:T(8,128)(2,1)S(1)} %rotate_near.1.near_ref, bf16[1536,384]{1,0:T(8,128)(2,1)S(1)} %collective-permute-done.4.slow_ref, bf16[784,128]{1,0:T(8,128)(2,1)S(1)} %collective-permute-done.1.slow_turn_ref), custom_call_target="tpu_custom_call" | custom-call | flops 589824 | bytes 2359296 | tf_op jit(solution)/shard_map/fill_rows/pallas_call | solution.py:545
  71.9 3.6 %collective-permute-done.6.slow_ref = bf16[4608,128]{1,0:T(8,128)(2,1)S(1)} collective-permute-done((bf16[4608,128]{1,0:T(8,128)(2,1)}, bf16[4608,128]{1,0:T(8,128)(2,1)S(1)}, u32[]{:S(2)}, u32[]{:S(2)}) %collective-permute-start.6) | collective-permute-done | bytes 1179680 | tf_op jit(solution)/shard_map/ppermute | solution.py:562
  75.5 2.4 %fill_rows.4.refs_0_ = bf16[6144,384]{1,0:T(8,128)(2,1)} custom-call(s32[32]{0:T(128)S(1)} %copy-done, bf16[9216,128]{1,0:T(8,128)(2,1)S(1)} %rotate_near.1.near_ref, bf16[4608,128]{1,0:T(8,128)(2,1)S(1)} %collective-permute-done.6.slow_ref, bf16[6144,384]{1,0:T(8,128)(2,1)} %fill_rows.3.refs_0_), custom_call_target="tpu_custom_call", output_to_operand_aliasing={{}: (3, {})} | custom-call | flops 1179648 | bytes 4718592 | tf_op jit(solution)/shard_map/fill_rows/pallas_call | solution.py:545
  77.8 0.0 collective-permute-done.9
  77.9 0.6 fusion.17
  79.9 3.6 %collective-permute-done.5.slow_ref = bf16[2304,128]{1,0:T(8,128)(2,1)S(1)} collective-permute-done((bf16[2304,128]{1,0:T(8,128)(2,1)S(1)}, bf16[2304,128]{1,0:T(8,128)(2,1)S(1)}, u32[]{:S(2)}, u32[]{:S(2)}) %collective-permute-start.5) | collective-permute-done | bytes 589856 | tf_op jit(solution)/shard_map/ppermute | solution.py:562
  83.5 2.4 %fill_rows.5 = bf16[6144,384]{1,0:T(8,128)(2,1)} custom-call(s32[32]{0:T(128)S(1)} %copy-done, bf16[9216,128]{1,0:T(8,128)(2,1)S(1)} %rotate_near.1.near_ref, bf16[2304,128]{1,0:T(8,128)(2,1)S(1)} %collective-permute-done.5.slow_ref, bf16[6144,384]{1,0:T(8,128)(2,1)} %fill_rows.4.refs_0_), custom_call_target="tpu_custom_call", output_to_operand_aliasing={{}: (3, {})} | custom-call | flops 589824 | bytes 2359296 | tf_op jit(solution)/shard_map/fill_rows/pallas_call | solution.py:545
  (9 shorter events, 0.1 us)
Async XLA Ops:
  6.0 50.5 %collective-permute-start.2 = (bf16[6144,384]{1,0:T(8,128)(2,1)}, bf16[6144,384]{1,0:T(8,128)(2,1)}, u32[]{:S(2)}, u32[]{:S(2)}) collective-permute-start(bf16[6144,384]{1,0:T(8,128)(2,1)} %refs_2_.1), channel_id=1, source_target_pairs={{0,2},{2,0},{4,6},{6,4},{8,10},{10,8},{12,14},{14,12},{16,18},{18,... | collective-permute-start | bytes 14155784 | tf_op jit(solution)/shard_map/ppermute | solution.py:562
  6.1 54.8 %collective-permute-start.4 = (bf16[1536,384]{1,0:T(8,128)(2,1)}, bf16[1536,384]{1,0:T(8,128)(2,1)S(1)}, u32[]{:S(2)}, u32[]{:S(2)}) collective-permute-start(bf16[1536,384]{1,0:T(8,128)(2,1)} %get-tuple-element.21), channel_id=1, source_target_pairs={{0,30},{2,4},{4,2},{6,8},{8,6},{10,12},{12,10},{14,16},{16,14},{18... | collective-permute-start | bytes 3538952 | tf_op jit(solution)/shard_map/ppermute | solution.py:562
  8.8 7.4 %collective-permute-start = (f32[256,384]{1,0:T(8,128)}, f32[256,384]{1,0:T(8,128)S(1)}, u32[]{:S(2)}, u32[]{:S(2)}) collective-permute-start(f32[256,384]{1,0:T(8,128)} %get-tuple-element.17.refs_0_), channel_id=1, source_target_pairs={{0,1},{1,0},{2,3},{3,2},{4,5},{5,4},{6,7},{7,6},{8,9},{9,8},{10,11... | collective-permute-start | bytes 1179656 | tf_op jit(solution)/shard_map/ppermute | solution.py:562
  16.1 0.8 copy-start.1
  33.6 31.8 %copy-start.2 = (bf16[2304,128]{1,0:T(8,128)(2,1)S(1)}, bf16[2304,128]{1,0:T(8,128)(2,1)}, u32[]{:S(2)}) copy-start(bf16[2304,128]{1,0:T(8,128)(2,1)} %get-tuple-element.23) | copy-start | bytes 1769476
  33.6 35.4 %copy-start = (s32[32]{0:T(128)S(1)}, s32[32]{0:T(128)}, u32[]{:S(2)}) copy-start(s32[32]{0:T(128)} %plan_ref.7) | copy-start | bytes 388
  33.6 22.9 %collective-permute-start.3 = (bf16[384,384]{1,0:T(8,128)(2,1)}, bf16[384,384]{1,0:T(8,128)(2,1)S(1)}, u32[]{:S(2)}, u32[]{:S(2)}) collective-permute-start(bf16[384,384]{1,0:T(8,128)(2,1)} %get-tuple-element.20), channel_id=1, source_target_pairs={{0,2},{2,0},{4,6},{6,4},{8,10},{10,8},{12,14},{14,12},{16,18},{18,... | collective-permute-start | bytes 884744 | tf_op jit(solution)/shard_map/ppermute | solution.py:562
  38.1 18.4 %collective-permute-start.1 = (bf16[784,128]{1,0:T(8,128)(2,1)}, bf16[784,128]{1,0:T(8,128)(2,1)S(1)}, u32[]{:S(2)}, u32[]{:S(2)}) collective-permute-start(bf16[784,128]{1,0:T(8,128)(2,1)} %get-tuple-element.18), channel_id=1, source_target_pairs={{0,30},{2,4},{4,2},{6,8},{8,6},{10,12},{12,10},{14,16},{16,14},{18... | collective-permute-start | bytes 602120 | tf_op jit(solution)/shard_map/ppermute | solution.py:562
  39.4 36.1 %collective-permute-start.6 = (bf16[4608,128]{1,0:T(8,128)(2,1)}, bf16[4608,128]{1,0:T(8,128)(2,1)S(1)}, u32[]{:S(2)}, u32[]{:S(2)}) collective-permute-start(bf16[4608,128]{1,0:T(8,128)(2,1)} %get-tuple-element.24), channel_id=1, source_target_pairs={{0,30},{2,4},{4,2},{6,8},{8,6},{10,12},{12,10},{14,16},{16,14},{18... | collective-permute-start | bytes 3538952 | tf_op jit(solution)/shard_map/ppermute | solution.py:562
  61.1 1.2 %collective-permute-start.7 = (f32[16,128]{1,0:T(8,128)S(1)}, f32[16,128]{1,0:T(8,128)S(1)}, u32[]{:S(2)}, u32[]{:S(2)}) collective-permute-start(f32[16,128]{1,0:T(8,128)S(1)} %pad_maximum_fusion), channel_id=1, source_target_pairs={{0,2},{2,0},{4,6},{6,4},{8,10},{10,8},{12,14},{14,12},{16,18},{18,... | collective-permute-start | bytes 24584 | tf_op jit(solution)/shard_map/ppermute | solution.py:574
  62.4 4.4 %collective-permute-start.8 = (f32[16,128]{1,0:T(8,128)S(1)}, f32[16,128]{1,0:T(8,128)S(1)}, u32[]{:S(2)}, u32[]{:S(2)}) collective-permute-start(f32[16,128]{1,0:T(8,128)S(1)} %pad_maximum_fusion.1), channel_id=1, source_target_pairs={{0,8},{2,10},{4,12},{6,14},{8,0},{10,2},{12,4},{14,6},{16,24},{18,... | collective-permute-start | bytes 24584 | tf_op jit(solution)/shard_map/ppermute | solution.py:574
  65.4 18.1 %collective-permute-start.5 = (bf16[2304,128]{1,0:T(8,128)(2,1)S(1)}, bf16[2304,128]{1,0:T(8,128)(2,1)S(1)}, u32[]{:S(2)}, u32[]{:S(2)}) collective-permute-start(bf16[2304,128]{1,0:T(8,128)(2,1)S(1)} %copy-done.2), channel_id=1, source_target_pairs={{0,30},{2,4},{4,2},{6,8},{8,6},{10,12},{12,10},{14,16},{16,14},{18... | collective-permute-start | bytes 1769480 | tf_op jit(solution)/shard_map/ppermute | solution.py:562
  66.8 11.0 %collective-permute-start.9 = (f32[16,128]{1,0:T(8,128)S(1)}, f32[16,128]{1,0:T(8,128)S(1)}, u32[]{:S(2)}, u32[]{:S(2)}) collective-permute-start(f32[16,128]{1,0:T(8,128)S(1)} %pad_maximum_fusion.2), channel_id=1, source_target_pairs={{0,16},{2,18},{4,20},{6,22},{8,24},{10,26},{12,28},{14,30},{16,0},... | collective-permute-start | bytes 24584 | tf_op jit(solution)/shard_map/ppermute | solution.py:574

commit v11 on v10

--- a/solution.py
+++ b/solution.py
@@ -18,6 +18,7 @@
 SUM_ROWS = 16
 IN_FLIGHT = 2
 VMEM_LIMIT = 60 * 1024 * 1024
+JACOBI_VMEM_LIMIT = 58 * 1024 * 1024
 FILL_VMEM_LIMIT = 32 * 1024 * 1024
 
 
@@ -136,19 +137,13 @@
 
 
 def jacobi_kernel(plan_ref, *refs):
-    jacobi_body(plan_ref, refs[:-17], *refs[-17:])
+    jacobi_body(plan_ref, refs[:-15], *refs[-15:])
 
 
 def jacobi_body(
     plan_ref, gram_refs, matrix_ref, head_ref, first_ref, last_ref, fast_ref, sums_ref,
-    gram_a, gram_b, basis_a, basis_b, cos_buf, sin_buf, held, packs, gram_held, gram_sems, sems,
+    gram_a, gram_b, basis_a, basis_b, cos_buf, sin_buf, held, packs, sems,
 ):
-    gram_copies = [
-        pltpu.make_async_copy(ref, gram_held.at[index], gram_sems.at[index])
-        for index, ref in enumerate(gram_refs)
-    ]
-    for copy in gram_copies:
-        copy.start()
     matrix_copy = pltpu.make_async_copy(matrix_ref.at[pl.ds(RAW_ROWS, held.shape[0])], held, sems.at[0])
     size = gram_refs[0].shape[1]
     half = size // 2
@@ -168,12 +163,10 @@
     lane_slot = slot_of_lane(lax.broadcasted_iota(jnp.int32, (1, 4 * LANES), 1), half)
     take_cols = onehot(lax.broadcasted_iota(jnp.int32, (size, 4 * LANES), 0), lane_slot)
     arranged = jnp.zeros((size, 4 * LANES), jnp.float32)
-    for copy in gram_copies:
-        copy.wait()
     matrix_copy.start()
-    packed = gram_held[0]
-    for index in range(1, len(gram_refs)):
-        packed = packed + gram_held[index]
+    packed = gram_refs[0][...]
+    for other in gram_refs[1:]:
+        packed = packed + other[...]
     gram_sum = full_gram(packed)
     sums_ref[...] = block_sums(packed)
     for piece in split_three(gram_sum):
@@ -314,8 +307,9 @@
 
     fast_ref[...] = turned(half - slow_base, fast_slot)
     slow = turned(slow_base, slow_slot)
-    packs[:size] = slow[:, :LANES]
-    packs[size : 2 * size] = slow[:, LANES : 2 * LANES]
+    head_rows = size + half
+    packs[:size] = slow[:, LANES : 2 * LANES]
+    packs[size:head_rows] = slow[:half, :LANES] + slow[half:, 2 * LANES :]
     matrix_copy.wait()
     copies = []
 
@@ -325,8 +319,9 @@
         )
         copies[-1].start()
 
-    leave(0, PACK, head_ref.at[pl.ds(0, PACK)])
-    copies.append(pltpu.make_async_copy(sums_ref, head_ref.at[pl.ds(PACK, SUM_ROWS)], sems.at[2]))
+    leave(0, head_rows, head_ref.at[pl.ds(0, head_rows)])
+    tail = head_ref.at[pl.ds(head_rows, SUM_ROWS)]
+    copies.append(pltpu.make_async_copy(sums_ref, tail, sems.at[2]))
     copies[-1].start()
     first_count = first_ref.shape[0]
     for unit in range(held.shape[0] // UNIT):
@@ -350,14 +345,15 @@
     return pl.pallas_call(
         jacobi_kernel,
         out_shape=(
-            jax.ShapeDtypeStruct((PACK + SUM_ROWS, LANES), jnp.bfloat16),
+            jax.ShapeDtypeStruct((size + size // 2 + SUM_ROWS, LANES), jnp.bfloat16),
             jax.ShapeDtypeStruct(((blocks - 1) * PACK - last, LANES), jnp.bfloat16),
             jax.ShapeDtypeStruct((last, LANES), jnp.bfloat16),
             jax.ShapeDtypeStruct((size, size), jnp.bfloat16),
             jax.ShapeDtypeStruct((SUM_ROWS, LANES), jnp.bfloat16),
         ),
         in_specs=[pl.BlockSpec(memory_space=pltpu.SMEM)]
-        + [pl.BlockSpec(memory_space=pl.ANY)] * (len(grams) + 1),
+        + [pl.BlockSpec(memory_space=pltpu.VMEM)] * len(grams)
+        + [pl.BlockSpec(memory_space=pl.ANY)],
         out_specs=[pl.BlockSpec(memory_space=pl.ANY)] * 3
         + [pl.BlockSpec(memory_space=pltpu.VMEM)] * 2,
         scratch_shapes=[
@@ -369,11 +365,9 @@
             pltpu.VMEM((groups, SUBS, LANES), jnp.float32),
             pltpu.VMEM((moved, size), jnp.bfloat16),
             pltpu.VMEM((blocks * PACK, LANES), jnp.bfloat16),
-            pltpu.VMEM((len(grams), 2 * LANES, size), jnp.float32),
-            pltpu.SemaphoreType.DMA((len(grams),)),
             pltpu.SemaphoreType.DMA((2 + blocks,)),
         ],
-        compiler_params=pltpu.CompilerParams(vmem_limit_bytes=VMEM_LIMIT),
+        compiler_params=pltpu.CompilerParams(vmem_limit_bytes=JACOBI_VMEM_LIMIT),
         cost_estimate=pl.CostEstimate(
             flops=size, bytes_accessed=size, transcendentals=0
         ),
@@ -515,7 +509,12 @@
     slot = moves(plan_ref)[3]
     mask = slot_lanes(slot, half)
     middle = slice(LANES, 2 * LANES)
-    slow_turn = jnp.concatenate([slow_turn_ref[:size], slow_turn_ref[size:]], axis=1)
+    mixed = slow_turn_ref[size : size + size // 2].astype(jnp.float32)
+    side = slot_lanes(slot, size // 2)
+    mixed = jnp.concatenate(
+        [jnp.where(side, mixed, 0.0), pltpu.roll(jnp.where(side, 0.0, mixed), LANES // 2, 1)], axis=0
+    )
+    slow_turn = jnp.concatenate([mixed.astype(jnp.bfloat16), slow_turn_ref[:size]], axis=1)
     for unit in range(out_ref.shape[0] // UNIT):
         start, at = unit * UNIT, unit * PACK
         rows = slice(start, start + UNIT)
@@ -610,8 +609,7 @@
     own, early = gram_blocks(matrix)
     matrix_after, own = lax.optimization_barrier((matrix, own))
     if lax.axis_size("rows") == 2:
-        other = swapped_with(own, "rows", fast_partner)
-        grams = [own, other]
+        grams = [own, swapped_with(own, "rows", fast_partner)]
     else:
         grams = [lax.psum(own, "rows")]
     raw = swapped_with(early, "blk", slow_partner)
@@ -623,13 +621,13 @@
     last = swapped_with(last, "blk", slow_partner)
     near_turn = swapped_with(near_turn, "blk", fast_partner)
     near_pack = rotate_near(near, near_turn)
-    theirs = head[PACK:]
+    theirs = head[size + size // 2 :]
     theirs, near_pack, raw = lax.optimization_barrier((theirs, near_pack, raw))
     totals = cycle_sums(sums, theirs)
     off_ratio = jnp.sqrt(totals[0, 0] / totals[1, 0])
 
     shape = (rows, size)
-    turn_spec = pl.BlockSpec((PACK, LANES), lambda i: (0, 0))
+    turn_spec = pl.BlockSpec(head.shape, lambda i: (0, 0))
     raw_spec = pl.BlockSpec((UNIT, size), lambda i: (i, 0))
     wide_spec = pl.BlockSpec((WIDE_TILE // UNIT * PACK, LANES), lambda i: (i, 0))
     last_spec = pl.BlockSpec((PACK, LANES), lambda i: (i, 0))

time: 87.3 us -> 85.1 us (0.975)
  starting transfers between devices: 16.8 us -> 28.9 us
  waiting for transfers between devices: 30.5 us -> 19.3 us
  Pallas kernels: 34.1 us -> 31.8 us
    ppermute x3, starting transfers between devices: 5.27 us -> 18.5 us  [permuted(): return lax.ppermute(value, 'blk', pairs)]
    ppermute x7, waiting for transfers between devices: 29.4 us -> 17.7 us  [swapped_with(): lax.ppermute(value, axis, [(source, partner(source, count)) for source in...]
    pallas_call x1, Pallas kernels: 4.41 us -> 2.35 us  [rotate_near(): pl.pallas_call(near_kernel, grid=(rows // WIDE_TILE,), in_specs=[pl.Block...]
    ppermute x7, starting transfers between devices: 11.6 us -> 10.4 us  [swapped_with(): lax.ppermute(value, axis, [(source, partner(source, count)) for source in...]
  transfers between devices with their start and end apart: 10 -> 10, of which waited for: 5 -> 6; matrix products, arithmetic and copies ran while one was open for 2% -> 2% of each run, Pallas kernels for 30% -> 28%
where the time goes in v11:
time: 85.1 us; the launch traced here: 84.9 us
  Pallas kernels  31.8 us (37%)
  starting transfers between devices  28.9 us (34%)
  waiting for transfers between devices  19.3 us (23%)
  between operations  3.27 us (4%)
  other arithmetic  0.91 us (1%)
    ppermute x3, starting transfers between devices, permuted(): return lax.ppermute(value, 'blk', pairs)  18.5 us
    ppermute x7, waiting for transfers between devices, swapped_with(): lax.ppermute(value, axis, [(source, partner(source, count)) for source in...  17.7 us
    pallas_call x1, Pallas kernels, jacobi(): pl.pallas_call(jacobi_kernel, out_shape=(jax.ShapeDtypeStruct((size + siz...  16.2 us
    ppermute x7, starting transfers between devices, swapped_with(): lax.ppermute(value, axis, [(source, partner(source, count)) for source in...  10.4 us
    pallas_call x3, Pallas kernels, fill_rows(): pl.pallas_call(kernel, grid=(count // tile,), in_specs=in_specs, out_spec...  7.88 us
    pallas_call x1, Pallas kernels, gram_blocks(): pl.pallas_call(gram_kernel, in_specs=[pl.BlockSpec(memory_space=pl.ANY)],...  5.39 us
    pallas_call x1, Pallas kernels, rotate_near(): pl.pallas_call(near_kernel, grid=(rows // WIDE_TILE,), in_specs=[pl.Block...  2.35 us
  transfers between devices with their start and end apart: 10, of which 6 were waited for; matrix products, arithmetic and copies ran while one was open for 2% of the time, Pallas kernels for 28%

profile of v11, /device:TPU:1, one launch (start us, length us, event | category | flops | bytes accessed | tf_op | source)
XLA Modules:
  0.0 84.9 jit_solution(3188821401631686603)
XLA Ops:
  0.6 5.4 %gram_blocks.1 = (f32[256,384]{1,0:T(8,128)}, bf16[1536,384]{1,0:T(8,128)(2,1)}) custom-call(bf16[6144,384]{1,0:T(8,128)(2,1)} %refs_2_.1), custom_call_target="tpu_custom_call" | custom-call | flops 1811939328 | bytes 4718592 | tf_op jit(solution)/shard_map/gram_blocks/pallas_call | solution.py:424
  6.0 0.1 collective-permute-start.2
  6.2 2.7 %collective-permute-start.4 = (bf16[1536,384]{1,0:T(8,128)(2,1)}, bf16[1536,384]{1,0:T(8,128)(2,1)S(1)}, u32[]{:S(2)}, u32[]{:S(2)}) collective-permute-start(bf16[1536,384]{1,0:T(8,128)(2,1)} %get-tuple-element.21), channel_id=1, source_target_pairs={{0,30},{2,4},{4,2},{6,8},{8,6},{10,12},{12,10},{14,16},{16,14},{18... | collective-permute-start | bytes 3538952 | tf_op jit(solution)/shard_map/ppermute | solution.py:561
  8.8 1.2 %collective-permute-start = (f32[256,384]{1,0:T(8,128)}, f32[256,384]{1,0:T(8,128)}, u32[]{:S(2)}, u32[]{:S(2)}) collective-permute-start(f32[256,384]{1,0:T(8,128)} %get-tuple-element.17.refs_0_), channel_id=1, source_target_pairs={{0,1},{1,0},{2,3},{3,2},{4,5},{5,4},{6,7},{7,6},{8,9},{9,8},{10,11... | collective-permute-start | bytes 1179656 | tf_op jit(solution)/shard_map/ppermute | solution.py:561
  10.0 6.3 %collective-permute-done.refs_1_ = f32[256,384]{1,0:T(8,128)} collective-permute-done((f32[256,384]{1,0:T(8,128)}, f32[256,384]{1,0:T(8,128)}, u32[]{:S(2)}, u32[]{:S(2)}) %collective-permute-start) | collective-permute-done | bytes 393248 | tf_op jit(solution)/shard_map/ppermute | solution.py:561
  16.3 16.2 %jacobi_turns.1 = (bf16[592,128]{1,0:T(8,128)(2,1)}, bf16[4608,128]{1,0:T(8,128)(2,1)}, bf16[2304,128]{1,0:T(8,128)(2,1)}, bf16[384,384]{1,0:T(8,128)(2,1)}, bf16[16,128]{1,0:T(8,128)(2,1)}) custom-call(s32[32]{0:T(128)} %plan_ref.7, f32[256,384]{1,0:T(8,128)} %get-tuple-element.17.refs_0_, f32[256,384]{1,0:T(8,128)} %collective-permute-done.refs_1_, ...), custom_call_target="tpu_custom_call" | custom-call | flops 384 | bytes 384 | tf_op jit(solution)/shard_map/jacobi_turns/pallas_call | solution.py:345
  32.5 0.0 copy-start.1
  32.5 0.0 copy-start
  32.5 4.4 %collective-permute-start.3 = (bf16[384,384]{1,0:T(8,128)(2,1)}, bf16[384,384]{1,0:T(8,128)(2,1)S(1)}, u32[]{:S(2)}, u32[]{:S(2)}) collective-permute-start(bf16[384,384]{1,0:T(8,128)(2,1)} %get-tuple-element.20), channel_id=1, source_target_pairs={{0,2},{2,0},{4,6},{6,4},{8,10},{10,8},{12,14},{14,12},{16,18},{18,... | collective-permute-start | bytes 884744 | tf_op jit(solution)/shard_map/ppermute | solution.py:561
  37.0 0.5 collective-permute-start.1
  37.5 0.7 convert_element_type.6
  38.2 1.2 %collective-permute-start.6 = (bf16[4608,128]{1,0:T(8,128)(2,1)}, bf16[4608,128]{1,0:T(8,128)(2,1)S(1)}, u32[]{:S(2)}, u32[]{:S(2)}) collective-permute-start(bf16[4608,128]{1,0:T(8,128)(2,1)} %get-tuple-element.24), channel_id=1, source_target_pairs={{0,30},{2,4},{4,2},{6,8},{8,6},{10,12},{12,10},{14,16},{16,14},{18... | collective-permute-start | bytes 3538952 | tf_op jit(solution)/shard_map/ppermute | solution.py:561
  39.4 2.4 %collective-permute-done.1.slow_turn_ref = bf16[592,128]{1,0:T(8,128)(2,1)S(1)} collective-permute-done((bf16[592,128]{1,0:T(8,128)(2,1)}, bf16[592,128]{1,0:T(8,128)(2,1)S(1)}, u32[]{:S(2)}, u32[]{:S(2)}) %collective-permute-start.1) | collective-permute-done | bytes 151584 | tf_op jit(solution)/shard_map/ppermute | solution.py:561
  41.8 0.0 collective-permute-done.3.turn_ref
  41.8 0.0 collective-permute-done.2.near_ref
  41.8 2.3 %rotate_near.1.near_ref = bf16[9216,128]{1,0:T(8,128)(2,1)S(1)} custom-call(bf16[6144,384]{1,0:T(8,128)(2,1)S(1)} %collective-permute-done.2.near_ref, bf16[384,384]{1,0:T(8,128)(2,1)S(1)} %collective-permute-done.3.turn_ref), custom_call_target="tpu_custom_call" | custom-call | flops 384 | bytes 384 | tf_op jit(solution)/shard_map/rotate_near/pallas_call | solution.py:473
  44.2 0.0 collective-permute-done.4.slow_ref
  44.2 0.1 fusion.1
  44.3 2.9 %collective-permute-start.7 = (f32[16,128]{1,0:T(8,128)S(1)}, f32[16,128]{1,0:T(8,128)S(1)}, u32[]{:S(2)}, u32[]{:S(2)}) collective-permute-start(f32[16,128]{1,0:T(8,128)S(1)} %pad_maximum_fusion), channel_id=1, source_target_pairs={{0,2},{2,0},{4,6},{6,4},{8,10},{10,8},{12,14},{14,12},{16,18},{18,... | collective-permute-start | bytes 24584 | tf_op jit(solution)/shard_map/ppermute | solution.py:573
  47.2 0.8 collective-permute-done.7
  48.0 0.1 subtract_subtract_fusion.1
  48.1 13.1 %collective-permute-start.8 = (f32[16,128]{1,0:T(8,128)S(1)}, f32[16,128]{1,0:T(8,128)S(1)}, u32[]{:S(2)}, u32[]{:S(2)}) collective-permute-start(f32[16,128]{1,0:T(8,128)S(1)} %pad_maximum_fusion.1), channel_id=1, source_target_pairs={{0,8},{2,10},{4,12},{6,14},{8,0},{10,2},{12,4},{14,6},{16,24},{18,... | collective-permute-start | bytes 24584 | tf_op jit(solution)/shard_map/ppermute | solution.py:573
  61.2 0.0 copy-done.1
  61.2 0.2 collective-permute-start.5
  61.4 0.8 collective-permute-done.8
  62.3 2.5 %collective-permute-start.9 = (f32[16,128]{1,0:T(8,128)S(1)}, f32[16,128]{1,0:T(8,128)S(1)}, u32[]{:S(2)}, u32[]{:S(2)}) collective-permute-start(f32[16,128]{1,0:T(8,128)S(1)} %pad_maximum_fusion.2), channel_id=1, source_target_pairs={{0,16},{2,18},{4,20},{6,22},{8,24},{10,26},{12,28},{14,30},{16,0},... | collective-permute-start | bytes 24584 | tf_op jit(solution)/shard_map/ppermute | solution.py:573
  64.8 0.0 copy-done
  64.8 3.0 %fill_rows.3.refs_0_ = bf16[6144,384]{1,0:T(8,128)(2,1)} custom-call(s32[32]{0:T(128)S(1)} %copy-done, bf16[9216,128]{1,0:T(8,128)(2,1)S(1)} %rotate_near.1.near_ref, bf16[1536,384]{1,0:T(8,128)(2,1)S(1)} %collective-permute-done.4.slow_ref, bf16[592,128]{1,0:T(8,128)(2,1)S(1)} %collective-permute-done.1.slow_turn_ref), custom_call_target="tpu_custom_call" | custom-call | flops 589824 | bytes 2359296 | tf_op jit(solution)/shard_map/fill_rows/pallas_call | solution.py:544
  67.9 7.2 %collective-permute-done.6.slow_ref = bf16[4608,128]{1,0:T(8,128)(2,1)S(1)} collective-permute-done((bf16[4608,128]{1,0:T(8,128)(2,1)}, bf16[4608,128]{1,0:T(8,128)(2,1)S(1)}, u32[]{:S(2)}, u32[]{:S(2)}) %collective-permute-start.6) | collective-permute-done | bytes 1179680 | tf_op jit(solution)/shard_map/ppermute | solution.py:561
  75.0 2.5 %fill_rows.4.refs_0_ = bf16[6144,384]{1,0:T(8,128)(2,1)} custom-call(s32[32]{0:T(128)S(1)} %copy-done, bf16[9216,128]{1,0:T(8,128)(2,1)S(1)} %rotate_near.1.near_ref, bf16[4608,128]{1,0:T(8,128)(2,1)S(1)} %collective-permute-done.6.slow_ref, bf16[6144,384]{1,0:T(8,128)(2,1)} %fill_rows.3.refs_0_), custom_call_target="tpu_custom_call", output_to_operand_aliasing={{}: (3, {})} | custom-call | flops 1179648 | bytes 4718592 | tf_op jit(solution)/shard_map/fill_rows/pallas_call | solution.py:544
  77.5 0.0 collective-permute-done.9
  77.5 0.6 fusion.17
  79.5 1.8 %collective-permute-done.5.slow_ref = bf16[2304,128]{1,0:T(8,128)(2,1)S(1)} collective-permute-done((bf16[2304,128]{1,0:T(8,128)(2,1)S(1)}, bf16[2304,128]{1,0:T(8,128)(2,1)S(1)}, u32[]{:S(2)}, u32[]{:S(2)}) %collective-permute-start.5) | collective-permute-done | bytes 589856 | tf_op jit(solution)/shard_map/ppermute | solution.py:561
  81.3 2.4 %fill_rows.5 = bf16[6144,384]{1,0:T(8,128)(2,1)} custom-call(s32[32]{0:T(128)S(1)} %copy-done, bf16[9216,128]{1,0:T(8,128)(2,1)S(1)} %rotate_near.1.near_ref, bf16[2304,128]{1,0:T(8,128)(2,1)S(1)} %collective-permute-done.5.slow_ref, bf16[6144,384]{1,0:T(8,128)(2,1)} %fill_rows.4.refs_0_), custom_call_target="tpu_custom_call", output_to_operand_aliasing={{}: (3, {})} | custom-call | flops 589824 | bytes 2359296 | tf_op jit(solution)/shard_map/fill_rows/pallas_call | solution.py:544
  (9 shorter events, 0.1 us)
Async XLA Ops:
  6.0 35.8 %collective-permute-start.2 = (bf16[6144,384]{1,0:T(8,128)(2,1)}, bf16[6144,384]{1,0:T(8,128)(2,1)S(1)}, u32[]{:S(2)}, u32[]{:S(2)}) collective-permute-start(bf16[6144,384]{1,0:T(8,128)(2,1)} %refs_2_.1), channel_id=1, source_target_pairs={{0,2},{2,0},{4,6},{6,4},{8,10},{10,8},{12,14},{14,12},{16,18},{18,... | collective-permute-start | bytes 14155784 | tf_op jit(solution)/shard_map/ppermute | solution.py:561
  6.2 38.0 %collective-permute-start.4 = (bf16[1536,384]{1,0:T(8,128)(2,1)}, bf16[1536,384]{1,0:T(8,128)(2,1)S(1)}, u32[]{:S(2)}, u32[]{:S(2)}) collective-permute-start(bf16[1536,384]{1,0:T(8,128)(2,1)} %get-tuple-element.21), channel_id=1, source_target_pairs={{0,30},{2,4},{4,2},{6,8},{8,6},{10,12},{12,10},{14,16},{16,14},{18... | collective-permute-start | bytes 3538952 | tf_op jit(solution)/shard_map/ppermute | solution.py:561
  8.8 7.5 %collective-permute-start = (f32[256,384]{1,0:T(8,128)}, f32[256,384]{1,0:T(8,128)}, u32[]{:S(2)}, u32[]{:S(2)}) collective-permute-start(f32[256,384]{1,0:T(8,128)} %get-tuple-element.17.refs_0_), channel_id=1, source_target_pairs={{0,1},{1,0},{2,3},{3,2},{4,5},{5,4},{6,7},{7,6},{8,9},{9,8},{10,11... | collective-permute-start | bytes 1179656 | tf_op jit(solution)/shard_map/ppermute | solution.py:561
  32.5 28.7 %copy-start.1 = (bf16[2304,128]{1,0:T(8,128)(2,1)S(1)}, bf16[2304,128]{1,0:T(8,128)(2,1)}, u32[]{:S(2)}) copy-start(bf16[2304,128]{1,0:T(8,128)(2,1)} %get-tuple-element.23) | copy-start | bytes 1769476
  32.5 32.3 %copy-start = (s32[32]{0:T(128)S(1)}, s32[32]{0:T(128)}, u32[]{:S(2)}) copy-start(s32[32]{0:T(128)} %plan_ref.7) | copy-start | bytes 388
  32.5 9.3 %collective-permute-start.3 = (bf16[384,384]{1,0:T(8,128)(2,1)}, bf16[384,384]{1,0:T(8,128)(2,1)S(1)}, u32[]{:S(2)}, u32[]{:S(2)}) collective-permute-start(bf16[384,384]{1,0:T(8,128)(2,1)} %get-tuple-element.20), channel_id=1, source_target_pairs={{0,2},{2,0},{4,6},{6,4},{8,10},{10,8},{12,14},{14,12},{16,18},{18,... | collective-permute-start | bytes 884744 | tf_op jit(solution)/shard_map/ppermute | solution.py:561
  37.0 4.8 %collective-permute-start.1 = (bf16[592,128]{1,0:T(8,128)(2,1)}, bf16[592,128]{1,0:T(8,128)(2,1)S(1)}, u32[]{:S(2)}, u32[]{:S(2)}) collective-permute-start(bf16[592,128]{1,0:T(8,128)(2,1)} %get-tuple-element.18), channel_id=1, source_target_pairs={{0,30},{2,4},{4,2},{6,8},{8,6},{10,12},{12,10},{14,16},{16,14},{18... | collective-permute-start | bytes 454664 | tf_op jit(solution)/shard_map/ppermute | solution.py:561
  38.2 36.8 %collective-permute-start.6 = (bf16[4608,128]{1,0:T(8,128)(2,1)}, bf16[4608,128]{1,0:T(8,128)(2,1)S(1)}, u32[]{:S(2)}, u32[]{:S(2)}) collective-permute-start(bf16[4608,128]{1,0:T(8,128)(2,1)} %get-tuple-element.24), channel_id=1, source_target_pairs={{0,30},{2,4},{4,2},{6,8},{8,6},{10,12},{12,10},{14,16},{16,14},{18... | collective-permute-start | bytes 3538952 | tf_op jit(solution)/shard_map/ppermute | solution.py:561
  44.3 3.8 %collective-permute-start.7 = (f32[16,128]{1,0:T(8,128)S(1)}, f32[16,128]{1,0:T(8,128)S(1)}, u32[]{:S(2)}, u32[]{:S(2)}) collective-permute-start(f32[16,128]{1,0:T(8,128)S(1)} %pad_maximum_fusion), channel_id=1, source_target_pairs={{0,2},{2,0},{4,6},{6,4},{8,10},{10,8},{12,14},{14,12},{16,18},{18,... | collective-permute-start | bytes 24584 | tf_op jit(solution)/shard_map/ppermute | solution.py:573
  48.1 14.1 %collective-permute-start.8 = (f32[16,128]{1,0:T(8,128)S(1)}, f32[16,128]{1,0:T(8,128)S(1)}, u32[]{:S(2)}, u32[]{:S(2)}) collective-permute-start(f32[16,128]{1,0:T(8,128)S(1)} %pad_maximum_fusion.1), channel_id=1, source_target_pairs={{0,8},{2,10},{4,12},{6,14},{8,0},{10,2},{12,4},{14,6},{16,24},{18,... | collective-permute-start | bytes 24584 | tf_op jit(solution)/shard_map/ppermute | solution.py:573
  61.2 20.1 %collective-permute-start.5 = (bf16[2304,128]{1,0:T(8,128)(2,1)S(1)}, bf16[2304,128]{1,0:T(8,128)(2,1)S(1)}, u32[]{:S(2)}, u32[]{:S(2)}) collective-permute-start(bf16[2304,128]{1,0:T(8,128)(2,1)S(1)} %copy-done.1), channel_id=1, source_target_pairs={{0,30},{2,4},{4,2},{6,8},{8,6},{10,12},{12,10},{14,16},{16,14},{18... | collective-permute-start | bytes 1769480 | tf_op jit(solution)/shard_map/ppermute | solution.py:561
  62.3 15.2 %collective-permute-start.9 = (f32[16,128]{1,0:T(8,128)S(1)}, f32[16,128]{1,0:T(8,128)S(1)}, u32[]{:S(2)}, u32[]{:S(2)}) collective-permute-start(f32[16,128]{1,0:T(8,128)S(1)} %pad_maximum_fusion.2), channel_id=1, source_target_pairs={{0,16},{2,18},{4,20},{6,22},{8,24},{10,26},{12,28},{14,30},{16,0},... | collective-permute-start | bytes 24584 | tf_op jit(solution)/shard_map/ppermute | solution.py:573

commit v12 on v11

--- a/solution.py
+++ b/solution.py
@@ -73,12 +73,24 @@
     return cos_sq * half_root, 0.5 * (across * root) * half_root
 
 
+def triangle():
+    rows = lax.broadcasted_iota(jnp.int32, (LANES, LANES), 0)
+    cols = lax.broadcasted_iota(jnp.int32, (LANES, LANES), 1)
+    return rows, cols
+
+
 def full_gram(packed):
-    first = packed[:LANES]
-    block01, block02 = first[:, LANES : 2 * LANES], first[:, 2 * LANES :]
-    block12 = packed[LANES:, LANES : 2 * LANES]
-    second = jnp.concatenate([block01.T, packed[LANES:, : 2 * LANES]], axis=1)
-    third = jnp.concatenate([block02.T, block12.T, packed[LANES:, 2 * LANES :]], axis=1)
+    shared, block01, block02, block12, block22 = (
+        packed[index * LANES : (index + 1) * LANES] for index in range(5)
+    )
+    diag11 = packed[5 * LANES : 5 * LANES + 1]
+    rows, cols = triangle()
+    flipped = shared.T
+    block00 = jnp.where(rows <= cols, shared, flipped)
+    block11 = jnp.where(rows > cols, shared, jnp.where(rows < cols, flipped, diag11))
+    first = jnp.concatenate([block00, block01, block02], axis=1)
+    second = jnp.concatenate([block01.T, block11, block12], axis=1)
+    third = jnp.concatenate([block02.T, block12.T, block22], axis=1)
     return jnp.concatenate([first, second, third], axis=0)
 
 
@@ -94,19 +106,12 @@
     return jnp.where(section == 1, main_start + lane, mixed)
 
 
-def block_sums(packed):
-    squares = packed * packed
-    total = jnp.zeros((1, 1), jnp.float32)
-    diag_sq = jnp.zeros((1, 1), jnp.float32)
-    rows = lax.broadcasted_iota(jnp.int32, (LANES, LANES), 0)
-    cols = lax.broadcasted_iota(jnp.int32, (LANES, LANES), 1)
-    for row, col, weight in (
-        (0, 0, 1.0), (0, 1, 2.0), (0, 2, 2.0), (1, 0, 1.0), (1, 1, 2.0), (1, 2, 1.0)
-    ):
-        block = squares[row * LANES : (row + 1) * LANES, col * LANES : (col + 1) * LANES]
-        total = total + weight * jnp.sum(block, keepdims=True)
-        if weight == 1.0:
-            diag_sq = diag_sq + jnp.sum(jnp.where(rows == cols, block, 0.0), keepdims=True)
+def block_sums(gram_sum):
+    squares = gram_sum * gram_sum
+    rows = lax.broadcasted_iota(jnp.int32, squares.shape, 0)
+    cols = lax.broadcasted_iota(jnp.int32, squares.shape, 1)
+    total = jnp.sum(squares, keepdims=True)
+    diag_sq = jnp.sum(jnp.where(rows == cols, squares, 0.0), keepdims=True)
     row = lax.broadcasted_iota(jnp.int32, (SUM_ROWS, LANES), 0)
     pieces = jnp.zeros((SUM_ROWS, LANES), jnp.float32)
     for index, piece in enumerate(split_three(total - diag_sq) + split_three(diag_sq)):
@@ -145,7 +150,7 @@
     gram_a, gram_b, basis_a, basis_b, cos_buf, sin_buf, held, packs, sems,
 ):
     matrix_copy = pltpu.make_async_copy(matrix_ref.at[pl.ds(RAW_ROWS, held.shape[0])], held, sems.at[0])
-    size = gram_refs[0].shape[1]
+    size = matrix_ref.shape[1]
     half = size // 2
     groups = half // SUBS
     last = groups - 1
@@ -168,7 +173,7 @@
     for other in gram_refs[1:]:
         packed = packed + other[...]
     gram_sum = full_gram(packed)
-    sums_ref[...] = block_sums(packed)
+    sums_ref[...] = block_sums(gram_sum)
     for piece in split_three(gram_sum):
         moved = dot32(take_rows, piece).astype(jnp.bfloat16)
         arranged = arranged + dot32(moved, take_cols)
@@ -413,9 +418,15 @@
         else:
             upper_ref[...] += upper
             corner_ref[...] += corner
-    packed_ref[:LANES] = upper_ref[:LANES]
-    packed_ref[LANES:, : 2 * LANES] = upper_ref[LANES:, LANES:]
-    packed_ref[LANES:, 2 * LANES :] = corner_ref[...]
+    rows_at, cols_at = triangle()
+    block11 = upper_ref[LANES:, LANES : 2 * LANES]
+    packed_ref[:LANES] = jnp.where(rows_at <= cols_at, upper_ref[:LANES, :LANES], block11)
+    packed_ref[LANES : 2 * LANES] = upper_ref[:LANES, LANES : 2 * LANES]
+    packed_ref[2 * LANES : 3 * LANES] = upper_ref[:LANES, 2 * LANES :]
+    packed_ref[3 * LANES : 4 * LANES] = upper_ref[LANES:, 2 * LANES :]
+    packed_ref[4 * LANES : 5 * LANES] = corner_ref[...]
+    diag11 = jnp.sum(jnp.where(rows_at == cols_at, block11, 0.0), axis=0, keepdims=True)
+    packed_ref[5 * LANES :] = jnp.broadcast_to(diag11, (SUBS, LANES))
     leave.wait()
 
 
@@ -426,7 +437,7 @@
         in_specs=[pl.BlockSpec(memory_space=pl.ANY)],
         out_specs=[pl.BlockSpec(memory_space=pltpu.VMEM), pl.BlockSpec(memory_space=pl.ANY)],
         out_shape=(
-            jax.ShapeDtypeStruct((2 * LANES, size), jnp.float32),
+            jax.ShapeDtypeStruct((5 * LANES + SUBS, LANES), jnp.float32),
             jax.ShapeDtypeStruct((RAW_ROWS, size), jnp.bfloat16),
         ),
         scratch_shapes=[

time: 85.1 us -> 84.2 us (0.989)
  transfers between devices with their start and end apart: 10 -> 10, of which waited for: 6 -> 6; matrix products, arithmetic and copies ran while one was open for 2% -> 2% of each run, Pallas kernels for 28% -> 29%
where the time goes in v12:
time: 84.2 us; the launch traced here: 83.9 us
  Pallas kernels  31.7 us (38%)
  starting transfers between devices  28.6 us (34%)
  waiting for transfers between devices  18.8 us (22%)
  between operations  3.27 us (4%)
  other arithmetic  0.89 us (1%)
    ppermute x3, starting transfers between devices, permuted(): return lax.ppermute(value, 'blk', pairs)  18.2 us
    ppermute x7, waiting for transfers between devices, swapped_with(): lax.ppermute(value, axis, [(source, partner(source, count)) for source in...  17.1 us
    pallas_call x1, Pallas kernels, jacobi(): pl.pallas_call(jacobi_kernel, out_shape=(jax.ShapeDtypeStruct((size + siz...  16.2 us
    ppermute x7, starting transfers between devices, swapped_with(): lax.ppermute(value, axis, [(source, partner(source, count)) for source in...  10.4 us
    pallas_call x3, Pallas kernels, fill_rows(): pl.pallas_call(kernel, grid=(count // tile,), in_specs=in_specs, out_spec...  7.79 us
    pallas_call x1, Pallas kernels, gram_blocks(): pl.pallas_call(gram_kernel, in_specs=[pl.BlockSpec(memory_space=pl.ANY)],...  5.37 us
    pallas_call x1, Pallas kernels, rotate_near(): pl.pallas_call(near_kernel, grid=(rows // WIDE_TILE,), in_specs=[pl.Block...  2.35 us
  transfers between devices with their start and end apart: 10, of which 6 were waited for; matrix products, arithmetic and copies ran while one was open for 2% of the time, Pallas kernels for 29%

profile of v12, /device:TPU:1, one launch (start us, length us, event | category | flops | bytes accessed | tf_op | source)
XLA Modules:
  0.0 83.9 jit_solution(15678834229894098845)
XLA Ops:
  0.6 5.4 %gram_blocks.1 = (f32[648,128]{1,0:T(8,128)}, bf16[1536,384]{1,0:T(8,128)(2,1)}) custom-call(bf16[6144,384]{1,0:T(8,128)(2,1)} %refs_2_.1), custom_call_target="tpu_custom_call" | custom-call | flops 1811939328 | bytes 4718592 | tf_op jit(solution)/shard_map/gram_blocks/pallas_call | solution.py:435
  6.0 0.1 collective-permute-start.2
  6.1 2.7 %collective-permute-start.4 = (bf16[1536,384]{1,0:T(8,128)(2,1)}, bf16[1536,384]{1,0:T(8,128)(2,1)S(1)}, u32[]{:S(2)}, u32[]{:S(2)}) collective-permute-start(bf16[1536,384]{1,0:T(8,128)(2,1)} %get-tuple-element.21), channel_id=1, source_target_pairs={{0,30},{2,4},{4,2},{6,8},{8,6},{10,12},{12,10},{14,16},{16,14},{18... | collective-permute-start | bytes 3538952 | tf_op jit(solution)/shard_map/ppermute | solution.py:572
  8.8 1.2 %collective-permute-start = (f32[648,128]{1,0:T(8,128)}, f32[648,128]{1,0:T(8,128)}, u32[]{:S(2)}, u32[]{:S(2)}) collective-permute-start(f32[648,128]{1,0:T(8,128)} %get-tuple-element.17.refs_0_), channel_id=1, source_target_pairs={{0,1},{1,0},{2,3},{3,2},{4,5},{5,4},{6,7},{7,6},{8,9},{9,8},{10,11... | collective-permute-start | bytes 995336 | tf_op jit(solution)/shard_map/ppermute | solution.py:572
  10.0 5.3 %collective-permute-done.refs_1_ = f32[648,128]{1,0:T(8,128)} collective-permute-done((f32[648,128]{1,0:T(8,128)}, f32[648,128]{1,0:T(8,128)}, u32[]{:S(2)}, u32[]{:S(2)}) %collective-permute-start) | collective-permute-done | bytes 331808 | tf_op jit(solution)/shard_map/ppermute | solution.py:572
  15.3 16.2 %jacobi_turns.1 = (bf16[592,128]{1,0:T(8,128)(2,1)}, bf16[4608,128]{1,0:T(8,128)(2,1)}, bf16[2304,128]{1,0:T(8,128)(2,1)}, bf16[384,384]{1,0:T(8,128)(2,1)}, bf16[16,128]{1,0:T(8,128)(2,1)}) custom-call(s32[32]{0:T(128)} %plan_ref.7, f32[648,128]{1,0:T(8,128)} %get-tuple-element.17.refs_0_, f32[648,128]{1,0:T(8,128)} %collective-permute-done.refs_1_, ...), custom_call_target="tpu_custom_call" | custom-call | flops 384 | bytes 384 | tf_op jit(solution)/shard_map/jacobi_turns/pallas_call | solution.py:350
  31.5 0.0 copy-start.1
  31.5 0.0 copy-start
  31.5 4.5 %collective-permute-start.3 = (bf16[384,384]{1,0:T(8,128)(2,1)}, bf16[384,384]{1,0:T(8,128)(2,1)S(1)}, u32[]{:S(2)}, u32[]{:S(2)}) collective-permute-start(bf16[384,384]{1,0:T(8,128)(2,1)} %get-tuple-element.20), channel_id=1, source_target_pairs={{0,2},{2,0},{4,6},{6,4},{8,10},{10,8},{12,14},{14,12},{16,18},{18,... | collective-permute-start | bytes 884744 | tf_op jit(solution)/shard_map/ppermute | solution.py:572
  36.0 0.2 collective-permute-start.1
  36.2 0.7 convert_element_type.6
  36.9 1.6 %collective-permute-start.6 = (bf16[4608,128]{1,0:T(8,128)(2,1)}, bf16[4608,128]{1,0:T(8,128)(2,1)S(1)}, u32[]{:S(2)}, u32[]{:S(2)}) collective-permute-start(bf16[4608,128]{1,0:T(8,128)(2,1)} %get-tuple-element.24), channel_id=1, source_target_pairs={{0,30},{2,4},{4,2},{6,8},{8,6},{10,12},{12,10},{14,16},{16,14},{18... | collective-permute-start | bytes 3538952 | tf_op jit(solution)/shard_map/ppermute | solution.py:572
  38.4 2.4 %collective-permute-done.1.slow_turn_ref = bf16[592,128]{1,0:T(8,128)(2,1)S(1)} collective-permute-done((bf16[592,128]{1,0:T(8,128)(2,1)}, bf16[592,128]{1,0:T(8,128)(2,1)S(1)}, u32[]{:S(2)}, u32[]{:S(2)}) %collective-permute-start.1) | collective-permute-done | bytes 151584 | tf_op jit(solution)/shard_map/ppermute | solution.py:572
  40.8 0.0 collective-permute-done.3.turn_ref
  40.8 0.0 collective-permute-done.2.near_ref
  40.8 2.3 %rotate_near.1.near_ref = bf16[9216,128]{1,0:T(8,128)(2,1)S(1)} custom-call(bf16[6144,384]{1,0:T(8,128)(2,1)S(1)} %collective-permute-done.2.near_ref, bf16[384,384]{1,0:T(8,128)(2,1)S(1)} %collective-permute-done.3.turn_ref), custom_call_target="tpu_custom_call" | custom-call | flops 384 | bytes 384 | tf_op jit(solution)/shard_map/rotate_near/pallas_call | solution.py:484
  43.2 0.0 collective-permute-done.4.slow_ref
  43.2 0.1 fusion.1
  43.3 2.9 %collective-permute-start.7 = (f32[16,128]{1,0:T(8,128)S(1)}, f32[16,128]{1,0:T(8,128)S(1)}, u32[]{:S(2)}, u32[]{:S(2)}) collective-permute-start(f32[16,128]{1,0:T(8,128)S(1)} %pad_maximum_fusion), channel_id=1, source_target_pairs={{0,2},{2,0},{4,6},{6,4},{8,10},{10,8},{12,14},{14,12},{16,18},{18,... | collective-permute-start | bytes 24584 | tf_op jit(solution)/shard_map/ppermute | solution.py:584
  46.3 0.8 collective-permute-done.7
  47.1 0.1 subtract_subtract_fusion.1
  47.2 12.7 %collective-permute-start.8 = (f32[16,128]{1,0:T(8,128)S(1)}, f32[16,128]{1,0:T(8,128)S(1)}, u32[]{:S(2)}, u32[]{:S(2)}) collective-permute-start(f32[16,128]{1,0:T(8,128)S(1)} %pad_maximum_fusion.1), channel_id=1, source_target_pairs={{0,8},{2,10},{4,12},{6,14},{8,0},{10,2},{12,4},{14,6},{16,24},{18,... | collective-permute-start | bytes 24584 | tf_op jit(solution)/shard_map/ppermute | solution.py:584
  59.9 0.0 copy-done.1
  59.9 0.2 collective-permute-start.5
  60.1 0.8 collective-permute-done.8
  61.0 2.5 %collective-permute-start.9 = (f32[16,128]{1,0:T(8,128)S(1)}, f32[16,128]{1,0:T(8,128)S(1)}, u32[]{:S(2)}, u32[]{:S(2)}) collective-permute-start(f32[16,128]{1,0:T(8,128)S(1)} %pad_maximum_fusion.2), channel_id=1, source_target_pairs={{0,16},{2,18},{4,20},{6,22},{8,24},{10,26},{12,28},{14,30},{16,0},... | collective-permute-start | bytes 24584 | tf_op jit(solution)/shard_map/ppermute | solution.py:584
  63.5 0.0 copy-done
  63.5 3.0 %fill_rows.3.refs_0_ = bf16[6144,384]{1,0:T(8,128)(2,1)} custom-call(s32[32]{0:T(128)S(1)} %copy-done, bf16[9216,128]{1,0:T(8,128)(2,1)S(1)} %rotate_near.1.near_ref, bf16[1536,384]{1,0:T(8,128)(2,1)S(1)} %collective-permute-done.4.slow_ref, bf16[592,128]{1,0:T(8,128)(2,1)S(1)} %collective-permute-done.1.slow_turn_ref), custom_call_target="tpu_custom_call" | custom-call | flops 589824 | bytes 2359296 | tf_op jit(solution)/shard_map/fill_rows/pallas_call | solution.py:555
  66.5 7.6 %collective-permute-done.6.slow_ref = bf16[4608,128]{1,0:T(8,128)(2,1)S(1)} collective-permute-done((bf16[4608,128]{1,0:T(8,128)(2,1)}, bf16[4608,128]{1,0:T(8,128)(2,1)S(1)}, u32[]{:S(2)}, u32[]{:S(2)}) %collective-permute-start.6) | collective-permute-done | bytes 1179680 | tf_op jit(solution)/shard_map/ppermute | solution.py:572
  74.1 2.4 %fill_rows.4.refs_0_ = bf16[6144,384]{1,0:T(8,128)(2,1)} custom-call(s32[32]{0:T(128)S(1)} %copy-done, bf16[9216,128]{1,0:T(8,128)(2,1)S(1)} %rotate_near.1.near_ref, bf16[4608,128]{1,0:T(8,128)(2,1)S(1)} %collective-permute-done.6.slow_ref, bf16[6144,384]{1,0:T(8,128)(2,1)} %fill_rows.3.refs_0_), custom_call_target="tpu_custom_call", output_to_operand_aliasing={{}: (3, {})} | custom-call | flops 1179648 | bytes 4718592 | tf_op jit(solution)/shard_map/fill_rows/pallas_call | solution.py:555
  76.4 0.0 collective-permute-done.9
  76.5 0.6 fusion.17
  78.5 1.9 %collective-permute-done.5.slow_ref = bf16[2304,128]{1,0:T(8,128)(2,1)S(1)} collective-permute-done((bf16[2304,128]{1,0:T(8,128)(2,1)S(1)}, bf16[2304,128]{1,0:T(8,128)(2,1)S(1)}, u32[]{:S(2)}, u32[]{:S(2)}) %collective-permute-start.5) | collective-permute-done | bytes 589856 | tf_op jit(solution)/shard_map/ppermute | solution.py:572
  80.4 2.4 %fill_rows.5 = bf16[6144,384]{1,0:T(8,128)(2,1)} custom-call(s32[32]{0:T(128)S(1)} %copy-done, bf16[9216,128]{1,0:T(8,128)(2,1)S(1)} %rotate_near.1.near_ref, bf16[2304,128]{1,0:T(8,128)(2,1)S(1)} %collective-permute-done.5.slow_ref, bf16[6144,384]{1,0:T(8,128)(2,1)} %fill_rows.4.refs_0_), custom_call_target="tpu_custom_call", output_to_operand_aliasing={{}: (3, {})} | custom-call | flops 589824 | bytes 2359296 | tf_op jit(solution)/shard_map/fill_rows/pallas_call | solution.py:555
  (9 shorter events, 0.1 us)
Async XLA Ops:
  6.0 34.8 %collective-permute-start.2 = (bf16[6144,384]{1,0:T(8,128)(2,1)}, bf16[6144,384]{1,0:T(8,128)(2,1)S(1)}, u32[]{:S(2)}, u32[]{:S(2)}) collective-permute-start(bf16[6144,384]{1,0:T(8,128)(2,1)} %refs_2_.1), channel_id=1, source_target_pairs={{0,2},{2,0},{4,6},{6,4},{8,10},{10,8},{12,14},{14,12},{16,18},{18,... | collective-permute-start | bytes 14155784 | tf_op jit(solution)/shard_map/ppermute | solution.py:572
  6.1 37.1 %collective-permute-start.4 = (bf16[1536,384]{1,0:T(8,128)(2,1)}, bf16[1536,384]{1,0:T(8,128)(2,1)S(1)}, u32[]{:S(2)}, u32[]{:S(2)}) collective-permute-start(bf16[1536,384]{1,0:T(8,128)(2,1)} %get-tuple-element.21), channel_id=1, source_target_pairs={{0,30},{2,4},{4,2},{6,8},{8,6},{10,12},{12,10},{14,16},{16,14},{18... | collective-permute-start | bytes 3538952 | tf_op jit(solution)/shard_map/ppermute | solution.py:572
  8.8 6.5 %collective-permute-start = (f32[648,128]{1,0:T(8,128)}, f32[648,128]{1,0:T(8,128)}, u32[]{:S(2)}, u32[]{:S(2)}) collective-permute-start(f32[648,128]{1,0:T(8,128)} %get-tuple-element.17.refs_0_), channel_id=1, source_target_pairs={{0,1},{1,0},{2,3},{3,2},{4,5},{5,4},{6,7},{7,6},{8,9},{9,8},{10,11... | collective-permute-start | bytes 995336 | tf_op jit(solution)/shard_map/ppermute | solution.py:572
  31.5 28.4 %copy-start.1 = (bf16[2304,128]{1,0:T(8,128)(2,1)S(1)}, bf16[2304,128]{1,0:T(8,128)(2,1)}, u32[]{:S(2)}) copy-start(bf16[2304,128]{1,0:T(8,128)(2,1)} %get-tuple-element.23) | copy-start | bytes 1769476
  31.5 32.0 %copy-start = (s32[32]{0:T(128)S(1)}, s32[32]{0:T(128)}, u32[]{:S(2)}) copy-start(s32[32]{0:T(128)} %plan_ref.7) | copy-start | bytes 388
  31.5 9.3 %collective-permute-start.3 = (bf16[384,384]{1,0:T(8,128)(2,1)}, bf16[384,384]{1,0:T(8,128)(2,1)S(1)}, u32[]{:S(2)}, u32[]{:S(2)}) collective-permute-start(bf16[384,384]{1,0:T(8,128)(2,1)} %get-tuple-element.20), channel_id=1, source_target_pairs={{0,2},{2,0},{4,6},{6,4},{8,10},{10,8},{12,14},{14,12},{16,18},{18,... | collective-permute-start | bytes 884744 | tf_op jit(solution)/shard_map/ppermute | solution.py:572
  36.0 4.8 %collective-permute-start.1 = (bf16[592,128]{1,0:T(8,128)(2,1)}, bf16[592,128]{1,0:T(8,128)(2,1)S(1)}, u32[]{:S(2)}, u32[]{:S(2)}) collective-permute-start(bf16[592,128]{1,0:T(8,128)(2,1)} %get-tuple-element.18), channel_id=1, source_target_pairs={{0,30},{2,4},{4,2},{6,8},{8,6},{10,12},{12,10},{14,16},{16,14},{18... | collective-permute-start | bytes 454664 | tf_op jit(solution)/shard_map/ppermute | solution.py:572
  36.9 37.2 %collective-permute-start.6 = (bf16[4608,128]{1,0:T(8,128)(2,1)}, bf16[4608,128]{1,0:T(8,128)(2,1)S(1)}, u32[]{:S(2)}, u32[]{:S(2)}) collective-permute-start(bf16[4608,128]{1,0:T(8,128)(2,1)} %get-tuple-element.24), channel_id=1, source_target_pairs={{0,30},{2,4},{4,2},{6,8},{8,6},{10,12},{12,10},{14,16},{16,14},{18... | collective-permute-start | bytes 3538952 | tf_op jit(solution)/shard_map/ppermute | solution.py:572
  43.3 3.8 %collective-permute-start.7 = (f32[16,128]{1,0:T(8,128)S(1)}, f32[16,128]{1,0:T(8,128)S(1)}, u32[]{:S(2)}, u32[]{:S(2)}) collective-permute-start(f32[16,128]{1,0:T(8,128)S(1)} %pad_maximum_fusion), channel_id=1, source_target_pairs={{0,2},{2,0},{4,6},{6,4},{8,10},{10,8},{12,14},{14,12},{16,18},{18,... | collective-permute-start | bytes 24584 | tf_op jit(solution)/shard_map/ppermute | solution.py:584
  47.2 13.8 %collective-permute-start.8 = (f32[16,128]{1,0:T(8,128)S(1)}, f32[16,128]{1,0:T(8,128)S(1)}, u32[]{:S(2)}, u32[]{:S(2)}) collective-permute-start(f32[16,128]{1,0:T(8,128)S(1)} %pad_maximum_fusion.1), channel_id=1, source_target_pairs={{0,8},{2,10},{4,12},{6,14},{8,0},{10,2},{12,4},{14,6},{16,24},{18,... | collective-permute-start | bytes 24584 | tf_op jit(solution)/shard_map/ppermute | solution.py:584
  59.9 20.5 %collective-permute-start.5 = (bf16[2304,128]{1,0:T(8,128)(2,1)S(1)}, bf16[2304,128]{1,0:T(8,128)(2,1)S(1)}, u32[]{:S(2)}, u32[]{:S(2)}) collective-permute-start(bf16[2304,128]{1,0:T(8,128)(2,1)S(1)} %copy-done.1), channel_id=1, source_target_pairs={{0,30},{2,4},{4,2},{6,8},{8,6},{10,12},{12,10},{14,16},{16,14},{18... | collective-permute-start | bytes 1769480 | tf_op jit(solution)/shard_map/ppermute | solution.py:572
  61.0 15.5 %collective-permute-start.9 = (f32[16,128]{1,0:T(8,128)S(1)}, f32[16,128]{1,0:T(8,128)S(1)}, u32[]{:S(2)}, u32[]{:S(2)}) collective-permute-start(f32[16,128]{1,0:T(8,128)S(1)} %pad_maximum_fusion.2), channel_id=1, source_target_pairs={{0,16},{2,18},{4,20},{6,22},{8,24},{10,26},{12,28},{14,30},{16,0},... | collective-permute-start | bytes 24584 | tf_op jit(solution)/shard_map/ppermute | solution.py:584

commit v13 on v12

--- a/solution.py
+++ b/solution.py
@@ -80,7 +80,7 @@
 
 
 def full_gram(packed):
-    shared, block01, block02, block12, block22 = (
+    shared, block01, block20, block21, block22 = (
         packed[index * LANES : (index + 1) * LANES] for index in range(5)
     )
     diag11 = packed[5 * LANES : 5 * LANES + 1]
@@ -88,9 +88,9 @@
     flipped = shared.T
     block00 = jnp.where(rows <= cols, shared, flipped)
     block11 = jnp.where(rows > cols, shared, jnp.where(rows < cols, flipped, diag11))
-    first = jnp.concatenate([block00, block01, block02], axis=1)
-    second = jnp.concatenate([block01.T, block11, block12], axis=1)
-    third = jnp.concatenate([block02.T, block12.T, block22], axis=1)
+    first = jnp.concatenate([block00, block01, block20.T], axis=1)
+    second = jnp.concatenate([block01.T, block11, block21.T], axis=1)
+    third = jnp.concatenate([block20, block21, block22], axis=1)
     return jnp.concatenate([first, second, third], axis=0)
 
 
@@ -410,7 +410,7 @@
             leave.start()
         values = held[start : start + count]
         right = values[:, 2 * LANES :]
-        upper = dot32(values[:, : 2 * LANES], values, ((0,), (0,)))
+        upper = dot32(values, values[:, : 2 * LANES], ((0,), (0,)))
         corner = dot32(right, right, ((0,), (0,)))
         if index == 0:
             upper_ref[...] = upper
@@ -419,11 +419,11 @@
             upper_ref[...] += upper
             corner_ref[...] += corner
     rows_at, cols_at = triangle()
-    block11 = upper_ref[LANES:, LANES : 2 * LANES]
+    block11 = upper_ref[LANES : 2 * LANES, LANES:]
     packed_ref[:LANES] = jnp.where(rows_at <= cols_at, upper_ref[:LANES, :LANES], block11)
-    packed_ref[LANES : 2 * LANES] = upper_ref[:LANES, LANES : 2 * LANES]
-    packed_ref[2 * LANES : 3 * LANES] = upper_ref[:LANES, 2 * LANES :]
-    packed_ref[3 * LANES : 4 * LANES] = upper_ref[LANES:, 2 * LANES :]
+    packed_ref[LANES : 2 * LANES] = upper_ref[:LANES, LANES:]
+    packed_ref[2 * LANES : 3 * LANES] = upper_ref[2 * LANES :, :LANES]
+    packed_ref[3 * LANES : 4 * LANES] = upper_ref[2 * LANES :, LANES:]
     packed_ref[4 * LANES : 5 * LANES] = corner_ref[...]
     diag11 = jnp.sum(jnp.where(rows_at == cols_at, block11, 0.0), axis=0, keepdims=True)
     packed_ref[5 * LANES :] = jnp.broadcast_to(diag11, (SUBS, LANES))
@@ -442,7 +442,7 @@
         ),
         scratch_shapes=[
             pltpu.VMEM((rows, size), jnp.bfloat16),
-            pltpu.VMEM((2 * LANES, size), jnp.float32),
+            pltpu.VMEM((size, 2 * LANES), jnp.float32),
             pltpu.VMEM((LANES, LANES), jnp.float32),
             pltpu.SemaphoreType.DMA((len(gram_spans(rows)),)),
             pltpu.SemaphoreType.DMA,

time: 84.2 us -> 84.4 us (level)
  no operation moved by 1% of the time
where the time goes in v13:
time: 84.4 us; the launch traced here: 84.1 us
  Pallas kernels  32 us (38%)
  starting transfers between devices  28.6 us (34%)
  waiting for transfers between devices  18.7 us (22%)
  between operations  3.27 us (4%)
  other arithmetic  0.89 us (1%)
    ppermute x3, starting transfers between devices, permuted(): return lax.ppermute(value, 'blk', pairs)  18.2 us
    ppermute x7, waiting for transfers between devices, swapped_with(): lax.ppermute(value, axis, [(source, partner(source, count)) for source in...  17 us
    pallas_call x1, Pallas kernels, jacobi(): pl.pallas_call(jacobi_kernel, out_shape=(jax.ShapeDtypeStruct((size + siz...  16.3 us
    ppermute x7, starting transfers between devices, swapped_with(): lax.ppermute(value, axis, [(source, partner(source, count)) for source in...  10.4 us
    pallas_call x3, Pallas kernels, fill_rows(): pl.pallas_call(kernel, grid=(count // tile,), in_specs=in_specs, out_spec...  7.88 us
    pallas_call x1, Pallas kernels, gram_blocks(): pl.pallas_call(gram_kernel, in_specs=[pl.BlockSpec(memory_space=pl.ANY)],...  5.54 us
    pallas_call x1, Pallas kernels, rotate_near(): pl.pallas_call(near_kernel, grid=(rows // WIDE_TILE,), in_specs=[pl.Block...  2.35 us
  transfers between devices with their start and end apart: 10, of which 6 were waited for; matrix products, arithmetic and copies ran while one was open for 2% of the time, Pallas kernels for 29%

profile of v13, /device:TPU:1, one launch (start us, length us, event | category | flops | bytes accessed | tf_op | source)
XLA Modules:
  0.0 84.1 jit_solution(4902346327504230676)
XLA Ops:
  0.6 5.5 %gram_blocks.1 = (f32[648,128]{1,0:T(8,128)}, bf16[1536,384]{1,0:T(8,128)(2,1)}) custom-call(bf16[6144,384]{1,0:T(8,128)(2,1)} %refs_2_.1), custom_call_target="tpu_custom_call" | custom-call | flops 1811939328 | bytes 4718592 | tf_op jit(solution)/shard_map/gram_blocks/pallas_call | solution.py:435
  6.2 0.1 collective-permute-start.2
  6.3 2.7 %collective-permute-start.4 = (bf16[1536,384]{1,0:T(8,128)(2,1)}, bf16[1536,384]{1,0:T(8,128)(2,1)S(1)}, u32[]{:S(2)}, u32[]{:S(2)}) collective-permute-start(bf16[1536,384]{1,0:T(8,128)(2,1)} %get-tuple-element.21), channel_id=1, source_target_pairs={{0,30},{2,4},{4,2},{6,8},{8,6},{10,12},{12,10},{14,16},{16,14},{18... | collective-permute-start | bytes 3538952 | tf_op jit(solution)/shard_map/ppermute | solution.py:572
  8.9 1.2 %collective-permute-start = (f32[648,128]{1,0:T(8,128)}, f32[648,128]{1,0:T(8,128)}, u32[]{:S(2)}, u32[]{:S(2)}) collective-permute-start(f32[648,128]{1,0:T(8,128)} %get-tuple-element.17.refs_0_), channel_id=1, source_target_pairs={{0,1},{1,0},{2,3},{3,2},{4,5},{5,4},{6,7},{7,6},{8,9},{9,8},{10,11... | collective-permute-start | bytes 995336 | tf_op jit(solution)/shard_map/ppermute | solution.py:572
  10.2 5.3 %collective-permute-done.refs_1_ = f32[648,128]{1,0:T(8,128)} collective-permute-done((f32[648,128]{1,0:T(8,128)}, f32[648,128]{1,0:T(8,128)}, u32[]{:S(2)}, u32[]{:S(2)}) %collective-permute-start) | collective-permute-done | bytes 331808 | tf_op jit(solution)/shard_map/ppermute | solution.py:572
  15.4 16.3 %jacobi_turns.1 = (bf16[592,128]{1,0:T(8,128)(2,1)}, bf16[4608,128]{1,0:T(8,128)(2,1)}, bf16[2304,128]{1,0:T(8,128)(2,1)}, bf16[384,384]{1,0:T(8,128)(2,1)}, bf16[16,128]{1,0:T(8,128)(2,1)}) custom-call(s32[32]{0:T(128)} %plan_ref.7, f32[648,128]{1,0:T(8,128)} %get-tuple-element.17.refs_0_, f32[648,128]{1,0:T(8,128)} %collective-permute-done.refs_1_, ...), custom_call_target="tpu_custom_call" | custom-call | flops 384 | bytes 384 | tf_op jit(solution)/shard_map/jacobi_turns/pallas_call | solution.py:350
  31.7 0.0 copy-start.1
  31.7 0.0 copy-start
  31.7 4.5 %collective-permute-start.3 = (bf16[384,384]{1,0:T(8,128)(2,1)}, bf16[384,384]{1,0:T(8,128)(2,1)S(1)}, u32[]{:S(2)}, u32[]{:S(2)}) collective-permute-start(bf16[384,384]{1,0:T(8,128)(2,1)} %get-tuple-element.20), channel_id=1, source_target_pairs={{0,2},{2,0},{4,6},{6,4},{8,10},{10,8},{12,14},{14,12},{16,18},{18,... | collective-permute-start | bytes 884744 | tf_op jit(solution)/shard_map/ppermute | solution.py:572
  36.2 0.2 collective-permute-start.1
  36.4 0.7 convert_element_type.6
  37.0 1.6 %collective-permute-start.6 = (bf16[4608,128]{1,0:T(8,128)(2,1)}, bf16[4608,128]{1,0:T(8,128)(2,1)S(1)}, u32[]{:S(2)}, u32[]{:S(2)}) collective-permute-start(bf16[4608,128]{1,0:T(8,128)(2,1)} %get-tuple-element.24), channel_id=1, source_target_pairs={{0,30},{2,4},{4,2},{6,8},{8,6},{10,12},{12,10},{14,16},{16,14},{18... | collective-permute-start | bytes 3538952 | tf_op jit(solution)/shard_map/ppermute | solution.py:572
  38.6 2.4 %collective-permute-done.1.slow_turn_ref = bf16[592,128]{1,0:T(8,128)(2,1)S(1)} collective-permute-done((bf16[592,128]{1,0:T(8,128)(2,1)}, bf16[592,128]{1,0:T(8,128)(2,1)S(1)}, u32[]{:S(2)}, u32[]{:S(2)}) %collective-permute-start.1) | collective-permute-done | bytes 151584 | tf_op jit(solution)/shard_map/ppermute | solution.py:572
  41.0 0.0 collective-permute-done.3.turn_ref
  41.0 0.0 collective-permute-done.2.near_ref
  41.0 2.4 %rotate_near.1.near_ref = bf16[9216,128]{1,0:T(8,128)(2,1)S(1)} custom-call(bf16[6144,384]{1,0:T(8,128)(2,1)S(1)} %collective-permute-done.2.near_ref, bf16[384,384]{1,0:T(8,128)(2,1)S(1)} %collective-permute-done.3.turn_ref), custom_call_target="tpu_custom_call" | custom-call | flops 384 | bytes 384 | tf_op jit(solution)/shard_map/rotate_near/pallas_call | solution.py:484
  43.4 0.0 collective-permute-done.4.slow_ref
  43.4 0.1 fusion.1
  43.5 2.9 %collective-permute-start.7 = (f32[16,128]{1,0:T(8,128)S(1)}, f32[16,128]{1,0:T(8,128)S(1)}, u32[]{:S(2)}, u32[]{:S(2)}) collective-permute-start(f32[16,128]{1,0:T(8,128)S(1)} %pad_maximum_fusion), channel_id=1, source_target_pairs={{0,2},{2,0},{4,6},{6,4},{8,10},{10,8},{12,14},{14,12},{16,18},{18,... | collective-permute-start | bytes 24584 | tf_op jit(solution)/shard_map/ppermute | solution.py:584
  46.4 0.8 collective-permute-done.7
  47.3 0.1 subtract_subtract_fusion.1
  47.4 12.7 %collective-permute-start.8 = (f32[16,128]{1,0:T(8,128)S(1)}, f32[16,128]{1,0:T(8,128)S(1)}, u32[]{:S(2)}, u32[]{:S(2)}) collective-permute-start(f32[16,128]{1,0:T(8,128)S(1)} %pad_maximum_fusion.1), channel_id=1, source_target_pairs={{0,8},{2,10},{4,12},{6,14},{8,0},{10,2},{12,4},{14,6},{16,24},{18,... | collective-permute-start | bytes 24584 | tf_op jit(solution)/shard_map/ppermute | solution.py:584
  60.1 0.0 copy-done.1
  60.1 0.2 collective-permute-start.5
  60.3 0.8 collective-permute-done.8
  61.1 2.5 %collective-permute-start.9 = (f32[16,128]{1,0:T(8,128)S(1)}, f32[16,128]{1,0:T(8,128)S(1)}, u32[]{:S(2)}, u32[]{:S(2)}) collective-permute-start(f32[16,128]{1,0:T(8,128)S(1)} %pad_maximum_fusion.2), channel_id=1, source_target_pairs={{0,16},{2,18},{4,20},{6,22},{8,24},{10,26},{12,28},{14,30},{16,0},... | collective-permute-start | bytes 24584 | tf_op jit(solution)/shard_map/ppermute | solution.py:584
  63.7 0.0 copy-done
  63.7 3.0 %fill_rows.3.refs_0_ = bf16[6144,384]{1,0:T(8,128)(2,1)} custom-call(s32[32]{0:T(128)S(1)} %copy-done, bf16[9216,128]{1,0:T(8,128)(2,1)S(1)} %rotate_near.1.near_ref, bf16[1536,384]{1,0:T(8,128)(2,1)S(1)} %collective-permute-done.4.slow_ref, bf16[592,128]{1,0:T(8,128)(2,1)S(1)} %collective-permute-done.1.slow_turn_ref), custom_call_target="tpu_custom_call" | custom-call | flops 589824 | bytes 2359296 | tf_op jit(solution)/shard_map/fill_rows/pallas_call | solution.py:555
  66.7 7.5 %collective-permute-done.6.slow_ref = bf16[4608,128]{1,0:T(8,128)(2,1)S(1)} collective-permute-done((bf16[4608,128]{1,0:T(8,128)(2,1)}, bf16[4608,128]{1,0:T(8,128)(2,1)S(1)}, u32[]{:S(2)}, u32[]{:S(2)}) %collective-permute-start.6) | collective-permute-done | bytes 1179680 | tf_op jit(solution)/shard_map/ppermute | solution.py:572
  74.2 2.5 %fill_rows.4.refs_0_ = bf16[6144,384]{1,0:T(8,128)(2,1)} custom-call(s32[32]{0:T(128)S(1)} %copy-done, bf16[9216,128]{1,0:T(8,128)(2,1)S(1)} %rotate_near.1.near_ref, bf16[4608,128]{1,0:T(8,128)(2,1)S(1)} %collective-permute-done.6.slow_ref, bf16[6144,384]{1,0:T(8,128)(2,1)} %fill_rows.3.refs_0_), custom_call_target="tpu_custom_call", output_to_operand_aliasing={{}: (3, {})} | custom-call | flops 1179648 | bytes 4718592 | tf_op jit(solution)/shard_map/fill_rows/pallas_call | solution.py:555
  76.7 0.0 collective-permute-done.9
  76.7 0.6 fusion.17
  78.7 1.8 %collective-permute-done.5.slow_ref = bf16[2304,128]{1,0:T(8,128)(2,1)S(1)} collective-permute-done((bf16[2304,128]{1,0:T(8,128)(2,1)S(1)}, bf16[2304,128]{1,0:T(8,128)(2,1)S(1)}, u32[]{:S(2)}, u32[]{:S(2)}) %collective-permute-start.5) | collective-permute-done | bytes 589856 | tf_op jit(solution)/shard_map/ppermute | solution.py:572
  80.6 2.4 %fill_rows.5 = bf16[6144,384]{1,0:T(8,128)(2,1)} custom-call(s32[32]{0:T(128)S(1)} %copy-done, bf16[9216,128]{1,0:T(8,128)(2,1)S(1)} %rotate_near.1.near_ref, bf16[2304,128]{1,0:T(8,128)(2,1)S(1)} %collective-permute-done.5.slow_ref, bf16[6144,384]{1,0:T(8,128)(2,1)} %fill_rows.4.refs_0_), custom_call_target="tpu_custom_call", output_to_operand_aliasing={{}: (3, {})} | custom-call | flops 589824 | bytes 2359296 | tf_op jit(solution)/shard_map/fill_rows/pallas_call | solution.py:555
  (9 shorter events, 0.1 us)
Async XLA Ops:
  6.2 34.9 %collective-permute-start.2 = (bf16[6144,384]{1,0:T(8,128)(2,1)}, bf16[6144,384]{1,0:T(8,128)(2,1)S(1)}, u32[]{:S(2)}, u32[]{:S(2)}) collective-permute-start(bf16[6144,384]{1,0:T(8,128)(2,1)} %refs_2_.1), channel_id=1, source_target_pairs={{0,2},{2,0},{4,6},{6,4},{8,10},{10,8},{12,14},{14,12},{16,18},{18,... | collective-permute-start | bytes 14155784 | tf_op jit(solution)/shard_map/ppermute | solution.py:572
  6.3 37.1 %collective-permute-start.4 = (bf16[1536,384]{1,0:T(8,128)(2,1)}, bf16[1536,384]{1,0:T(8,128)(2,1)S(1)}, u32[]{:S(2)}, u32[]{:S(2)}) collective-permute-start(bf16[1536,384]{1,0:T(8,128)(2,1)} %get-tuple-element.21), channel_id=1, source_target_pairs={{0,30},{2,4},{4,2},{6,8},{8,6},{10,12},{12,10},{14,16},{16,14},{18... | collective-permute-start | bytes 3538952 | tf_op jit(solution)/shard_map/ppermute | solution.py:572
  8.9 6.5 %collective-permute-start = (f32[648,128]{1,0:T(8,128)}, f32[648,128]{1,0:T(8,128)}, u32[]{:S(2)}, u32[]{:S(2)}) collective-permute-start(f32[648,128]{1,0:T(8,128)} %get-tuple-element.17.refs_0_), channel_id=1, source_target_pairs={{0,1},{1,0},{2,3},{3,2},{4,5},{5,4},{6,7},{7,6},{8,9},{9,8},{10,11... | collective-permute-start | bytes 995336 | tf_op jit(solution)/shard_map/ppermute | solution.py:572
  31.7 28.4 %copy-start.1 = (bf16[2304,128]{1,0:T(8,128)(2,1)S(1)}, bf16[2304,128]{1,0:T(8,128)(2,1)}, u32[]{:S(2)}) copy-start(bf16[2304,128]{1,0:T(8,128)(2,1)} %get-tuple-element.23) | copy-start | bytes 1769476
  31.7 32.0 %copy-start = (s32[32]{0:T(128)S(1)}, s32[32]{0:T(128)}, u32[]{:S(2)}) copy-start(s32[32]{0:T(128)} %plan_ref.7) | copy-start | bytes 388
  31.7 9.3 %collective-permute-start.3 = (bf16[384,384]{1,0:T(8,128)(2,1)}, bf16[384,384]{1,0:T(8,128)(2,1)S(1)}, u32[]{:S(2)}, u32[]{:S(2)}) collective-permute-start(bf16[384,384]{1,0:T(8,128)(2,1)} %get-tuple-element.20), channel_id=1, source_target_pairs={{0,2},{2,0},{4,6},{6,4},{8,10},{10,8},{12,14},{14,12},{16,18},{18,... | collective-permute-start | bytes 884744 | tf_op jit(solution)/shard_map/ppermute | solution.py:572
  36.2 4.8 %collective-permute-start.1 = (bf16[592,128]{1,0:T(8,128)(2,1)}, bf16[592,128]{1,0:T(8,128)(2,1)S(1)}, u32[]{:S(2)}, u32[]{:S(2)}) collective-permute-start(bf16[592,128]{1,0:T(8,128)(2,1)} %get-tuple-element.18), channel_id=1, source_target_pairs={{0,30},{2,4},{4,2},{6,8},{8,6},{10,12},{12,10},{14,16},{16,14},{18... | collective-permute-start | bytes 454664 | tf_op jit(solution)/shard_map/ppermute | solution.py:572
  37.0 37.2 %collective-permute-start.6 = (bf16[4608,128]{1,0:T(8,128)(2,1)}, bf16[4608,128]{1,0:T(8,128)(2,1)S(1)}, u32[]{:S(2)}, u32[]{:S(2)}) collective-permute-start(bf16[4608,128]{1,0:T(8,128)(2,1)} %get-tuple-element.24), channel_id=1, source_target_pairs={{0,30},{2,4},{4,2},{6,8},{8,6},{10,12},{12,10},{14,16},{16,14},{18... | collective-permute-start | bytes 3538952 | tf_op jit(solution)/shard_map/ppermute | solution.py:572
  43.5 3.7 %collective-permute-start.7 = (f32[16,128]{1,0:T(8,128)S(1)}, f32[16,128]{1,0:T(8,128)S(1)}, u32[]{:S(2)}, u32[]{:S(2)}) collective-permute-start(f32[16,128]{1,0:T(8,128)S(1)} %pad_maximum_fusion), channel_id=1, source_target_pairs={{0,2},{2,0},{4,6},{6,4},{8,10},{10,8},{12,14},{14,12},{16,18},{18,... | collective-permute-start | bytes 24584 | tf_op jit(solution)/shard_map/ppermute | solution.py:584
  47.4 13.8 %collective-permute-start.8 = (f32[16,128]{1,0:T(8,128)S(1)}, f32[16,128]{1,0:T(8,128)S(1)}, u32[]{:S(2)}, u32[]{:S(2)}) collective-permute-start(f32[16,128]{1,0:T(8,128)S(1)} %pad_maximum_fusion.1), channel_id=1, source_target_pairs={{0,8},{2,10},{4,12},{6,14},{8,0},{10,2},{12,4},{14,6},{16,24},{18,... | collective-permute-start | bytes 24584 | tf_op jit(solution)/shard_map/ppermute | solution.py:584
  60.1 20.5 %collective-permute-start.5 = (bf16[2304,128]{1,0:T(8,128)(2,1)S(1)}, bf16[2304,128]{1,0:T(8,128)(2,1)S(1)}, u32[]{:S(2)}, u32[]{:S(2)}) collective-permute-start(bf16[2304,128]{1,0:T(8,128)(2,1)S(1)} %copy-done.1), channel_id=1, source_target_pairs={{0,30},{2,4},{4,2},{6,8},{8,6},{10,12},{12,10},{14,16},{16,14},{18... | collective-permute-start | bytes 1769480 | tf_op jit(solution)/shard_map/ppermute | solution.py:572
  61.1 15.6 %collective-permute-start.9 = (f32[16,128]{1,0:T(8,128)S(1)}, f32[16,128]{1,0:T(8,128)S(1)}, u32[]{:S(2)}, u32[]{:S(2)}) collective-permute-start(f32[16,128]{1,0:T(8,128)S(1)} %pad_maximum_fusion.2), channel_id=1, source_target_pairs={{0,16},{2,18},{4,20},{6,22},{8,24},{10,26},{12,28},{14,30},{16,0},... | collective-permute-start | bytes 24584 | tf_op jit(solution)/shard_map/ppermute | solution.py:584
